TPU v7x, 32 devices: a whole 2x2x4 slice. The times are simulated.
32 devices in a mesh: dp: 4 (over z), context: 2 (over x), tensor: 4 (over y, core).
Axes of the slice: x: 2, y: 2, z: 4, core: 2. Of those that a mesh axis runs over, the one named last changes fastest.
Arguments:
- tokens: bfloat16 [2048, 2304], P(('dp', 'context')), may hold values from -6 to 6
- segments: int32 [2048], P(('dp', 'context')), may hold values from 0 to 3, as said below
- w_query: bfloat16 [2304, 2048], P('dp', 'tensor'), as said below
- key_weight: bfloat16 [2304, 1024], P('dp', 'tensor'), may hold values from -0.125 to 0.125
- value_weight: bfloat16 [2304, 1024], P('dp', 'tensor'), may hold values from -0.125 to 0.125
- w_output: bfloat16 [2048, 2304], P('tensor', 'dp'), may hold values from -0.125 to 0.125
- w_gate: bfloat16 [2304, 9216], P('dp', 'tensor'), may hold values from -0.125 to 0.125
- w_up: bfloat16 [2304, 9216], P('dp', 'tensor'), may hold values from -0.125 to 0.125
- w_down: bfloat16 [9216, 2304], P('tensor', 'dp'), may hold values from -0.0625 to 0.0625
- pre_attn_gain: bfloat16 [2304], P('dp'), may hold values from -0.5 to 0.5
- post_attn_gain: bfloat16 [2304], P('dp'), may hold values from -0.5 to 0.5
- pre_ffw_gain: bfloat16 [2304], P('dp'), may hold values from -0.5 to 0.5
- post_ffw_gain: bfloat16 [2304], P('dp'), may hold values from -0.5 to 0.5
- cotangent: bfloat16 [2048, 2304], P(('dp', 'context')), may hold values from -6 to 6
Outputs:
- output: bfloat16 [2048, 2304], P(('dp', 'context'))
- tokens_grad: float32 [2048, 2304], P(('dp', 'context'))
- w_query_grad: float32 [2304, 2048], P(('dp', 'context'), 'tensor')
- w_key_grad: float32 [2304, 1024], P(('dp', 'context'), 'tensor')
- w_value_grad: float32 [2304, 1024], P(('dp', 'context'), 'tensor')
- w_output_grad: float32 [2048, 2304], P('tensor', ('dp', 'context'))
- w_gate_grad: float32 [2304, 9216], P(('dp', 'context'), 'tensor')
- w_up_grad: float32 [2304, 9216], P(('dp', 'context'), 'tensor')
- w_down_grad: float32 [9216, 2304], P('tensor', ('dp', 'context'))
- pre_attn_gain_grad: float32 [2304], P(('dp', 'context'))
- post_attn_gain_grad: float32 [2304], P(('dp', 'context'))
- pre_ffw_gain_grad: float32 [2304], P(('dp', 'context'))
- post_ffw_gain_grad: float32 [2304], P(('dp', 'context'))
Inputs may be any that keep to these rules, and one draw needn't show every extreme that they name: `segments`: segment numbers never fall along the packed sequence; each of the 4 documents is a run of one token or more. `w_query`: every entry lies within -48 / sqrt(2304) and 48 / sqrt(2304).
All inputs are finite; a program needn't handle non-finite values.
Results may differ from a plain program's by a relative error of at most 0.017.
The roundings to bfloat16 on the way count: a program that leaves them out, or rounds other values in their place, can miss the bound.
Values may be sent and summed in bfloat16 or wider, within the bound.
No kernel may reach another device: no remote copies, remote signals or barrier semaphores. Data moves between devices by JAX's collectives and lax.ppermute only.
A program may use at most 256 MiB of HBM per device.

v0:
```python
import jax
import jax.numpy as jnp
from jax import lax
from jax.sharding import PartitionSpec as P

HEAD_SIZE = 256
SLIDE_WINDOW = 4096


eps = 1e-06
softcap = 50.0
negative = -1e30


def passed_along(value, axis, steps):
    count = lax.axis_size(axis)
    initial, last = (max(0, -steps), min(count, count - steps))
    return lax.ppermute(value, axis, [(source, source + steps) for source in range(initial, last)])


def rms_scale(value_rows):
    return lax.rsqrt(jnp.mean(value_rows * value_rows, axis=-1, keepdims=True) + eps)


def rms_back(grad, normed, scale):
    return scale * (grad - normed * jnp.mean(grad * normed, axis=-1, keepdims=True))


def rotary_tables(positions):
    inverse = 1.0 / 10000.0 ** (jnp.arange(0, HEAD_SIZE, 2, dtype=jnp.float32) / HEAD_SIZE)
    angles = positions.astype(jnp.float32)[:, None] * inverse[None, :]
    return (jnp.cos(angles), jnp.sin(angles))


def apply_rotary(value_rows, cosine_table, sine_table):
    half = value_rows.shape[-1] // 2
    first = value_rows[..., :half]
    second = value_rows[..., half:]
    cos_part = cosine_table[:, None, :]
    sin_part = sine_table[:, None, :]
    return jnp.concatenate(
        [first * cos_part - second * sin_part, second * cos_part + first * sin_part], axis=-1
    )


def rotate_back(grads, cosine_table, sine_table):
    half = grads.shape[-1] // 2
    first = grads[..., :half]
    second = grads[..., half:]
    cos_part = cosine_table[:, None, :]
    sin_part = sine_table[:, None, :]
    return jnp.concatenate(
        [first * cos_part + second * sin_part, second * cos_part - first * sin_part], axis=-1
    )


def gated(gate_value, up_value):
    return jax.nn.gelu(gate_value, approximate=True) * up_value


def on_device(
    tokens,
    segments,
    w_query,
    key_weight,
    value_weight,
    w_output,
    w_gate,
    w_up,
    w_down,
    pre_attn_gain,
    post_attn_gain,
    pre_ffw_gain,
    post_ffw_gain,
    cotangent,
):
    rows = tokens.shape[0]
    blocks_total = lax.axis_size(("dp", "context"))
    reach = min((SLIDE_WINDOW + rows - 2) // rows, blocks_total - 1)
    span = (reach + 1) * rows
    block_index = lax.axis_index(("dp", "context"))
    positions = block_index * rows + jnp.arange(rows, dtype=jnp.int32)
    f32 = jnp.float32
    b16 = jnp.bfloat16
    gate_part, up_part, down_part = (w_gate, w_up, w_down)
    gathered = (
        lax.all_gather(w_query, "dp", axis=0, tiled=True),
        lax.all_gather(key_weight, "dp", axis=0, tiled=True),
        lax.all_gather(value_weight, "dp", axis=0, tiled=True),
        lax.all_gather(w_output, "dp", axis=1, tiled=True),
        lax.all_gather(gate_part, "dp", axis=0, tiled=True),
        lax.all_gather(up_part, "dp", axis=0, tiled=True),
        lax.all_gather(down_part, "dp", axis=1, tiled=True),
        lax.all_gather(pre_attn_gain, "dp", axis=0, tiled=True),
        lax.all_gather(post_attn_gain, "dp", axis=0, tiled=True),
        lax.all_gather(pre_ffw_gain, "dp", axis=0, tiled=True),
        lax.all_gather(post_ffw_gain, "dp", axis=0, tiled=True),
    )
    (
        full_query,
        full_key,
        full_value,
        full_output,
        full_gate,
        full_up,
        full_down,
        gain_one,
        gain_two,
        gain_three,
        gain_four,
    ) = gathered
    key_heads = full_key.shape[1] // HEAD_SIZE
    query_heads = full_query.shape[1] // HEAD_SIZE
    each_key_head = query_heads // key_heads
    inputs = tokens.astype(f32)
    scale_one = rms_scale(inputs)
    normed_one = inputs * scale_one
    factor_one = 1.0 + gain_one.astype(f32)
    lifted_one = (normed_one * factor_one).astype(b16)
    query_pre = jnp.dot(lifted_one, full_query, preferred_element_type=f32)
    key_unrotated = jnp.dot(lifted_one, full_key, preferred_element_type=f32)
    value_pre = jnp.dot(lifted_one, full_value, preferred_element_type=f32)
    cosine_table, sine_table = rotary_tables(positions)
    query_rows = (
        apply_rotary(query_pre.reshape(rows, query_heads, HEAD_SIZE), cosine_table, sine_table)
        * HEAD_SIZE ** (-0.5)
    ).astype(b16)
    query_rows = query_rows.reshape(rows, key_heads, each_key_head, HEAD_SIZE)
    key_rows = apply_rotary(
        key_unrotated.reshape(rows, key_heads, HEAD_SIZE), cosine_table, sine_table
    ).astype(b16)
    value_rows = value_pre.astype(b16).reshape(rows, key_heads, HEAD_SIZE)
    key_list = [key_rows]
    value_list = [value_rows]
    segment_list = [segments]
    for offset in range(1, reach + 1):
        moved = passed_along((key_rows, value_rows, segments), ("dp", "context"), offset)
        key_list = [moved[0]] + key_list
        value_list = [moved[1]] + value_list
        segment_list = [moved[2]] + segment_list
    all_keys = jnp.concatenate(key_list, axis=0)
    all_values = jnp.concatenate(value_list, axis=0)
    all_segments = jnp.concatenate(segment_list, axis=0)
    key_positions = block_index * rows - reach * rows + jnp.arange(span, dtype=jnp.int32)
    valid = (key_positions[None, :] <= positions[:, None]) & (
        positions[:, None] - key_positions[None, :] < SLIDE_WINDOW
    )
    valid = valid & (key_positions[None, :] >= 0) & (all_segments[None, :] == segments[:, None])

    def scores(query_values):
        raw = jnp.einsum("qkgd,skd->kgqs", query_values, all_keys, preferred_element_type=f32)
        bent = jnp.tanh(raw / softcap)
        return (jnp.where(valid, softcap * bent, negative), bent)

    masked, bent = scores(query_rows)
    highest = jnp.max(masked, axis=-1, keepdims=True)
    log_total = highest + jnp.log(jnp.sum(jnp.exp(masked - highest), axis=-1, keepdims=True))
    probs_low = jnp.exp(masked - log_total).astype(b16)
    mixed = jnp.einsum("kgqs,skd->qkgd", probs_low, all_values, preferred_element_type=f32)
    mixed = mixed.astype(b16).reshape(rows, query_heads * HEAD_SIZE)
    branch = lax.psum(jnp.dot(mixed, full_output, preferred_element_type=f32), "tensor")
    scale_two = rms_scale(branch)
    normed_two = branch * scale_two
    factor_two = 1.0 + gain_two.astype(f32)
    middle = inputs + normed_two * factor_two
    scale_three = rms_scale(middle)
    normed_three = middle * scale_three
    factor_three = 1.0 + gain_three.astype(f32)
    lifted_two = (normed_three * factor_three).astype(b16)
    feed_rows, feed_cotangent = (lifted_two, cotangent)
    gate = jnp.dot(feed_rows, full_gate, preferred_element_type=f32)
    upper = jnp.dot(feed_rows, full_up, preferred_element_type=f32)
    hidden = gated(gate, upper).astype(b16)
    partial_down = jnp.dot(hidden, full_down, preferred_element_type=f32)
    down = lax.psum(partial_down, "tensor")
    scale_four = rms_scale(down)
    normed_four = down * scale_four
    factor_four = 1.0 + gain_four.astype(f32)
    output = (middle + normed_four * factor_four).astype(b16)
    grad_out = cotangent.astype(f32)
    grad_gain_four = jnp.sum(grad_out * normed_four, axis=0)
    grad_down = rms_back(feed_cotangent.astype(f32) * factor_four, normed_four, scale_four).astype(
        b16
    )
    grad_hidden = jnp.einsum("td,fd->tf", grad_down, full_down, preferred_element_type=f32)
    unused, pull = jax.vjp(gated, gate, upper)
    grad_gate, grad_upper = pull(grad_hidden)
    grad_gate = grad_gate.astype(b16)
    grad_upper = grad_upper.astype(b16)
    grad_w_gate = jnp.einsum("td,tf->df", feed_rows, grad_gate, preferred_element_type=f32)
    grad_w_up = jnp.einsum("td,tf->df", feed_rows, grad_upper, preferred_element_type=f32)
    lifted_grad = jnp.einsum("tf,df->td", grad_gate, full_gate, preferred_element_type=f32)
    lifted_grad = lifted_grad + jnp.einsum(
        "tf,df->td", grad_upper, full_up, preferred_element_type=f32
    )
    lifted_grad = lax.psum(lifted_grad, "tensor")
    grad_w_down = jnp.einsum("tf,td->fd", hidden, grad_down, preferred_element_type=f32)
    feed_results = (
        lax.psum_scatter(grad_w_gate, ("dp", "context"), scatter_dimension=0, tiled=True),
        lax.psum_scatter(grad_w_up, ("dp", "context"), scatter_dimension=0, tiled=True),
        lax.psum_scatter(grad_w_down, ("dp", "context"), scatter_dimension=1, tiled=True),
    )
    grad_gain_three = jnp.sum(lifted_grad * normed_three, axis=0)
    grad_middle = grad_out + rms_back(lifted_grad * factor_three, normed_three, scale_three)
    grad_gain_two = jnp.sum(grad_middle * normed_two, axis=0)
    grad_branch = rms_back(grad_middle * factor_two, normed_two, scale_two).astype(b16)
    grad_w_output = jnp.einsum("th,td->hd", mixed, grad_branch, preferred_element_type=f32)
    grad_mixed = jnp.einsum("td,hd->th", grad_branch, full_output, preferred_element_type=f32)
    grad_mixed = grad_mixed.astype(b16).reshape(rows, key_heads, each_key_head, HEAD_SIZE)
    masked_again, bent_again = scores(query_rows)
    probs = jnp.exp(masked_again - log_total)
    grad_probs = jnp.einsum("qkgd,skd->kgqs", grad_mixed, all_values, preferred_element_type=f32)
    grad_capped = probs * (grad_probs - jnp.sum(probs * grad_probs, axis=-1, keepdims=True))
    grad_raw = (grad_capped * (1.0 - bent_again * bent_again)).astype(b16)
    grad_queries = jnp.einsum("kgqs,skd->qkgd", grad_raw, all_keys, preferred_element_type=f32)
    grad_keys_all = jnp.einsum("kgqs,qkgd->skd", grad_raw, query_rows, preferred_element_type=f32)
    grad_values_all = jnp.einsum(
        "kgqs,qkgd->skd", probs.astype(b16), grad_mixed, preferred_element_type=f32
    )
    grad_keys = grad_keys_all[reach * rows :]
    grad_values = grad_values_all[reach * rows :]
    for offset in range(1, reach + 1):
        lower = (reach - offset) * rows
        returned = passed_along(
            (grad_keys_all[lower : lower + rows], grad_values_all[lower : lower + rows]),
            ("dp", "context"),
            -offset,
        )
        grad_keys = grad_keys + returned[0]
        grad_values = grad_values + returned[1]
    grad_query_pre = rotate_back(
        grad_queries.reshape(rows, query_heads, HEAD_SIZE), cosine_table, sine_table
    ) * HEAD_SIZE ** (-0.5)
    grad_query_pre = grad_query_pre.astype(b16).reshape(rows, query_heads * HEAD_SIZE)
    grad_key_pre = (
        rotate_back(grad_keys, cosine_table, sine_table)
        .astype(b16)
        .reshape(rows, key_heads * HEAD_SIZE)
    )
    grad_value_pre = grad_values.astype(b16).reshape(rows, key_heads * HEAD_SIZE)
    grad_w_query = jnp.einsum("td,th->dh", lifted_one, grad_query_pre, preferred_element_type=f32)
    grad_w_key = jnp.einsum("td,th->dh", lifted_one, grad_key_pre, preferred_element_type=f32)
    grad_w_value = jnp.einsum("td,th->dh", lifted_one, grad_value_pre, preferred_element_type=f32)
    first_grad = jnp.einsum("th,dh->td", grad_query_pre, full_query, preferred_element_type=f32)
    first_grad = first_grad + jnp.einsum(
        "th,dh->td", grad_key_pre, full_key, preferred_element_type=f32
    )
    first_grad = first_grad + jnp.einsum(
        "th,dh->td", grad_value_pre, full_value, preferred_element_type=f32
    )
    first_grad = lax.psum(first_grad, "tensor")
    grad_gain_one = jnp.sum(first_grad * normed_one, axis=0)
    grad_inputs = grad_middle + rms_back(first_grad * factor_one, normed_one, scale_one)
    reduced = (
        lax.psum_scatter(grad_w_query, ("dp", "context"), scatter_dimension=0, tiled=True),
        lax.psum_scatter(grad_w_key, ("dp", "context"), scatter_dimension=0, tiled=True),
        lax.psum_scatter(grad_w_value, ("dp", "context"), scatter_dimension=0, tiled=True),
        lax.psum_scatter(grad_w_output, ("dp", "context"), scatter_dimension=1, tiled=True),
        lax.psum_scatter(grad_gain_one, ("dp", "context"), scatter_dimension=0, tiled=True),
        lax.psum_scatter(grad_gain_two, ("dp", "context"), scatter_dimension=0, tiled=True),
        lax.psum_scatter(grad_gain_three, ("dp", "context"), scatter_dimension=0, tiled=True),
        lax.psum_scatter(grad_gain_four, ("dp", "context"), scatter_dimension=0, tiled=True),
    )
    return (
        output,
        grad_inputs,
        reduced[0],
        reduced[1],
        reduced[2],
        reduced[3],
        feed_results[0],
        feed_results[1],
        feed_results[2],
        reduced[4],
        reduced[5],
        reduced[6],
        reduced[7],
    )


def solution(mesh):
    return jax.shard_map(
        on_device,
        mesh=mesh,
        in_specs=(
            P(("dp", "context"), None),
            P(("dp", "context")),
            P("dp", "tensor"),
            P("dp", "tensor"),
            P("dp", "tensor"),
            P("tensor", "dp"),
            P("dp", "tensor"),
            P("dp", "tensor"),
            P("tensor", "dp"),
            P("dp"),
            P("dp"),
            P("dp"),
            P("dp"),
            P(("dp", "context"), None),
        ),
        out_specs=(
            P(("dp", "context"), None),
            P(("dp", "context"), None),
            P(("dp", "context"), "tensor"),
            P(("dp", "context"), "tensor"),
            P(("dp", "context"), "tensor"),
            P("tensor", ("dp", "context")),
            P(("dp", "context"), "tensor"),
            P(("dp", "context"), "tensor"),
            P("tensor", ("dp", "context")),
            P(("dp", "context")),
            P(("dp", "context")),
            P(("dp", "context")),
            P(("dp", "context")),
        ),
        check_vma=False,
    )
```

profile of v0, /device:TPU:0, one launch (start us, length us, event | category | flops | bytes accessed | tf_op | source)
XLA Modules:
  0.0 2560.1 jit_solution(8721327989254465212)
XLA Ops:
  9.5 7.9 collective-permute-start.7
  21.2 2.5 collective-permute-start.11
  29.3 17.2 all-reduce.9
  54.2 2.2 convolution_bitcast_fusion.2
  57.0 4.9 collective-permute-start.14
  61.9 2.1 collective-permute-start.15
  68.3 15.4 all-gather.8.cloned.1.call-done
  85.4 8.5 collective-permute-start.19
  94.0 3.2 collective-permute-start.20
  97.2 3.1 collective-permute-start
  105.0 4.2 collective-permute-start.4
  112.2 5.7 collective-permute-start.6
  119.3 4.1 collective-permute-done.3
  124.1 5.0 collective-permute-done.4
  129.7 4.8 collective-permute-done.5
  136.5 19.2 all-gather.12.cloned.1.call-done
  155.7 2.5 fusion.97
  163.1 2.8 convolution_convert_fusion.1
  166.0 50.1 %all-gather.14.cloned.1.call-done = bf16[512,2304]{0,1:T(8,128)(2,1)} async-done(((bf16[512,576]{0,1:T(8,128)(2,1)}), bf16[512,2304]{0,1:T(8,128)(2,1)}) %all-gather.14.cloned.1.call-update) | async-done | bytes 2359312 | tf_op jit(solution)/shard_map/all_gather | solution.py:90
  216.1 3.9 fusion.104
  223.9 50.7 %all-reduce.15.cloned.1.call-done = f32[256,2304]{1,0:T(8,128)} async-done(((f32[256,2304]{1,0:T(8,128)}), f32[256,2304]{1,0:T(8,128)}) %all-reduce.15.cloned.1.call-update) | async-done | bytes 2359312 | tf_op jit(solution)/shard_map/psum | solution.py:161
  274.6 2.1 multiply_reduce_fusion.6
  280.2 182.0 %all-gather.16.cloned.1.call-done = bf16[2304,2304]{1,0:T(8,128)(2,1)} async-done(((bf16[576,2304]{1,0:T(8,128)(2,1)}), bf16[2304,2304]{1,0:T(8,128)(2,1)}) %all-gather.16.cloned.1.call-update) | async-done | bytes 10616848 | tf_op jit(solution)/shard_map/all_gather | solution.py:91
  462.2 8.7 fusion.105
  470.9 177.1 %all-gather.18.cloned.1.call-done = bf16[2304,2304]{1,0:T(8,128)(2,1)} async-done(((bf16[576,2304]{1,0:T(8,128)(2,1)}), bf16[2304,2304]{1,0:T(8,128)(2,1)}) %all-gather.18.cloned.1.call-update) | async-done | bytes 10616848 | tf_op jit(solution)/shard_map/all_gather | solution.py:92
  648.1 9.8 multiply_convert_fusion.2
  657.9 176.1 %all-gather.20.cloned.1.call-done = bf16[2304,2304]{0,1:T(8,128)(2,1)} async-done(((bf16[2304,576]{0,1:T(8,128)(2,1)}), bf16[2304,2304]{0,1:T(8,128)(2,1)}) %all-gather.20.cloned.1.call-update) | async-done | bytes 10616848 | tf_op jit(solution)/shard_map/all_gather | solution.py:93
  833.9 8.7 fusion.106
  844.2 52.5 %all-reduce.17.cloned.1.call-done = f32[256,2304]{1,0:T(8,128)} async-done(((f32[256,2304]{1,0:T(8,128)}), f32[256,2304]{1,0:T(8,128)}) %all-reduce.17.cloned.1.call-update) | async-done | bytes 2359312 | tf_op jit(solution)/shard_map/psum | solution.py:175
  896.7 2.1 multiply_reduce_fusion.4
  899.1 2.9 fusion.27
  904.0 9.1 multiply_convert_fusion.1
  913.1 2.9 fusion.107
  916.1 8.4 convolution_add_fusion.2
  924.8 55.6 %all-reduce.19.cloned.1.call-done = f32[256,2304]{1,0:T(8,128)} async-done(((f32[256,2304]{1,0:T(8,128)}), f32[256,2304]{1,0:T(8,128)}) %all-reduce.19.cloned.1.call-update) | async-done | bytes 2359312 | tf_op jit(solution)/shard_map/psum | solution.py:196
  980.4 3.1 multiply_reduce_fusion
  983.5 3.7 multiply_reduce_fusion.1
  991.2 5.4 convolution_bitcast_fusion
  996.6 2.8 fusion.1
  999.3 2.0 fusion
  1013.2 2.6 fusion.108
  1017.2 4.6 collective-permute-done.22
  1025.5 31.9 %collective-permute-done.24 = f32[256,1,256]{0,2,1:T(8,128)} collective-permute-done((f32[256,1,256]{0,2,1:T(8,128)}, f32[256,1,256]{0,2,1:T(8,128)}, u32[]{:S(2)}, u32[]{:S(2)}) %collective-permute-start.24) | collective-permute-done | bytes 262176 | tf_op jit(solution)/shard_map/ppermute | solution.py:18
  1070.3 30.6 %collective-permute-done.31 = f32[256,1,256]{0,2,1:T(8,128)S(1)} collective-permute-done((f32[256,1,256]{0,2,1:T(8,128)S(1)}, f32[256,1,256]{0,2,1:T(8,128)S(1)}, u32[]{:S(2)}, u32[]{:S(2)}) %collective-permute-start.31) | collective-permute-done | bytes 262176 | tf_op jit(solution)/shard_map/ppermute | solution.py:18
  1100.9 2.3 collective-permute-done.32
  1103.4 1.9 convolution_add_fusion
  1105.4 2.0 fusion.78
  1107.5 2.1 fusion.92
  1109.7 3.0 fusion.109
  1112.8 3.1 fusion.95
  1117.5 8.8 fusion.112
  1127.9 9.1 fusion.110
  1138.3 8.9 fusion.111
  1149.3 8.4 all-reduce.21.cloned.1.call-done
  1157.7 3.0 fusion.25
  1160.7 39.2 %all-reduce.8 = (f32[2304]{0:T(1024)}, f32[2304]{0:T(1024)}, f32[2304]{0:T(1024)}, f32[2304]{0:T(1024)}) all-reduce(f32[2304]{0:T(1024)} %get-tuple-element.19, f32[2304]{0:T(1024)} %get-tuple-element.15, f32[2304]{0:T(1024)} %get-tuple-element.13, ...), channel_id=9, replica_groups=mesh['dp'=4,'context'=2,'tensor'=4] {'dp','context'}, use_global_device_ids=true, to_apply=%region_23.24.clone | all-reduce | flops 9216 | bytes 73728
  1206.0 3.7 fusion.24
  1209.7 21.2 reduce-scatter.10.cloned.1.call-done
  1230.9 72.1 %reduce-scatter.12.cloned.1.call-done = f32[288,256]{1,0:T(8,128)} async-done(((f32[2304,256]{1,0:T(8,128)}), f32[288,256]{1,0:T(8,128)}) %reduce-scatter.12.cloned.1.call-update) | async-done | bytes 294928 | tf_op jit(solution)/shard_map/reduce_scatter | solution.py:257
  1303.0 98.4 %reduce-scatter.14.cloned.1.call-done = f32[512,288]{0,1:T(8,128)} async-done(((f32[512,2304]{0,1:T(8,128)}), f32[512,288]{0,1:T(8,128)}) %reduce-scatter.14.cloned.1.call-update) | async-done | bytes 589840 | tf_op jit(solution)/shard_map/reduce_scatter | solution.py:258
  1401.4 99.1 %reduce-scatter.8.cloned.1.call-done = f32[288,512]{1,0:T(8,128)} async-done(((f32[2304,512]{1,0:T(8,128)}), f32[288,512]{1,0:T(8,128)}) %reduce-scatter.8.cloned.1.call-update) | async-done | bytes 589840 | tf_op jit(solution)/shard_map/reduce_scatter | solution.py:255
  1500.5 351.4 %reduce-scatter.20.cloned.1.call-done = f32[2304,288]{0,1:T(8,128)} async-done(((f32[2304,2304]{0,1:T(8,128)}), f32[2304,288]{0,1:T(8,128)}) %reduce-scatter.20.cloned.1.call-update) | async-done | bytes 2654224 | tf_op jit(solution)/shard_map/reduce_scatter | solution.py:201
  1851.9 350.7 %reduce-scatter.16.cloned.1.call-done = f32[288,2304]{1,0:T(8,128)} async-done(((f32[2304,2304]{1,0:T(8,128)}), f32[288,2304]{1,0:T(8,128)}) %reduce-scatter.16.cloned.1.call-update) | async-done | bytes 2654224 | tf_op jit(solution)/shard_map/reduce_scatter | solution.py:199
  2202.6 350.2 %reduce-scatter.18.cloned.1.call-done = f32[288,2304]{1,0:T(8,128)} async-done(((f32[2304,2304]{1,0:T(8,128)}), f32[288,2304]{1,0:T(8,128)}) %reduce-scatter.18.cloned.1.call-update) | async-done | bytes 2654224 | tf_op jit(solution)/shard_map/reduce_scatter | solution.py:200
  (301 shorter events, 99.4 us)
Async XLA Ops:
  7.2 40.2 %copy-start.56 = (s32[256]{0:T(256)S(1)}, s32[256]{0:T(256)}, u32[]{:S(2)}) copy-start(s32[256]{0:T(256)} %param.15) | copy-start | bytes 3076
  7.2 39.3 %copy-start = (bf16[256,2304]{1,0:T(8,128)(2,1)S(1)}, bf16[256,2304]{1,0:T(8,128)(2,1)}, u32[]{:S(2)}) copy-start(bf16[256,2304]{1,0:T(8,128)(2,1)} %param.14) | copy-start | bytes 3538948
  7.2 47.0 %all-gather.10.cloned.1.call-start = ((), (), s32[]{:S(2)}) async-start(), calls=%async_computation.8 | async-start | bytes 1474560 | tf_op jit(solution)/shard_map/all_gather | solution.py:88
  7.9 75.7 %all-gather.8.cloned.1.call-start = ((), (), s32[]{:S(2)}) async-start(), calls=%async_computation.7 | async-start | bytes 1474560 | tf_op jit(solution)/shard_map/all_gather | solution.py:89
  8.7 147.0 %all-gather.12.cloned.1.call-start = ((), (), s32[]{:S(2)}) async-start(), calls=%async_computation.9 | async-start | bytes 2949120 | tf_op jit(solution)/shard_map/all_gather | solution.py:87
  9.4 206.7 %all-gather.14.cloned.1.call-start = ((), (), s32[]{:S(2)}) async-start(), calls=%async_computation.10 | async-start | bytes 2949120 | tf_op jit(solution)/shard_map/all_gather | solution.py:90
  9.5 37.9 %collective-permute-start.7 = (s32[256]{0:T(256)}, s32[256]{0:T(256)S(1)}, u32[]{:S(2)}, u32[]{:S(2)}) collective-permute-start(s32[256]{0:T(256)} %param.15), channel_id=1, source_target_pairs={{0,28},{1,29},{2,30},{3,31}} | collective-permute-start | bytes 3080 | tf_op jit(solution)/shard_map/ppermute | solution.py:18
  17.4 31.8 %collective-permute-start.8 = (s32[256]{0:T(256)}, s32[256]{0:T(256)S(1)}, u32[]{:S(2)}, u32[]{:S(2)}) collective-permute-start(s32[256]{0:T(256)} %param.15), channel_id=1, source_target_pairs={{0,24},{4,28},{1,25},{5,29},{2,26},{6,30},{3,27},{7,31}} | collective-permute-start | bytes 3080 | tf_op jit(solution)/shard_map/ppermute | solution.py:18
  18.6 32.5 %collective-permute-start.9 = (s32[256]{0:T(256)}, s32[256]{0:T(256)S(1)}, u32[]{:S(2)}, u32[]{:S(2)}) collective-permute-start(s32[256]{0:T(256)} %param.15), channel_id=1, source_target_pairs={{0,20},{4,24},{8,28},{1,21},{5,25},{9,29},{2,22},{6,26},{10,30},{3... | collective-permute-start | bytes 3080 | tf_op jit(solution)/shard_map/ppermute | solution.py:18
  19.9 31.2 %collective-permute-start.10 = (s32[256]{0:T(256)}, s32[256]{0:T(256)S(1)}, u32[]{:S(2)}, u32[]{:S(2)}) collective-permute-start(s32[256]{0:T(256)} %param.15), channel_id=1, source_target_pairs={{0,16},{4,20},{8,24},{12,28},{1,17},{5,21},{9,25},{13,29},{2,18},{... | collective-permute-start | bytes 3080 | tf_op jit(solution)/shard_map/ppermute | solution.py:18
  21.2 29.9 %collective-permute-start.11 = (s32[256]{0:T(256)}, s32[256]{0:T(256)S(1)}, u32[]{:S(2)}, u32[]{:S(2)}) collective-permute-start(s32[256]{0:T(256)} %param.15), channel_id=1, source_target_pairs={{0,12},{4,16},{8,20},{12,24},{16,28},{1,13},{5,17},{9,21},{13,25},... | collective-permute-start | bytes 3080 | tf_op jit(solution)/shard_map/ppermute | solution.py:18
  23.8 250.9 %all-reduce.15.cloned.1.call-start = ((), (), s32[]{:S(2)}) async-start(), calls=%async_computation.11 | async-start | bytes 4718592 | tf_op jit(solution)/shard_map/psum | solution.py:161
  47.3 111.4 %copy-start.20 = (f32[256,128]{1,0:T(8,128)}, f32[256,128]{1,0:T(8,128)S(1)}, u32[]{:S(2)}) copy-start(f32[256,128]{1,0:T(8,128)S(1)} %get-tuple-element.60) | copy-start | bytes 393220
  47.3 111.4 %copy-start.22 = (f32[256,128]{1,0:T(8,128)}, f32[256,128]{1,0:T(8,128)S(1)}, u32[]{:S(2)}) copy-start(f32[256,128]{1,0:T(8,128)S(1)} %get-tuple-element.61) | copy-start | bytes 393220
  47.4 3.8 collective-permute-start.12
  49.2 3.2 collective-permute-start.13
  54.2 108.2 %copy-start.15 = (pred[256,2048]{0,1:T(8,128)(4,1)}, pred[256,2048]{0,1:T(8,128)(4,1)S(1)}, u32[]{:S(2)}) copy-start(pred[256,2048]{0,1:T(8,128)(4,1)S(1)} %fusion.35) | copy-start | bytes 1572868
  57.0 28.4 %collective-permute-start.14 = (bf16[256,1,256]{0,2,1:T(8,128)(2,1)S(1)}, bf16[256,1,256]{0,2,1:T(8,128)(2,1)S(1)}, u32[]{:S(2)}, u32[]{:S(2)}) collective-permute-start(bf16[256,1,256]{0,2,1:T(8,128)(2,1)S(1)} %pad_maximum_fusion), channel_id=1, source_target_pairs={{0,28},{1,29},{2,30},{3,31}} | collective-permute-start | bytes 393224 | tf_op jit(solution)/shard_map/ppermute | solution.py:18
  61.9 32.1 %collective-permute-start.15 = (bf16[256,1,256]{0,2,1:T(8,128)(2,1)S(1)}, bf16[256,1,256]{0,2,1:T(8,128)(2,1)S(1)}, u32[]{:S(2)}, u32[]{:S(2)}) collective-permute-start(bf16[256,1,256]{0,2,1:T(8,128)(2,1)S(1)} %pad_maximum_fusion), channel_id=1, source_target_pairs={{0,24},{4,28},{1,25},{5,29},{2,26},{6,30},{3,27},{7,31}} | collective-permute-start | bytes 393224 | tf_op jit(solution)/shard_map/ppermute | solution.py:18
  64.0 33.2 %collective-permute-start.16 = (bf16[256,1,256]{0,2,1:T(8,128)(2,1)S(1)}, bf16[256,1,256]{0,2,1:T(8,128)(2,1)S(1)}, u32[]{:S(2)}, u32[]{:S(2)}) collective-permute-start(bf16[256,1,256]{0,2,1:T(8,128)(2,1)S(1)} %pad_maximum_fusion), channel_id=1, source_target_pairs={{0,20},{4,24},{8,28},{1,21},{5,25},{9,29},{2,22},{6,26},{10,30},{3... | collective-permute-start | bytes 393224 | tf_op jit(solution)/shard_map/ppermute | solution.py:18
  65.3 35.1 %collective-permute-start.17 = (bf16[256,1,256]{0,2,1:T(8,128)(2,1)S(1)}, bf16[256,1,256]{0,2,1:T(8,128)(2,1)S(1)}, u32[]{:S(2)}, u32[]{:S(2)}) collective-permute-start(bf16[256,1,256]{0,2,1:T(8,128)(2,1)S(1)} %pad_maximum_fusion), channel_id=1, source_target_pairs={{0,16},{4,20},{8,24},{12,28},{1,17},{5,21},{9,25},{13,29},{2,18},{... | collective-permute-start | bytes 393224 | tf_op jit(solution)/shard_map/ppermute | solution.py:18
  66.6 35.7 %collective-permute-start.18 = (bf16[256,1,256]{0,2,1:T(8,128)(2,1)S(1)}, bf16[256,1,256]{0,2,1:T(8,128)(2,1)S(1)}, u32[]{:S(2)}, u32[]{:S(2)}) collective-permute-start(bf16[256,1,256]{0,2,1:T(8,128)(2,1)S(1)} %pad_maximum_fusion), channel_id=1, source_target_pairs={{0,12},{4,16},{8,20},{12,24},{16,28},{1,13},{5,17},{9,21},{13,25},... | collective-permute-start | bytes 393224 | tf_op jit(solution)/shard_map/ppermute | solution.py:18
  85.4 18.2 collective-permute-start.19
  94.0 11.0 collective-permute-start.20
  97.2 12.0 collective-permute-start
  100.4 11.8 collective-permute-start.1
  102.3 16.4 collective-permute-start.2
  103.6 19.8 collective-permute-start.3
  105.0 24.1 collective-permute-start.4
  109.2 25.3 collective-permute-start.5
  112.2 23.0 collective-permute-start.6
  166.0 54.0 %copy-start.30 = (bf16[256,2,256]{2,0,1:T(8,128)(2,1)}, bf16[256,2,256]{2,0,1:T(8,128)(2,1)S(1)}, u32[]{:S(2)}) copy-start(bf16[256,2,256]{2,0,1:T(8,128)(2,1)S(1)} %convolution_convert_fusion.1) | copy-start | bytes 786436
  220.0 242.2 %all-gather.16.cloned.1.call-start = ((), (), s32[]{:S(2)}) async-start(), calls=%async_computation.12 | async-start | bytes 13271040 | tf_op jit(solution)/shard_map/all_gather | solution.py:91
  220.6 427.5 %all-gather.18.cloned.1.call-start = ((), (), s32[]{:S(2)}) async-start(), calls=%async_computation.13 | async-start | bytes 13271040 | tf_op jit(solution)/shard_map/all_gather | solution.py:92
  221.4 612.6 %all-gather.20.cloned.1.call-start = ((), (), s32[]{:S(2)}) async-start(), calls=%async_computation.14 | async-start | bytes 13271040 | tf_op jit(solution)/shard_map/all_gather | solution.py:93
  222.1 674.6 %all-reduce.17.cloned.1.call-start = ((), (), s32[]{:S(2)}) async-start(), calls=%async_computation.15 | async-start | bytes 4718592 | tf_op jit(solution)/shard_map/psum | solution.py:175
  842.7 137.7 %all-reduce.19.cloned.1.call-start = ((), (), s32[]{:S(2)}) async-start(), calls=%async_computation.16 | async-start | bytes 4718592 | tf_op jit(solution)/shard_map/psum | solution.py:196
  924.5 233.2 %all-reduce.21.cloned.1.call-start = ((), (), s32[]{:S(2)}) async-start(), calls=%async_computation.17 | async-start | bytes 4718592 | tf_op jit(solution)/shard_map/psum | solution.py:251
  1004.8 11.1 collective-permute-start.21
  1006.1 15.7 collective-permute-start.22
  1007.4 16.8 collective-permute-start.23
  1008.7 48.7 %collective-permute-start.24 = (f32[256,1,256]{0,2,1:T(8,128)}, f32[256,1,256]{0,2,1:T(8,128)}, u32[]{:S(2)}, u32[]{:S(2)}) collective-permute-start(f32[256,1,256]{0,2,1:T(8,128)} %get-tuple-element.47), channel_id=1, source_target_pairs={{16,0},{20,4},{24,8},{28,12},{17,1},{21,5},{25,9},{29,13},{18,2},{... | collective-permute-start | bytes 786440 | tf_op jit(solution)/shard_map/ppermute | solution.py:18
  1010.0 49.9 %collective-permute-start.25 = (f32[256,1,256]{0,2,1:T(8,128)}, f32[256,1,256]{0,2,1:T(8,128)}, u32[]{:S(2)}, u32[]{:S(2)}) collective-permute-start(f32[256,1,256]{0,2,1:T(8,128)} %get-tuple-element.46), channel_id=1, source_target_pairs={{20,0},{24,4},{28,8},{21,1},{25,5},{29,9},{22,2},{26,6},{30,10},{2... | collective-permute-start | bytes 786440 | tf_op jit(solution)/shard_map/ppermute | solution.py:18
  1015.9 45.3 %collective-permute-start.26 = (f32[256,1,256]{0,2,1:T(8,128)S(1)}, f32[256,1,256]{0,2,1:T(8,128)S(1)}, u32[]{:S(2)}, u32[]{:S(2)}) collective-permute-start(f32[256,1,256]{0,2,1:T(8,128)S(1)} %copy-done.37), channel_id=1, source_target_pairs={{24,0},{28,4},{25,1},{29,5},{26,2},{30,6},{27,3},{31,7}} | collective-permute-start | bytes 786440 | tf_op jit(solution)/shard_map/ppermute | solution.py:18
  1021.8 43.5 %copy-start.49 = (f32[256]{0:T(256)S(1)}, f32[256]{0:T(256)}, u32[]{:S(2)}) copy-start(f32[256]{0:T(256)} %copy-done.48) | copy-start | bytes 3076
  1021.8 43.5 %copy-start.55 = (f32[128]{0:T(128)S(1)}, f32[128]{0:T(128)}, u32[]{:S(2)}) copy-start(f32[128]{0:T(128)} %copy-done.54) | copy-start | bytes 1540
  1021.8 47.0 %copy-start.25 = (bf16[2304,256]{1,0:T(8,128)(2,1)S(1)}, bf16[2304,256]{1,0:T(8,128)(2,1)}, u32[]{:S(2)}) copy-start(bf16[2304,256]{1,0:T(8,128)(2,1)} %all-gather.10.cloned.1.call-done) | copy-start | bytes 3538948
  1021.8 40.7 %collective-permute-start.27 = (f32[256,1,256]{0,2,1:T(8,128)S(1)}, f32[256,1,256]{0,2,1:T(8,128)S(1)}, u32[]{:S(2)}, u32[]{:S(2)}) collective-permute-start(f32[256,1,256]{0,2,1:T(8,128)S(1)} %copy-done.36), channel_id=1, source_target_pairs={{28,0},{29,1},{30,2},{31,3}} | collective-permute-start | bytes 786440 | tf_op jit(solution)/shard_map/ppermute | solution.py:18
  1024.2 41.7 %collective-permute-start.28 = (f32[256,1,256]{0,2,1:T(8,128)S(1)}, f32[256,1,256]{0,2,1:T(8,128)S(1)}, u32[]{:S(2)}, u32[]{:S(2)}) collective-permute-start(f32[256,1,256]{0,2,1:T(8,128)S(1)} %get-tuple-element.36), channel_id=1, source_target_pairs={{4,0},{8,4},{12,8},{16,12},{20,16},{24,20},{28,24},{5,1},{9,5},{13... | collective-permute-start | bytes 786440 | tf_op jit(solution)/shard_map/ppermute | solution.py:18
  1057.3 9.9 collective-permute-start.29
  1059.9 10.4 collective-permute-start.30
  1061.2 39.7 %collective-permute-start.31 = (f32[256,1,256]{0,2,1:T(8,128)S(1)}, f32[256,1,256]{0,2,1:T(8,128)S(1)}, u32[]{:S(2)}, u32[]{:S(2)}) collective-permute-start(f32[256,1,256]{0,2,1:T(8,128)S(1)} %get-tuple-element.40), channel_id=1, source_target_pairs={{16,0},{20,4},{24,8},{28,12},{17,1},{21,5},{25,9},{29,13},{18,2},{... | collective-permute-start | bytes 786440 | tf_op jit(solution)/shard_map/ppermute | solution.py:18
  1062.5 40.7 %collective-permute-start.32 = (f32[256,1,256]{0,2,1:T(8,128)S(1)}, f32[256,1,256]{0,2,1:T(8,128)S(1)}, u32[]{:S(2)}, u32[]{:S(2)}) collective-permute-start(f32[256,1,256]{0,2,1:T(8,128)S(1)} %get-tuple-element.39), channel_id=1, source_target_pairs={{20,0},{24,4},{28,8},{21,1},{25,5},{29,9},{22,2},{26,6},{30,10},{2... | collective-permute-start | bytes 786440 | tf_op jit(solution)/shard_map/ppermute | solution.py:18
  1065.8 37.3 %collective-permute-start.33 = (f32[256,1,256]{0,2,1:T(8,128)S(1)}, f32[256,1,256]{0,2,1:T(8,128)S(1)}, u32[]{:S(2)}, u32[]{:S(2)}) collective-permute-start(f32[256,1,256]{0,2,1:T(8,128)S(1)} %get-tuple-element.38), channel_id=1, source_target_pairs={{24,0},{28,4},{25,1},{29,5},{26,2},{30,6},{27,3},{31,7}} | collective-permute-start | bytes 786440 | tf_op jit(solution)/shard_map/ppermute | solution.py:18
  1067.2 36.0 %collective-permute-start.34 = (f32[256,1,256]{0,2,1:T(8,128)S(1)}, f32[256,1,256]{0,2,1:T(8,128)S(1)}, u32[]{:S(2)}, u32[]{:S(2)}) collective-permute-start(f32[256,1,256]{0,2,1:T(8,128)S(1)} %get-tuple-element.37), channel_id=1, source_target_pairs={{28,0},{29,1},{30,2},{31,3}} | collective-permute-start | bytes 786440 | tf_op jit(solution)/shard_map/ppermute | solution.py:18
  1069.3 34.0 %copy-start.24 = (bf16[2304,256]{1,0:T(8,128)(2,1)S(1)}, bf16[2304,256]{1,0:T(8,128)(2,1)}, u32[]{:S(2)}) copy-start(bf16[2304,256]{1,0:T(8,128)(2,1)} %all-gather.8.cloned.1.call-done) | copy-start | bytes 3538948
  1105.3 125.5 %reduce-scatter.10.cloned.1.call-start = ((), (), s32[]{:S(2)}) async-start(), calls=%async_computation.19 | async-start | bytes 2654208 | tf_op jit(solution)/shard_map/reduce_scatter | solution.py:256
  1107.5 195.5 %reduce-scatter.12.cloned.1.call-start = ((), (), s32[]{:S(2)}) async-start(), calls=%async_computation.20 | async-start | bytes 2654208 | tf_op jit(solution)/shard_map/reduce_scatter | solution.py:257
  1109.6 291.7 %reduce-scatter.14.cloned.1.call-start = ((), (), s32[]{:S(2)}) async-start(), calls=%async_computation.21 | async-start | bytes 5308416 | tf_op jit(solution)/shard_map/reduce_scatter | solution.py:258
  1112.7 387.8 %reduce-scatter.8.cloned.1.call-start = ((), (), s32[]{:S(2)}) async-start(), calls=%async_computation.18 | async-start | bytes 5308416 | tf_op jit(solution)/shard_map/reduce_scatter | solution.py:255
  1115.9 736.0 %reduce-scatter.20.cloned.1.call-start = ((), (), s32[]{:S(2)}) async-start(), calls=%async_computation.24 | async-start | bytes 23887872 | tf_op jit(solution)/shard_map/reduce_scatter | solution.py:201
  1126.3 1076.3 %reduce-scatter.16.cloned.1.call-start = ((), (), s32[]{:S(2)}) async-start(), calls=%async_computation.22 | async-start | bytes 23887872 | tf_op jit(solution)/shard_map/reduce_scatter | solution.py:199
  1137.0 1415.8 %reduce-scatter.18.cloned.1.call-start = ((), (), s32[]{:S(2)}) async-start(), calls=%async_computation.23 | async-start | bytes 23887872 | tf_op jit(solution)/shard_map/reduce_scatter | solution.py:200
  1147.3 58.7 %copy-start.5 = (f32[256,2304]{1,0:T(8,128)S(1)}, f32[256,2304]{1,0:T(8,128)}, u32[]{:S(2)}) copy-start(f32[256,2304]{1,0:T(8,128)} %copy-done.4) | copy-start | bytes 7077892
  (51 other events, 255.9 us)
Sparse Core Ops, SparseCore 0:
  9.6 34.0 all-gather.9
  45.3 38.2 all-gather.7
  85.2 70.4 all-gather.11
  157.1 58.9 all-gather.13
  220.1 54.4 all-reduce.14
  276.1 186.1 all-gather.15
  463.8 184.2 all-gather.17
  649.6 184.2 all-gather.19
  842.8 53.8 all-reduce.16
  924.7 55.7 all-reduce.18
  1105.5 52.2 all-reduce.20
  1161.6 69.2 reduce-scatter.9
  1235.0 67.9 reduce-scatter.11
  1307.1 94.2 reduce-scatter.13
  1405.5 94.9 reduce-scatter.7
  1504.8 347.0 reduce-scatter.19
  1856.7 345.8 reduce-scatter.15
  2206.9 345.8 reduce-scatter.17
where the time goes:
time: 2570 us; the launch traced here: 2560 us
  waiting for transfers between devices  2220 us (86%)
  matrix products  115 us (4%)
  starting transfers between devices  79.7 us (3%)
  blocking collectives  56.4 us (2%)
  other arithmetic  38.3 us (1%)
  local copies, waits for them, and re-layouts  30.3 us (1%)
    reduce_scatter x1, waiting for transfers between devices, on_device(): lax.psum_scatter(grad_w_down, ('dp', 'context'), scatter_dimension=1, til...  351 us
    reduce_scatter x1, waiting for transfers between devices, on_device(): lax.psum_scatter(grad_w_gate, ('dp', 'context'), scatter_dimension=0, til...  351 us
    reduce_scatter x1, waiting for transfers between devices, on_device(): lax.psum_scatter(grad_w_up, ('dp', 'context'), scatter_dimension=0, tiled...  350 us
    all_gather x1, waiting for transfers between devices, on_device(): lax.all_gather(gate_part, 'dp', axis=0, tiled=True)  182 us
    all_gather x1, waiting for transfers between devices, on_device(): lax.all_gather(up_part, 'dp', axis=0, tiled=True)  177 us
    all_gather x1, waiting for transfers between devices, on_device(): lax.all_gather(down_part, 'dp', axis=1, tiled=True)  176 us
    reduce_scatter x1, waiting for transfers between devices, on_device(): lax.psum_scatter(grad_w_query, ('dp', 'context'), scatter_dimension=0, ti...  99.1 us
    reduce_scatter x1, waiting for transfers between devices, on_device(): lax.psum_scatter(grad_w_output, ('dp', 'context'), scatter_dimension=1, t...  98.4 us
  transfers between devices with their start and end apart: 53, of which 30 were waited for; matrix products, arithmetic and copies ran while one was open for 4% of the time, Pallas kernels for 0%

commit v1 on v0

v1 whole, which is shorter than its diff:
```python
import jax
import jax.numpy as jnp
from jax import lax
from jax.sharding import PartitionSpec as P

HEAD_SIZE = 256
SLIDE_WINDOW = 4096


eps = 1e-06
softcap = 50.0
negative = -1e30
f32 = jnp.float32
b16 = jnp.bfloat16


def rms_scale(value_rows):
    return lax.rsqrt(jnp.mean(value_rows * value_rows, axis=-1, keepdims=True) + eps)


def rms_back(grad, normed, scale):
    return scale * (grad - normed * jnp.mean(grad * normed, axis=-1, keepdims=True))


def rotary_tables(positions):
    inverse = 1.0 / 10000.0 ** (jnp.arange(0, HEAD_SIZE, 2, dtype=f32) / HEAD_SIZE)
    angles = positions.astype(f32)[:, None] * inverse[None, :]
    return (jnp.cos(angles), jnp.sin(angles))


def apply_rotary(value_rows, cosine_table, sine_table):
    half = value_rows.shape[-1] // 2
    first, second = value_rows[:, :half], value_rows[:, half:]
    return jnp.concatenate(
        [first * cosine_table - second * sine_table, second * cosine_table + first * sine_table],
        axis=-1,
    )


def rotate_back(grads, cosine_table, sine_table):
    return apply_rotary(grads, cosine_table, -sine_table)


def gated(gate_value, up_value):
    return jax.nn.gelu(gate_value, approximate=True) * up_value


def exchange(blocks, axis):
    return lax.all_to_all(blocks, axis, 0, 0, tiled=True)


def gathered(block, axis):
    count = lax.axis_size(axis)
    return exchange(jnp.broadcast_to(block[None], (count,) + block.shape), axis)


def swapped(value, axis, bit):
    count = lax.axis_size(axis)
    return lax.ppermute(value, axis, [(place, place ^ bit) for place in range(count)])


def shifted(value, axis, steps):
    count = lax.axis_size(axis)
    return lax.ppermute(
        value, axis, [(s, s + steps) for s in range(count) if 0 <= s + steps < count]
    )


def summed(blocks):
    return jnp.sum(blocks.astype(f32), axis=0)


def dot(left, right):
    return jnp.dot(left, right, preferred_element_type=f32)


def dot_nt(left, right):
    return lax.dot_general(left, right, (((1,), (1,)), ((), ())), preferred_element_type=f32)


def dot_tn(left, right):
    return lax.dot_general(left, right, (((0,), (0,)), ((), ())), preferred_element_type=f32)


def spread_rows(block):
    stacked = gathered(block, "dp")[None]
    stacked = jnp.concatenate([stacked, swapped(stacked, "tensor", 2)], axis=0)
    stacked = stacked[:, None]
    other = swapped(stacked, "tensor", 1)
    stacked = jnp.concatenate([stacked, other], axis=1)
    return stacked.reshape((-1,) + block.shape[1:])


def collect_rows(partial, sub):
    n = lax.axis_size("dp")
    width = partial.shape[-1]
    stacked = partial.reshape(2, 2, n, sub, width)
    stacked = stacked[:, 0] + swapped(stacked[:, 1].astype(b16), "tensor", 1).astype(f32)
    stacked = stacked[0] + swapped(stacked[1].astype(b16), "tensor", 2).astype(f32)
    return summed(exchange(stacked.astype(b16), "dp"))


def on_device(
    tokens,
    segments,
    w_query,
    key_weight,
    value_weight,
    w_output,
    w_gate,
    w_up,
    w_down,
    pre_attn_gain,
    post_attn_gain,
    pre_ffw_gain,
    post_ffw_gain,
    cotangent,
):
    n = lax.axis_size("dp")
    place = lax.axis_index("dp")
    side = lax.axis_index("context")
    lane = lax.axis_index("tensor")
    lanes = lax.axis_size("tensor")
    rows, width = tokens.shape
    group = 2 * rows
    sub = rows // lanes
    deep = width // n
    reach = min((SLIDE_WINDOW + group - 2) // group, n - 1)
    is_first = side == 0

    def ordered(own, other, axis):
        return jnp.concatenate(
            [jnp.where(is_first, own, other), jnp.where(is_first, other, own)], axis=axis
        )

    def half_of(value, which, axis):
        size = value.shape[axis] // 2
        low = lax.slice_in_dim(value, 0, size, axis=axis)
        high = lax.slice_in_dim(value, size, 2 * size, axis=axis)
        return jnp.where(which == 0, low, high)

    head_cols = jnp.concatenate(
        [half_of(w_query, side, 1), jnp.where(is_first, key_weight, value_weight)], axis=1
    )
    attn_in = gathered(head_cols, "dp").reshape(width, 2 * HEAD_SIZE)
    gains = gathered(
        jnp.stack([pre_attn_gain, post_attn_gain, pre_ffw_gain, post_ffw_gain]), "dp"
    )
    gains = 1.0 + jnp.swapaxes(gains, 0, 1).reshape(4, width).astype(f32)
    all_segments = gathered(segments, ("dp", "context")).reshape(-1)
    tokens_other = swapped(tokens, "context", 1)
    group_tokens = ordered(tokens, tokens_other, 0).astype(f32)
    w_out = jnp.swapaxes(gathered(half_of(w_output, side, 0), "dp"), 0, 1).reshape(
        HEAD_SIZE, width
    )

    units = w_gate.shape[1] // n

    def own_units(weight):
        blocks = jnp.swapaxes(half_of(weight.reshape(deep, n, units), side, 2), 0, 1)
        mine = exchange(blocks, "dp").reshape(width, units // 2)
        return ordered(mine, swapped(mine, "context", 1), 1)

    gate_w = own_units(w_gate)
    up_w = own_units(w_up)
    blocks = half_of(w_down.reshape(n, units, deep), side, 1)
    mine = jnp.swapaxes(exchange(blocks, "dp"), 0, 1).reshape(units // 2, width)
    down_w = ordered(mine, swapped(mine, "context", 1), 0)

    scale_one = rms_scale(group_tokens)
    normed_one = group_tokens * scale_one
    lifted_one = (normed_one * gains[0]).astype(b16)
    projected = dot(lifted_one, attn_in)
    positions = place * group + jnp.arange(group, dtype=jnp.int32)
    cosine_table, sine_table = rotary_tables(positions)
    queries = (
        apply_rotary(projected[:, :HEAD_SIZE], cosine_table, sine_table) * HEAD_SIZE ** (-0.5)
    ).astype(b16)
    mine = projected[:, HEAD_SIZE:]
    mine = jnp.where(is_first, apply_rotary(mine, cosine_table, sine_table), mine).astype(b16)
    mine = [mine] + [shifted(mine, "dp", steps) for steps in range(1, reach + 1)]
    theirs = [swapped(block, "context", 1) for block in mine]
    mine = jnp.concatenate(mine[::-1], axis=0)
    theirs = jnp.concatenate(theirs[::-1], axis=0)
    keys = jnp.where(is_first, mine, theirs)
    values = jnp.where(is_first, theirs, mine)
    span = (reach + 1) * group
    key_positions = (place - reach) * group + jnp.arange(span, dtype=jnp.int32)
    padded = jnp.concatenate([jnp.full((reach * group,), -1, jnp.int32), all_segments])
    key_segments = lax.dynamic_slice_in_dim(padded, place * group, span)
    query_segments = key_segments[reach * group :]
    valid = (key_positions[None, :] <= positions[:, None]) & (
        positions[:, None] - key_positions[None, :] < SLIDE_WINDOW
    )
    valid = valid & (key_positions[None, :] >= 0)
    valid = valid & (key_segments[None, :] == query_segments[:, None])
    bent = jnp.tanh(dot_nt(queries, keys) / softcap)
    masked = jnp.where(valid, softcap * bent, negative)
    weights = jnp.exp(masked - jnp.max(masked, axis=-1, keepdims=True))
    probs = weights / jnp.sum(weights, axis=-1, keepdims=True)
    probs_low = probs.astype(b16)
    mixed = dot(probs_low, values).astype(b16)
    branch = dot(mixed, w_out).astype(b16)
    branch = summed(exchange(branch.reshape(2 * lanes, sub, width), ("context", "tensor")))

    own_tokens = lax.dynamic_slice_in_dim(tokens, lane * sub, sub).astype(f32)
    grad_out = lax.dynamic_slice_in_dim(cotangent, lane * sub, sub).astype(f32)
    scale_two = rms_scale(branch)
    normed_two = branch * scale_two
    middle = own_tokens + normed_two * gains[1]
    scale_three = rms_scale(middle)
    normed_three = middle * scale_three
    lifted_two = spread_rows((normed_three * gains[2]).astype(b16))
    gate = dot(lifted_two, gate_w)
    upper = dot(lifted_two, up_w)
    hidden = gated(gate, upper).astype(b16)
    down = collect_rows(dot(hidden, down_w), sub)
    scale_four = rms_scale(down)
    normed_four = down * scale_four
    output = (middle + normed_four * gains[3]).astype(b16)
    output = gathered(output, "tensor").reshape(rows, width)

    grad_gain_four = jnp.sum(grad_out * normed_four, axis=0)
    grad_down = spread_rows(rms_back(grad_out * gains[3], normed_four, scale_four).astype(b16))
    grad_hidden = dot_nt(grad_down, down_w)
    unused, pull = jax.vjp(gated, gate, upper)
    grad_gate, grad_upper = pull(grad_hidden)
    grad_gate = grad_gate.astype(b16)
    grad_upper = grad_upper.astype(b16)
    lifted_grad = collect_rows(dot_nt(grad_gate, gate_w) + dot_nt(grad_upper, up_w), sub)

    def weight_grad(left, right):
        partial = dot_tn(left, right).reshape(n, 2, deep // 2, units)
        kept = jnp.where(is_first, partial[:, 0], partial[:, 1])
        sent = jnp.where(is_first, partial[:, 1], partial[:, 0])
        total = kept + swapped(sent.astype(b16), "context", 1).astype(f32)
        return exchange(total.astype(b16), "dp")

    grad_w_down = weight_grad(grad_down, hidden)
    grad_w_gate = weight_grad(lifted_two, grad_gate)
    grad_w_up = weight_grad(lifted_two, grad_upper)
    grad_w_down = jnp.swapaxes(grad_w_down, 1, 2).reshape(n * units, deep // 2).astype(f32)
    grad_w_gate = jnp.swapaxes(grad_w_gate, 0, 1).reshape(deep // 2, n * units).astype(f32)
    grad_w_up = jnp.swapaxes(grad_w_up, 0, 1).reshape(deep // 2, n * units).astype(f32)

    grad_gain_three = jnp.sum(lifted_grad * normed_three, axis=0)
    grad_middle = grad_out + rms_back(lifted_grad * gains[2], normed_three, scale_three)
    grad_gain_two = jnp.sum(grad_middle * normed_two, axis=0)
    grad_branch = rms_back(grad_middle * gains[1], normed_two, scale_two).astype(b16)
    grad_branch = gathered(grad_branch, ("context", "tensor")).reshape(group, width)

    grad_w_out = dot_tn(mixed, grad_branch)
    grad_mixed = dot_nt(grad_branch, w_out).astype(b16)
    grad_probs = dot_nt(grad_mixed, values)
    grad_capped = probs * (grad_probs - jnp.sum(probs * grad_probs, axis=-1, keepdims=True))
    grad_raw = (grad_capped * (1.0 - bent * bent)).astype(b16)
    grad_queries = dot(grad_raw, keys)
    grad_keys = dot_tn(grad_raw, queries)
    grad_values = dot_tn(probs_low, grad_mixed)
    kept = jnp.where(is_first, grad_keys, grad_values)
    sent = jnp.where(is_first, grad_values, grad_keys).astype(b16)
    kept = kept + swapped(sent, "context", 1).astype(f32)
    kept = kept.reshape(reach + 1, group, HEAD_SIZE)
    mine = kept[reach]
    for steps in range(1, reach + 1):
        mine = mine + shifted(kept[reach - steps].astype(b16), "dp", -steps).astype(f32)
    grad_query_pre = rotate_back(grad_queries, cosine_table, sine_table) * HEAD_SIZE ** (-0.5)
    mine = jnp.where(is_first, rotate_back(mine, cosine_table, sine_table), mine)
    grad_projected = jnp.concatenate([grad_query_pre, mine], axis=1).astype(b16)
    first_grad = dot_nt(grad_projected, attn_in).astype(b16)
    first_grad = summed(
        exchange(first_grad.reshape(2 * lanes, sub, width), ("context", "tensor"))
    )
    own_scale = rms_scale(own_tokens)
    own_normed = own_tokens * own_scale
    grad_gain_one = jnp.sum(first_grad * own_normed, axis=0)
    grad_inputs = grad_middle + rms_back(first_grad * gains[0], own_normed, own_scale)
    grad_inputs = gathered(grad_inputs.astype(b16), "tensor").reshape(rows, width).astype(f32)

    grad_attn_in = dot_tn(lifted_one, grad_projected).astype(b16)
    grad_attn_in = summed(exchange(grad_attn_in.reshape(n, deep, 2 * HEAD_SIZE), "dp"))
    kept = half_of(grad_attn_in, side, 0)
    got = swapped(half_of(grad_attn_in, 1 - side, 0).astype(b16), "context", 1).astype(f32)
    grad_w_query = ordered(kept[:, :HEAD_SIZE], got[:, :HEAD_SIZE], 1)
    grad_w_key = jnp.where(is_first, kept[:, HEAD_SIZE:], got[:, HEAD_SIZE:])
    grad_w_value = jnp.where(is_first, got[:, HEAD_SIZE:], kept[:, HEAD_SIZE:])
    grad_w_out = jnp.swapaxes(grad_w_out.astype(b16).reshape(HEAD_SIZE, n, deep), 0, 1)
    grad_w_out = summed(exchange(grad_w_out, "dp"))
    kept = half_of(grad_w_out, side, 1)
    got = swapped(half_of(grad_w_out, 1 - side, 1).astype(b16), "context", 1).astype(f32)
    grad_w_out = ordered(kept, got, 0)

    grad_gains = jnp.stack([grad_gain_one, grad_gain_two, grad_gain_three, grad_gain_four])
    grad_gains = jnp.swapaxes(grad_gains.reshape(4, 2 * n, deep // 2), 0, 1)
    grad_gains = jnp.sum(exchange(grad_gains, ("dp", "context")), axis=0)
    grad_gains = jnp.sum(gathered(grad_gains, "tensor"), axis=0)
    return (
        output,
        grad_inputs,
        grad_w_query,
        grad_w_key,
        grad_w_value,
        grad_w_out,
        grad_w_gate,
        grad_w_up,
        grad_w_down,
        grad_gains[0],
        grad_gains[1],
        grad_gains[2],
        grad_gains[3],
    )


def solution(mesh):
    return jax.shard_map(
        on_device,
        mesh=mesh,
        in_specs=(
            P(("dp", "context"), None),
            P(("dp", "context")),
            P("dp", "tensor"),
            P("dp", "tensor"),
            P("dp", "tensor"),
            P("tensor", "dp"),
            P("dp", "tensor"),
            P("dp", "tensor"),
            P("tensor", "dp"),
            P("dp"),
            P("dp"),
            P("dp"),
            P("dp"),
            P(("dp", "context"), None),
        ),
        out_specs=(
            P(("dp", "context"), None),
            P(("dp", "context"), None),
            P(("dp", "context"), "tensor"),
            P(("dp", "context"), "tensor"),
            P(("dp", "context"), "tensor"),
            P("tensor", ("dp", "context")),
            P(("dp", "context"), "tensor"),
            P(("dp", "context"), "tensor"),
            P("tensor", ("dp", "context")),
            P(("dp", "context")),
            P(("dp", "context")),
            P(("dp", "context")),
            P(("dp", "context")),
        ),
        check_vma=False,
    )
```

time: 2570 us -> 1060 us (0.41)
  waiting for transfers between devices: 2220 us -> 635 us
  local copies, waits for them, and re-layouts: 30.3 us -> 91.2 us
  starting transfers between devices: 79.7 us -> 135 us
  other arithmetic: 38.3 us -> 76.6 us
  matrix products: 115 us -> 81.1 us
  blocking collectives: 56.4 us -> 30.7 us
    reduce_scatter x7 -> x0, waiting for transfers between devices: 1340 us -> none  [the longest x1 351 us: on_device(): lax.psum_scatter(grad_w_down, ('dp', 'context'), scatter_dimension=1, til...]
    all_gather x7 -> x0, waiting for transfers between devices: 620 us -> none  [the longest x1 182 us: on_device(): lax.all_gather(gate_part, 'dp', axis=0, tiled=True)]
    all_to_all x0 -> x22, waiting for transfers between devices: none -> 320 us  [exchange(): return lax.all_to_all(blocks, axis, 0, 0, tiled=True)]
    ppermute x35 -> x28, waiting for transfers between devices: 88.6 us -> 315 us  [the longest x22 252 us: swapped(): lax.ppermute(value, axis, [(place, place ^ bit) for place in range(count)])]
    psum x4 -> x0, waiting for transfers between devices: 167 us -> none  [the longest x1 55.6 us: on_device(): lifted_grad = lax.psum(lifted_grad, 'tensor')]
    all_to_all x0 -> x22, starting transfers between devices: none -> 101 us  [exchange(): return lax.all_to_all(blocks, axis, 0, 0, tiled=True)]
    unnamed x2 -> x0, blocking collectives: 56.4 us -> none
    ppermute x35 -> x28, starting transfers between devices: 78.1 us -> 34 us  [the longest x22 19.3 us: swapped(): lax.ppermute(value, axis, [(place, place ^ bit) for place in range(count)])]
  transfers between devices with their start and end apart: 53 -> 50, of which waited for: 30 -> 36; matrix products, arithmetic and copies ran while one was open for 4% -> 18% of each run, Pallas kernels for 0% -> 0%
where the time goes in v1:
time: 1060 us; the launch traced here: 1050 us
  waiting for transfers between devices  635 us (60%)
  starting transfers between devices  135 us (13%)
  local copies, waits for them, and re-layouts  91.2 us (9%)
  matrix products  81.1 us (8%)
  other arithmetic  76.6 us (7%)
  blocking collectives  30.7 us (3%)
    all_to_all x22, waiting for transfers between devices, exchange(): return lax.all_to_all(blocks, axis, 0, 0, tiled=True)  320 us
    ppermute x22, waiting for transfers between devices, swapped(): lax.ppermute(value, axis, [(place, place ^ bit) for place in range(count)])  252 us
    all_to_all x22, starting transfers between devices, exchange(): return lax.all_to_all(blocks, axis, 0, 0, tiled=True)  101 us
    ppermute x6, waiting for transfers between devices, shifted(): lax.ppermute(value, axis, [(s, s + steps) for s in range(count) if 0 <= s...  63.8 us
    dot_general x7, matrix products, dot_tn(): lax.dot_general(left, right, (((0,), (0,)), ((), ())), preferred_element_...  31.4 us
    all_to_all x1, blocking collectives, exchange(): return lax.all_to_all(blocks, axis, 0, 0, tiled=True)  30.7 us
    dot_general x7, matrix products, dot_nt(): lax.dot_general(left, right, (((1,), (1,)), ((), ())), preferred_element_...  28.1 us
    unnamed x185, local copies, waits for them, and re-layouts  26.3 us
  transfers between devices with their start and end apart: 50, of which 36 were waited for; matrix products, arithmetic and copies ran while one was open for 18% of the time, Pallas kernels for 0%

profile of v1, /device:TPU:0, one launch (start us, length us, event | category | flops | bytes accessed | tf_op | source)
XLA Modules:
  0.0 1052.4 jit_solution(17828411720642850708)
XLA Ops:
  1.9 7.3 all-to-all-start
  19.6 5.5 all-to-all-done.1
  26.8 4.5 all-to-all-start.2
  32.1 4.0 copy.84
  40.5 16.3 %collective-permute-done = bf16[256,2304]{1,0:T(8,128)(2,1)} collective-permute-done((bf16[256,2304]{1,0:T(8,128)(2,1)}, bf16[256,2304]{1,0:T(8,128)(2,1)}, u32[]{:S(2)}, u32[]{:S(2)}) %collective-permute-start) | collective-permute-done | bytes 1179680 | tf_op jit(solution)/shard_map/ppermute | solution.py:59
  59.9 22.9 %all-to-all-done.2 = bf16[4,576,512]{2,1,0:T(8,128)(2,1)} async-done(((bf16[4,576,512]{2,1,0:T(8,128)(2,1)}), bf16[4,576,512]{2,1,0:T(8,128)(2,1)}, u32[]{:S(2)}, u32[]{:S(2)}) %all-to-all-start.2) | async-done | bytes 2359328 | tf_op jit(solution)/shard_map/all_to_all | solution.py:49
  92.0 5.7 collective-permute-start.1
  103.7 9.8 collective-permute-done.1
  126.6 5.8 collective-permute-done.5
  136.3 12.1 %all-to-all-start.6 = ((bf16[4,576,288]{1,2,0:T(8,128)(2,1)}), bf16[4,576,288]{1,2,0:T(8,128)(2,1)S(1)}, u32[]{:S(2)}, u32[]{:S(2)}) async-start(bf16[4,576,288]{1,2,0:T(8,128)(2,1)} %fusion.41), calls=%async_computation.6 | async-start | bytes 2949120 | tf_op jit(solution)/shard_map/all_to_all | solution.py:49
  148.4 5.6 fusion.123
  160.9 19.7 %all-to-all-done.6 = bf16[4,576,288]{1,2,0:T(8,128)(2,1)S(1)} async-done(((bf16[4,576,288]{1,2,0:T(8,128)(2,1)}), bf16[4,576,288]{1,2,0:T(8,128)(2,1)S(1)}, u32[]{:S(2)}, u32[]{:S(2)}) %all-to-all-start.6) | async-done | bytes 1327136 | tf_op jit(solution)/shard_map/all_to_all | solution.py:49
  181.7 4.6 all-to-all-start.4
  186.3 4.0 copy.86
  191.6 23.2 %all-to-all-done.4 = bf16[8,64,2304]{2,1,0:T(8,128)(2,1)} async-done(((bf16[8,64,2304]{2,1,0:T(8,128)(2,1)}), bf16[8,64,2304]{2,1,0:T(8,128)(2,1)}, u32[]{:S(2)}, u32[]{:S(2)}) %all-to-all-start.4) | async-done | bytes 2359328 | tf_op jit(solution)/shard_map/all_to_all | solution.py:49
  222.7 30.6 %all-to-all-done.7 = bf16[4,576,288]{1,2,0:T(8,128)(2,1)S(1)} async-done(((bf16[4,576,288]{1,2,0:T(8,128)(2,1)}), bf16[4,576,288]{1,2,0:T(8,128)(2,1)S(1)}, u32[]{:S(2)}, u32[]{:S(2)}) %all-to-all-start.7) | async-done | bytes 1327136 | tf_op jit(solution)/shard_map/all_to_all | solution.py:49
  254.5 4.3 all-to-all-start.5
  258.7 4.5 copy.88
  266.3 20.5 %all-to-all-done.5 = bf16[4,64,2304]{2,1,0:T(8,128)(2,1)} async-done(((bf16[4,64,2304]{2,1,0:T(8,128)(2,1)}), bf16[4,64,2304]{2,1,0:T(8,128)(2,1)}, u32[]{:S(2)}, u32[]{:S(2)}) %all-to-all-start.5) | async-done | bytes 1179680 | tf_op jit(solution)/shard_map/all_to_all | solution.py:49
  286.8 4.3 all-to-all-start.8
  294.6 3.8 reshape.254
  304.6 21.0 %all-to-all-done.8 = bf16[4,288,576]{2,1,0:T(8,128)(2,1)} async-done(((bf16[4,288,576]{2,1,0:T(8,128)(2,1)}), bf16[4,288,576]{2,1,0:T(8,128)(2,1)}, u32[]{:S(2)}, u32[]{:S(2)}) %all-to-all-start.8) | async-done | bytes 1327136 | tf_op jit(solution)/shard_map/all_to_all | solution.py:49
  334.7 24.5 %collective-permute-done.11 = bf16[2304,288]{0,1:T(8,128)(2,1)} collective-permute-done((bf16[2304,288]{0,1:T(8,128)(2,1)}, bf16[2304,288]{0,1:T(8,128)(2,1)}, u32[]{:S(2)}, u32[]{:S(2)}) %collective-permute-start.11) | collective-permute-done | bytes 1327136 | tf_op jit(solution)/shard_map/ppermute | solution.py:59
  360.7 24.6 %collective-permute-done.12 = bf16[288,2304]{1,0:T(8,128)(2,1)S(1)} collective-permute-done((bf16[288,2304]{1,0:T(8,128)(2,1)}, bf16[288,2304]{1,0:T(8,128)(2,1)S(1)}, u32[]{:S(2)}, u32[]{:S(2)}) %collective-permute-start.12) | collective-permute-done | bytes 1327136 | tf_op jit(solution)/shard_map/ppermute | solution.py:59
  388.9 4.6 multiply_convert_fusion.2
  393.5 4.0 fusion.33
  397.8 4.5 collective-permute-done.13
  403.6 27.4 %collective-permute-done.14 = bf16[4,64,2304]{2,1,0:T(8,128)(2,1)S(1)} collective-permute-done((bf16[4,64,2304]{2,1,0:T(8,128)(2,1)S(1)}, bf16[4,64,2304]{2,1,0:T(8,128)(2,1)S(1)}, u32[]{:S(2)}, u32[]{:S(2)}) %collective-permute-start.14) | collective-permute-done | bytes 1179680 | tf_op jit(solution)/shard_map/ppermute | solution.py:59
  432.3 4.8 all-to-all-start.9
  437.2 28.0 %all-to-all-done.9 = bf16[4,64,2304]{2,1,0:T(8,128)(2,1)} async-done(((bf16[4,64,2304]{2,1,0:T(8,128)(2,1)}), bf16[4,64,2304]{2,1,0:T(8,128)(2,1)}, u32[]{:S(2)}, u32[]{:S(2)}) %all-to-all-start.9) | async-done | bytes 1179680 | tf_op jit(solution)/shard_map/all_to_all | solution.py:49
  468.8 30.7 %all_to_all.116 = bf16[4,64,2304]{2,1,0:T(8,128)(2,1)S(1)} all-to-all(bf16[4,64,2304]{2,1,0:T(8,128)(2,1)S(1)} %broadcast_in_dim.41), channel_id=1, replica_groups=mesh['dp'=4,'context'=2,'tensor'=4] {'dp'}, dimensions={0} | all-to-all | bytes 2359296 | tf_op jit(solution)/shard_map/all_to_all | solution.py:49
  500.1 25.9 %collective-permute-done.15 = bf16[1,4,64,2304]{3,2,1,0:T(8,128)(2,1)S(1)} collective-permute-done((bf16[1,4,64,2304]{3,2,1,0:T(8,128)(2,1)S(1)}, bf16[1,4,64,2304]{3,2,1,0:T(8,128)(2,1)S(1)}, u32[]{:S(2)}, u32[]{:S(2)}) %collective-permute-start.15) | collective-permute-done | bytes 1179680 | tf_op jit(solution)/shard_map/ppermute | solution.py:59
  526.4 4.5 collective-permute-done.16
  531.4 5.0 fusion.25
  536.5 4.0 fusion.34
  540.5 3.9 convolution_add_fusion
  544.9 4.4 collective-permute-done.17
  550.6 27.4 %collective-permute-done.18 = bf16[4,64,2304]{2,1,0:T(8,128)(2,1)S(1)} collective-permute-done((bf16[4,64,2304]{2,1,0:T(8,128)(2,1)S(1)}, bf16[4,64,2304]{2,1,0:T(8,128)(2,1)S(1)}, u32[]{:S(2)}, u32[]{:S(2)}) %collective-permute-start.18) | collective-permute-done | bytes 1179680 | tf_op jit(solution)/shard_map/ppermute | solution.py:59
  582.8 6.7 copy.102
  589.4 21.6 %all-to-all-done.12 = bf16[4,64,2304]{2,1,0:T(8,128)(2,1)S(1)} async-done(((bf16[4,64,2304]{2,1,0:T(8,128)(2,1)}), bf16[4,64,2304]{2,1,0:T(8,128)(2,1)S(1)}, u32[]{:S(2)}, u32[]{:S(2)}) %all-to-all-start.12) | async-done | bytes 1179680 | tf_op jit(solution)/shard_map/all_to_all | solution.py:49
  618.7 6.1 fusion.5
  630.7 6.6 copy.93
  637.3 6.2 fusion.7
  647.6 31.7 %collective-permute-done.27 = bf16[4,288,576]{2,1,0:T(8,128)(2,1)} collective-permute-done((bf16[4,288,576]{2,1,0:T(8,128)(2,1)}, bf16[4,288,576]{2,1,0:T(8,128)(2,1)}, u32[]{:S(2)}, u32[]{:S(2)}) %collective-permute-start.27) | collective-permute-done | bytes 1327136 | tf_op jit(solution)/shard_map/ppermute | solution.py:59
  683.5 4.4 all-to-all-start.10
  696.2 7.6 all-to-all-done.10
  703.9 4.3 all-to-all-start.20
  711.1 4.7 select_convert_fusion.3
  721.9 21.3 %all-to-all-done.20 = bf16[4,288,576]{2,1,0:T(8,128)(2,1)} async-done(((bf16[4,288,576]{2,1,0:T(8,128)(2,1)}), bf16[4,288,576]{2,1,0:T(8,128)(2,1)}, u32[]{:S(2)}, u32[]{:S(2)}) %all-to-all-start.20) | async-done | bytes 1327136 | tf_op jit(solution)/shard_map/all_to_all | solution.py:49
  743.2 4.3 all-to-all-start.19
  755.7 16.1 %collective-permute-done.20 = bf16[512,256]{0,1:T(8,128)(2,1)S(1)} collective-permute-done((bf16[512,256]{0,1:T(8,128)(2,1)S(1)}, bf16[512,256]{0,1:T(8,128)(2,1)S(1)}, u32[]{:S(2)}, u32[]{:S(2)}) %collective-permute-start.20) | collective-permute-done | bytes 262176 | tf_op jit(solution)/shard_map/ppermute | solution.py:64
  771.8 32.5 %collective-permute-done.21 = bf16[512,256]{0,1:T(8,128)(2,1)S(1)} collective-permute-done((bf16[512,256]{0,1:T(8,128)(2,1)S(1)}, bf16[512,256]{0,1:T(8,128)(2,1)S(1)}, u32[]{:S(2)}, u32[]{:S(2)}) %collective-permute-start.21) | collective-permute-done | bytes 262176 | tf_op jit(solution)/shard_map/ppermute | solution.py:64
  806.5 4.5 convolution_convert_fusion.1
  811.0 4.4 all-to-all-start.14
  815.4 6.1 fusion.44
  823.7 51.6 %collective-permute-done.25 = bf16[4,288,576]{2,1,0:T(8,128)(2,1)S(1)} collective-permute-done((bf16[4,288,576]{2,1,0:T(8,128)(2,1)S(1)}, bf16[4,288,576]{2,1,0:T(8,128)(2,1)S(1)}, u32[]{:S(2)}, u32[]{:S(2)}) %collective-permute-start.25) | collective-permute-done | bytes 1327136 | tf_op jit(solution)/shard_map/ppermute | solution.py:59
  877.0 4.5 all-to-all-start.18
  890.4 26.0 %all-to-all-done.18 = bf16[4,288,576]{2,1,0:T(8,128)(2,1)} async-done(((bf16[4,288,576]{2,1,0:T(8,128)(2,1)}), bf16[4,288,576]{2,1,0:T(8,128)(2,1)}, u32[]{:S(2)}, u32[]{:S(2)}) %all-to-all-start.18) | async-done | bytes 1327136 | tf_op jit(solution)/shard_map/all_to_all | solution.py:49
  916.4 4.0 all-to-all-start.21
  927.2 4.3 all-to-all-start.17
  932.4 26.1 %all-to-all-done.17 = bf16[4,256,576]{1,2,0:T(8,128)(2,1)} async-done(((bf16[4,256,576]{1,2,0:T(8,128)(2,1)}), bf16[4,256,576]{1,2,0:T(8,128)(2,1)}, u32[]{:S(2)}, u32[]{:S(2)}) %all-to-all-start.17) | async-done | bytes 1179680 | tf_op jit(solution)/shard_map/all_to_all | solution.py:49
  966.9 4.7 all-to-all-start.16
  995.5 30.1 %all-to-all-done.16 = bf16[4,576,512]{2,1,0:T(8,128)(2,1)} async-done(((bf16[4,576,512]{2,1,0:T(8,128)(2,1)}), bf16[4,576,512]{2,1,0:T(8,128)(2,1)}, u32[]{:S(2)}, u32[]{:S(2)}) %all-to-all-start.16) | async-done | bytes 2359328 | tf_op jit(solution)/shard_map/all_to_all | solution.py:49
  1035.6 10.6 %all-to-all-done.15 = bf16[4,64,2304]{2,1,0:T(8,128)(2,1)S(1)} async-done(((bf16[4,64,2304]{2,1,0:T(8,128)(2,1)}), bf16[4,64,2304]{2,1,0:T(8,128)(2,1)S(1)}, u32[]{:S(2)}, u32[]{:S(2)}) %all-to-all-start.15) | async-done | bytes 1179680 | tf_op jit(solution)/shard_map/all_to_all | solution.py:49
  (376 shorter events, 230.2 us)
Async XLA Ops:
  1.9 13.8 %all-to-all-start = ((s32[8,1,256]{2,1,0:T(1,128)}), s32[8,1,256]{2,1,0:T(1,128)S(1)}, u32[]{:S(2)}, u32[]{:S(2)}) async-start(s32[8,1,256]{2,1,0:T(1,128)} %broadcast_in_dim.32), calls=%async_computation | async-start | bytes 16384 | tf_op jit(solution)/shard_map/all_to_all | solution.py:49
  16.3 8.9 all-to-all-start.1
  26.8 56.1 %all-to-all-start.2 = ((bf16[4,576,512]{2,1,0:T(8,128)(2,1)}), bf16[4,576,512]{2,1,0:T(8,128)(2,1)}, u32[]{:S(2)}, u32[]{:S(2)}) async-start(bf16[4,576,512]{2,1,0:T(8,128)(2,1)} %broadcast_in_dim.34), calls=%async_computation.2 | async-start | bytes 4718592 | tf_op jit(solution)/shard_map/all_to_all | solution.py:49
  31.3 25.5 %collective-permute-start = (bf16[256,2304]{1,0:T(8,128)(2,1)}, bf16[256,2304]{1,0:T(8,128)(2,1)}, u32[]{:S(2)}, u32[]{:S(2)}) collective-permute-start(bf16[256,2304]{1,0:T(8,128)(2,1)} %param.14), channel_id=1, source_target_pairs={{0,4},{4,0},{1,5},{5,1},{2,6},{6,2},{3,7},{7,3},{8,12},{12,8},{9,1... | collective-permute-start | bytes 3538952 | tf_op jit(solution)/shard_map/ppermute | solution.py:59
  40.5 47.0 %copy-start.53 = (f32[2304]{0:T(1024)}, f32[2304]{0:T(1024)S(1)}, u32[]{:S(2)}) copy-start(f32[2304]{0:T(1024)S(1)} %mul.360) | copy-start | bytes 27652
  83.9 51.4 %all-to-all-start.3 = ((bf16[4,256,576]{1,2,0:T(8,128)(2,1)}), bf16[4,256,576]{1,2,0:T(8,128)(2,1)S(1)}, u32[]{:S(2)}, u32[]{:S(2)}) async-start(bf16[4,256,576]{1,2,0:T(8,128)(2,1)} %broadcast_in_dim.36), calls=%async_computation.3 | async-start | bytes 2359296 | tf_op jit(solution)/shard_map/all_to_all | solution.py:49
  92.0 43.3 %copy-start.46 = (bf16[512,256]{0,1:T(8,128)(2,1)}, bf16[512,256]{0,1:T(8,128)(2,1)S(1)}, u32[]{:S(2)}) copy-start(bf16[512,256]{0,1:T(8,128)(2,1)S(1)} %fusion.69) | copy-start | bytes 786436
  92.0 21.4 %collective-permute-start.1 = (bf16[512,256]{0,1:T(8,128)(2,1)S(1)}, bf16[512,256]{0,1:T(8,128)(2,1)S(1)}, u32[]{:S(2)}, u32[]{:S(2)}) collective-permute-start(bf16[512,256]{0,1:T(8,128)(2,1)S(1)} %fusion.69), channel_id=1, source_target_pairs={{0,24},{1,25},{2,26},{3,27},{4,28},{5,29},{6,30},{7,31}} | collective-permute-start | bytes 786440 | tf_op jit(solution)/shard_map/ppermute | solution.py:64
  97.7 21.4 %collective-permute-start.2 = (bf16[512,256]{0,1:T(8,128)(2,1)S(1)}, bf16[512,256]{0,1:T(8,128)(2,1)}, u32[]{:S(2)}, u32[]{:S(2)}) collective-permute-start(bf16[512,256]{0,1:T(8,128)(2,1)S(1)} %fusion.69), channel_id=1, source_target_pairs={{0,16},{8,24},{1,17},{9,25},{2,18},{10,26},{3,19},{11,27},{4,20},{... | collective-permute-start | bytes 786440 | tf_op jit(solution)/shard_map/ppermute | solution.py:64
  99.7 23.3 %collective-permute-start.3 = (bf16[512,256]{0,1:T(8,128)(2,1)S(1)}, bf16[512,256]{0,1:T(8,128)(2,1)}, u32[]{:S(2)}, u32[]{:S(2)}) collective-permute-start(bf16[512,256]{0,1:T(8,128)(2,1)S(1)} %fusion.69), channel_id=1, source_target_pairs={{0,8},{8,16},{16,24},{1,9},{9,17},{17,25},{2,10},{10,18},{18,26},{... | collective-permute-start | bytes 786440 | tf_op jit(solution)/shard_map/ppermute | solution.py:64
  113.5 13.1 %collective-permute-start.4 = (bf16[512,256]{0,1:T(8,128)(2,1)S(1)}, bf16[512,256]{0,1:T(8,128)(2,1)S(1)}, u32[]{:S(2)}, u32[]{:S(2)}) collective-permute-start(bf16[512,256]{0,1:T(8,128)(2,1)S(1)} %collective-permute-done.1), channel_id=1, source_target_pairs={{0,4},{4,0},{1,5},{5,1},{2,6},{6,2},{3,7},{7,3},{8,12},{12,8},{9,1... | collective-permute-start | bytes 786440 | tf_op jit(solution)/shard_map/ppermute | solution.py:59
  115.6 19.6 %collective-permute-start.7 = (bf16[512,256]{0,1:T(8,128)(2,1)S(1)}, bf16[512,256]{0,1:T(8,128)(2,1)S(1)}, u32[]{:S(2)}, u32[]{:S(2)}) collective-permute-start(bf16[512,256]{0,1:T(8,128)(2,1)S(1)} %fusion.69), channel_id=1, source_target_pairs={{0,4},{4,0},{1,5},{5,1},{2,6},{6,2},{3,7},{7,3},{8,12},{12,8},{9,1... | collective-permute-start | bytes 786440 | tf_op jit(solution)/shard_map/ppermute | solution.py:59
  119.1 13.3 %collective-permute-start.5 = (bf16[512,256]{0,1:T(8,128)(2,1)}, bf16[512,256]{0,1:T(8,128)(2,1)S(1)}, u32[]{:S(2)}, u32[]{:S(2)}) collective-permute-start(bf16[512,256]{0,1:T(8,128)(2,1)} %collective-permute-done.2), channel_id=1, source_target_pairs={{0,4},{4,0},{1,5},{5,1},{2,6},{6,2},{3,7},{7,3},{8,12},{12,8},{9,1... | collective-permute-start | bytes 786440 | tf_op jit(solution)/shard_map/ppermute | solution.py:59
  123.0 12.2 %collective-permute-start.6 = (bf16[512,256]{0,1:T(8,128)(2,1)}, bf16[512,256]{0,1:T(8,128)(2,1)S(1)}, u32[]{:S(2)}, u32[]{:S(2)}) collective-permute-start(bf16[512,256]{0,1:T(8,128)(2,1)} %collective-permute-done.3), channel_id=1, source_target_pairs={{0,4},{4,0},{1,5},{5,1},{2,6},{6,2},{3,7},{7,3},{8,12},{12,8},{9,1... | collective-permute-start | bytes 786440 | tf_op jit(solution)/shard_map/ppermute | solution.py:59
  136.3 44.3 %all-to-all-start.6 = ((bf16[4,576,288]{1,2,0:T(8,128)(2,1)}), bf16[4,576,288]{1,2,0:T(8,128)(2,1)S(1)}, u32[]{:S(2)}, u32[]{:S(2)}) async-start(bf16[4,576,288]{1,2,0:T(8,128)(2,1)} %fusion.41), calls=%async_computation.6 | async-start | bytes 2949120 | tf_op jit(solution)/shard_map/all_to_all | solution.py:49
  181.7 33.1 %all-to-all-start.4 = ((bf16[8,64,2304]{2,1,0:T(8,128)(2,1)}), bf16[8,64,2304]{2,1,0:T(8,128)(2,1)}, u32[]{:S(2)}, u32[]{:S(2)}) async-start(bf16[8,64,2304]{2,1,0:T(8,128)(2,1)} %bitcast.5), calls=%async_computation.4 | async-start | bytes 4718592 | tf_op jit(solution)/shard_map/all_to_all | solution.py:49
  214.8 38.5 %all-to-all-start.7 = ((bf16[4,576,288]{1,2,0:T(8,128)(2,1)}), bf16[4,576,288]{1,2,0:T(8,128)(2,1)S(1)}, u32[]{:S(2)}, u32[]{:S(2)}) async-start(bf16[4,576,288]{1,2,0:T(8,128)(2,1)} %fusion.40), calls=%async_computation.7 | async-start | bytes 2949120 | tf_op jit(solution)/shard_map/all_to_all | solution.py:49
  218.6 392.6 %copy-start.52 = (f32[2304]{0:T(1024)}, f32[2304]{0:T(1024)S(1)}, u32[]{:S(2)}) copy-start(f32[2304]{0:T(1024)S(1)} %mul.385) | copy-start | bytes 27652
  222.6 388.6 %copy-start.74 = (f32[64]{0:T(128)}, f32[64]{0:T(128)S(1)}, u32[]{:S(2)}) copy-start(f32[64]{0:T(128)S(1)} %add_rsqrt_fusion.3) | copy-start | bytes 772
  254.5 32.4 %all-to-all-start.5 = ((bf16[4,64,2304]{2,1,0:T(8,128)(2,1)}), bf16[4,64,2304]{2,1,0:T(8,128)(2,1)}, u32[]{:S(2)}, u32[]{:S(2)}) async-start(bf16[4,64,2304]{2,1,0:T(8,128)(2,1)} %broadcast_in_dim.37), calls=%async_computation.5 | async-start | bytes 2359296 | tf_op jit(solution)/shard_map/all_to_all | solution.py:49
  286.8 38.7 %all-to-all-start.8 = ((bf16[4,288,576]{2,1,0:T(8,128)(2,1)}), bf16[4,288,576]{2,1,0:T(8,128)(2,1)}, u32[]{:S(2)}, u32[]{:S(2)}) async-start(bf16[4,288,576]{2,1,0:T(8,128)(2,1)} %slice_select_fusion), calls=%async_computation.8 | async-start | bytes 2949120 | tf_op jit(solution)/shard_map/all_to_all | solution.py:49
  291.2 39.6 %collective-permute-start.8 = (bf16[1,4,64,2304]{3,2,1,0:T(8,128)(2,1)}, bf16[1,4,64,2304]{3,2,1,0:T(8,128)(2,1)}, u32[]{:S(2)}, u32[]{:S(2)}) collective-permute-start(bf16[1,4,64,2304]{3,2,1,0:T(8,128)(2,1)} %bitcast.6), channel_id=1, source_target_pairs={{0,2},{1,3},{2,0},{3,1},{4,6},{5,7},{6,4},{7,5},{8,10},{9,11},{10,... | collective-permute-start | bytes 3538952 | tf_op jit(solution)/shard_map/ppermute | solution.py:59
  298.4 34.3 %collective-permute-start.10 = (bf16[2304,288]{0,1:T(8,128)(2,1)}, bf16[2304,288]{0,1:T(8,128)(2,1)}, u32[]{:S(2)}, u32[]{:S(2)}) collective-permute-start(bf16[2304,288]{0,1:T(8,128)(2,1)} %reshape.254), channel_id=1, source_target_pairs={{0,4},{4,0},{1,5},{5,1},{2,6},{6,2},{3,7},{7,3},{8,12},{12,8},{9,1... | collective-permute-start | bytes 3981320 | tf_op jit(solution)/shard_map/ppermute | solution.py:59
  303.1 56.2 %collective-permute-start.11 = (bf16[2304,288]{0,1:T(8,128)(2,1)}, bf16[2304,288]{0,1:T(8,128)(2,1)}, u32[]{:S(2)}, u32[]{:S(2)}) collective-permute-start(bf16[2304,288]{0,1:T(8,128)(2,1)} %reshape.256), channel_id=1, source_target_pairs={{0,4},{4,0},{1,5},{5,1},{2,6},{6,2},{3,7},{7,3},{8,12},{12,8},{9,1... | collective-permute-start | bytes 3981320 | tf_op jit(solution)/shard_map/ppermute | solution.py:59
  330.1 55.2 %collective-permute-start.12 = (bf16[288,2304]{1,0:T(8,128)(2,1)}, bf16[288,2304]{1,0:T(8,128)(2,1)S(1)}, u32[]{:S(2)}, u32[]{:S(2)}) collective-permute-start(bf16[288,2304]{1,0:T(8,128)(2,1)} %reshape.258), channel_id=1, source_target_pairs={{0,4},{4,0},{1,5},{5,1},{2,6},{6,2},{3,7},{7,3},{8,12},{12,8},{9,1... | collective-permute-start | bytes 3981320 | tf_op jit(solution)/shard_map/ppermute | solution.py:59
  332.6 52.9 %collective-permute-start.9 = (bf16[2,1,4,64,2304]{4,3,2,1,0:T(8,128)(2,1)S(1)}, bf16[2,1,4,64,2304]{4,3,2,1,0:T(8,128)(2,1)S(1)}, u32[]{:S(2)}, u32[]{:S(2)}) collective-permute-start(bf16[2,1,4,64,2304]{4,3,2,1,0:T(8,128)(2,1)S(1)} %maximum_bitcast_fusion), channel_id=1, source_target_pairs={{0,1},{1,0},{2,3},{3,2},{4,5},{5,4},{6,7},{7,6},{8,9},{9,8},{10,11... | collective-permute-start | bytes 7077896 | tf_op jit(solution)/shard_map/ppermute | solution.py:59
  334.7 51.3 %copy-start.22 = (bf16[2304,288]{0,1:T(8,128)(2,1)}, bf16[2304,288]{0,1:T(8,128)(2,1)S(1)}, u32[]{:S(2)}) copy-start(bf16[2304,288]{0,1:T(8,128)(2,1)S(1)} %get-tuple-element.40) | copy-start | bytes 3981316
  334.7 51.3 %copy-start.24 = (bf16[2304,288]{0,1:T(8,128)(2,1)}, bf16[2304,288]{0,1:T(8,128)(2,1)S(1)}, u32[]{:S(2)}) copy-start(bf16[2304,288]{0,1:T(8,128)(2,1)S(1)} %get-tuple-element.41) | copy-start | bytes 3981316
  334.7 50.6 %copy-start.21 = (bf16[288,2304]{1,0:T(8,128)(2,1)S(1)}, bf16[288,2304]{1,0:T(8,128)(2,1)}, u32[]{:S(2)}) copy-start(bf16[288,2304]{1,0:T(8,128)(2,1)} %reshape.258) | copy-start | bytes 3981316
  397.8 4.6 collective-permute-start.13
  403.0 28.1 %collective-permute-start.14 = (bf16[4,64,2304]{2,1,0:T(8,128)(2,1)S(1)}, bf16[4,64,2304]{2,1,0:T(8,128)(2,1)S(1)}, u32[]{:S(2)}, u32[]{:S(2)}) collective-permute-start(bf16[4,64,2304]{2,1,0:T(8,128)(2,1)S(1)} %fusion.42), channel_id=1, source_target_pairs={{0,2},{1,3},{2,0},{3,1},{4,6},{5,7},{6,4},{7,5},{8,10},{9,11},{10,... | collective-permute-start | bytes 3538952 | tf_op jit(solution)/shard_map/ppermute | solution.py:59
  432.3 33.0 %all-to-all-start.9 = ((bf16[4,64,2304]{2,1,0:T(8,128)(2,1)}), bf16[4,64,2304]{2,1,0:T(8,128)(2,1)}, u32[]{:S(2)}, u32[]{:S(2)}) async-start(bf16[4,64,2304]{2,1,0:T(8,128)(2,1)} %fusion.31), calls=%async_computation.9 | async-start | bytes 2359296 | tf_op jit(solution)/shard_map/all_to_all | solution.py:49
  499.5 26.5 %collective-permute-start.15 = (bf16[1,4,64,2304]{3,2,1,0:T(8,128)(2,1)S(1)}, bf16[1,4,64,2304]{3,2,1,0:T(8,128)(2,1)S(1)}, u32[]{:S(2)}, u32[]{:S(2)}) collective-permute-start(bf16[1,4,64,2304]{3,2,1,0:T(8,128)(2,1)S(1)} %bitcast.178), channel_id=1, source_target_pairs={{0,2},{1,3},{2,0},{3,1},{4,6},{5,7},{6,4},{7,5},{8,10},{9,11},{10,... | collective-permute-start | bytes 3538952 | tf_op jit(solution)/shard_map/ppermute | solution.py:59
  526.3 4.6 collective-permute-start.16
  544.7 4.6 collective-permute-start.17
  549.9 28.1 %collective-permute-start.18 = (bf16[4,64,2304]{2,1,0:T(8,128)(2,1)S(1)}, bf16[4,64,2304]{2,1,0:T(8,128)(2,1)S(1)}, u32[]{:S(2)}, u32[]{:S(2)}) collective-permute-start(bf16[4,64,2304]{2,1,0:T(8,128)(2,1)S(1)} %fusion.43), channel_id=1, source_target_pairs={{0,2},{1,3},{2,0},{3,1},{4,6},{5,7},{6,4},{7,5},{8,10},{9,11},{10,... | collective-permute-start | bytes 3538952 | tf_op jit(solution)/shard_map/ppermute | solution.py:59
  579.2 31.8 %all-to-all-start.12 = ((bf16[4,64,2304]{2,1,0:T(8,128)(2,1)}), bf16[4,64,2304]{2,1,0:T(8,128)(2,1)S(1)}, u32[]{:S(2)}, u32[]{:S(2)}) async-start(bf16[4,64,2304]{2,1,0:T(8,128)(2,1)} %fusion.29), calls=%async_computation.12 | async-start | bytes 2359296 | tf_op jit(solution)/shard_map/all_to_all | solution.py:49
  614.8 67.6 %all-to-all-start.13 = ((bf16[8,64,2304]{2,1,0:T(8,128)(2,1)}), bf16[8,64,2304]{2,1,0:T(8,128)(2,1)S(1)}, u32[]{:S(2)}, u32[]{:S(2)}) async-start(bf16[8,64,2304]{2,1,0:T(8,128)(2,1)} %broadcast_in_dim.44), calls=%async_computation.13 | async-start | bytes 4718592 | tf_op jit(solution)/shard_map/all_to_all | solution.py:49
  628.7 50.5 %collective-permute-start.27 = (bf16[4,288,576]{2,1,0:T(8,128)(2,1)}, bf16[4,288,576]{2,1,0:T(8,128)(2,1)}, u32[]{:S(2)}, u32[]{:S(2)}) collective-permute-start(bf16[4,288,576]{2,1,0:T(8,128)(2,1)} %fusion.39), channel_id=1, source_target_pairs={{0,4},{4,0},{1,5},{5,1},{2,6},{6,2},{3,7},{7,3},{8,12},{12,8},{9,1... | collective-permute-start | bytes 3981320 | tf_op jit(solution)/shard_map/ppermute | solution.py:59
  637.3 41.9 %slice-start.2 = ((s8[5898240]{0:T(1024)(128)(4,1)}), s8[4194304]{0:T(1024)(128)(4,1)S(1)}, s32[]{:S(2)}) async-start(s8[5898240]{0:T(1024)(128)(4,1)} %bitcast.165), calls=%async_computation.25 | async-start | bytes 8388608
  637.3 41.9 %slice-start.3 = ((s8[5898240]{0:T(1024)(128)(4,1)}), s8[1703936]{0:T(1024)(128)(4,1)S(1)}, s32[]{:S(2)}) async-start(s8[5898240]{0:T(1024)(128)(4,1)} %bitcast.165), calls=%async_computation.26 | async-start | bytes 3407872
  647.5 68.5 %collective-permute-start.26 = (bf16[4,288,576]{2,1,0:T(8,128)(2,1)}, bf16[4,288,576]{2,1,0:T(8,128)(2,1)}, u32[]{:S(2)}, u32[]{:S(2)}) collective-permute-start(bf16[4,288,576]{2,1,0:T(8,128)(2,1)} %fusion.38), channel_id=1, source_target_pairs={{0,4},{4,0},{1,5},{5,1},{2,6},{6,2},{3,7},{7,3},{8,12},{12,8},{9,1... | collective-permute-start | bytes 3981320 | tf_op jit(solution)/shard_map/ppermute | solution.py:59
  683.5 20.3 %all-to-all-start.10 = ((bf16[4,64,2304]{2,1,0:T(8,128)(2,1)}), bf16[4,64,2304]{2,1,0:T(8,128)(2,1)}, u32[]{:S(2)}, u32[]{:S(2)}) async-start(bf16[4,64,2304]{2,1,0:T(8,128)(2,1)} %broadcast_in_dim.40), calls=%async_computation.10 | async-start | bytes 2359296 | tf_op jit(solution)/shard_map/all_to_all | solution.py:49
  703.9 39.3 %all-to-all-start.20 = ((bf16[4,288,576]{2,1,0:T(8,128)(2,1)}), bf16[4,288,576]{2,1,0:T(8,128)(2,1)}, u32[]{:S(2)}, u32[]{:S(2)}) async-start(bf16[4,288,576]{2,1,0:T(8,128)(2,1)} %fusion.17), calls=%async_computation.20 | async-start | bytes 2949120 | tf_op jit(solution)/shard_map/all_to_all | solution.py:49
  715.8 31.7 %collective-permute-start.19 = (bf16[2048,256]{0,1:T(8,128)(2,1)}, bf16[2048,256]{0,1:T(8,128)(2,1)}, u32[]{:S(2)}, u32[]{:S(2)}) collective-permute-start(bf16[2048,256]{0,1:T(8,128)(2,1)} %get-tuple-element.71), channel_id=1, source_target_pairs={{0,4},{4,0},{1,5},{5,1},{2,6},{6,2},{3,7},{7,3},{8,12},{12,8},{9,1... | collective-permute-start | bytes 3145736 | tf_op jit(solution)/shard_map/ppermute | solution.py:59
  743.2 67.8 %all-to-all-start.19 = ((bf16[4,288,576]{2,1,0:T(8,128)(2,1)}), bf16[4,288,576]{2,1,0:T(8,128)(2,1)}, u32[]{:S(2)}, u32[]{:S(2)}) async-start(bf16[4,288,576]{2,1,0:T(8,128)(2,1)} %fusion.18), calls=%async_computation.19 | async-start | bytes 2949120 | tf_op jit(solution)/shard_map/all_to_all | solution.py:49
  750.1 21.7 %collective-permute-start.20 = (bf16[512,256]{0,1:T(8,128)(2,1)S(1)}, bf16[512,256]{0,1:T(8,128)(2,1)S(1)}, u32[]{:S(2)}, u32[]{:S(2)}) collective-permute-start(bf16[512,256]{0,1:T(8,128)(2,1)S(1)} %get-tuple-element.55), channel_id=1, source_target_pairs={{8,0},{16,8},{24,16},{9,1},{17,9},{25,17},{10,2},{18,10},{26,18},{... | collective-permute-start | bytes 786440 | tf_op jit(solution)/shard_map/ppermute | solution.py:64
  751.4 52.9 %collective-permute-start.21 = (bf16[512,256]{0,1:T(8,128)(2,1)S(1)}, bf16[512,256]{0,1:T(8,128)(2,1)S(1)}, u32[]{:S(2)}, u32[]{:S(2)}) collective-permute-start(bf16[512,256]{0,1:T(8,128)(2,1)S(1)} %get-tuple-element.57), channel_id=1, source_target_pairs={{16,0},{24,8},{17,1},{25,9},{18,2},{26,10},{19,3},{27,11},{20,4},{... | collective-permute-start | bytes 786440 | tf_op jit(solution)/shard_map/ppermute | solution.py:64
  752.7 51.6 %collective-permute-start.22 = (bf16[512,256]{0,1:T(8,128)(2,1)S(1)}, bf16[512,256]{0,1:T(8,128)(2,1)S(1)}, u32[]{:S(2)}, u32[]{:S(2)}) collective-permute-start(bf16[512,256]{0,1:T(8,128)(2,1)S(1)} %get-tuple-element.56), channel_id=1, source_target_pairs={{24,0},{25,1},{26,2},{27,3},{28,4},{29,5},{30,6},{31,7}} | collective-permute-start | bytes 786440 | tf_op jit(solution)/shard_map/ppermute | solution.py:64
  755.7 50.1 %copy-start.44 = (bf16[512,256]{0,1:T(8,128)(2,1)}, bf16[512,256]{0,1:T(8,128)(2,1)S(1)}, u32[]{:S(2)}) copy-start(bf16[512,256]{0,1:T(8,128)(2,1)S(1)} %fusion.71) | copy-start | bytes 786436
  811.0 66.0 %all-to-all-start.14 = ((bf16[8,64,2304]{2,1,0:T(8,128)(2,1)}), bf16[8,64,2304]{2,1,0:T(8,128)(2,1)}, u32[]{:S(2)}, u32[]{:S(2)}) async-start(bf16[8,64,2304]{2,1,0:T(8,128)(2,1)} %bitcast.181), calls=%async_computation.14 | async-start | bytes 4718592 | tf_op jit(solution)/shard_map/all_to_all | solution.py:49
  821.8 53.6 %collective-permute-start.25 = (bf16[4,288,576]{2,1,0:T(8,128)(2,1)S(1)}, bf16[4,288,576]{2,1,0:T(8,128)(2,1)S(1)}, u32[]{:S(2)}, u32[]{:S(2)}) collective-permute-start(bf16[4,288,576]{2,1,0:T(8,128)(2,1)S(1)} %fusion.37), channel_id=1, source_target_pairs={{0,4},{4,0},{1,5},{5,1},{2,6},{6,2},{3,7},{7,3},{8,12},{12,8},{9,1... | collective-permute-start | bytes 3981320 | tf_op jit(solution)/shard_map/ppermute | solution.py:59
  877.0 39.5 %all-to-all-start.18 = ((bf16[4,288,576]{2,1,0:T(8,128)(2,1)}), bf16[4,288,576]{2,1,0:T(8,128)(2,1)}, u32[]{:S(2)}, u32[]{:S(2)}) async-start(bf16[4,288,576]{2,1,0:T(8,128)(2,1)} %fusion.16), calls=%async_computation.18 | async-start | bytes 2949120 | tf_op jit(solution)/shard_map/all_to_all | solution.py:49
  885.6 37.6 %copy-start.18 = (f32[64,2304]{1,0:T(8,128)}, f32[64,2304]{1,0:T(8,128)S(1)}, u32[]{:S(2)}) copy-start(f32[64,2304]{1,0:T(8,128)S(1)} %convert_reduce_fusion.1) | copy-start | bytes 1769476
  916.4 10.8 %all-to-all-start.21 = ((f32[8,4,288]{2,1,0:T(4,128)}), f32[8,4,288]{2,1,0:T(4,128)}, u32[]{:S(2)}, u32[]{:S(2)}) async-start(f32[8,4,288]{2,1,0:T(4,128)} %maximum_bitcast_fusion.2), calls=%async_computation.21 | async-start | bytes 98304 | tf_op jit(solution)/shard_map/all_to_all | solution.py:49
  923.2 39.2 %copy-start.27 = (bf16[256,2304]{1,0:T(8,128)(2,1)S(1)}, bf16[256,2304]{1,0:T(8,128)(2,1)}, u32[]{:S(2)}) copy-start(bf16[256,2304]{1,0:T(8,128)(2,1)} %copy-done.26) | copy-start | bytes 3538948
  923.2 39.2 %copy-start.29 = (bf16[256,2304]{1,0:T(8,128)(2,1)S(1)}, bf16[256,2304]{1,0:T(8,128)(2,1)}, u32[]{:S(2)}) copy-start(bf16[256,2304]{1,0:T(8,128)(2,1)} %copy-done.28) | copy-start | bytes 3538948
  925.7 36.7 %copy-start.75 = (f32[512]{0:T(512)S(1)}, f32[512]{0:T(512)}, u32[]{:S(2)}) copy-start(f32[512]{0:T(512)} %add_rsqrt_fusion) | copy-start | bytes 6148
  927.2 31.3 %all-to-all-start.17 = ((bf16[4,256,576]{1,2,0:T(8,128)(2,1)}), bf16[4,256,576]{1,2,0:T(8,128)(2,1)}, u32[]{:S(2)}, u32[]{:S(2)}) async-start(bf16[4,256,576]{1,2,0:T(8,128)(2,1)} %bitcast.175), calls=%async_computation.17 | async-start | bytes 2359296 | tf_op jit(solution)/shard_map/all_to_all | solution.py:49
  959.1 7.1 all-to-all-start.22
  966.9 58.7 %all-to-all-start.16 = ((bf16[4,576,512]{2,1,0:T(8,128)(2,1)}), bf16[4,576,512]{2,1,0:T(8,128)(2,1)}, u32[]{:S(2)}, u32[]{:S(2)}) async-start(bf16[4,576,512]{2,1,0:T(8,128)(2,1)} %bitcast.180), calls=%async_computation.16 | async-start | bytes 4718592 | tf_op jit(solution)/shard_map/all_to_all | solution.py:49
  992.2 38.1 %collective-permute-start.24 = (bf16[256,288]{0,1:T(8,128)(2,1)S(1)}, bf16[256,288]{0,1:T(8,128)(2,1)S(1)}, u32[]{:S(2)}, u32[]{:S(2)}) collective-permute-start(bf16[256,288]{0,1:T(8,128)(2,1)S(1)} %select_convert_fusion.5), channel_id=1, source_target_pairs={{0,4},{4,0},{1,5},{5,1},{2,6},{6,2},{3,7},{7,3},{8,12},{12,8},{9,1... | collective-permute-start | bytes 442376 | tf_op jit(solution)/shard_map/ppermute | solution.py:59
  1026.7 19.5 %all-to-all-start.15 = ((bf16[4,64,2304]{2,1,0:T(8,128)(2,1)}), bf16[4,64,2304]{2,1,0:T(8,128)(2,1)S(1)}, u32[]{:S(2)}, u32[]{:S(2)}) async-start(bf16[4,64,2304]{2,1,0:T(8,128)(2,1)} %broadcast_in_dim.45), calls=%async_computation.15 | async-start | bytes 2359296 | tf_op jit(solution)/shard_map/all_to_all | solution.py:49
  1034.1 13.8 %collective-permute-start.23 = (bf16[288,512]{1,0:T(8,128)(2,1)S(1)}, bf16[288,512]{1,0:T(8,128)(2,1)S(1)}, u32[]{:S(2)}, u32[]{:S(2)}) collective-permute-start(bf16[288,512]{1,0:T(8,128)(2,1)S(1)} %select_convert_fusion.4), channel_id=1, source_target_pairs={{0,4},{4,0},{1,5},{5,1},{2,6},{6,2},{3,7},{7,3},{8,12},{12,8},{9,1... | collective-permute-start | bytes 884744 | tf_op jit(solution)/shard_map/ppermute | solution.py:59
  (75 other events, 675.9 us)

commit v2 on v1

v2 whole, which is shorter than its diff:
```python
import jax
import jax.numpy as jnp
from jax import lax
from jax.sharding import PartitionSpec as P

HEAD_SIZE = 256
SLIDE_WINDOW = 4096


eps = 1e-06
softcap = 50.0
negative = -1e30
f32 = jnp.float32
b16 = jnp.bfloat16


def rms_scale(value_rows):
    return lax.rsqrt(jnp.mean(value_rows * value_rows, axis=-1, keepdims=True) + eps)


def rms_back(grad, normed, scale):
    return scale * (grad - normed * jnp.mean(grad * normed, axis=-1, keepdims=True))


def rotary_tables(positions):
    inverse = 1.0 / 10000.0 ** (jnp.arange(0, HEAD_SIZE, 2, dtype=f32) / HEAD_SIZE)
    angles = positions.astype(f32)[:, None] * inverse[None, :]
    return (jnp.cos(angles), jnp.sin(angles))


def apply_rotary(value_rows, cosine_table, sine_table):
    half = value_rows.shape[-1] // 2
    first, second = value_rows[:, :half], value_rows[:, half:]
    return jnp.concatenate(
        [first * cosine_table - second * sine_table, second * cosine_table + first * sine_table],
        axis=-1,
    )


def rotate_back(grads, cosine_table, sine_table):
    return apply_rotary(grads, cosine_table, -sine_table)


def gated(gate_value, up_value):
    return jax.nn.gelu(gate_value, approximate=True) * up_value


def exchange(blocks, axis):
    return lax.all_to_all(blocks, axis, 0, 0, tiled=True)


def gathered(block, axis):
    count = lax.axis_size(axis)
    return exchange(jnp.broadcast_to(block[None], (count,) + block.shape), axis)


def swapped(value, axis, bit):
    count = lax.axis_size(axis)
    return lax.ppermute(value, axis, [(place, place ^ bit) for place in range(count)])


def passed_on(value, steps, way):
    n = lax.axis_size("dp")
    pairs = [(s, s + 1) for s in range(steps - 1, n - 1)]
    if way < 0:
        pairs = [(n - 1 - s, n - 1 - t) for s, t in pairs]
    return lax.ppermute(value, "dp", pairs)


def shifted(value, axis, steps):
    count = lax.axis_size(axis)
    return lax.ppermute(
        value, axis, [(s, s + steps) for s in range(count) if 0 <= s + steps < count]
    )


def summed(blocks):
    return jnp.sum(blocks.astype(f32), axis=0)


def dot(left, right):
    return jnp.dot(left, right, preferred_element_type=f32)


def dot_nt(left, right):
    return lax.dot_general(left, right, (((1,), (1,)), ((), ())), preferred_element_type=f32)


def dot_tn(left, right):
    return lax.dot_general(left, right, (((0,), (0,)), ((), ())), preferred_element_type=f32)


def rotated(value, steps):
    n = lax.axis_size("dp")
    return lax.ppermute(value, "dp", [(s, (s + steps) % n) for s in range(n)])


def picked(first, pair):
    low, high = pair
    return jnp.where(first, low, high), jnp.where(first, high, low)


def after(value, *earlier):
    return lax.optimization_barrier((value,) + earlier)[0]


def bits():
    lane = lax.axis_index("tensor")
    return lax.axis_index("context") == 0, lane < 2, lane % 2 == 0


AXES = (("context", 1), ("tensor", 2), ("tensor", 1))


def join(own, step, axis):
    low, high = picked(bits()[step], (own, swapped(own, *AXES[step])))
    return jnp.stack([low, high], axis=axis)


def fold(partial, step, axis):
    low = lax.index_in_dim(partial, 0, axis, keepdims=False)
    high = lax.index_in_dim(partial, 1, axis, keepdims=False)
    kept, sent = picked(bits()[step], (low, high))
    return kept + swapped(sent.astype(b16), *AXES[step]).astype(f32)


def collect_group(partial, sub):
    width = partial.shape[-1]
    partial = fold(partial.reshape(2, 2, 2, sub, width), 2, 2)
    left, right = partial[..., : width // 2], partial[..., width // 2 :]
    left = fold(fold(left, 0, 0), 1, 0)
    right = fold(fold(right, 1, 1), 0, 0)
    return jnp.concatenate([left, right], axis=-1)


def spread_group(block):
    width = block.shape[-1]
    left, right = block[:, : width // 2], block[:, width // 2 :]
    left = join(join(left, 0, 0), 1, 1)
    right = join(join(right, 1, 0), 0, 0)
    whole = join(jnp.concatenate([left, right], axis=-1), 2, 2)
    return whole.reshape(-1, width)


def spread_lanes(block):
    return join(join(block, 1, 0), 2, 1).reshape(-1, block.shape[-1])


def spread_chunk(block):
    block = jnp.concatenate([block, swapped(block, "tensor", 2)], axis=0)
    return jnp.concatenate([block, swapped(block, "tensor", 1)], axis=0)


def collect_chunk(partial):
    half = partial.shape[0] // 2
    partial = partial[:half] + swapped(partial[half:].astype(b16), "tensor", 1).astype(f32)
    half = half // 2
    return partial[:half] + swapped(partial[half:].astype(b16), "tensor", 2).astype(f32)


def on_device(
    tokens,
    segments,
    w_query,
    key_weight,
    value_weight,
    w_output,
    w_gate,
    w_up,
    w_down,
    pre_attn_gain,
    post_attn_gain,
    pre_ffw_gain,
    post_ffw_gain,
    cotangent,
):
    n = lax.axis_size("dp")
    place = lax.axis_index("dp")
    side = lax.axis_index("context")
    lane = lax.axis_index("tensor")
    lanes = lax.axis_size("tensor")
    rows, width = tokens.shape
    group = 2 * rows
    sub = rows // lanes
    deep = width // n
    reach = min((SLIDE_WINDOW + group - 2) // group, n - 1)
    is_first = side == 0

    def half_of(value, which, axis):
        size = value.shape[axis] // 2
        low = lax.slice_in_dim(value, 0, size, axis=axis)
        high = lax.slice_in_dim(value, size, 2 * size, axis=axis)
        return jnp.where(which == 0, low, high)

    def with_rider(block, values):
        rider = jnp.zeros((16 * HEAD_SIZE - values.size,), b16)
        rider = jnp.concatenate([values.astype(b16).reshape(-1), rider])
        return jnp.concatenate([block, rider.reshape(16, HEAD_SIZE)], axis=0)

    def split_rider(blocks, count):
        size = blocks.shape[1] - 16
        rider = blocks[:, size:].reshape(blocks.shape[0], -1)[:, :count]
        return blocks[:, :size], rider

    gains = jnp.concatenate([pre_attn_gain, post_attn_gain, pre_ffw_gain, post_ffw_gain])
    pair_got = gathered(
        with_rider(jnp.where(is_first, key_weight, value_weight), gains), "dp"
    )
    group_tokens = join(tokens, 0, 0).reshape(group, width).astype(f32)
    segment_pair = join(segments[None].astype(b16), 0, 0)
    pair_in, gains = split_rider(pair_got, 4 * deep)
    pair_in = pair_in.reshape(width, HEAD_SIZE)
    gains = 1.0 + jnp.swapaxes(gains.reshape(n, 4, deep), 0, 1).reshape(4, width).astype(f32)
    query_got = gathered(
        after(with_rider(half_of(w_query, side, 1), segment_pair), pair_got), "dp"
    )
    query_in, all_segments = split_rider(query_got, group)
    query_in = query_in.reshape(width, HEAD_SIZE)
    all_segments = all_segments.reshape(-1).astype(jnp.int32)
    w_out_got = gathered(after(half_of(w_output, side, 0), query_got), "dp")
    w_out = jnp.swapaxes(w_out_got, 0, 1).reshape(HEAD_SIZE, width)

    units = w_gate.shape[1] // n

    def unit_blocks(weight):
        return jnp.swapaxes(half_of(weight, side, 0).reshape(deep // 2, n, units), 0, 1)

    gate_blocks = unit_blocks(after(w_gate, pair_got))
    up_blocks = unit_blocks(after(w_up, pair_got))
    down_blocks = half_of(after(w_down, pair_got).reshape(n, units, deep), side, 1)
    gate_got = exchange(after(gate_blocks, w_out_got), "dp")
    up_got = exchange(after(up_blocks, gate_got), "dp")
    down_got = exchange(after(down_blocks, up_got), "dp")
    gate_w = join(gate_got, 0, 1).reshape(width, units)
    up_w = join(after(up_got, gate_w), 0, 1).reshape(width, units)
    down_half = jnp.swapaxes(after(down_got, up_w), 0, 1).reshape(units // 2, width)
    down_w = join(down_half, 0, 0).reshape(units, width)

    scale_one = rms_scale(group_tokens)
    normed_one = group_tokens * scale_one
    lifted_one = (normed_one * gains[0]).astype(b16)
    positions = place * group + jnp.arange(group, dtype=jnp.int32)
    cosine_table, sine_table = rotary_tables(positions)
    mine = dot(lifted_one, pair_in)
    mine = jnp.where(is_first, apply_rotary(mine, cosine_table, sine_table), mine).astype(b16)
    mine = [mine] + [shifted(mine, "dp", steps) for steps in range(1, reach + 1)]
    theirs = [swapped(block, "context", 1) for block in mine]
    mine[0] = after(mine[0], gate_blocks, up_blocks, down_blocks)
    mine = jnp.concatenate(mine[::-1], axis=0)
    theirs = jnp.concatenate(theirs[::-1], axis=0)
    keys = jnp.where(is_first, mine, theirs)
    values = jnp.where(is_first, theirs, mine)
    queries = (
        apply_rotary(dot(lifted_one, query_in), cosine_table, sine_table) * HEAD_SIZE ** (-0.5)
    ).astype(b16)
    span = (reach + 1) * group
    key_positions = (place - reach) * group + jnp.arange(span, dtype=jnp.int32)
    padded = jnp.concatenate([jnp.full((reach * group,), -1, jnp.int32), all_segments])
    key_segments = lax.dynamic_slice_in_dim(padded, place * group, span)
    query_segments = key_segments[reach * group :]
    valid = (key_positions[None, :] <= positions[:, None]) & (
        positions[:, None] - key_positions[None, :] < SLIDE_WINDOW
    )
    valid = valid & (key_positions[None, :] >= 0)
    valid = valid & (key_segments[None, :] == query_segments[:, None])
    bent = jnp.tanh(dot_nt(queries, keys) / softcap)
    masked = jnp.where(valid, softcap * bent, negative)
    weights = jnp.exp(masked - jnp.max(masked, axis=-1, keepdims=True))
    probs = weights / jnp.sum(weights, axis=-1, keepdims=True)
    probs_low = probs.astype(b16)
    mixed = dot(after(probs_low, w_out_got), values).astype(b16)
    branch = collect_group(dot(mixed, w_out), sub)
    branch = after(branch, gate_got)

    own_tokens = lax.dynamic_slice_in_dim(tokens, lane * sub, sub).astype(f32)
    grad_out = lax.dynamic_slice_in_dim(cotangent, lane * sub, sub).astype(f32)
    scale_two = rms_scale(branch)
    normed_two = branch * scale_two
    middle = own_tokens + normed_two * gains[1]
    scale_three = rms_scale(middle)
    normed_three = middle * scale_three
    lifted_two = (normed_three * gains[2]).astype(b16)
    lifted_two = after(lifted_two, up_got, gate_w)
    lifted_two = [lifted_two] + [
        rotated(after(lifted_two, down_got), steps) for steps in range(1, n)
    ]
    lifted_two = [spread_chunk(block) for block in lifted_two]
    lifted_two[0] = after(lifted_two[0], up_w, down_got)
    gate = [dot(chunk, gate_w) for chunk in lifted_two]
    upper = [dot(chunk, up_w) for chunk in lifted_two]
    hidden = [gated(*pair).astype(b16) for pair in zip(gate, upper)]
    down = [collect_chunk(dot(chunk, down_w)) for chunk in hidden]
    down = down[0] + sum(
        rotated(down[steps].astype(b16), -steps).astype(f32) for steps in range(1, n)
    )
    scale_four = rms_scale(down)
    normed_four = down * scale_four
    output = (middle + normed_four * gains[3]).astype(b16)

    def unit_grad(left, right):
        partial = dot_tn(jnp.concatenate(left, axis=0), jnp.concatenate(right, axis=0))
        return fold(partial.reshape(n, 2, deep // 2, units), 0, 1).astype(b16)

    grad_down = rms_back(grad_out * gains[3], normed_four, scale_four).astype(b16)
    grad_down = [grad_down] + [rotated(grad_down, steps) for steps in range(1, n)]
    grad_down = [spread_chunk(block) for block in grad_down]
    output = spread_lanes(after(output, *grad_down))
    grad_gate, grad_upper, lifted_grad = [], [], []
    for steps in range(n):
        unused, pull = jax.vjp(gated, gate[steps], upper[steps])
        pair = [side.astype(b16) for side in pull(dot_nt(grad_down[steps], down_w))]
        grad_gate.append(pair[0])
        grad_upper.append(pair[1])
        lifted_grad.append(collect_chunk(dot_nt(pair[0], gate_w) + dot_nt(pair[1], up_w)))
    down_part = unit_grad(grad_down, hidden)
    grad_gate[0] = after(grad_gate[0], *lifted_grad)
    gate_part = unit_grad(lifted_two, grad_gate)
    lifted_grad = lifted_grad[0] + sum(
        rotated(lifted_grad[steps].astype(b16), -steps).astype(f32) for steps in range(1, n)
    )
    lifted_grad = after(lifted_grad, down_part)
    grad_middle = grad_out + rms_back(lifted_grad * gains[2], normed_three, scale_three)
    grad_branch = rms_back(grad_middle * gains[1], normed_two, scale_two).astype(b16)
    grad_branch = after(grad_branch, gate_part, output)
    grad_w_down = exchange(after(down_part, grad_branch), "dp")
    grad_upper[0] = after(grad_upper[0], grad_branch)
    up_part = unit_grad(lifted_two, grad_upper)
    grad_branch = spread_group(grad_branch)

    grad_branch = after(grad_branch, grad_w_down, up_part)
    grad_w_gate = exchange(after(gate_part, grad_w_down), "dp")
    grad_mixed = dot_nt(grad_branch, w_out).astype(b16)
    grad_probs = dot_nt(grad_mixed, values)
    grad_capped = probs * (grad_probs - jnp.sum(probs * grad_probs, axis=-1, keepdims=True))
    grad_raw = (grad_capped * (1.0 - bent * bent)).astype(b16)
    grad_keys = dot_tn(grad_raw, queries)
    grad_values = dot_tn(probs_low, grad_mixed)
    kept = jnp.where(is_first, grad_keys, grad_values)
    sent = jnp.where(is_first, grad_values, grad_keys).astype(b16)
    sent = after(sent, grad_w_gate)
    grad_w_up = exchange(after(up_part, grad_w_gate), "dp")
    kept = kept + swapped(sent, "context", 1).astype(f32)
    kept = after(kept, grad_w_up)
    kept = kept.reshape(reach + 1, group, HEAD_SIZE)
    mine = kept[reach]
    for steps in range(1, reach + 1):
        mine = mine + shifted(kept[reach - steps].astype(b16), "dp", -steps).astype(f32)
    grad_queries = dot(grad_raw, keys)
    grad_query_pre = rotate_back(grad_queries, cosine_table, sine_table) * HEAD_SIZE ** (-0.5)
    grad_query_pre = grad_query_pre.astype(b16)
    grad_w_out = dot_tn(mixed, grad_branch)
    grad_w_out = jnp.swapaxes(grad_w_out.astype(b16).reshape(HEAD_SIZE, n, deep), 0, 1)
    grad_w_out = exchange(after(grad_w_out, mine), "dp")
    mine = jnp.where(is_first, rotate_back(mine, cosine_table, sine_table), mine).astype(b16)
    first_grad = dot_nt(grad_query_pre, query_in) + dot_nt(mine, pair_in)
    first_grad = collect_group(first_grad, sub)
    own_scale = rms_scale(own_tokens)
    own_normed = own_tokens * own_scale
    grad_inputs = grad_middle + rms_back(first_grad * gains[0], own_normed, own_scale)
    grad_inputs = spread_lanes(grad_inputs.astype(b16)).astype(f32)
    grad_gains = jnp.stack(
        [
            jnp.sum(first_grad * own_normed, axis=0),
            jnp.sum(grad_middle * normed_two, axis=0),
            jnp.sum(lifted_grad * normed_three, axis=0),
            jnp.sum(grad_out * normed_four, axis=0),
        ]
    )

    def row_blocks(right):
        return dot_tn(lifted_one, right).astype(b16).reshape(n, deep, HEAD_SIZE)

    grad_w_query = exchange(after(row_blocks(grad_query_pre), grad_w_out), "dp")
    rider = jnp.swapaxes(grad_gains.astype(b16).reshape(4, n, deep), 0, 1).reshape(n, -1)
    rider = jnp.pad(rider, ((0, 0), (0, 16 * HEAD_SIZE - rider.shape[1])))
    rider = jnp.concatenate([row_blocks(mine), rider.reshape(n, 16, HEAD_SIZE)], axis=1)
    grad_pair = summed(exchange(after(rider, grad_w_query), "dp"))
    grad_gains = grad_pair[deep:].reshape(-1)[: 4 * deep].reshape(4, 2, deep // 2)
    grad_gains, sent = picked(is_first, (grad_gains[:, 0], grad_gains[:, 1]))
    grad_gains = grad_gains + swapped(sent, "context", 1)
    grad_gains = grad_gains + swapped(grad_gains, "tensor", 2)
    grad_gains = grad_gains + swapped(grad_gains, "tensor", 1)

    def halves(total):
        kept, sent = picked(is_first, (total[: deep // 2], total[deep // 2 : deep]))
        return kept, swapped(sent.astype(b16), "context", 1).astype(f32)

    grad_w_query = jnp.concatenate(picked(is_first, halves(summed(grad_w_query))), axis=1)
    grad_w_key, grad_w_value = picked(is_first, halves(grad_pair))
    grad_w_out = summed(grad_w_out)
    kept = half_of(grad_w_out, side, 1)
    got = swapped(half_of(grad_w_out, 1 - side, 1).astype(b16), "context", 1).astype(f32)
    grad_w_out = jnp.concatenate(picked(is_first, (kept, got)), axis=0)

    grad_w_down = jnp.swapaxes(grad_w_down, 1, 2).reshape(n * units, deep // 2).astype(f32)
    grad_w_gate = jnp.swapaxes(grad_w_gate, 0, 1).reshape(deep // 2, n * units).astype(f32)
    grad_w_up = jnp.swapaxes(grad_w_up, 0, 1).reshape(deep // 2, n * units).astype(f32)
    return (
        output,
        grad_inputs,
        grad_w_query,
        grad_w_key,
        grad_w_value,
        grad_w_out,
        grad_w_gate,
        grad_w_up,
        grad_w_down,
        grad_gains[0],
        grad_gains[1],
        grad_gains[2],
        grad_gains[3],
    )


def solution(mesh):
    return jax.shard_map(
        on_device,
        mesh=mesh,
        in_specs=(
            P(("dp", "context"), None),
            P(("dp", "context")),
            P("dp", "tensor"),
            P("dp", "tensor"),
            P("dp", "tensor"),
            P("tensor", "dp"),
            P("dp", "tensor"),
            P("dp", "tensor"),
            P("tensor", "dp"),
            P("dp"),
            P("dp"),
            P("dp"),
            P("dp"),
            P(("dp", "context"), None),
        ),
        out_specs=(
            P(("dp", "context"), None),
            P(("dp", "context"), None),
            P(("dp", "context"), "tensor"),
            P(("dp", "context"), "tensor"),
            P(("dp", "context"), "tensor"),
            P("tensor", ("dp", "context")),
            P(("dp", "context"), "tensor"),
            P(("dp", "context"), "tensor"),
            P("tensor", ("dp", "context")),
            P(("dp", "context")),
            P(("dp", "context")),
            P(("dp", "context")),
            P(("dp", "context")),
        ),
        check_vma=False,
    )
```

time: 1060 us -> 855 us (0.81)
  waiting for transfers between devices: 635 us -> 439 us
  blocking collectives: 30.7 us -> 0 us
  other arithmetic: 76.6 us -> 89 us
    all_to_all x22 -> x12, waiting for transfers between devices: 320 us -> 116 us  [exchange(): return lax.all_to_all(blocks, axis, 0, 0, tiled=True)]
    ppermute x0 -> x12, waiting for transfers between devices: none -> 54.8 us  [rotated(): return lax.ppermute(value, 'dp', [(s, (s + steps) % n) for s in range(n)])]
    ppermute x6, waiting for transfers between devices: 63.8 us -> 19.1 us  [shifted(): lax.ppermute(value, axis, [(s, s + steps) for s in range(count) if 0 <= s...]
    all_to_all x22 -> x12, starting transfers between devices: 101 us -> 57.1 us  [exchange(): return lax.all_to_all(blocks, axis, 0, 0, tiled=True)]
    ppermute x22 -> x70, starting transfers between devices: 19.3 us -> 53.4 us  [swapped(): lax.ppermute(value, axis, [(place, place ^ bit) for place in range(count)])]
    all_to_all x1 -> x0, blocking collectives: 30.7 us -> none  [exchange(): return lax.all_to_all(blocks, axis, 0, 0, tiled=True)]
    ppermute x0 -> x12, starting transfers between devices: none -> 16.8 us  [rotated(): return lax.ppermute(value, 'dp', [(s, (s + steps) % n) for s in range(n)])]
    dot_general x2 -> x0, local copies, waits for them, and re-layouts: 13.3 us -> none  [dot_tn(): lax.dot_general(left, right, (((0,), (0,)), ((), ())), preferred_element_...]
  transfers between devices with their start and end apart: 50 -> 100, of which waited for: 36 -> 52; matrix products, arithmetic and copies ran while one was open for 18% -> 26% of each run, Pallas kernels for 0% -> 0%
where the time goes in v2:
time: 855 us; the launch traced here: 846 us
  waiting for transfers between devices  439 us (51%)
  starting transfers between devices  142 us (17%)
  local copies, waits for them, and re-layouts  93 us (11%)
  other arithmetic  89 us (10%)
  matrix products  79.7 us (9%)
    ppermute x70, waiting for transfers between devices, swapped(): lax.ppermute(value, axis, [(place, place ^ bit) for place in range(count)])  249 us
    all_to_all x12, waiting for transfers between devices, exchange(): return lax.all_to_all(blocks, axis, 0, 0, tiled=True)  116 us
    all_to_all x12, starting transfers between devices, exchange(): return lax.all_to_all(blocks, axis, 0, 0, tiled=True)  57.1 us
    ppermute x12, waiting for transfers between devices, rotated(): return lax.ppermute(value, 'dp', [(s, (s + steps) % n) for s in range(n)])  54.8 us
    ppermute x70, starting transfers between devices, swapped(): lax.ppermute(value, axis, [(place, place ^ bit) for place in range(count)])  53.4 us
    dot_general x8, matrix products, dot_tn(): lax.dot_general(left, right, (((0,), (0,)), ((), ())), preferred_element_...  27.3 us
    dot_general x17, matrix products, dot(): return jnp.dot(left, right, preferred_element_type=f32)  27 us
    dot_general x17, matrix products, dot_nt(): lax.dot_general(left, right, (((1,), (1,)), ((), ())), preferred_element_...  25.3 us
  transfers between devices with their start and end apart: 100, of which 52 were waited for; matrix products, arithmetic and copies ran while one was open for 26% of the time, Pallas kernels for 0%

profile of v2, /device:TPU:0, one launch (start us, length us, event | category | flops | bytes accessed | tf_op | source)
XLA Modules:
  0.0 846.1 jit_solution(8566335260936832453)
XLA Ops:
  9.3 4.9 all-to-all-start
  18.6 22.8 %collective-permute-done.1 = bf16[256,2304]{1,0:T(8,128)(2,1)} collective-permute-done((bf16[256,2304]{1,0:T(8,128)(2,1)S(1)}, bf16[256,2304]{1,0:T(8,128)(2,1)}, u32[]{:S(2)}, u32[]{:S(2)}) %collective-permute-start.1) | collective-permute-done | bytes 1179680 | tf_op jit(solution)/shard_map/ppermute | solution.py:59
  51.5 4.3 collective-permute-start.4
  55.8 4.3 collective-permute-start.3
  63.2 4.3 all-to-all-start.1
  67.5 3.8 slice_select_fusion.1
  71.4 3.4 reshape.434
  79.1 4.0 copy.173
  92.1 9.4 %collective-permute-done.5 = bf16[512,256]{0,1:T(8,128)(2,1)S(1)} collective-permute-done((bf16[512,256]{0,1:T(8,128)(2,1)}, bf16[512,256]{0,1:T(8,128)(2,1)S(1)}, u32[]{:S(2)}, u32[]{:S(2)}) %collective-permute-start.5) | collective-permute-done | bytes 262176 | tf_op jit(solution)/shard_map/ppermute | solution.py:59
  103.7 5.7 all-to-all-start.2
  113.5 4.2 fusion.164
  120.6 14.0 %all-to-all-done.2 = bf16[4,256,576]{1,2,0:T(8,128)(2,1)S(1)} async-done(((bf16[4,256,576]{1,2,0:T(8,128)(2,1)}), bf16[4,256,576]{1,2,0:T(8,128)(2,1)S(1)}, u32[]{:S(2)}, u32[]{:S(2)}) %all-to-all-start.2) | async-done | bytes 1179680 | tf_op jit(solution)/shard_map/all_to_all | solution.py:49
  148.8 4.4 all-to-all-start.3
  161.0 27.4 %all-to-all-done.3 = bf16[4,288,576]{2,1,0:T(8,128)(2,1)} async-done(((bf16[4,288,576]{2,1,0:T(8,128)(2,1)}), bf16[4,288,576]{2,1,0:T(8,128)(2,1)}, u32[]{:S(2)}, u32[]{:S(2)}) %all-to-all-start.3) | async-done | bytes 1327136 | tf_op jit(solution)/shard_map/all_to_all | solution.py:49
  188.4 4.3 all-to-all-start.4
  196.9 29.5 %collective-permute-done.14 = bf16[4,288,576]{2,1,0:T(8,128)(2,1)S(1)} collective-permute-done((bf16[4,288,576]{2,1,0:T(8,128)(2,1)}, bf16[4,288,576]{2,1,0:T(8,128)(2,1)S(1)}, u32[]{:S(2)}, u32[]{:S(2)}) %collective-permute-start.14) | collective-permute-done | bytes 1327136 | tf_op jit(solution)/shard_map/ppermute | solution.py:59
  229.4 4.8 all-to-all-start.5
  241.7 24.5 %collective-permute-done.17 = bf16[4,288,576]{2,1,0:T(8,128)(2,1)S(1)} collective-permute-done((bf16[4,288,576]{2,1,0:T(8,128)(2,1)}, bf16[4,288,576]{2,1,0:T(8,128)(2,1)S(1)}, u32[]{:S(2)}, u32[]{:S(2)}) %collective-permute-start.17) | collective-permute-done | bytes 1327136 | tf_op jit(solution)/shard_map/ppermute | solution.py:59
  269.9 3.4 collective-permute-start.33
  277.7 4.2 reshape.439
  289.1 6.4 collective-permute-done.27
  299.6 7.5 collective-permute-done.22
  335.9 11.7 %collective-permute-done.37 = bf16[64,2304]{1,0:T(8,128)(2,1)S(1)} collective-permute-done((bf16[64,2304]{1,0:T(8,128)(2,1)S(1)}, bf16[64,2304]{1,0:T(8,128)(2,1)S(1)}, u32[]{:S(2)}, u32[]{:S(2)}) %collective-permute-start.37) | collective-permute-done | bytes 294944 | tf_op jit(solution)/shard_map/ppermute | solution.py:59
  350.5 3.4 collective-permute-done.31
  365.1 6.5 collective-permute-done.32
  382.8 4.2 collective-permute-start.47
  387.7 6.8 collective-permute-done.47
  394.9 16.9 %collective-permute-done.44 = bf16[64,2304]{1,0:T(8,128)(2,1)S(1)} collective-permute-done((bf16[64,2304]{1,0:T(8,128)(2,1)S(1)}, bf16[64,2304]{1,0:T(8,128)(2,1)S(1)}, u32[]{:S(2)}, u32[]{:S(2)}) %collective-permute-start.44) | collective-permute-done | bytes 294944 | tf_op jit(solution)/shard_map/ppermute | solution.py:95
  414.0 7.8 collective-permute-done.45
  431.6 3.9 fusion.20
  456.5 12.1 %collective-permute-done.61 = bf16[64,2304]{1,0:T(8,128)(2,1)S(1)} collective-permute-done((bf16[64,2304]{1,0:T(8,128)(2,1)S(1)}, bf16[64,2304]{1,0:T(8,128)(2,1)S(1)}, u32[]{:S(2)}, u32[]{:S(2)}) %collective-permute-start.61) | collective-permute-done | bytes 294944 | tf_op jit(solution)/shard_map/ppermute | solution.py:59
  470.1 4.9 collective-permute-done.58
  475.1 5.3 collective-permute-done.55
  482.0 4.8 collective-permute-done.62
  486.8 9.9 %collective-permute-done.59 = bf16[64,2304]{1,0:T(8,128)(2,1)S(1)} collective-permute-done((bf16[64,2304]{1,0:T(8,128)(2,1)S(1)}, bf16[64,2304]{1,0:T(8,128)(2,1)S(1)}, u32[]{:S(2)}, u32[]{:S(2)}) %collective-permute-start.59) | collective-permute-done | bytes 294944 | tf_op jit(solution)/shard_map/ppermute | solution.py:95
  497.4 3.9 fusion.28
  505.5 29.9 %collective-permute-done.64 = bf16[4,288,576]{2,1,0:T(8,128)(2,1)S(1)} collective-permute-done((bf16[4,288,576]{2,1,0:T(8,128)(2,1)S(1)}, bf16[4,288,576]{2,1,0:T(8,128)(2,1)S(1)}, u32[]{:S(2)}, u32[]{:S(2)}) %collective-permute-start.64) | collective-permute-done | bytes 1327136 | tf_op jit(solution)/shard_map/ppermute | solution.py:59
  538.7 5.7 fusion.36
  544.5 8.2 all-to-all-start.6
  558.9 3.3 collective-permute-done.68
  567.4 24.6 %collective-permute-done.70 = bf16[4,288,576]{2,1,0:T(8,128)(2,1)S(1)} collective-permute-done((bf16[4,288,576]{2,1,0:T(8,128)(2,1)S(1)}, bf16[4,288,576]{2,1,0:T(8,128)(2,1)S(1)}, u32[]{:S(2)}, u32[]{:S(2)}) %collective-permute-start.70) | collective-permute-done | bytes 1327136 | tf_op jit(solution)/shard_map/ppermute | solution.py:59
  594.4 5.0 all-to-all-start.7
  608.7 24.1 %all-to-all-done.7 = bf16[4,288,576]{2,1,0:T(8,128)(2,1)} async-done(((bf16[4,288,576]{2,1,0:T(8,128)(2,1)}), bf16[4,288,576]{2,1,0:T(8,128)(2,1)}, u32[]{:S(2)}, u32[]{:S(2)}) %all-to-all-start.7) | async-done | bytes 1327136 | tf_op jit(solution)/shard_map/all_to_all | solution.py:49
  632.8 4.3 all-to-all-start.8
  637.2 4.1 select_convert_fusion.5
  644.0 3.5 convolution_convert_fusion.1
  653.8 11.9 %collective-permute-done.71 = bf16[2048,256]{0,1:T(8,128)(2,1)} collective-permute-done((bf16[2048,256]{0,1:T(8,128)(2,1)}, bf16[2048,256]{0,1:T(8,128)(2,1)}, u32[]{:S(2)}, u32[]{:S(2)}) %collective-permute-start.71) | collective-permute-done | bytes 1048608 | tf_op jit(solution)/shard_map/ppermute | solution.py:59
  678.1 11.2 %collective-permute-done.72 = bf16[512,256]{0,1:T(8,128)(2,1)S(1)} collective-permute-done((bf16[512,256]{0,1:T(8,128)(2,1)S(1)}, bf16[512,256]{0,1:T(8,128)(2,1)S(1)}, u32[]{:S(2)}, u32[]{:S(2)}) %collective-permute-start.72) | collective-permute-done | bytes 262176 | tf_op jit(solution)/shard_map/ppermute | solution.py:72
  689.3 7.9 collective-permute-done.73
  704.7 3.5 copy.161
  708.3 4.5 reshape.457
  712.8 3.6 convolution_convert_fusion.2
  718.0 3.5 copy.159
  721.5 4.5 reshape.455
  727.6 3.5 copy.160
  731.1 4.7 reshape.456
  735.8 4.3 all-to-all-start.9
  746.0 6.2 collective-permute-done.76
  760.9 8.7 %all-to-all-done.9 = bf16[4,256,576]{1,2,0:T(8,128)(2,1)} async-done(((bf16[4,256,576]{1,2,0:T(8,128)(2,1)}), bf16[4,256,576]{1,2,0:T(8,128)(2,1)}, u32[]{:S(2)}, u32[]{:S(2)}) %all-to-all-start.9) | async-done | bytes 1179680 | tf_op jit(solution)/shard_map/all_to_all | solution.py:49
  769.6 3.5 all-to-all-start.10
  778.5 5.9 collective-permute-done.80
  787.9 13.9 %all-to-all-done.10 = bf16[4,576,256]{2,1,0:T(8,128)(2,1)S(1)} async-done(((bf16[4,576,256]{2,1,0:T(8,128)(2,1)}), bf16[4,576,256]{2,1,0:T(8,128)(2,1)S(1)}, u32[]{:S(2)}, u32[]{:S(2)}) %all-to-all-start.10) | async-done | bytes 1179680 | tf_op jit(solution)/shard_map/all_to_all | solution.py:49
  802.9 3.5 all-to-all-start.11
  810.3 24.9 %all-to-all-done.11 = bf16[4,592,256]{2,1,0:T(8,128)(2,1)S(1)} async-done(((bf16[4,592,256]{2,1,0:T(8,128)(2,1)}), bf16[4,592,256]{2,1,0:T(8,128)(2,1)S(1)}, u32[]{:S(2)}, u32[]{:S(2)}) %all-to-all-start.11) | async-done | bytes 1212448 | tf_op jit(solution)/shard_map/all_to_all | solution.py:49
  (643 shorter events, 296.4 us)
Async XLA Ops:
  1.3 16.5 %collective-permute-start = (bf16[1,256]{1,0:T(2,128)(2,1)S(1)}, bf16[1,256]{1,0:T(2,128)(2,1)S(1)}, u32[]{:S(2)}, u32[]{:S(2)}) collective-permute-start(bf16[1,256]{1,0:T(2,128)(2,1)S(1)} %convert_element_type.461), channel_id=1, source_target_pairs={{0,4},{4,0},{1,5},{5,1},{2,6},{6,2},{3,7},{7,3},{8,12},{12,8},{9,1... | collective-permute-start | bytes 1544 | tf_op jit(solution)/shard_map/ppermute | solution.py:59
  9.3 34.9 %all-to-all-start = ((bf16[4,592,256]{2,1,0:T(8,128)(2,1)}), bf16[4,592,256]{2,1,0:T(8,128)(2,1)}, u32[]{:S(2)}, u32[]{:S(2)}) async-start(bf16[4,592,256]{2,1,0:T(8,128)(2,1)} %broadcast_in_dim.12), calls=%async_computation | async-start | bytes 2424832 | tf_op jit(solution)/shard_map/all_to_all | solution.py:49
  14.2 27.3 %collective-permute-start.1 = (bf16[256,2304]{1,0:T(8,128)(2,1)S(1)}, bf16[256,2304]{1,0:T(8,128)(2,1)}, u32[]{:S(2)}, u32[]{:S(2)}) collective-permute-start(bf16[256,2304]{1,0:T(8,128)(2,1)S(1)} %copy-done.28), channel_id=1, source_target_pairs={{0,4},{4,0},{1,5},{5,1},{2,6},{6,2},{3,7},{7,3},{8,12},{12,8},{9,1... | collective-permute-start | bytes 3538952 | tf_op jit(solution)/shard_map/ppermute | solution.py:59
  50.9 50.6 %collective-permute-start.8 = (bf16[512,256]{0,1:T(8,128)(2,1)S(1)}, bf16[512,256]{0,1:T(8,128)(2,1)S(1)}, u32[]{:S(2)}, u32[]{:S(2)}) collective-permute-start(bf16[512,256]{0,1:T(8,128)(2,1)S(1)} %fusion.97), channel_id=1, source_target_pairs={{0,4},{4,0},{1,5},{5,1},{2,6},{6,2},{3,7},{7,3},{8,12},{12,8},{9,1... | collective-permute-start | bytes 786440 | tf_op jit(solution)/shard_map/ppermute | solution.py:59
  51.5 33.0 %collective-permute-start.4 = (bf16[512,256]{0,1:T(8,128)(2,1)S(1)}, bf16[512,256]{0,1:T(8,128)(2,1)}, u32[]{:S(2)}, u32[]{:S(2)}) collective-permute-start(bf16[512,256]{0,1:T(8,128)(2,1)S(1)} %fusion.97), channel_id=1, source_target_pairs={{0,8},{8,16},{16,24},{1,9},{9,17},{17,25},{2,10},{10,18},{18,26},{... | collective-permute-start | bytes 786440 | tf_op jit(solution)/shard_map/ppermute | solution.py:72
  55.8 30.2 %collective-permute-start.3 = (bf16[512,256]{0,1:T(8,128)(2,1)S(1)}, bf16[512,256]{0,1:T(8,128)(2,1)}, u32[]{:S(2)}, u32[]{:S(2)}) collective-permute-start(bf16[512,256]{0,1:T(8,128)(2,1)S(1)} %fusion.97), channel_id=1, source_target_pairs={{0,16},{8,24},{1,17},{9,25},{2,18},{10,26},{3,19},{11,27},{4,20},{... | collective-permute-start | bytes 786440 | tf_op jit(solution)/shard_map/ppermute | solution.py:72
  60.1 26.5 %collective-permute-start.2 = (bf16[512,256]{0,1:T(8,128)(2,1)S(1)}, bf16[512,256]{0,1:T(8,128)(2,1)}, u32[]{:S(2)}, u32[]{:S(2)}) collective-permute-start(bf16[512,256]{0,1:T(8,128)(2,1)S(1)} %fusion.97), channel_id=1, source_target_pairs={{0,24},{1,25},{2,26},{3,27},{4,28},{5,29},{6,30},{7,31}} | collective-permute-start | bytes 786440 | tf_op jit(solution)/shard_map/ppermute | solution.py:72
  63.2 38.4 %all-to-all-start.1 = ((bf16[4,592,256]{2,1,0:T(8,128)(2,1)}), bf16[4,592,256]{2,1,0:T(8,128)(2,1)}, u32[]{:S(2)}, u32[]{:S(2)}) async-start(bf16[4,592,256]{2,1,0:T(8,128)(2,1)} %broadcast_in_dim.13), calls=%async_computation.1 | async-start | bytes 2424832 | tf_op jit(solution)/shard_map/all_to_all | solution.py:49
  84.5 17.0 %collective-permute-start.7 = (bf16[512,256]{0,1:T(8,128)(2,1)}, bf16[512,256]{0,1:T(8,128)(2,1)S(1)}, u32[]{:S(2)}, u32[]{:S(2)}) collective-permute-start(bf16[512,256]{0,1:T(8,128)(2,1)} %collective-permute-done.4), channel_id=1, source_target_pairs={{0,4},{4,0},{1,5},{5,1},{2,6},{6,2},{3,7},{7,3},{8,12},{12,8},{9,1... | collective-permute-start | bytes 786440 | tf_op jit(solution)/shard_map/ppermute | solution.py:59
  86.0 15.4 %collective-permute-start.6 = (bf16[512,256]{0,1:T(8,128)(2,1)}, bf16[512,256]{0,1:T(8,128)(2,1)S(1)}, u32[]{:S(2)}, u32[]{:S(2)}) collective-permute-start(bf16[512,256]{0,1:T(8,128)(2,1)} %collective-permute-done.3), channel_id=1, source_target_pairs={{0,4},{4,0},{1,5},{5,1},{2,6},{6,2},{3,7},{7,3},{8,12},{12,8},{9,1... | collective-permute-start | bytes 786440 | tf_op jit(solution)/shard_map/ppermute | solution.py:59
  86.6 14.9 %collective-permute-start.5 = (bf16[512,256]{0,1:T(8,128)(2,1)}, bf16[512,256]{0,1:T(8,128)(2,1)S(1)}, u32[]{:S(2)}, u32[]{:S(2)}) collective-permute-start(bf16[512,256]{0,1:T(8,128)(2,1)} %collective-permute-done.2), channel_id=1, source_target_pairs={{0,4},{4,0},{1,5},{5,1},{2,6},{6,2},{3,7},{7,3},{8,12},{12,8},{9,1... | collective-permute-start | bytes 786440 | tf_op jit(solution)/shard_map/ppermute | solution.py:59
  103.7 31.0 %all-to-all-start.2 = ((bf16[4,256,576]{1,2,0:T(8,128)(2,1)}), bf16[4,256,576]{1,2,0:T(8,128)(2,1)S(1)}, u32[]{:S(2)}, u32[]{:S(2)}) async-start(bf16[4,256,576]{1,2,0:T(8,128)(2,1)} %broadcast_in_dim.15), calls=%async_computation.2 | async-start | bytes 2359296 | tf_op jit(solution)/shard_map/all_to_all | solution.py:49
  148.8 39.6 %all-to-all-start.3 = ((bf16[4,288,576]{2,1,0:T(8,128)(2,1)}), bf16[4,288,576]{2,1,0:T(8,128)(2,1)}, u32[]{:S(2)}, u32[]{:S(2)}) async-start(bf16[4,288,576]{2,1,0:T(8,128)(2,1)} %bitcast.373), calls=%async_computation.3 | async-start | bytes 2949120 | tf_op jit(solution)/shard_map/all_to_all | solution.py:49
  188.4 40.4 %all-to-all-start.4 = ((bf16[4,288,576]{2,1,0:T(8,128)(2,1)}), bf16[4,288,576]{2,1,0:T(8,128)(2,1)}, u32[]{:S(2)}, u32[]{:S(2)}) async-start(bf16[4,288,576]{2,1,0:T(8,128)(2,1)} %bitcast.331), calls=%async_computation.4 | async-start | bytes 2949120 | tf_op jit(solution)/shard_map/all_to_all | solution.py:49
  192.9 33.6 %collective-permute-start.14 = (bf16[4,288,576]{2,1,0:T(8,128)(2,1)}, bf16[4,288,576]{2,1,0:T(8,128)(2,1)S(1)}, u32[]{:S(2)}, u32[]{:S(2)}) collective-permute-start(bf16[4,288,576]{2,1,0:T(8,128)(2,1)} %all-to-all-done.3), channel_id=1, source_target_pairs={{0,4},{4,0},{1,5},{5,1},{2,6},{6,2},{3,7},{7,3},{8,12},{12,8},{9,1... | collective-permute-start | bytes 3981320 | tf_op jit(solution)/shard_map/ppermute | solution.py:59
  229.4 40.5 %all-to-all-start.5 = ((bf16[4,288,576]{2,1,0:T(8,128)(2,1)}), bf16[4,288,576]{2,1,0:T(8,128)(2,1)}, u32[]{:S(2)}, u32[]{:S(2)}) async-start(bf16[4,288,576]{2,1,0:T(8,128)(2,1)} %slice_select_fusion), calls=%async_computation.5 | async-start | bytes 2949120 | tf_op jit(solution)/shard_map/all_to_all | solution.py:49
  234.1 32.1 %collective-permute-start.17 = (bf16[4,288,576]{2,1,0:T(8,128)(2,1)}, bf16[4,288,576]{2,1,0:T(8,128)(2,1)S(1)}, u32[]{:S(2)}, u32[]{:S(2)}) collective-permute-start(bf16[4,288,576]{2,1,0:T(8,128)(2,1)} %all-to-all-done.4), channel_id=1, source_target_pairs={{0,4},{4,0},{1,5},{5,1},{2,6},{6,2},{3,7},{7,3},{8,12},{12,8},{9,1... | collective-permute-start | bytes 3981320 | tf_op jit(solution)/shard_map/ppermute | solution.py:59
  269.9 17.6 %collective-permute-start.33 = (bf16[64,2304]{1,0:T(8,128)(2,1)}, bf16[64,2304]{1,0:T(8,128)(2,1)}, u32[]{:S(2)}, u32[]{:S(2)}) collective-permute-start(bf16[64,2304]{1,0:T(8,128)(2,1)} %multiply_convert_fusion.11), channel_id=1, source_target_pairs={{0,24},{8,0},{16,8},{24,16},{1,25},{9,1},{17,9},{25,17},{2,26},{10... | collective-permute-start | bytes 884744 | tf_op jit(solution)/shard_map/ppermute | solution.py:95
  273.3 22.2 %collective-permute-start.27 = (bf16[64,2304]{1,0:T(8,128)(2,1)}, bf16[64,2304]{1,0:T(8,128)(2,1)}, u32[]{:S(2)}, u32[]{:S(2)}) collective-permute-start(bf16[64,2304]{1,0:T(8,128)(2,1)} %multiply_convert_fusion.11), channel_id=1, source_target_pairs={{0,16},{8,24},{16,0},{24,8},{1,17},{9,25},{17,1},{25,9},{2,18},{10... | collective-permute-start | bytes 884744 | tf_op jit(solution)/shard_map/ppermute | solution.py:95
  273.3 23.7 %collective-permute-start.21 = (bf16[64,2304]{1,0:T(8,128)(2,1)}, bf16[64,2304]{1,0:T(8,128)(2,1)}, u32[]{:S(2)}, u32[]{:S(2)}) collective-permute-start(bf16[64,2304]{1,0:T(8,128)(2,1)} %multiply_convert_fusion.11), channel_id=1, source_target_pairs={{0,8},{8,16},{16,24},{24,0},{1,9},{9,17},{17,25},{25,1},{2,10},{10... | collective-permute-start | bytes 884744 | tf_op jit(solution)/shard_map/ppermute | solution.py:95
  281.9 41.7 %collective-permute-start.18 = (bf16[288,2304]{1,0:T(8,128)(2,1)}, bf16[288,2304]{1,0:T(8,128)(2,1)S(1)}, u32[]{:S(2)}, u32[]{:S(2)}) collective-permute-start(bf16[288,2304]{1,0:T(8,128)(2,1)} %reshape.439), channel_id=1, source_target_pairs={{0,4},{4,0},{1,5},{5,1},{2,6},{6,2},{3,7},{7,3},{8,12},{12,8},{9,1... | collective-permute-start | bytes 3981320 | tf_op jit(solution)/shard_map/ppermute | solution.py:59
  295.5 12.8 %collective-permute-start.28 = (bf16[64,2304]{1,0:T(8,128)(2,1)}, bf16[64,2304]{1,0:T(8,128)(2,1)S(1)}, u32[]{:S(2)}, u32[]{:S(2)}) collective-permute-start(bf16[64,2304]{1,0:T(8,128)(2,1)} %collective-permute-done.27), channel_id=1, source_target_pairs={{0,2},{1,3},{2,0},{3,1},{4,6},{5,7},{6,4},{7,5},{8,10},{9,11},{10,... | collective-permute-start | bytes 884744 | tf_op jit(solution)/shard_map/ppermute | solution.py:59
  299.6 15.5 %collective-permute-start.35 = (bf16[128,2304]{1,0:T(8,128)(2,1)S(1)}, bf16[128,2304]{1,0:T(8,128)(2,1)S(1)}, u32[]{:S(2)}, u32[]{:S(2)}) collective-permute-start(bf16[128,2304]{1,0:T(8,128)(2,1)S(1)} %pad_maximum_fusion.12), channel_id=1, source_target_pairs={{0,1},{1,0},{2,3},{3,2},{4,5},{5,4},{6,7},{7,6},{8,9},{9,8},{10,11... | collective-permute-start | bytes 1769480 | tf_op jit(solution)/shard_map/ppermute | solution.py:59
  331.2 33.8 %collective-permute-start.20 = (bf16[64,2304]{1,0:T(8,128)(2,1)}, bf16[64,2304]{1,0:T(8,128)(2,1)}, u32[]{:S(2)}, u32[]{:S(2)}) collective-permute-start(bf16[64,2304]{1,0:T(8,128)(2,1)} %slice.793), channel_id=1, source_target_pairs={{0,2},{1,3},{2,0},{3,1},{4,6},{5,7},{6,4},{7,5},{8,10},{9,11},{10,... | collective-permute-start | bytes 884744 | tf_op jit(solution)/shard_map/ppermute | solution.py:59
  332.9 14.7 %collective-permute-start.37 = (bf16[64,2304]{1,0:T(8,128)(2,1)S(1)}, bf16[64,2304]{1,0:T(8,128)(2,1)S(1)}, u32[]{:S(2)}, u32[]{:S(2)}) collective-permute-start(bf16[64,2304]{1,0:T(8,128)(2,1)S(1)} %slice.790), channel_id=1, source_target_pairs={{0,2},{1,3},{2,0},{3,1},{4,6},{5,7},{6,4},{7,5},{8,10},{9,11},{10,... | collective-permute-start | bytes 884744 | tf_op jit(solution)/shard_map/ppermute | solution.py:59
  333.6 20.3 %collective-permute-start.31 = (bf16[64,2304]{1,0:T(8,128)(2,1)S(1)}, bf16[64,2304]{1,0:T(8,128)(2,1)S(1)}, u32[]{:S(2)}, u32[]{:S(2)}) collective-permute-start(bf16[64,2304]{1,0:T(8,128)(2,1)S(1)} %slice.791), channel_id=1, source_target_pairs={{0,2},{1,3},{2,0},{3,1},{4,6},{5,7},{6,4},{7,5},{8,10},{9,11},{10,... | collective-permute-start | bytes 884744 | tf_op jit(solution)/shard_map/ppermute | solution.py:59
  335.4 24.1 %collective-permute-start.25 = (bf16[64,2304]{1,0:T(8,128)(2,1)S(1)}, bf16[64,2304]{1,0:T(8,128)(2,1)S(1)}, u32[]{:S(2)}, u32[]{:S(2)}) collective-permute-start(bf16[64,2304]{1,0:T(8,128)(2,1)S(1)} %slice.792), channel_id=1, source_target_pairs={{0,2},{1,3},{2,0},{3,1},{4,6},{5,7},{6,4},{7,5},{8,10},{9,11},{10,... | collective-permute-start | bytes 884744 | tf_op jit(solution)/shard_map/ppermute | solution.py:59
  348.4 16.7 %collective-permute-start.38 = (bf16[64,2304]{1,0:T(8,128)(2,1)}, bf16[64,2304]{1,0:T(8,128)(2,1)}, u32[]{:S(2)}, u32[]{:S(2)}) collective-permute-start(bf16[64,2304]{1,0:T(8,128)(2,1)} %fusion.88), channel_id=1, source_target_pairs={{0,8},{8,16},{16,24},{24,0},{1,9},{9,17},{17,25},{25,1},{2,10},{10... | collective-permute-start | bytes 884744 | tf_op jit(solution)/shard_map/ppermute | solution.py:95
  354.7 16.8 %collective-permute-start.32 = (bf16[64,2304]{1,0:T(8,128)(2,1)}, bf16[64,2304]{1,0:T(8,128)(2,1)}, u32[]{:S(2)}, u32[]{:S(2)}) collective-permute-start(bf16[64,2304]{1,0:T(8,128)(2,1)} %fusion.89), channel_id=1, source_target_pairs={{0,16},{8,24},{16,0},{24,8},{1,17},{9,25},{17,1},{25,9},{2,18},{10... | collective-permute-start | bytes 884744 | tf_op jit(solution)/shard_map/ppermute | solution.py:95
  360.3 14.4 %collective-permute-start.26 = (bf16[64,2304]{1,0:T(8,128)(2,1)}, bf16[64,2304]{1,0:T(8,128)(2,1)}, u32[]{:S(2)}, u32[]{:S(2)}) collective-permute-start(bf16[64,2304]{1,0:T(8,128)(2,1)} %fusion.90), channel_id=1, source_target_pairs={{0,24},{8,0},{16,8},{24,16},{1,25},{9,1},{17,9},{25,17},{2,26},{10... | collective-permute-start | bytes 884744 | tf_op jit(solution)/shard_map/ppermute | solution.py:95
  386.9 24.9 %collective-permute-start.44 = (bf16[64,2304]{1,0:T(8,128)(2,1)S(1)}, bf16[64,2304]{1,0:T(8,128)(2,1)S(1)}, u32[]{:S(2)}, u32[]{:S(2)}) collective-permute-start(bf16[64,2304]{1,0:T(8,128)(2,1)S(1)} %get-tuple-element.91), channel_id=1, source_target_pairs={{0,16},{8,24},{16,0},{24,8},{1,17},{9,25},{17,1},{25,9},{2,18},{10... | collective-permute-start | bytes 884744 | tf_op jit(solution)/shard_map/ppermute | solution.py:95
  387.1 25.3 %collective-permute-start.41 = (bf16[64,2304]{1,0:T(8,128)(2,1)S(1)}, bf16[64,2304]{1,0:T(8,128)(2,1)S(1)}, u32[]{:S(2)}, u32[]{:S(2)}) collective-permute-start(bf16[64,2304]{1,0:T(8,128)(2,1)S(1)} %get-tuple-element.91), channel_id=1, source_target_pairs={{0,8},{8,16},{16,24},{24,0},{1,9},{9,17},{17,25},{25,1},{2,10},{10... | collective-permute-start | bytes 884744 | tf_op jit(solution)/shard_map/ppermute | solution.py:95
  387.6 37.6 %collective-permute-start.40 = (bf16[128,2304]{1,0:T(8,128)(2,1)S(1)}, bf16[128,2304]{1,0:T(8,128)(2,1)S(1)}, u32[]{:S(2)}, u32[]{:S(2)}) collective-permute-start(bf16[128,2304]{1,0:T(8,128)(2,1)S(1)} %pad_maximum_fusion.13), channel_id=1, source_target_pairs={{0,1},{1,0},{2,3},{3,2},{4,5},{5,4},{6,7},{7,6},{8,9},{9,8},{10,11... | collective-permute-start | bytes 1769480 | tf_op jit(solution)/shard_map/ppermute | solution.py:59
  394.5 19.4 %collective-permute-start.48 = (bf16[64,2304]{1,0:T(8,128)(2,1)S(1)}, bf16[64,2304]{1,0:T(8,128)(2,1)S(1)}, u32[]{:S(2)}, u32[]{:S(2)}) collective-permute-start(bf16[64,2304]{1,0:T(8,128)(2,1)S(1)} %collective-permute-done.47), channel_id=1, source_target_pairs={{0,2},{1,3},{2,0},{3,1},{4,6},{5,7},{6,4},{7,5},{8,10},{9,11},{10,... | collective-permute-start | bytes 884744 | tf_op jit(solution)/shard_map/ppermute | solution.py:59
  412.4 12.6 %collective-permute-start.42 = (bf16[64,2304]{1,0:T(8,128)(2,1)S(1)}, bf16[64,2304]{1,0:T(8,128)(2,1)S(1)}, u32[]{:S(2)}, u32[]{:S(2)}) collective-permute-start(bf16[64,2304]{1,0:T(8,128)(2,1)S(1)} %collective-permute-done.41), channel_id=1, source_target_pairs={{0,2},{1,3},{2,0},{3,1},{4,6},{5,7},{6,4},{7,5},{8,10},{9,11},{10,... | collective-permute-start | bytes 884744 | tf_op jit(solution)/shard_map/ppermute | solution.py:59
  413.9 16.7 %collective-permute-start.49 = (bf16[128,2304]{1,0:T(8,128)(2,1)S(1)}, bf16[128,2304]{1,0:T(8,128)(2,1)S(1)}, u32[]{:S(2)}, u32[]{:S(2)}) collective-permute-start(bf16[128,2304]{1,0:T(8,128)(2,1)S(1)} %pad_maximum_fusion.16), channel_id=1, source_target_pairs={{0,1},{1,0},{2,3},{3,2},{4,5},{5,4},{6,7},{7,6},{8,9},{9,8},{10,11... | collective-permute-start | bytes 1769480 | tf_op jit(solution)/shard_map/ppermute | solution.py:59
  429.5 22.2 %collective-permute-start.52 = (bf16[128,2304]{1,0:T(8,128)(2,1)S(1)}, bf16[128,2304]{1,0:T(8,128)(2,1)S(1)}, u32[]{:S(2)}, u32[]{:S(2)}) collective-permute-start(bf16[128,2304]{1,0:T(8,128)(2,1)S(1)} %slice.781), channel_id=1, source_target_pairs={{0,1},{1,0},{2,3},{3,2},{4,5},{5,4},{6,7},{7,6},{8,9},{9,8},{10,11... | collective-permute-start | bytes 1769480 | tf_op jit(solution)/shard_map/ppermute | solution.py:59
  439.2 12.2 %collective-permute-start.50 = (bf16[64,2304]{1,0:T(8,128)(2,1)S(1)}, bf16[64,2304]{1,0:T(8,128)(2,1)S(1)}, u32[]{:S(2)}, u32[]{:S(2)}) collective-permute-start(bf16[64,2304]{1,0:T(8,128)(2,1)S(1)} %get-tuple-element.59), channel_id=1, source_target_pairs={{0,2},{1,3},{2,0},{3,1},{4,6},{5,7},{6,4},{7,5},{8,10},{9,11},{10,... | collective-permute-start | bytes 884744 | tf_op jit(solution)/shard_map/ppermute | solution.py:59
  440.2 61.8 %collective-permute-start.63 = (bf16[4,288,576]{2,1,0:T(8,128)(2,1)S(1)}, bf16[4,288,576]{2,1,0:T(8,128)(2,1)S(1)}, u32[]{:S(2)}, u32[]{:S(2)}) collective-permute-start(bf16[4,288,576]{2,1,0:T(8,128)(2,1)S(1)} %fusion.15), channel_id=1, source_target_pairs={{0,4},{4,0},{1,5},{5,1},{2,6},{6,2},{3,7},{7,3},{8,12},{12,8},{9,1... | collective-permute-start | bytes 3981320 | tf_op jit(solution)/shard_map/ppermute | solution.py:59
  451.7 28.7 %collective-permute-start.51 = (bf16[2,64,2304]{2,1,0:T(8,128)(2,1)S(1)}, bf16[2,64,2304]{2,1,0:T(8,128)(2,1)S(1)}, u32[]{:S(2)}, u32[]{:S(2)}) collective-permute-start(bf16[2,64,2304]{2,1,0:T(8,128)(2,1)S(1)} %pad_maximum_fusion.17), channel_id=1, source_target_pairs={{0,1},{1,0},{2,3},{3,2},{4,5},{5,4},{6,7},{7,6},{8,9},{9,8},{10,11... | collective-permute-start | bytes 1769480 | tf_op jit(solution)/shard_map/ppermute | solution.py:59
  452.4 29.6 %collective-permute-start.53 = (bf16[64,2304]{1,0:T(8,128)(2,1)S(1)}, bf16[64,2304]{1,0:T(8,128)(2,1)S(1)}, u32[]{:S(2)}, u32[]{:S(2)}) collective-permute-start(bf16[64,2304]{1,0:T(8,128)(2,1)S(1)} %slice.789), channel_id=1, source_target_pairs={{0,2},{1,3},{2,0},{3,1},{4,6},{5,7},{6,4},{7,5},{8,10},{9,11},{10,... | collective-permute-start | bytes 884744 | tf_op jit(solution)/shard_map/ppermute | solution.py:59
  454.0 14.6 %collective-permute-start.61 = (bf16[64,2304]{1,0:T(8,128)(2,1)S(1)}, bf16[64,2304]{1,0:T(8,128)(2,1)S(1)}, u32[]{:S(2)}, u32[]{:S(2)}) collective-permute-start(bf16[64,2304]{1,0:T(8,128)(2,1)S(1)} %slice.786), channel_id=1, source_target_pairs={{0,2},{1,3},{2,0},{3,1},{4,6},{5,7},{6,4},{7,5},{8,10},{9,11},{10,... | collective-permute-start | bytes 884744 | tf_op jit(solution)/shard_map/ppermute | solution.py:59
  454.9 20.1 %collective-permute-start.58 = (bf16[64,2304]{1,0:T(8,128)(2,1)S(1)}, bf16[64,2304]{1,0:T(8,128)(2,1)S(1)}, u32[]{:S(2)}, u32[]{:S(2)}) collective-permute-start(bf16[64,2304]{1,0:T(8,128)(2,1)S(1)} %slice.787), channel_id=1, source_target_pairs={{0,2},{1,3},{2,0},{3,1},{4,6},{5,7},{6,4},{7,5},{8,10},{9,11},{10,... | collective-permute-start | bytes 884744 | tf_op jit(solution)/shard_map/ppermute | solution.py:59
  480.4 16.4 %collective-permute-start.59 = (bf16[64,2304]{1,0:T(8,128)(2,1)S(1)}, bf16[64,2304]{1,0:T(8,128)(2,1)S(1)}, u32[]{:S(2)}, u32[]{:S(2)}) collective-permute-start(bf16[64,2304]{1,0:T(8,128)(2,1)S(1)} %slice_add_fusion.9), channel_id=1, source_target_pairs={{0,16},{8,24},{16,0},{24,8},{1,17},{9,25},{17,1},{25,9},{2,18},{10... | collective-permute-start | bytes 884744 | tf_op jit(solution)/shard_map/ppermute | solution.py:95
  480.5 16.8 %collective-permute-start.56 = (bf16[64,2304]{1,0:T(8,128)(2,1)S(1)}, bf16[64,2304]{1,0:T(8,128)(2,1)S(1)}, u32[]{:S(2)}, u32[]{:S(2)}) collective-permute-start(bf16[64,2304]{1,0:T(8,128)(2,1)S(1)} %slice_add_fusion.10), channel_id=1, source_target_pairs={{0,24},{8,0},{16,8},{24,16},{1,25},{9,1},{17,9},{25,17},{2,26},{10... | collective-permute-start | bytes 884744 | tf_op jit(solution)/shard_map/ppermute | solution.py:95
  501.7 33.7 %collective-permute-start.64 = (bf16[4,288,576]{2,1,0:T(8,128)(2,1)S(1)}, bf16[4,288,576]{2,1,0:T(8,128)(2,1)S(1)}, u32[]{:S(2)}, u32[]{:S(2)}) collective-permute-start(bf16[4,288,576]{2,1,0:T(8,128)(2,1)S(1)} %fusion.16), channel_id=1, source_target_pairs={{0,4},{4,0},{1,5},{5,1},{2,6},{6,2},{3,7},{7,3},{8,12},{12,8},{9,1... | collective-permute-start | bytes 3981320 | tf_op jit(solution)/shard_map/ppermute | solution.py:59
  537.0 15.6 %collective-permute-start.65 = (bf16[64,1152]{1,0:T(8,128)(2,1)S(1)}, bf16[64,1152]{1,0:T(8,128)(2,1)S(1)}, u32[]{:S(2)}, u32[]{:S(2)}) collective-permute-start(bf16[64,1152]{1,0:T(8,128)(2,1)S(1)} %get-tuple-element.175), channel_id=1, source_target_pairs={{0,4},{4,0},{1,5},{5,1},{2,6},{6,2},{3,7},{7,3},{8,12},{12,8},{9,1... | collective-permute-start | bytes 442376 | tf_op jit(solution)/shard_map/ppermute | solution.py:59
  537.3 15.3 %collective-permute-start.67 = (bf16[64,1152]{1,0:T(8,128)(2,1)S(1)}, bf16[64,1152]{1,0:T(8,128)(2,1)S(1)}, u32[]{:S(2)}, u32[]{:S(2)}) collective-permute-start(bf16[64,1152]{1,0:T(8,128)(2,1)S(1)} %get-tuple-element.176), channel_id=1, source_target_pairs={{0,2},{1,3},{2,0},{3,1},{4,6},{5,7},{6,4},{7,5},{8,10},{9,11},{10,... | collective-permute-start | bytes 442376 | tf_op jit(solution)/shard_map/ppermute | solution.py:59
  544.5 50.0 %all-to-all-start.6 = ((bf16[4,288,576]{2,1,0:T(8,128)(2,1)}), bf16[4,288,576]{2,1,0:T(8,128)(2,1)}, u32[]{:S(2)}, u32[]{:S(2)}) async-start(bf16[4,288,576]{2,1,0:T(8,128)(2,1)} %fusion.13), calls=%async_computation.6 | async-start | bytes 2949120 | tf_op jit(solution)/shard_map/all_to_all | solution.py:49
  557.7 34.3 %collective-permute-start.70 = (bf16[4,288,576]{2,1,0:T(8,128)(2,1)S(1)}, bf16[4,288,576]{2,1,0:T(8,128)(2,1)S(1)}, u32[]{:S(2)}, u32[]{:S(2)}) collective-permute-start(bf16[4,288,576]{2,1,0:T(8,128)(2,1)S(1)} %fusion.17), channel_id=1, source_target_pairs={{0,4},{4,0},{1,5},{5,1},{2,6},{6,2},{3,7},{7,3},{8,12},{12,8},{9,1... | collective-permute-start | bytes 3981320 | tf_op jit(solution)/shard_map/ppermute | solution.py:59
  565.4 28.2 %collective-permute-start.69 = (bf16[2,2,64,2304]{3,2,1,0:T(8,128)(2,1)S(1)}, bf16[2,2,64,2304]{3,2,1,0:T(8,128)(2,1)S(1)}, u32[]{:S(2)}, u32[]{:S(2)}) collective-permute-start(bf16[2,2,64,2304]{3,2,1,0:T(8,128)(2,1)S(1)} %maximum_maximum_fusion), channel_id=1, source_target_pairs={{0,1},{1,0},{2,3},{3,2},{4,5},{5,4},{6,7},{7,6},{8,9},{9,8},{10,11... | collective-permute-start | bytes 3538952 | tf_op jit(solution)/shard_map/ppermute | solution.py:59
  594.4 38.4 %all-to-all-start.7 = ((bf16[4,288,576]{2,1,0:T(8,128)(2,1)}), bf16[4,288,576]{2,1,0:T(8,128)(2,1)}, u32[]{:S(2)}, u32[]{:S(2)}) async-start(bf16[4,288,576]{2,1,0:T(8,128)(2,1)} %fusion.9), calls=%async_computation.7 | async-start | bytes 2949120 | tf_op jit(solution)/shard_map/all_to_all | solution.py:49
  632.8 38.7 %all-to-all-start.8 = ((bf16[4,288,576]{2,1,0:T(8,128)(2,1)}), bf16[4,288,576]{2,1,0:T(8,128)(2,1)}, u32[]{:S(2)}, u32[]{:S(2)}) async-start(bf16[4,288,576]{2,1,0:T(8,128)(2,1)} %fusion.12), calls=%async_computation.8 | async-start | bytes 2949120 | tf_op jit(solution)/shard_map/all_to_all | solution.py:49
  641.3 24.4 %collective-permute-start.71 = (bf16[2048,256]{0,1:T(8,128)(2,1)}, bf16[2048,256]{0,1:T(8,128)(2,1)}, u32[]{:S(2)}, u32[]{:S(2)}) collective-permute-start(bf16[2048,256]{0,1:T(8,128)(2,1)} %get-tuple-element.67), channel_id=1, source_target_pairs={{0,4},{4,0},{1,5},{5,1},{2,6},{6,2},{3,7},{7,3},{8,12},{12,8},{9,1... | collective-permute-start | bytes 3145736 | tf_op jit(solution)/shard_map/ppermute | solution.py:59
  673.4 15.9 %collective-permute-start.72 = (bf16[512,256]{0,1:T(8,128)(2,1)S(1)}, bf16[512,256]{0,1:T(8,128)(2,1)S(1)}, u32[]{:S(2)}, u32[]{:S(2)}) collective-permute-start(bf16[512,256]{0,1:T(8,128)(2,1)S(1)} %get-tuple-element.131), channel_id=1, source_target_pairs={{8,0},{16,8},{24,16},{9,1},{17,9},{25,17},{10,2},{18,10},{26,18},{... | collective-permute-start | bytes 786440 | tf_op jit(solution)/shard_map/ppermute | solution.py:72
  674.7 14.6 %collective-permute-start.74 = (bf16[512,256]{0,1:T(8,128)(2,1)S(1)}, bf16[512,256]{0,1:T(8,128)(2,1)S(1)}, u32[]{:S(2)}, u32[]{:S(2)}) collective-permute-start(bf16[512,256]{0,1:T(8,128)(2,1)S(1)} %get-tuple-element.132), channel_id=1, source_target_pairs={{24,0},{25,1},{26,2},{27,3},{28,4},{29,5},{30,6},{31,7}} | collective-permute-start | bytes 786440 | tf_op jit(solution)/shard_map/ppermute | solution.py:72
  676.0 21.2 %collective-permute-start.73 = (bf16[512,256]{0,1:T(8,128)(2,1)S(1)}, bf16[512,256]{0,1:T(8,128)(2,1)S(1)}, u32[]{:S(2)}, u32[]{:S(2)}) collective-permute-start(bf16[512,256]{0,1:T(8,128)(2,1)S(1)} %get-tuple-element.133), channel_id=1, source_target_pairs={{16,0},{24,8},{17,1},{25,9},{18,2},{26,10},{19,3},{27,11},{20,4},{... | collective-permute-start | bytes 786440 | tf_op jit(solution)/shard_map/ppermute | solution.py:72
  703.2 36.9 %collective-permute-start.75 = (bf16[2,2,64,2304]{3,2,0,1:T(8,128)(2,1)}, bf16[2,2,64,2304]{3,2,0,1:T(8,128)(2,1)}, u32[]{:S(2)}, u32[]{:S(2)}) collective-permute-start(bf16[2,2,64,2304]{3,2,0,1:T(8,128)(2,1)} %fusion.19), channel_id=1, source_target_pairs={{0,1},{1,0},{2,3},{3,2},{4,5},{5,4},{6,7},{7,6},{8,9},{9,8},{10,11... | collective-permute-start | bytes 3538952 | tf_op jit(solution)/shard_map/ppermute | solution.py:59
  735.8 33.8 %all-to-all-start.9 = ((bf16[4,256,576]{1,2,0:T(8,128)(2,1)}), bf16[4,256,576]{1,2,0:T(8,128)(2,1)}, u32[]{:S(2)}, u32[]{:S(2)}) async-start(bf16[4,256,576]{1,2,0:T(8,128)(2,1)} %bitcast.376), calls=%async_computation.9 | async-start | bytes 2359296 | tf_op jit(solution)/shard_map/all_to_all | solution.py:49
  769.6 32.2 %all-to-all-start.10 = ((bf16[4,576,256]{2,1,0:T(8,128)(2,1)}), bf16[4,576,256]{2,1,0:T(8,128)(2,1)S(1)}, u32[]{:S(2)}, u32[]{:S(2)}) async-start(bf16[4,576,256]{2,1,0:T(8,128)(2,1)} %bitcast.385), calls=%async_computation.10 | async-start | bytes 2359296 | tf_op jit(solution)/shard_map/all_to_all | solution.py:49
  777.7 28.7 %collective-permute-start.84 = (bf16[256,288]{0,1:T(8,128)(2,1)S(1)}, bf16[256,288]{0,1:T(8,128)(2,1)S(1)}, u32[]{:S(2)}, u32[]{:S(2)}) collective-permute-start(bf16[256,288]{0,1:T(8,128)(2,1)S(1)} %select_convert_fusion.10), channel_id=1, source_target_pairs={{0,4},{4,0},{1,5},{5,1},{2,6},{6,2},{3,7},{7,3},{8,12},{12,8},{9,1... | collective-permute-start | bytes 442376 | tf_op jit(solution)/shard_map/ppermute | solution.py:59
  785.3 22.1 %collective-permute-start.81 = (bf16[2,64,2304]{2,1,0:T(8,128)(2,1)}, bf16[2,64,2304]{2,1,0:T(8,128)(2,1)S(1)}, u32[]{:S(2)}, u32[]{:S(2)}) collective-permute-start(bf16[2,64,2304]{2,1,0:T(8,128)(2,1)} %pad_maximum_fusion.19), channel_id=1, source_target_pairs={{0,1},{1,0},{2,3},{3,2},{4,5},{5,4},{6,7},{7,6},{8,9},{9,8},{10,11... | collective-permute-start | bytes 1769480 | tf_op jit(solution)/shard_map/ppermute | solution.py:59
  802.9 32.3 %all-to-all-start.11 = ((bf16[4,592,256]{2,1,0:T(8,128)(2,1)}), bf16[4,592,256]{2,1,0:T(8,128)(2,1)S(1)}, u32[]{:S(2)}, u32[]{:S(2)}) async-start(bf16[4,592,256]{2,1,0:T(8,128)(2,1)} %pad_maximum_fusion.4), calls=%async_computation.11 | async-start | bytes 2424832 | tf_op jit(solution)/shard_map/all_to_all | solution.py:49
  809.5 26.7 %collective-permute-start.82 = (bf16[288,256]{1,0:T(8,128)(2,1)S(1)}, bf16[288,256]{1,0:T(8,128)(2,1)S(1)}, u32[]{:S(2)}, u32[]{:S(2)}) collective-permute-start(bf16[288,256]{1,0:T(8,128)(2,1)S(1)} %select_convert_fusion.12), channel_id=1, source_target_pairs={{0,4},{4,0},{1,5},{5,1},{2,6},{6,2},{3,7},{7,3},{8,12},{12,8},{9,1... | collective-permute-start | bytes 442376 | tf_op jit(solution)/shard_map/ppermute | solution.py:59
  (142 other events, 1136.2 us)

commit v3 on v2

v3 whole, which is shorter than its diff:
```python
import jax
import jax.numpy as jnp
from jax import lax
from jax.experimental import pallas as pl
from jax.experimental.pallas import tpu as pltpu
from jax.sharding import PartitionSpec as P

HEAD_SIZE = 256
SLIDE_WINDOW = 4096


eps = 1e-06
softcap = 50.0
negative = -1e30
f32 = jnp.float32
b16 = jnp.bfloat16


def rms_scale(value_rows):
    return lax.rsqrt(jnp.mean(value_rows * value_rows, axis=-1, keepdims=True) + eps)


def rms_back(grad, normed, scale):
    return scale * (grad - normed * jnp.mean(grad * normed, axis=-1, keepdims=True))


def rotary_tables(positions):
    inverse = 1.0 / 10000.0 ** (jnp.arange(0, HEAD_SIZE, 2, dtype=f32) / HEAD_SIZE)
    angles = positions.astype(f32)[:, None] * inverse[None, :]
    return (jnp.cos(angles), jnp.sin(angles))


def apply_rotary(value_rows, cosine_table, sine_table):
    half = value_rows.shape[-1] // 2
    first, second = value_rows[:, :half], value_rows[:, half:]
    return jnp.concatenate(
        [first * cosine_table - second * sine_table, second * cosine_table + first * sine_table],
        axis=-1,
    )


def rotate_back(grads, cosine_table, sine_table):
    return apply_rotary(grads, cosine_table, -sine_table)


def gated(gate_value, up_value):
    return jax.nn.gelu(gate_value, approximate=True) * up_value


def exchange(blocks, axis):
    return lax.all_to_all(blocks, axis, 0, 0, tiled=True)


def gathered(block, axis):
    count = lax.axis_size(axis)
    return exchange(jnp.broadcast_to(block[None], (count,) + block.shape), axis)


def swapped(value, axis, bit):
    count = lax.axis_size(axis)
    return lax.ppermute(value, axis, [(place, place ^ bit) for place in range(count)])


def passed_on(value, steps, way):
    n = lax.axis_size("dp")
    pairs = [(s, s + 1) for s in range(steps - 1, n - 1)]
    if way < 0:
        pairs = [(n - 1 - s, n - 1 - t) for s, t in pairs]
    return lax.ppermute(value, "dp", pairs)


def shifted(value, axis, steps):
    count = lax.axis_size(axis)
    return lax.ppermute(
        value, axis, [(s, s + steps) for s in range(count) if 0 <= s + steps < count]
    )


def summed(blocks):
    return jnp.sum(blocks.astype(f32), axis=0)


def dot(left, right):
    return jnp.dot(left, right, preferred_element_type=f32)


def dot_nt(left, right):
    return lax.dot_general(left, right, (((1,), (1,)), ((), ())), preferred_element_type=f32)


def dot_tn(left, right):
    return lax.dot_general(left, right, (((0,), (0,)), ((), ())), preferred_element_type=f32)


def rotated(value, steps):
    n = lax.axis_size("dp")
    return lax.ppermute(value, "dp", [(s, (s + steps) % n) for s in range(n)])


def picked(first, pair):
    low, high = pair
    return jnp.where(first, low, high), jnp.where(first, high, low)


def after(value, *earlier):
    return lax.optimization_barrier((value,) + earlier)[0]


def ring_blocks(block):
    n = lax.axis_size("dp")
    return [block] + [rotated(block, steps) for steps in range(1, n)]


def in_order(blocks):
    n = lax.axis_size("dp")
    place = lax.axis_index("dp")
    blocks = [blocks[-j % n] for j in range(n)]
    for bit in range((n - 1).bit_length()):
        shift = 1 << bit
        odd = (place >> bit) % 2 == 1
        blocks = [jnp.where(odd, blocks[(j - shift) % n], blocks[j]) for j in range(n)]
    return jnp.stack(blocks)


def ring_summed(blocks):
    n = lax.axis_size("dp")
    place = lax.axis_index("dp")
    total = lax.dynamic_index_in_dim(blocks, place, 0, keepdims=False)
    for steps in range(1, n):
        sent = lax.dynamic_index_in_dim(blocks, (place + steps) % n, 0, keepdims=False)
        total = total + rotated(sent.astype(b16), steps).astype(f32)
    return total


def unit_blocks(weights, side, n):
    deep, total = weights[0].shape
    units = total // n
    shape = (n, deep // 2, units)
    if deep % 32:
        halves = [lax.dynamic_slice_in_dim(w, side * (deep // 2), deep // 2) for w in weights]
        return [jnp.swapaxes(w.reshape(deep // 2, n, units), 0, 1) for w in halves]

    def kernel(side_ref, *refs):
        for source, target in zip(refs[: len(weights)], refs[len(weights) :]):
            for j in range(n):
                target[j] = source[:, j * units : (j + 1) * units]

    return pl.pallas_call(
        kernel,
        grid_spec=pltpu.PrefetchScalarGridSpec(
            num_scalar_prefetch=1,
            grid=(1,),
            in_specs=[pl.BlockSpec((deep // 2, total), lambda g, s: (s[0], 0))] * len(weights),
            out_specs=[pl.BlockSpec(shape, lambda g, s: (0, 0, 0))] * len(weights),
        ),
        out_shape=[jax.ShapeDtypeStruct(shape, w.dtype) for w in weights],
        compiler_params=pltpu.CompilerParams(vmem_limit_bytes=48 << 20),
        name="unit_blocks",
    )(side.astype(jnp.int32).reshape(1), *weights)


def side_by_side(blocks):
    n, rows, units = blocks.shape
    if rows % 16:
        return jnp.swapaxes(blocks, 0, 1).reshape(rows, n * units).astype(f32)

    def kernel(source, target):
        for j in range(n):
            target[:, j * units : (j + 1) * units] = source[j].astype(f32)

    return pl.pallas_call(
        kernel,
        out_shape=jax.ShapeDtypeStruct((rows, n * units), f32),
        compiler_params=pltpu.CompilerParams(vmem_limit_bytes=32 << 20),
        name="side_by_side",
    )(blocks)


def bits():
    lane = lax.axis_index("tensor")
    return lax.axis_index("context") == 0, lane < 2, lane % 2 == 0


AXES = (("context", 1), ("tensor", 2), ("tensor", 1))


def join(own, step, axis):
    low, high = picked(bits()[step], (own, swapped(own, *AXES[step])))
    return jnp.stack([low, high], axis=axis)


def fold(partial, step, axis):
    low = lax.index_in_dim(partial, 0, axis, keepdims=False)
    high = lax.index_in_dim(partial, 1, axis, keepdims=False)
    kept, sent = picked(bits()[step], (low, high))
    return kept + swapped(sent.astype(b16), *AXES[step]).astype(f32)


def collect_group(partial, sub, *earlier):
    width = partial.shape[-1]
    partial = after(fold(partial.reshape(2, 2, 2, sub, width), 2, 2), *earlier)
    left, right = partial[..., : width // 2], partial[..., width // 2 :]
    left = fold(fold(left, 0, 0), 1, 0)
    right = fold(fold(right, 1, 1), 0, 0)
    return jnp.concatenate([left, right], axis=-1)


def spread_group(block, *earlier):
    width = block.shape[-1]
    left, right = block[:, : width // 2], block[:, width // 2 :]
    left = join(join(left, 0, 0), 1, 1)
    right = join(join(right, 1, 0), 0, 0)
    whole = after(jnp.concatenate([left, right], axis=-1), *earlier)
    whole = join(whole, 2, 2)
    return whole.reshape(-1, width)


def spread_lanes(block):
    return join(join(block, 1, 0), 2, 1).reshape(-1, block.shape[-1])


SMEM = pltpu.SMEM


def params(megabytes=48):
    return pltpu.CompilerParams(vmem_limit_bytes=megabytes << 20)


def scalar(value):
    return value.astype(jnp.int32).reshape(1)


def whole(shape):
    return pl.BlockSpec(shape, lambda *_: (0,) * len(shape))


def row_grad(left, right):
    width = left.shape[1]
    step = 384

    def kernel(left_ref, right_ref, out):
        for start in range(0, width, step):
            here = slice(start, start + step)
            out[here, :] = dot_tn(left_ref[:, here], right_ref[...]).astype(b16)

    return pl.pallas_call(
        kernel,
        out_shape=jax.ShapeDtypeStruct((width, right.shape[1]), b16),
        compiler_params=params(),
        name="row_grad",
    )(left, right)


def attend_back(rows, w_out, keys, values, queries, probs, bent, tables, side):
    group, width = rows.shape
    span, size = keys.shape
    block = 128
    steps = group // block

    def kernel(
        side_ref, rows_ref, out_ref, key_ref, value_ref, query_ref, probs_ref, bent_ref, cos_ref, sin_ref,
        query_grad, kept, sent, key_sum, value_sum,
    ):
        step = pl.program_id(0)
        mixed = dot(rows_ref[...], out_ref[...]).astype(b16)
        grads = dot_nt(mixed, value_ref[...])
        probs = probs_ref[...]
        bent = bent_ref[...]
        grads = probs * (grads - jnp.sum(probs * grads, axis=-1, keepdims=True))
        grads = (grads * (1.0 - bent * bent)).astype(b16)
        turned = rotate_back(dot(grads, key_ref[...]), cos_ref[...], sin_ref[...])
        query_grad[...] = (turned * HEAD_SIZE ** (-0.5)).astype(b16)
        key_part = dot_tn(grads, query_ref[...])
        value_part = dot_tn(probs.astype(b16), mixed)

        @pl.when(step == 0)
        def _():
            key_sum[...] = key_part
            value_sum[...] = value_part

        @pl.when(step > 0)
        def _():
            key_sum[...] += key_part
            value_sum[...] += value_part

        @pl.when((step == steps - 1) & (side_ref[0] == 0))
        def _():
            kept[...] = key_sum[...]
            sent[...] = value_sum[...].astype(b16)

        @pl.when((step == steps - 1) & (side_ref[0] == 1))
        def _():
            kept[...] = value_sum[...]
            sent[...] = key_sum[...].astype(b16)

    def by_rows(columns):
        return pl.BlockSpec((block, columns), lambda g: (g, 0))

    return pl.pallas_call(
        kernel,
        grid=(steps,),
        in_specs=[
            pl.BlockSpec(memory_space=SMEM),
            by_rows(width),
            whole((width, size)),
            whole((span, size)),
            whole((span, size)),
            by_rows(size),
            by_rows(span),
            by_rows(span),
            by_rows(size // 2),
            by_rows(size // 2),
        ],
        out_specs=[by_rows(size), whole((span, size)), whole((span, size))],
        out_shape=[
            jax.ShapeDtypeStruct((group, size), b16),
            jax.ShapeDtypeStruct((span, size), f32),
            jax.ShapeDtypeStruct((span, size), b16),
        ],
        scratch_shapes=[pltpu.VMEM((span, size), f32)] * 2,
        compiler_params=params(),
        name="attend_back",
    )(scalar(side), rows, w_out, keys, values, queries, probs, bent, *tables)


def together(*values):
    return lax.optimization_barrier(values)


def spread_chunk(block, *earlier):
    block = jnp.concatenate([block, swapped(block, "tensor", 2)], axis=0)
    block = after(block, *earlier)
    return jnp.concatenate([block, swapped(block, "tensor", 1)], axis=0)


def folded(partial, bit):
    half = partial.shape[0] // 2
    return partial[:half] + swapped(partial[half:].astype(b16), "tensor", bit).astype(f32)


def pipelined(block, work):
    n = lax.axis_size("dp")
    sub = block.shape[0]
    groups = [[0], [1, n - 1], list(range(2, n - 1))] if n > 3 else [[0], list(range(1, n))]
    rows, partial, rest = [], [], []
    sent = block
    for group in groups:
        got = [rotated(sent, steps) if steps else block for steps in group]
        if group[0]:
            sent = after(block, *got)
        rows.append(got)
    for number, got in enumerate(rows):
        got = jnp.concatenate(got, axis=0) if len(got) > 1 else got[0]
        rows[number] = spread_chunk(got, *partial[:1])
        first, *others = work(number, after(rows[number], *partial[-1:]))
        partial.append(first)
        rest.append(others)

    total = 0.0
    for number, group in enumerate(groups):
        back = folded(folded(partial[number], 1), 2)
        for place, steps in enumerate(group):
            part = back[place * sub : (place + 1) * sub]
            if steps:
                part = rotated(part.astype(b16), -steps).astype(f32)
            total = total + part
    return rows, total, list(zip(*rest)), partial + [back]


def on_device(
    tokens,
    segments,
    w_query,
    key_weight,
    value_weight,
    w_output,
    w_gate,
    w_up,
    w_down,
    pre_attn_gain,
    post_attn_gain,
    pre_ffw_gain,
    post_ffw_gain,
    cotangent,
):
    n = lax.axis_size("dp")
    place = lax.axis_index("dp")
    side = lax.axis_index("context")
    lane = lax.axis_index("tensor")
    lanes = lax.axis_size("tensor")
    rows, width = tokens.shape
    group = 2 * rows
    sub = rows // lanes
    deep = width // n
    reach = min((SLIDE_WINDOW + group - 2) // group, n - 1)
    is_first = side == 0

    def half_of(value, which, axis):
        size = value.shape[axis] // 2
        low = lax.slice_in_dim(value, 0, size, axis=axis)
        high = lax.slice_in_dim(value, size, 2 * size, axis=axis)
        return jnp.where(which == 0, low, high)

    def with_rider(block, values):
        rider = jnp.zeros((16 * HEAD_SIZE - values.size,), b16)
        rider = jnp.concatenate([values.astype(b16).reshape(-1), rider])
        return jnp.concatenate([block, rider.reshape(16, HEAD_SIZE)], axis=0)

    def split_rider(blocks, count):
        size = blocks.shape[1] - 16
        rider = blocks[:, size:].reshape(blocks.shape[0], -1)[:, :count]
        return blocks[:, :size], rider

    gains = jnp.concatenate([pre_attn_gain, post_attn_gain, pre_ffw_gain, post_ffw_gain])
    pair_got = ring_blocks(with_rider(jnp.where(is_first, key_weight, value_weight), gains))
    group_tokens = join(tokens, 0, 0).reshape(group, width).astype(f32)
    segment_pair = join(segments[None].astype(b16), 0, 0)
    pair_in, gains = split_rider(in_order(pair_got), 4 * deep)
    pair_in = pair_in.reshape(width, HEAD_SIZE)
    gains = 1.0 + jnp.swapaxes(gains.reshape(n, 4, deep), 0, 1).reshape(4, width).astype(f32)
    scale_one = rms_scale(group_tokens)
    normed_one = group_tokens * scale_one
    lifted_one = (normed_one * gains[0]).astype(b16)
    positions = place * group + jnp.arange(group, dtype=jnp.int32)
    cosine_table, sine_table = rotary_tables(positions)
    mine = dot(lifted_one, pair_in)
    mine = jnp.where(is_first, apply_rotary(mine, cosine_table, sine_table), mine).astype(b16)
    mine = [mine] + [shifted(mine, "dp", steps) for steps in range(1, reach + 1)]
    query_got = ring_blocks(after(with_rider(half_of(w_query, side, 1), segment_pair), mine[0]))
    query_in, all_segments = split_rider(in_order(query_got), group)
    query_in = query_in.reshape(width, HEAD_SIZE)
    all_segments = all_segments.reshape(-1).astype(jnp.int32)
    out_got = ring_blocks(after(half_of(w_output.T, side, 1), *query_got))
    w_out = in_order(out_got).reshape(width, HEAD_SIZE)

    units = w_gate.shape[1] // n
    gate_got, up_got, down_got = unit_blocks([w_gate, w_up, w_down.T], side, n)
    gate_got = exchange(after(gate_got, *mine), "dp")
    up_got = exchange(after(up_got, gate_got), "dp")
    down_got = exchange(after(down_got, up_got), "dp")
    gate_w = join(gate_got, 0, 1).reshape(width, units)
    up_w = join(up_got, 0, 1).reshape(width, units)
    down_w = join(down_got, 0, 1).reshape(width, units)

    theirs = [swapped(block, "context", 1) for block in mine]
    mine = jnp.concatenate(mine[::-1], axis=0)
    theirs = jnp.concatenate(theirs[::-1], axis=0)
    keys = jnp.where(is_first, mine, theirs)
    values = jnp.where(is_first, theirs, mine)
    queries = (
        apply_rotary(dot(lifted_one, query_in), cosine_table, sine_table) * HEAD_SIZE ** (-0.5)
    ).astype(b16)
    span = (reach + 1) * group
    key_positions = (place - reach) * group + jnp.arange(span, dtype=jnp.int32)
    padded = jnp.concatenate([jnp.full((reach * group,), -1, jnp.int32), all_segments])
    key_segments = lax.dynamic_slice_in_dim(padded, place * group, span)
    query_segments = key_segments[reach * group :]
    valid = (key_positions[None, :] <= positions[:, None]) & (
        positions[:, None] - key_positions[None, :] < SLIDE_WINDOW
    )
    valid = valid & (key_positions[None, :] >= 0)
    valid = valid & (key_segments[None, :] == query_segments[:, None])
    bent = jnp.tanh(dot_nt(queries, keys) / softcap)
    masked = jnp.where(valid, softcap * bent, negative)
    weights = jnp.exp(masked - jnp.max(masked, axis=-1, keepdims=True))
    probs = weights / jnp.sum(weights, axis=-1, keepdims=True)
    probs_low = probs.astype(b16)
    mixed = dot(after(probs_low, up_got, gate_w, *out_got), values).astype(b16)
    branch = collect_group(dot_nt(mixed, w_out), sub, up_w, down_got)

    own_tokens = lax.dynamic_slice_in_dim(tokens, lane * sub, sub).astype(f32)
    grad_out = lax.dynamic_slice_in_dim(cotangent, lane * sub, sub).astype(f32)
    scale_two = rms_scale(branch)
    normed_two = branch * scale_two
    middle = own_tokens + normed_two * gains[1]
    scale_three = rms_scale(middle)
    normed_three = middle * scale_three
    lifted_two = (normed_three * gains[2]).astype(b16)

    def feed(number, chunk):
        gate = dot(chunk, gate_w)
        upper = dot(chunk, up_w)
        hidden = gated(gate, upper).astype(b16)
        return dot_nt(hidden, down_w), gate, upper, hidden

    lifted_two, down, (gate, upper, hidden), unused = pipelined(lifted_two, feed)
    scale_four = rms_scale(down)
    normed_four = down * scale_four
    output = (middle + normed_four * gains[3]).astype(b16)

    def unit_grad(left, right):
        partial = dot_tn(jnp.concatenate(left, axis=0), jnp.concatenate(right, axis=0))
        return partial.reshape(n, 2, deep // 2, units)

    grad_down = rms_back(grad_out * gains[3], normed_four, scale_four).astype(b16)
    def feed_back(number, chunk):
        unused, pull = jax.vjp(gated, gate[number], upper[number])
        grad_gate, grad_upper = [side.astype(b16) for side in pull(dot(chunk, down_w))]
        partial = dot_nt(grad_gate, gate_w) + dot_nt(grad_upper, up_w)
        return partial, grad_gate, grad_upper

    grad_down, lifted_grad, (grad_gate, grad_upper), partial = pipelined(grad_down, feed_back)
    output = spread_lanes(after(output, *grad_down))
    down_sum = unit_grad(grad_down, after(hidden, partial[-3]))
    down_part = fold(down_sum, 0, 1).astype(b16)
    gate_sum = unit_grad(lifted_two, after(grad_gate, partial[-1]))
    gate_part = fold(after(gate_sum, down_part), 0, 1).astype(b16)
    up_sum = unit_grad(lifted_two, after(grad_upper, partial[-1]))
    up_part = fold(after(up_sum, gate_part), 0, 1).astype(b16)
    grad_w_down = exchange(down_part, "dp")
    lifted_grad = after(lifted_grad, down_part, gate_sum, up_sum)
    grad_middle = grad_out + rms_back(lifted_grad * gains[2], normed_three, scale_three)
    grad_branch = rms_back(grad_middle * gains[1], normed_two, scale_two).astype(b16)
    grad_w_gate = exchange(after(gate_part, grad_w_down), "dp")
    grad_branch = spread_group(after(grad_branch, output, grad_w_down, gate_part), grad_w_gate, up_part)

    def row_blocks(left, right):
        return row_grad(left, right).reshape(n, deep, HEAD_SIZE)

    grad_w_up = exchange(after(up_part, grad_w_gate), "dp")
    grad_w_out = ring_summed(after(row_blocks(grad_branch, mixed), grad_w_gate))
    grad_query_pre, kept, sent = attend_back(
        grad_branch, w_out, keys, values, queries, probs, bent, (cosine_table, sine_table), side
    )
    kept = kept.reshape(reach + 1, group, HEAD_SIZE)
    sent = sent.reshape(reach + 1, group, HEAD_SIZE)
    slots = [
        kept[slot] + swapped(sent[slot], "context", 1).astype(f32) for slot in range(reach + 1)
    ]
    slots[0] = after(slots[0], grad_w_up, grad_w_out)
    mine = slots[reach]
    for steps in range(reach, 0, -1):
        mine = mine + shifted(slots[reach - steps].astype(b16), "dp", -steps).astype(f32)
    grad_w_query = ring_summed(after(row_blocks(lifted_one, grad_query_pre), grad_w_out))
    mine = after(mine, grad_w_query)
    mine = jnp.where(is_first, rotate_back(mine, cosine_table, sine_table), mine).astype(b16)
    first_grad = dot_nt(grad_query_pre, query_in) + dot_nt(mine, pair_in)
    grad_gain_one = jnp.sum(first_grad * normed_one, axis=0)
    first_grad = collect_group(first_grad, sub)
    own_scale = rms_scale(own_tokens)
    own_normed = own_tokens * own_scale
    grad_inputs = grad_middle + rms_back(first_grad * gains[0], own_normed, own_scale)
    grad_inputs = grad_inputs.astype(b16)
    grad_gains = jnp.stack(
        [
            grad_gain_one,
            jnp.sum(grad_middle * normed_two, axis=0),
            jnp.sum(lifted_grad * normed_three, axis=0),
            jnp.sum(grad_out * normed_four, axis=0),
        ]
    )

    def halves(total):
        kept, sent = picked(is_first, (total[: deep // 2], total[deep // 2 : deep]))
        return kept, swapped(sent.astype(b16), "context", 1).astype(f32)

    rider = jnp.swapaxes(grad_gains.astype(b16).reshape(4, n, deep), 0, 1).reshape(n, -1)
    rider = jnp.pad(rider, ((0, 0), (0, 16 * HEAD_SIZE - rider.shape[1])))
    rider = jnp.concatenate([row_blocks(lifted_one, mine), rider.reshape(n, 16, HEAD_SIZE)], axis=1)
    grad_pair = ring_summed(rider)
    grad_inputs, grad_pair = together(grad_inputs, grad_pair)
    grad_inputs = spread_lanes(grad_inputs).astype(f32)
    grad_gains = grad_pair[deep:].reshape(-1)[: 4 * deep].reshape(4, 2, deep // 2)
    grad_gains, sent = picked(is_first, (grad_gains[:, 0], grad_gains[:, 1]))
    grad_gains = grad_gains + swapped(sent, "context", 1)
    grad_gains = grad_gains + swapped(grad_gains, "tensor", 2)
    grad_gains = grad_gains + swapped(grad_gains, "tensor", 1)
    grad_w_out = jnp.concatenate(picked(is_first, halves(grad_w_out)), axis=1).T
    grad_w_query = jnp.concatenate(picked(is_first, halves(grad_w_query)), axis=1)
    grad_w_key, grad_w_value = picked(is_first, halves(grad_pair))
    grad_w_down, grad_w_gate, grad_w_up = after(
        (grad_w_down, grad_w_gate, grad_w_up), grad_w_out
    )
    grad_w_down = side_by_side(grad_w_down).T
    grad_w_gate = side_by_side(grad_w_gate)
    grad_w_up = side_by_side(grad_w_up)
    return (
        output,
        grad_inputs,
        grad_w_query,
        grad_w_key,
        grad_w_value,
        grad_w_out,
        grad_w_gate,
        grad_w_up,
        grad_w_down,
        grad_gains[0],
        grad_gains[1],
        grad_gains[2],
        grad_gains[3],
    )


def solution(mesh):
    return jax.shard_map(
        on_device,
        mesh=mesh,
        in_specs=(
            P(("dp", "context"), None),
            P(("dp", "context")),
            P("dp", "tensor"),
            P("dp", "tensor"),
            P("dp", "tensor"),
            P("tensor", "dp"),
            P("dp", "tensor"),
            P("dp", "tensor"),
            P("tensor", "dp"),
            P("dp"),
            P("dp"),
            P("dp"),
            P("dp"),
            P(("dp", "context"), None),
        ),
        out_specs=(
            P(("dp", "context"), None),
            P(("dp", "context"), None),
            P(("dp", "context"), "tensor"),
            P(("dp", "context"), "tensor"),
            P(("dp", "context"), "tensor"),
            P("tensor", ("dp", "context")),
            P(("dp", "context"), "tensor"),
            P(("dp", "context"), "tensor"),
            P("tensor", ("dp", "context")),
            P(("dp", "context")),
            P(("dp", "context")),
            P(("dp", "context")),
            P(("dp", "context")),
        ),
        check_vma=False,
    )
```

time: 855 us -> 791 us (0.925)
  local copies, waits for them, and re-layouts: 93 us -> 39.8 us
  waiting for transfers between devices: 439 us -> 399 us
  Pallas kernels: 0 us -> 27.2 us
  matrix products: 79.7 us -> 57.5 us
  starting transfers between devices: 142 us -> 160 us
    ppermute x12 -> x30, waiting for transfers between devices: 54.8 us -> 171 us  [rotated(): return lax.ppermute(value, 'dp', [(s, (s + steps) % n) for s in range(n)])]
    all_to_all x12 -> x6, waiting for transfers between devices: 116 us -> 30.1 us  [exchange(): return lax.all_to_all(blocks, axis, 0, 0, tiled=True)]
    ppermute x70 -> x65, waiting for transfers between devices: 249 us -> 172 us  [swapped(): lax.ppermute(value, axis, [(place, place ^ bit) for place in range(count)])]
    pallas_call x0 -> x8, Pallas kernels: none -> 27.2 us  [the longest x1 12.9 us: attend_back(): pl.pallas_call(kernel, grid=(steps,), in_specs=[pl.BlockSpec(memory_space...]
    convert_element_type x8 -> x1, local copies, waits for them, and re-layouts: 28.3 us -> 1.58 us  [on_device(): grad_inputs = spread_lanes(grad_inputs).astype(f32)]
    ppermute x12 -> x30, starting transfers between devices: 16.8 us -> 43.1 us  [rotated(): return lax.ppermute(value, 'dp', [(s, (s + steps) % n) for s in range(n)])]
    reshape x6 -> x0, local copies, waits for them, and re-layouts: 16 us -> none  [the longest x4 7.76 us: unit_blocks(): half_of(weight, side, 0).reshape(deep // 2, n, units)]
    dot_general x8 -> x3, matrix products: 27.3 us -> 15.7 us  [dot_tn(): lax.dot_general(left, right, (((0,), (0,)), ((), ())), preferred_element_...]
  transfers between devices with their start and end apart: 100 -> 107, of which waited for: 52 -> 55; matrix products, arithmetic and copies ran while one was open for 26% -> 20% of each run, Pallas kernels for 0% -> 3%
where the time goes in v3:
time: 791 us; the launch traced here: 781 us
  waiting for transfers between devices  399 us (50%)
  starting transfers between devices  160 us (20%)
  other arithmetic  94.1 us (12%)
  matrix products  57.5 us (7%)
  local copies, waits for them, and re-layouts  39.8 us (5%)
  Pallas kernels  27.2 us (3%)
    ppermute x65, waiting for transfers between devices, swapped(): lax.ppermute(value, axis, [(place, place ^ bit) for place in range(count)])  172 us
    ppermute x30, waiting for transfers between devices, rotated(): return lax.ppermute(value, 'dp', [(s, (s + steps) % n) for s in range(n)])  171 us
    ppermute x65, starting transfers between devices, swapped(): lax.ppermute(value, axis, [(place, place ^ bit) for place in range(count)])  51.8 us
    all_to_all x6, starting transfers between devices, exchange(): return lax.all_to_all(blocks, axis, 0, 0, tiled=True)  47.6 us
    ppermute x30, starting transfers between devices, rotated(): return lax.ppermute(value, 'dp', [(s, (s + steps) % n) for s in range(n)])  43.1 us
    all_to_all x6, waiting for transfers between devices, exchange(): return lax.all_to_all(blocks, axis, 0, 0, tiled=True)  30.1 us
    ppermute x6, waiting for transfers between devices, shifted(): lax.ppermute(value, axis, [(s, s + steps) for s in range(count) if 0 <= s...  26.7 us
    dot_general x13, matrix products, dot_nt(): lax.dot_general(left, right, (((1,), (1,)), ((), ())), preferred_element_...  21 us
  transfers between devices with their start and end apart: 107, of which 55 were waited for; matrix products, arithmetic and copies ran while one was open for 20% of the time, Pallas kernels for 3%

profile of v3, /device:TPU:0, one launch (start us, length us, event | category | flops | bytes accessed | tf_op | source)
XLA Modules:
  0.0 781.1 jit_solution(15578154738872476366)
XLA Ops:
  0.7 2.8 concatenate.117
  4.5 5.1 collective-permute-start.2
  17.5 17.9 %collective-permute-done.3 = bf16[592,256]{1,0:T(8,128)(2,1)S(1)} collective-permute-done((bf16[592,256]{1,0:T(8,128)(2,1)S(1)}, bf16[592,256]{1,0:T(8,128)(2,1)S(1)}, u32[]{:S(2)}, u32[]{:S(2)}) %collective-permute-start.3) | collective-permute-done | bytes 303136 | tf_op jit(solution)/shard_map/ppermute | solution.py:97
  36.8 3.5 collective-permute-done.1
  46.5 5.7 collective-permute-start.8
  55.0 5.5 collective-permute-start.9
  63.2 5.0 unit_blocks.1
  68.9 14.7 %collective-permute-done.9 = bf16[512,256]{1,0:T(8,128)(2,1)} collective-permute-done((bf16[512,256]{1,0:T(8,128)(2,1)}, bf16[512,256]{1,0:T(8,128)(2,1)}, u32[]{:S(2)}, u32[]{:S(2)}) %collective-permute-start.9) | collective-permute-done | bytes 262176 | tf_op jit(solution)/shard_map/ppermute | solution.py:74
  86.4 16.7 %all-to-all-start = ((bf16[4,288,576]{2,1,0:T(8,128)(2,1)}), bf16[4,288,576]{2,1,0:T(8,128)(2,1)}, u32[]{:S(2)}, u32[]{:S(2)}) async-start(bf16[4,288,576]{2,1,0:T(8,128)(2,1)} %get-tuple-element.65), calls=%async_computation | async-start | bytes 2949120 | tf_op jit(solution)/shard_map/all_to_all | solution.py:51
  112.6 3.1 collective-permute-start.17
  118.2 3.9 collective-permute-start.18
  125.2 4.5 fusion.137
  130.8 21.2 %all-to-all-done = bf16[4,288,576]{2,1,0:T(8,128)(2,1)} async-done(((bf16[4,288,576]{2,1,0:T(8,128)(2,1)}), bf16[4,288,576]{2,1,0:T(8,128)(2,1)}, u32[]{:S(2)}, u32[]{:S(2)}) %all-to-all-start) | async-done | bytes 1327136 | tf_op jit(solution)/shard_map/all_to_all | solution.py:51
  151.9 4.5 all-to-all-start.1
  157.1 3.2 fusion.4
  160.3 3.5 fusion.135
  164.0 26.5 %collective-permute-done.15 = bf16[4,288,576]{2,1,0:T(8,128)(2,1)S(1)} collective-permute-done((bf16[4,288,576]{2,1,0:T(8,128)(2,1)}, bf16[4,288,576]{2,1,0:T(8,128)(2,1)S(1)}, u32[]{:S(2)}, u32[]{:S(2)}) %collective-permute-start.15) | collective-permute-done | bytes 1327136 | tf_op jit(solution)/shard_map/ppermute | solution.py:61
  202.4 3.6 all-to-all-start.2
  206.5 2.7 fusion.139
  209.3 3.0 copy_add_fusion
  212.3 28.6 %collective-permute-done.20 = bf16[4,288,576]{2,1,0:T(8,128)(2,1)S(1)} collective-permute-done((bf16[4,288,576]{2,1,0:T(8,128)(2,1)}, bf16[4,288,576]{2,1,0:T(8,128)(2,1)S(1)}, u32[]{:S(2)}, u32[]{:S(2)}) %collective-permute-start.20) | collective-permute-done | bytes 1327136 | tf_op jit(solution)/shard_map/ppermute | solution.py:61
  251.8 4.6 collective-permute-done.21
  271.5 2.9 collective-permute-start.31
  276.5 5.2 collective-permute-done.30
  289.3 10.1 %collective-permute-done.38 = bf16[64,2304]{1,0:T(8,128)(2,1)S(1)} collective-permute-done((bf16[64,2304]{1,0:T(8,128)(2,1)}, bf16[64,2304]{1,0:T(8,128)(2,1)S(1)}, u32[]{:S(2)}, u32[]{:S(2)}) %collective-permute-start.38) | collective-permute-done | bytes 294944 | tf_op jit(solution)/shard_map/ppermute | solution.py:97
  301.1 5.8 collective-permute-done.27
  315.6 2.8 collective-permute-done.40
  320.2 2.7 multiply_convert_fusion.3
  334.6 12.3 %collective-permute-done.42 = bf16[64,2304]{1,0:T(8,128)(2,1)S(1)} collective-permute-done((bf16[64,2304]{1,0:T(8,128)(2,1)S(1)}, bf16[64,2304]{1,0:T(8,128)(2,1)S(1)}, u32[]{:S(2)}, u32[]{:S(2)}) %collective-permute-start.42) | collective-permute-done | bytes 294944 | tf_op jit(solution)/shard_map/ppermute | solution.py:61
  347.2 11.6 %collective-permute-done.35 = bf16[128,2304]{1,0:T(8,128)(2,1)S(1)} collective-permute-done((bf16[128,2304]{1,0:T(8,128)(2,1)S(1)}, bf16[128,2304]{1,0:T(8,128)(2,1)S(1)}, u32[]{:S(2)}, u32[]{:S(2)}) %collective-permute-start.35) | collective-permute-done | bytes 589856 | tf_op jit(solution)/shard_map/ppermute | solution.py:61
  359.0 3.8 collective-permute-start.36
  362.9 7.9 %collective-permute-done.37 = bf16[64,2304]{1,0:T(8,128)(2,1)S(1)} collective-permute-done((bf16[64,2304]{1,0:T(8,128)(2,1)S(1)}, bf16[64,2304]{1,0:T(8,128)(2,1)S(1)}, u32[]{:S(2)}, u32[]{:S(2)}) %collective-permute-start.37) | collective-permute-done | bytes 294944 | tf_op jit(solution)/shard_map/ppermute | solution.py:97
  370.7 2.9 collective-permute-done.36
  377.7 4.7 collective-permute-done.44
  385.1 5.7 collective-permute-done.46
  393.1 11.1 %collective-permute-done.50 = bf16[64,2304]{1,0:T(8,128)(2,1)S(1)} collective-permute-done((bf16[64,2304]{1,0:T(8,128)(2,1)S(1)}, bf16[64,2304]{1,0:T(8,128)(2,1)S(1)}, u32[]{:S(2)}, u32[]{:S(2)}) %collective-permute-start.50) | collective-permute-done | bytes 294944 | tf_op jit(solution)/shard_map/ppermute | solution.py:97
  405.7 6.3 collective-permute-done.51
  417.2 3.7 collective-permute-done.55
  436.7 3.9 fusion.23
  442.5 7.8 collective-permute-done.62
  451.5 6.0 fusion.29
  457.5 5.8 fusion.35
  466.5 8.8 %collective-permute-done.64 = bf16[4,288,576]{2,1,0:T(8,128)(2,1)S(1)} collective-permute-done((bf16[4,288,576]{2,1,0:T(8,128)(2,1)S(1)}, bf16[4,288,576]{2,1,0:T(8,128)(2,1)S(1)}, u32[]{:S(2)}, u32[]{:S(2)}) %collective-permute-start.64) | collective-permute-done | bytes 1327136 | tf_op jit(solution)/shard_map/ppermute | solution.py:61
  476.8 5.8 all-to-all-start.3
  488.2 3.2 fusion.10
  491.7 26.6 %collective-permute-done.60 = bf16[64,2304]{1,0:T(8,128)(2,1)S(1)} collective-permute-done((bf16[64,2304]{1,0:T(8,128)(2,1)S(1)}, bf16[64,2304]{1,0:T(8,128)(2,1)S(1)}, u32[]{:S(2)}, u32[]{:S(2)}) %collective-permute-start.60) | collective-permute-done | bytes 294944 | tf_op jit(solution)/shard_map/ppermute | solution.py:97
  527.0 4.0 collective-permute-done.66
  534.5 4.1 fusion.11
  538.9 12.2 %all-to-all-start.4 = ((bf16[4,288,576]{2,1,0:T(8,128)(2,1)}), bf16[4,288,576]{2,1,0:T(8,128)(2,1)S(1)}, u32[]{:S(2)}, u32[]{:S(2)}) async-start(bf16[4,288,576]{2,1,0:T(8,128)(2,1)} %fusion.6), calls=%async_computation.4 | async-start | bytes 2949120 | tf_op jit(solution)/shard_map/all_to_all | solution.py:51
  553.1 4.8 collective-permute-done.67
  559.2 12.2 %collective-permute-done.70 = bf16[4,288,576]{2,1,0:T(8,128)(2,1)} collective-permute-done((bf16[4,288,576]{2,1,0:T(8,128)(2,1)}, bf16[4,288,576]{2,1,0:T(8,128)(2,1)}, u32[]{:S(2)}, u32[]{:S(2)}) %collective-permute-start.70) | collective-permute-done | bytes 1327136 | tf_op jit(solution)/shard_map/ppermute | solution.py:61
  571.4 4.7 fusion.5
  576.0 7.6 all-to-all-done.4.source
  583.7 4.8 all-to-all-start.5
  592.0 3.8 collective-permute-start.76
  598.8 12.9 %attend_back.1 = (bf16[512,256]{1,0:T(8,128)(2,1)S(1)}, f32[2048,256]{1,0:T(8,128)}, bf16[2048,256]{1,0:T(8,128)(2,1)S(1)}) custom-call(s32[1]{0:T(128)} %bitcast.16.side_ref, bf16[512,2304]{1,0:T(8,128)(2,1)} %bitcast.334, bf16[2304,256]{1,0:T(8,128)(2,1)S(1)} %bitcast.336, bf16[2048,256]{1,0:T(8,128)(2,1)S(1)} %copy-done.8, ...), custom_call_target="tpu_custom_call" | custom-call | tf_op jit(solution)/shard_map/attend_back/pallas_call | solution.py:299
  615.3 4.4 collective-permute-done.76
  621.5 28.3 %collective-permute-done.75 = bf16[576,256]{1,0:T(8,128)(2,1)S(1)} collective-permute-done((bf16[576,256]{1,0:T(8,128)(2,1)S(1)}, bf16[576,256]{1,0:T(8,128)(2,1)S(1)}, u32[]{:S(2)}, u32[]{:S(2)}) %collective-permute-start.75) | collective-permute-done | bytes 294944 | tf_op jit(solution)/shard_map/ppermute | solution.py:97
  658.5 6.3 collective-permute-done.84
  666.1 22.6 %collective-permute-done.83 = bf16[576,256]{1,0:T(8,128)(2,1)} collective-permute-done((bf16[576,256]{1,0:T(8,128)(2,1)}, bf16[576,256]{1,0:T(8,128)(2,1)}, u32[]{:S(2)}, u32[]{:S(2)}) %collective-permute-start.83) | collective-permute-done | bytes 294944 | tf_op jit(solution)/shard_map/ppermute | solution.py:97
  692.1 9.7 %collective-permute-done.79 = bf16[512,256]{1,0:T(8,128)(2,1)S(1)} collective-permute-done((bf16[512,256]{1,0:T(8,128)(2,1)}, bf16[512,256]{1,0:T(8,128)(2,1)S(1)}, u32[]{:S(2)}, u32[]{:S(2)}) %collective-permute-start.79) | collective-permute-done | bytes 262176 | tf_op jit(solution)/shard_map/ppermute | solution.py:74
  739.0 14.4 %collective-permute-done.91 = bf16[592,256]{1,0:T(8,128)(2,1)S(1)} collective-permute-done((bf16[592,256]{1,0:T(8,128)(2,1)S(1)}, bf16[592,256]{1,0:T(8,128)(2,1)S(1)}, u32[]{:S(2)}, u32[]{:S(2)}) %collective-permute-start.91) | collective-permute-done | bytes 303136 | tf_op jit(solution)/shard_map/ppermute | solution.py:97
  762.9 3.2 collective-permute-done.98
  772.4 3.3 side_by_side.4
  (591 shorter events, 257.8 us)
Async XLA Ops:
  9.6 25.8 %collective-permute-start.3 = (bf16[592,256]{1,0:T(8,128)(2,1)S(1)}, bf16[592,256]{1,0:T(8,128)(2,1)S(1)}, u32[]{:S(2)}, u32[]{:S(2)}) collective-permute-start(bf16[592,256]{1,0:T(8,128)(2,1)S(1)} %pad_maximum_fusion.31), channel_id=1, source_target_pairs={{0,16},{8,24},{16,0},{24,8},{1,17},{9,25},{17,1},{25,9},{2,18},{10... | collective-permute-start | bytes 909320 | tf_op jit(solution)/shard_map/ppermute | solution.py:97
  9.6 25.8 %collective-permute-start.4 = (bf16[592,256]{1,0:T(8,128)(2,1)S(1)}, bf16[592,256]{1,0:T(8,128)(2,1)S(1)}, u32[]{:S(2)}, u32[]{:S(2)}) collective-permute-start(bf16[592,256]{1,0:T(8,128)(2,1)S(1)} %pad_maximum_fusion.31), channel_id=1, source_target_pairs={{0,8},{8,16},{16,24},{24,0},{1,9},{9,17},{17,25},{25,1},{2,10},{10... | collective-permute-start | bytes 909320 | tf_op jit(solution)/shard_map/ppermute | solution.py:97
  11.9 40.3 %collective-permute-start = (bf16[1,256]{1,0:T(2,128)(2,1)}, bf16[1,256]{1,0:T(2,128)(2,1)}, u32[]{:S(2)}, u32[]{:S(2)}) collective-permute-start(bf16[1,256]{1,0:T(2,128)(2,1)} %convert_element_type.420), channel_id=1, source_target_pairs={{0,4},{4,0},{1,5},{5,1},{2,6},{6,2},{3,7},{7,3},{8,12},{12,8},{9,1... | collective-permute-start | bytes 1544 | tf_op jit(solution)/shard_map/ppermute | solution.py:61
  13.4 26.9 %collective-permute-start.1 = (bf16[256,2304]{1,0:T(8,128)(2,1)}, bf16[256,2304]{1,0:T(8,128)(2,1)}, u32[]{:S(2)}, u32[]{:S(2)}) collective-permute-start(bf16[256,2304]{1,0:T(8,128)(2,1)} %param.14), channel_id=1, source_target_pairs={{0,4},{4,0},{1,5},{5,1},{2,6},{6,2},{3,7},{7,3},{8,12},{12,8},{9,1... | collective-permute-start | bytes 3538952 | tf_op jit(solution)/shard_map/ppermute | solution.py:61
  46.5 14.0 %collective-permute-start.8 = (bf16[512,256]{1,0:T(8,128)(2,1)}, bf16[512,256]{1,0:T(8,128)(2,1)}, u32[]{:S(2)}, u32[]{:S(2)}) collective-permute-start(bf16[512,256]{1,0:T(8,128)(2,1)} %fusion.85), channel_id=1, source_target_pairs={{0,24},{1,25},{2,26},{3,27},{4,28},{5,29},{6,30},{7,31}} | collective-permute-start | bytes 786440 | tf_op jit(solution)/shard_map/ppermute | solution.py:74
  52.9 50.8 %collective-permute-start.5 = (bf16[592,256]{1,0:T(8,128)(2,1)S(1)}, bf16[592,256]{1,0:T(8,128)(2,1)}, u32[]{:S(2)}, u32[]{:S(2)}) collective-permute-start(bf16[592,256]{1,0:T(8,128)(2,1)S(1)} %pad_maximum_fusion.30), channel_id=1, source_target_pairs={{0,24},{8,0},{16,8},{24,16},{1,25},{9,1},{17,9},{25,17},{2,26},{10... | collective-permute-start | bytes 909320 | tf_op jit(solution)/shard_map/ppermute | solution.py:97
  53.0 52.2 %collective-permute-start.6 = (bf16[592,256]{1,0:T(8,128)(2,1)S(1)}, bf16[592,256]{1,0:T(8,128)(2,1)}, u32[]{:S(2)}, u32[]{:S(2)}) collective-permute-start(bf16[592,256]{1,0:T(8,128)(2,1)S(1)} %pad_maximum_fusion.30), channel_id=1, source_target_pairs={{0,16},{8,24},{16,0},{24,8},{1,17},{9,25},{17,1},{25,9},{2,18},{10... | collective-permute-start | bytes 909320 | tf_op jit(solution)/shard_map/ppermute | solution.py:97
  53.1 52.6 %collective-permute-start.7 = (bf16[592,256]{1,0:T(8,128)(2,1)S(1)}, bf16[592,256]{1,0:T(8,128)(2,1)}, u32[]{:S(2)}, u32[]{:S(2)}) collective-permute-start(bf16[592,256]{1,0:T(8,128)(2,1)S(1)} %pad_maximum_fusion.30), channel_id=1, source_target_pairs={{0,8},{8,16},{16,24},{24,0},{1,9},{9,17},{17,25},{25,1},{2,10},{10... | collective-permute-start | bytes 909320 | tf_op jit(solution)/shard_map/ppermute | solution.py:97
  55.0 28.6 %collective-permute-start.9 = (bf16[512,256]{1,0:T(8,128)(2,1)}, bf16[512,256]{1,0:T(8,128)(2,1)}, u32[]{:S(2)}, u32[]{:S(2)}) collective-permute-start(bf16[512,256]{1,0:T(8,128)(2,1)} %fusion.85), channel_id=1, source_target_pairs={{0,16},{8,24},{1,17},{9,25},{2,18},{10,26},{3,19},{11,27},{4,20},{... | collective-permute-start | bytes 786440 | tf_op jit(solution)/shard_map/ppermute | solution.py:74
  60.5 25.9 %collective-permute-start.10 = (bf16[512,256]{1,0:T(8,128)(2,1)}, bf16[512,256]{1,0:T(8,128)(2,1)}, u32[]{:S(2)}, u32[]{:S(2)}) collective-permute-start(bf16[512,256]{1,0:T(8,128)(2,1)} %fusion.85), channel_id=1, source_target_pairs={{0,8},{8,16},{16,24},{1,9},{9,17},{17,25},{2,10},{10,18},{18,26},{... | collective-permute-start | bytes 786440 | tf_op jit(solution)/shard_map/ppermute | solution.py:74
  83.6 39.0 %collective-permute-start.14 = (bf16[512,256]{1,0:T(8,128)(2,1)}, bf16[512,256]{1,0:T(8,128)(2,1)}, u32[]{:S(2)}, u32[]{:S(2)}) collective-permute-start(bf16[512,256]{1,0:T(8,128)(2,1)} %fusion.85), channel_id=1, source_target_pairs={{0,4},{4,0},{1,5},{5,1},{2,6},{6,2},{3,7},{7,3},{8,12},{12,8},{9,1... | collective-permute-start | bytes 786440 | tf_op jit(solution)/shard_map/ppermute | solution.py:61
  86.4 65.5 %all-to-all-start = ((bf16[4,288,576]{2,1,0:T(8,128)(2,1)}), bf16[4,288,576]{2,1,0:T(8,128)(2,1)}, u32[]{:S(2)}, u32[]{:S(2)}) async-start(bf16[4,288,576]{2,1,0:T(8,128)(2,1)} %get-tuple-element.65), calls=%async_computation | async-start | bytes 2949120 | tf_op jit(solution)/shard_map/all_to_all | solution.py:51
  103.7 14.5 %collective-permute-start.12 = (bf16[512,256]{1,0:T(8,128)(2,1)}, bf16[512,256]{1,0:T(8,128)(2,1)S(1)}, u32[]{:S(2)}, u32[]{:S(2)}) collective-permute-start(bf16[512,256]{1,0:T(8,128)(2,1)} %collective-permute-done.9), channel_id=1, source_target_pairs={{0,4},{4,0},{1,5},{5,1},{2,6},{6,2},{3,7},{7,3},{8,12},{12,8},{9,1... | collective-permute-start | bytes 786440 | tf_op jit(solution)/shard_map/ppermute | solution.py:61
  105.2 17.4 %collective-permute-start.13 = (bf16[512,256]{1,0:T(8,128)(2,1)}, bf16[512,256]{1,0:T(8,128)(2,1)S(1)}, u32[]{:S(2)}, u32[]{:S(2)}) collective-permute-start(bf16[512,256]{1,0:T(8,128)(2,1)} %collective-permute-done.10), channel_id=1, source_target_pairs={{0,4},{4,0},{1,5},{5,1},{2,6},{6,2},{3,7},{7,3},{8,12},{12,8},{9,1... | collective-permute-start | bytes 786440 | tf_op jit(solution)/shard_map/ppermute | solution.py:61
  109.9 53.8 %collective-permute-start.16 = (bf16[576,256]{1,0:T(8,128)(2,1)S(1)}, bf16[576,256]{1,0:T(8,128)(2,1)S(1)}, u32[]{:S(2)}, u32[]{:S(2)}) collective-permute-start(bf16[576,256]{1,0:T(8,128)(2,1)S(1)} %copy-done.60), channel_id=1, source_target_pairs={{0,8},{8,16},{16,24},{24,0},{1,9},{9,17},{17,25},{25,1},{2,10},{10... | collective-permute-start | bytes 884744 | tf_op jit(solution)/shard_map/ppermute | solution.py:97
  112.6 51.2 %collective-permute-start.17 = (bf16[576,256]{1,0:T(8,128)(2,1)S(1)}, bf16[576,256]{1,0:T(8,128)(2,1)S(1)}, u32[]{:S(2)}, u32[]{:S(2)}) collective-permute-start(bf16[576,256]{1,0:T(8,128)(2,1)S(1)} %copy-done.60), channel_id=1, source_target_pairs={{0,16},{8,24},{16,0},{24,8},{1,17},{9,25},{17,1},{25,9},{2,18},{10... | collective-permute-start | bytes 884744 | tf_op jit(solution)/shard_map/ppermute | solution.py:97
  118.2 45.6 %collective-permute-start.18 = (bf16[576,256]{1,0:T(8,128)(2,1)S(1)}, bf16[576,256]{1,0:T(8,128)(2,1)S(1)}, u32[]{:S(2)}, u32[]{:S(2)}) collective-permute-start(bf16[576,256]{1,0:T(8,128)(2,1)S(1)} %copy-done.60), channel_id=1, source_target_pairs={{0,24},{8,0},{16,8},{24,16},{1,25},{9,1},{17,9},{25,17},{2,26},{10... | collective-permute-start | bytes 884744 | tf_op jit(solution)/shard_map/ppermute | solution.py:97
  151.9 44.0 %all-to-all-start.1 = ((bf16[4,288,576]{2,1,0:T(8,128)(2,1)}), bf16[4,288,576]{2,1,0:T(8,128)(2,1)}, u32[]{:S(2)}, u32[]{:S(2)}) async-start(bf16[4,288,576]{2,1,0:T(8,128)(2,1)} %get-tuple-element.66), calls=%async_computation.1 | async-start | bytes 2949120 | tf_op jit(solution)/shard_map/all_to_all | solution.py:51
  156.5 34.1 %collective-permute-start.15 = (bf16[4,288,576]{2,1,0:T(8,128)(2,1)}, bf16[4,288,576]{2,1,0:T(8,128)(2,1)S(1)}, u32[]{:S(2)}, u32[]{:S(2)}) collective-permute-start(bf16[4,288,576]{2,1,0:T(8,128)(2,1)} %all-to-all-done), channel_id=1, source_target_pairs={{0,4},{4,0},{1,5},{5,1},{2,6},{6,2},{3,7},{7,3},{8,12},{12,8},{9,1... | collective-permute-start | bytes 3981320 | tf_op jit(solution)/shard_map/ppermute | solution.py:61
  202.4 42.6 %all-to-all-start.2 = ((bf16[4,288,576]{2,1,0:T(8,128)(2,1)}), bf16[4,288,576]{2,1,0:T(8,128)(2,1)S(1)}, u32[]{:S(2)}, u32[]{:S(2)}) async-start(bf16[4,288,576]{2,1,0:T(8,128)(2,1)} %get-tuple-element.70), calls=%async_computation.2 | async-start | bytes 2949120 | tf_op jit(solution)/shard_map/all_to_all | solution.py:51
  205.9 35.0 %collective-permute-start.20 = (bf16[4,288,576]{2,1,0:T(8,128)(2,1)}, bf16[4,288,576]{2,1,0:T(8,128)(2,1)S(1)}, u32[]{:S(2)}, u32[]{:S(2)}) collective-permute-start(bf16[4,288,576]{2,1,0:T(8,128)(2,1)} %all-to-all-done.1), channel_id=1, source_target_pairs={{0,4},{4,0},{1,5},{5,1},{2,6},{6,2},{3,7},{7,3},{8,12},{12,8},{9,1... | collective-permute-start | bytes 3981320 | tf_op jit(solution)/shard_map/ppermute | solution.py:61
  275.9 31.0 %collective-permute-start.27 = (bf16[4,288,576]{2,1,0:T(8,128)(2,1)}, bf16[4,288,576]{2,1,0:T(8,128)(2,1)S(1)}, u32[]{:S(2)}, u32[]{:S(2)}) collective-permute-start(bf16[4,288,576]{2,1,0:T(8,128)(2,1)} %copy-done.35), channel_id=1, source_target_pairs={{0,4},{4,0},{1,5},{5,1},{2,6},{6,2},{3,7},{7,3},{8,12},{12,8},{9,1... | collective-permute-start | bytes 3981320 | tf_op jit(solution)/shard_map/ppermute | solution.py:61
  284.1 15.4 %collective-permute-start.38 = (bf16[64,2304]{1,0:T(8,128)(2,1)}, bf16[64,2304]{1,0:T(8,128)(2,1)S(1)}, u32[]{:S(2)}, u32[]{:S(2)}) collective-permute-start(bf16[64,2304]{1,0:T(8,128)(2,1)} %multiply_convert_fusion.9), channel_id=1, source_target_pairs={{0,16},{8,24},{16,0},{24,8},{1,17},{9,25},{17,1},{25,9},{2,18},{10... | collective-permute-start | bytes 884744 | tf_op jit(solution)/shard_map/ppermute | solution.py:97
  286.5 14.5 %collective-permute-start.26 = (bf16[128,2304]{1,0:T(8,128)(2,1)S(1)}, bf16[128,2304]{1,0:T(8,128)(2,1)S(1)}, u32[]{:S(2)}, u32[]{:S(2)}) collective-permute-start(bf16[128,2304]{1,0:T(8,128)(2,1)S(1)} %pad_maximum_fusion.21), channel_id=1, source_target_pairs={{0,1},{1,0},{2,3},{3,2},{4,5},{5,4},{6,7},{7,6},{8,9},{9,8},{10,11... | collective-permute-start | bytes 1769480 | tf_op jit(solution)/shard_map/ppermute | solution.py:61
  287.7 25.7 %collective-permute-start.32 = (bf16[128,2304]{1,0:T(8,128)(2,1)S(1)}, bf16[128,2304]{1,0:T(8,128)(2,1)S(1)}, u32[]{:S(2)}, u32[]{:S(2)}) collective-permute-start(bf16[128,2304]{1,0:T(8,128)(2,1)S(1)} %pad_maximum_fusion.22), channel_id=1, source_target_pairs={{0,2},{1,3},{2,0},{3,1},{4,6},{5,7},{6,4},{7,5},{8,10},{9,11},{10,... | collective-permute-start | bytes 1769480 | tf_op jit(solution)/shard_map/ppermute | solution.py:61
  299.4 15.3 %collective-permute-start.39 = (bf16[64,2304]{1,0:T(8,128)(2,1)S(1)}, bf16[64,2304]{1,0:T(8,128)(2,1)S(1)}, u32[]{:S(2)}, u32[]{:S(2)}) collective-permute-start(bf16[64,2304]{1,0:T(8,128)(2,1)S(1)} %collective-permute-done.38), channel_id=1, source_target_pairs={{0,2},{1,3},{2,0},{3,1},{4,6},{5,7},{6,4},{7,5},{8,10},{9,11},{10,... | collective-permute-start | bytes 884744 | tf_op jit(solution)/shard_map/ppermute | solution.py:61
  315.4 15.1 %collective-permute-start.28 = (bf16[128,2304]{1,0:T(8,128)(2,1)S(1)}, bf16[128,2304]{1,0:T(8,128)(2,1)S(1)}, u32[]{:S(2)}, u32[]{:S(2)}) collective-permute-start(bf16[128,2304]{1,0:T(8,128)(2,1)S(1)} %slice.730), channel_id=1, source_target_pairs={{0,1},{1,0},{2,3},{3,2},{4,5},{5,4},{6,7},{7,6},{8,9},{9,8},{10,11... | collective-permute-start | bytes 1769480 | tf_op jit(solution)/shard_map/ppermute | solution.py:61
  330.7 32.2 %collective-permute-start.29 = (bf16[64,2304]{1,0:T(8,128)(2,1)S(1)}, bf16[64,2304]{1,0:T(8,128)(2,1)S(1)}, u32[]{:S(2)}, u32[]{:S(2)}) collective-permute-start(bf16[64,2304]{1,0:T(8,128)(2,1)S(1)} %slice.734), channel_id=1, source_target_pairs={{0,2},{1,3},{2,0},{3,1},{4,6},{5,7},{6,4},{7,5},{8,10},{9,11},{10,... | collective-permute-start | bytes 884744 | tf_op jit(solution)/shard_map/ppermute | solution.py:61
  332.2 14.7 %collective-permute-start.42 = (bf16[64,2304]{1,0:T(8,128)(2,1)S(1)}, bf16[64,2304]{1,0:T(8,128)(2,1)S(1)}, u32[]{:S(2)}, u32[]{:S(2)}) collective-permute-start(bf16[64,2304]{1,0:T(8,128)(2,1)S(1)} %slice.733), channel_id=1, source_target_pairs={{0,2},{1,3},{2,0},{3,1},{4,6},{5,7},{6,4},{7,5},{8,10},{9,11},{10,... | collective-permute-start | bytes 884744 | tf_op jit(solution)/shard_map/ppermute | solution.py:61
  334.0 24.7 %collective-permute-start.35 = (bf16[128,2304]{1,0:T(8,128)(2,1)S(1)}, bf16[128,2304]{1,0:T(8,128)(2,1)S(1)}, u32[]{:S(2)}, u32[]{:S(2)}) collective-permute-start(bf16[128,2304]{1,0:T(8,128)(2,1)S(1)} %slice.729), channel_id=1, source_target_pairs={{0,2},{1,3},{2,0},{3,1},{4,6},{5,7},{6,4},{7,5},{8,10},{9,11},{10,... | collective-permute-start | bytes 1769480 | tf_op jit(solution)/shard_map/ppermute | solution.py:61
  347.0 15.9 %collective-permute-start.43 = (bf16[64,2304]{1,0:T(8,128)(2,1)S(1)}, bf16[64,2304]{1,0:T(8,128)(2,1)S(1)}, u32[]{:S(2)}, u32[]{:S(2)}) collective-permute-start(bf16[64,2304]{1,0:T(8,128)(2,1)S(1)} %fusion.74), channel_id=1, source_target_pairs={{0,16},{8,24},{16,0},{24,8},{1,17},{9,25},{17,1},{25,9},{2,18},{10... | collective-permute-start | bytes 884744 | tf_op jit(solution)/shard_map/ppermute | solution.py:97
  359.0 14.6 %collective-permute-start.36 = (bf16[64,2304]{1,0:T(8,128)(2,1)S(1)}, bf16[64,2304]{1,0:T(8,128)(2,1)S(1)}, u32[]{:S(2)}, u32[]{:S(2)}) collective-permute-start(bf16[64,2304]{1,0:T(8,128)(2,1)S(1)} %get-tuple-element.218), channel_id=1, source_target_pairs={{0,24},{8,0},{16,8},{24,16},{1,25},{9,1},{17,9},{25,17},{2,26},{10... | collective-permute-start | bytes 884744 | tf_op jit(solution)/shard_map/ppermute | solution.py:97
  382.4 29.7 %collective-permute-start.45 = (bf16[128,2304]{1,0:T(8,128)(2,1)S(1)}, bf16[128,2304]{1,0:T(8,128)(2,1)S(1)}, u32[]{:S(2)}, u32[]{:S(2)}) collective-permute-start(bf16[128,2304]{1,0:T(8,128)(2,1)S(1)} %pad_maximum_fusion.24), channel_id=1, source_target_pairs={{0,1},{1,0},{2,3},{3,2},{4,5},{5,4},{6,7},{7,6},{8,9},{9,8},{10,11... | collective-permute-start | bytes 1769480 | tf_op jit(solution)/shard_map/ppermute | solution.py:61
  391.5 24.7 %collective-permute-start.48 = (bf16[128,2304]{1,0:T(8,128)(2,1)S(1)}, bf16[128,2304]{1,0:T(8,128)(2,1)S(1)}, u32[]{:S(2)}, u32[]{:S(2)}) collective-permute-start(bf16[128,2304]{1,0:T(8,128)(2,1)S(1)} %pad_maximum_fusion.25), channel_id=1, source_target_pairs={{0,2},{1,3},{2,0},{3,1},{4,6},{5,7},{6,4},{7,5},{8,10},{9,11},{10,... | collective-permute-start | bytes 1769480 | tf_op jit(solution)/shard_map/ppermute | solution.py:61
  421.8 69.9 %collective-permute-start.56 = (bf16[64,2304]{1,0:T(8,128)(2,1)}, bf16[64,2304]{1,0:T(8,128)(2,1)}, u32[]{:S(2)}, u32[]{:S(2)}) collective-permute-start(bf16[64,2304]{1,0:T(8,128)(2,1)} %slice.732), channel_id=1, source_target_pairs={{0,2},{1,3},{2,0},{3,1},{4,6},{5,7},{6,4},{7,5},{8,10},{9,11},{10,... | collective-permute-start | bytes 884744 | tf_op jit(solution)/shard_map/ppermute | solution.py:61
  436.2 27.1 %collective-permute-start.57 = (bf16[256,2304]{1,0:T(8,128)(2,1)S(1)}, bf16[256,2304]{1,0:T(8,128)(2,1)S(1)}, u32[]{:S(2)}, u32[]{:S(2)}) collective-permute-start(bf16[256,2304]{1,0:T(8,128)(2,1)S(1)} %slice.723), channel_id=1, source_target_pairs={{0,1},{1,0},{2,3},{3,2},{4,5},{5,4},{6,7},{7,6},{8,9},{9,8},{10,11... | collective-permute-start | bytes 3538952 | tf_op jit(solution)/shard_map/ppermute | solution.py:61
  440.9 34.3 %collective-permute-start.64 = (bf16[4,288,576]{2,1,0:T(8,128)(2,1)S(1)}, bf16[4,288,576]{2,1,0:T(8,128)(2,1)S(1)}, u32[]{:S(2)}, u32[]{:S(2)}) collective-permute-start(bf16[4,288,576]{2,1,0:T(8,128)(2,1)S(1)} %fusion.9), channel_id=1, source_target_pairs={{0,4},{4,0},{1,5},{5,1},{2,6},{6,2},{3,7},{7,3},{8,12},{12,8},{9,1... | collective-permute-start | bytes 3981320 | tf_op jit(solution)/shard_map/ppermute | solution.py:61
  451.0 40.7 %collective-permute-start.63 = (bf16[64,2304]{1,0:T(8,128)(2,1)}, bf16[64,2304]{1,0:T(8,128)(2,1)}, u32[]{:S(2)}, u32[]{:S(2)}) collective-permute-start(bf16[64,2304]{1,0:T(8,128)(2,1)} %slice_add_fusion.8), channel_id=1, source_target_pairs={{0,16},{8,24},{16,0},{24,8},{1,17},{9,25},{17,1},{25,9},{2,18},{10... | collective-permute-start | bytes 884744 | tf_op jit(solution)/shard_map/ppermute | solution.py:97
  464.4 18.2 %collective-permute-start.58 = (bf16[128,2304]{1,0:T(8,128)(2,1)}, bf16[128,2304]{1,0:T(8,128)(2,1)}, u32[]{:S(2)}, u32[]{:S(2)}) collective-permute-start(bf16[128,2304]{1,0:T(8,128)(2,1)} %slice.726), channel_id=1, source_target_pairs={{0,2},{1,3},{2,0},{3,1},{4,6},{5,7},{6,4},{7,5},{8,10},{9,11},{10,... | collective-permute-start | bytes 1769480 | tf_op jit(solution)/shard_map/ppermute | solution.py:61
  476.8 48.9 %all-to-all-start.3 = ((bf16[4,288,576]{2,1,0:T(8,128)(2,1)}), bf16[4,288,576]{2,1,0:T(8,128)(2,1)S(1)}, u32[]{:S(2)}, u32[]{:S(2)}) async-start(bf16[4,288,576]{2,1,0:T(8,128)(2,1)} %fusion.7), calls=%async_computation.3 | async-start | bytes 2949120 | tf_op jit(solution)/shard_map/all_to_all | solution.py:51
  484.2 34.1 %collective-permute-start.60 = (bf16[64,2304]{1,0:T(8,128)(2,1)S(1)}, bf16[64,2304]{1,0:T(8,128)(2,1)S(1)}, u32[]{:S(2)}, u32[]{:S(2)}) collective-permute-start(bf16[64,2304]{1,0:T(8,128)(2,1)S(1)} %get-tuple-element.215), channel_id=1, source_target_pairs={{0,8},{8,16},{16,24},{24,0},{1,9},{9,17},{17,25},{25,1},{2,10},{10... | collective-permute-start | bytes 884744 | tf_op jit(solution)/shard_map/ppermute | solution.py:97
  486.3 32.4 %collective-permute-start.59 = (bf16[64,2304]{1,0:T(8,128)(2,1)S(1)}, bf16[64,2304]{1,0:T(8,128)(2,1)S(1)}, u32[]{:S(2)}, u32[]{:S(2)}) collective-permute-start(bf16[64,2304]{1,0:T(8,128)(2,1)S(1)} %get-tuple-element.214), channel_id=1, source_target_pairs={{0,24},{8,0},{16,8},{24,16},{1,25},{9,1},{17,9},{25,17},{2,26},{10... | collective-permute-start | bytes 884744 | tf_op jit(solution)/shard_map/ppermute | solution.py:97
  491.4 32.8 %collective-permute-start.65 = (bf16[4,288,576]{2,1,0:T(8,128)(2,1)S(1)}, bf16[4,288,576]{2,1,0:T(8,128)(2,1)S(1)}, u32[]{:S(2)}, u32[]{:S(2)}) collective-permute-start(bf16[4,288,576]{2,1,0:T(8,128)(2,1)S(1)} %fusion.10), channel_id=1, source_target_pairs={{0,4},{4,0},{1,5},{5,1},{2,6},{6,2},{3,7},{7,3},{8,12},{12,8},{9,1... | collective-permute-start | bytes 3981320 | tf_op jit(solution)/shard_map/ppermute | solution.py:61
  532.7 19.4 %collective-permute-start.69 = (bf16[2,64,1152]{2,1,0:T(8,128)(2,1)}, bf16[2,64,1152]{2,1,0:T(8,128)(2,1)}, u32[]{:S(2)}, u32[]{:S(2)}) collective-permute-start(bf16[2,64,1152]{2,1,0:T(8,128)(2,1)} %pad_maximum_fusion.33), channel_id=1, source_target_pairs={{0,4},{4,0},{1,5},{5,1},{2,6},{6,2},{3,7},{7,3},{8,12},{12,8},{9,1... | collective-permute-start | bytes 884744 | tf_op jit(solution)/shard_map/ppermute | solution.py:61
  538.6 32.8 %collective-permute-start.70 = (bf16[4,288,576]{2,1,0:T(8,128)(2,1)}, bf16[4,288,576]{2,1,0:T(8,128)(2,1)}, u32[]{:S(2)}, u32[]{:S(2)}) collective-permute-start(bf16[4,288,576]{2,1,0:T(8,128)(2,1)} %fusion.11), channel_id=1, source_target_pairs={{0,4},{4,0},{1,5},{5,1},{2,6},{6,2},{3,7},{7,3},{8,12},{12,8},{9,1... | collective-permute-start | bytes 3981320 | tf_op jit(solution)/shard_map/ppermute | solution.py:61
  538.9 44.7 %all-to-all-start.4 = ((bf16[4,288,576]{2,1,0:T(8,128)(2,1)}), bf16[4,288,576]{2,1,0:T(8,128)(2,1)S(1)}, u32[]{:S(2)}, u32[]{:S(2)}) async-start(bf16[4,288,576]{2,1,0:T(8,128)(2,1)} %fusion.6), calls=%async_computation.4 | async-start | bytes 2949120 | tf_op jit(solution)/shard_map/all_to_all | solution.py:51
  583.7 74.9 %all-to-all-start.5 = ((bf16[4,288,576]{2,1,0:T(8,128)(2,1)}), bf16[4,288,576]{2,1,0:T(8,128)(2,1)}, u32[]{:S(2)}, u32[]{:S(2)}) async-start(bf16[4,288,576]{2,1,0:T(8,128)(2,1)} %fusion.5), calls=%async_computation.5 | async-start | bytes 2949120 | tf_op jit(solution)/shard_map/all_to_all | solution.py:51
  592.0 27.7 %collective-permute-start.76 = (bf16[576,256]{1,0:T(8,128)(2,1)S(1)}, bf16[576,256]{1,0:T(8,128)(2,1)S(1)}, u32[]{:S(2)}, u32[]{:S(2)}) collective-permute-start(bf16[576,256]{1,0:T(8,128)(2,1)S(1)} %get-tuple-element.176), channel_id=1, source_target_pairs={{0,24},{8,0},{16,8},{24,16},{1,25},{9,1},{17,9},{25,17},{2,26},{10... | collective-permute-start | bytes 884744 | tf_op jit(solution)/shard_map/ppermute | solution.py:97
  595.8 53.9 %collective-permute-start.75 = (bf16[576,256]{1,0:T(8,128)(2,1)S(1)}, bf16[576,256]{1,0:T(8,128)(2,1)S(1)}, u32[]{:S(2)}, u32[]{:S(2)}) collective-permute-start(bf16[576,256]{1,0:T(8,128)(2,1)S(1)} %get-tuple-element.177), channel_id=1, source_target_pairs={{0,16},{8,24},{16,0},{24,8},{1,17},{9,25},{17,1},{25,9},{2,18},{10... | collective-permute-start | bytes 884744 | tf_op jit(solution)/shard_map/ppermute | solution.py:97
  596.6 54.9 %collective-permute-start.74 = (bf16[576,256]{1,0:T(8,128)(2,1)S(1)}, bf16[576,256]{1,0:T(8,128)(2,1)S(1)}, u32[]{:S(2)}, u32[]{:S(2)}) collective-permute-start(bf16[576,256]{1,0:T(8,128)(2,1)S(1)} %get-tuple-element.175), channel_id=1, source_target_pairs={{0,8},{8,16},{16,24},{24,0},{1,9},{9,17},{17,25},{25,1},{2,10},{10... | collective-permute-start | bytes 884744 | tf_op jit(solution)/shard_map/ppermute | solution.py:97
  612.4 40.9 %collective-permute-start.78 = (bf16[512,256]{1,0:T(8,128)(2,1)S(1)}, bf16[512,256]{1,0:T(8,128)(2,1)S(1)}, u32[]{:S(2)}, u32[]{:S(2)}) collective-permute-start(bf16[512,256]{1,0:T(8,128)(2,1)S(1)} %get-tuple-element.194), channel_id=1, source_target_pairs={{0,4},{4,0},{1,5},{5,1},{2,6},{6,2},{3,7},{7,3},{8,12},{12,8},{9,1... | collective-permute-start | bytes 786440 | tf_op jit(solution)/shard_map/ppermute | solution.py:61
  614.1 39.2 %collective-permute-start.80 = (bf16[512,256]{1,0:T(8,128)(2,1)S(1)}, bf16[512,256]{1,0:T(8,128)(2,1)S(1)}, u32[]{:S(2)}, u32[]{:S(2)}) collective-permute-start(bf16[512,256]{1,0:T(8,128)(2,1)S(1)} %get-tuple-element.193), channel_id=1, source_target_pairs={{0,4},{4,0},{1,5},{5,1},{2,6},{6,2},{3,7},{7,3},{8,12},{12,8},{9,1... | collective-permute-start | bytes 786440 | tf_op jit(solution)/shard_map/ppermute | solution.py:61
  619.7 36.6 %collective-permute-start.73 = (bf16[512,256]{1,0:T(8,128)(2,1)S(1)}, bf16[512,256]{1,0:T(8,128)(2,1)S(1)}, u32[]{:S(2)}, u32[]{:S(2)}) collective-permute-start(bf16[512,256]{1,0:T(8,128)(2,1)S(1)} %get-tuple-element.195), channel_id=1, source_target_pairs={{0,4},{4,0},{1,5},{5,1},{2,6},{6,2},{3,7},{7,3},{8,12},{12,8},{9,1... | collective-permute-start | bytes 786440 | tf_op jit(solution)/shard_map/ppermute | solution.py:61
  649.7 42.4 %collective-permute-start.72 = (bf16[512,256]{1,0:T(8,128)(2,1)}, bf16[512,256]{1,0:T(8,128)(2,1)}, u32[]{:S(2)}, u32[]{:S(2)}) collective-permute-start(bf16[512,256]{1,0:T(8,128)(2,1)} %get-tuple-element.192), channel_id=1, source_target_pairs={{0,4},{4,0},{1,5},{5,1},{2,6},{6,2},{3,7},{7,3},{8,12},{12,8},{9,1... | collective-permute-start | bytes 786440 | tf_op jit(solution)/shard_map/ppermute | solution.py:61
  653.3 35.4 %collective-permute-start.83 = (bf16[576,256]{1,0:T(8,128)(2,1)}, bf16[576,256]{1,0:T(8,128)(2,1)}, u32[]{:S(2)}, u32[]{:S(2)}) collective-permute-start(bf16[576,256]{1,0:T(8,128)(2,1)} %get-tuple-element.174), channel_id=1, source_target_pairs={{0,16},{8,24},{16,0},{24,8},{1,17},{9,25},{17,1},{25,9},{2,18},{10... | collective-permute-start | bytes 884744 | tf_op jit(solution)/shard_map/ppermute | solution.py:97
  653.4 36.7 %collective-permute-start.82 = (bf16[576,256]{1,0:T(8,128)(2,1)}, bf16[576,256]{1,0:T(8,128)(2,1)}, u32[]{:S(2)}, u32[]{:S(2)}) collective-permute-start(bf16[576,256]{1,0:T(8,128)(2,1)} %get-tuple-element.172), channel_id=1, source_target_pairs={{0,8},{8,16},{16,24},{24,0},{1,9},{9,17},{17,25},{25,1},{2,10},{10... | collective-permute-start | bytes 884744 | tf_op jit(solution)/shard_map/ppermute | solution.py:97
  656.3 35.8 %collective-permute-start.81 = (bf16[512,256]{1,0:T(8,128)(2,1)}, bf16[512,256]{1,0:T(8,128)(2,1)}, u32[]{:S(2)}, u32[]{:S(2)}) collective-permute-start(bf16[512,256]{1,0:T(8,128)(2,1)} %get-tuple-element.155), channel_id=1, source_target_pairs={{8,0},{16,8},{24,16},{9,1},{17,9},{25,17},{10,2},{18,10},{26,18},{... | collective-permute-start | bytes 786440 | tf_op jit(solution)/shard_map/ppermute | solution.py:74
  664.9 37.0 %collective-permute-start.79 = (bf16[512,256]{1,0:T(8,128)(2,1)}, bf16[512,256]{1,0:T(8,128)(2,1)S(1)}, u32[]{:S(2)}, u32[]{:S(2)}) collective-permute-start(bf16[512,256]{1,0:T(8,128)(2,1)} %get-tuple-element.154), channel_id=1, source_target_pairs={{16,0},{24,8},{17,1},{25,9},{18,2},{26,10},{19,3},{27,11},{20,4},{... | collective-permute-start | bytes 786440 | tf_op jit(solution)/shard_map/ppermute | solution.py:74
  711.8 17.6 %collective-permute-start.85 = (bf16[2,2,64,2304]{3,2,0,1:T(8,128)(2,1)}, bf16[2,2,64,2304]{3,2,0,1:T(8,128)(2,1)}, u32[]{:S(2)}, u32[]{:S(2)}) collective-permute-start(bf16[2,2,64,2304]{3,2,0,1:T(8,128)(2,1)} %fusion.20), channel_id=1, source_target_pairs={{0,1},{1,0},{2,3},{3,2},{4,5},{5,4},{6,7},{7,6},{8,9},{9,8},{10,11... | collective-permute-start | bytes 3538952 | tf_op jit(solution)/shard_map/ppermute | solution.py:61
  727.2 26.2 %collective-permute-start.91 = (bf16[592,256]{1,0:T(8,128)(2,1)S(1)}, bf16[592,256]{1,0:T(8,128)(2,1)S(1)}, u32[]{:S(2)}, u32[]{:S(2)}) collective-permute-start(bf16[592,256]{1,0:T(8,128)(2,1)S(1)} %get-tuple-element.159), channel_id=1, source_target_pairs={{0,16},{8,24},{16,0},{24,8},{1,17},{9,25},{17,1},{25,9},{2,18},{10... | collective-permute-start | bytes 909320 | tf_op jit(solution)/shard_map/ppermute | solution.py:97
  727.3 26.1 %collective-permute-start.90 = (bf16[592,256]{1,0:T(8,128)(2,1)S(1)}, bf16[592,256]{1,0:T(8,128)(2,1)S(1)}, u32[]{:S(2)}, u32[]{:S(2)}) collective-permute-start(bf16[592,256]{1,0:T(8,128)(2,1)S(1)} %get-tuple-element.158), channel_id=1, source_target_pairs={{0,8},{8,16},{16,24},{24,0},{1,9},{9,17},{17,25},{25,1},{2,10},{10... | collective-permute-start | bytes 909320 | tf_op jit(solution)/shard_map/ppermute | solution.py:97
  731.9 21.6 %collective-permute-start.86 = (bf16[2,64,1152]{2,1,0:T(8,128)(2,1)S(1)}, bf16[2,64,1152]{2,1,0:T(8,128)(2,1)S(1)}, u32[]{:S(2)}, u32[]{:S(2)}) collective-permute-start(bf16[2,64,1152]{2,1,0:T(8,128)(2,1)S(1)} %fusion.111), channel_id=1, source_target_pairs={{0,4},{4,0},{1,5},{5,1},{2,6},{6,2},{3,7},{7,3},{8,12},{12,8},{9,1... | collective-permute-start | bytes 884744 | tf_op jit(solution)/shard_map/ppermute | solution.py:61
  733.7 19.8 %collective-permute-start.88 = (bf16[2,64,1152]{2,1,0:T(8,128)(2,1)S(1)}, bf16[2,64,1152]{2,1,0:T(8,128)(2,1)S(1)}, u32[]{:S(2)}, u32[]{:S(2)}) collective-permute-start(bf16[2,64,1152]{2,1,0:T(8,128)(2,1)S(1)} %fusion.112), channel_id=1, source_target_pairs={{0,2},{1,3},{2,0},{3,1},{4,6},{5,7},{6,4},{7,5},{8,10},{9,11},{10,... | collective-permute-start | bytes 884744 | tf_op jit(solution)/shard_map/ppermute | solution.py:61
  737.3 25.6 %collective-permute-start.95 = (bf16[288,256]{1,0:T(8,128)(2,1)}, bf16[288,256]{1,0:T(8,128)(2,1)S(1)}, u32[]{:S(2)}, u32[]{:S(2)}) collective-permute-start(bf16[288,256]{1,0:T(8,128)(2,1)} %select_convert_fusion.10), channel_id=1, source_target_pairs={{0,4},{4,0},{1,5},{5,1},{2,6},{6,2},{3,7},{7,3},{8,12},{12,8},{9,1... | collective-permute-start | bytes 442376 | tf_op jit(solution)/shard_map/ppermute | solution.py:61
  (136 other events, 1274.3 us)

commit v4 on v3

--- a/solution.py
+++ b/solution.py
@@ -1,3 +1,5 @@
+import math
+
 import jax
 import jax.numpy as jnp
 from jax import lax
@@ -122,13 +124,19 @@
     return jnp.stack(blocks)
 
 
-def ring_summed(blocks):
+def ring_summed(blocks, *earlier):
     n = lax.axis_size("dp")
     place = lax.axis_index("dp")
-    total = lax.dynamic_index_in_dim(blocks, place, 0, keepdims=False)
-    for steps in range(1, n):
-        sent = lax.dynamic_index_in_dim(blocks, (place + steps) % n, 0, keepdims=False)
-        total = total + rotated(sent.astype(b16), steps).astype(f32)
+    total = lax.dynamic_index_in_dim(blocks, place, 0, keepdims=False).astype(f32)
+    got = [
+        rotated(
+            lax.dynamic_index_in_dim(blocks, (place + steps) % n, 0, keepdims=False), steps
+        )
+        for steps in range(1, n)
+    ]
+    got = after(got, *earlier)
+    for block in got:
+        total = total + block.astype(f32)
     return total
 
 
@@ -171,7 +179,7 @@
     return pl.pallas_call(
         kernel,
         out_shape=jax.ShapeDtypeStruct((rows, n * units), f32),
-        compiler_params=pltpu.CompilerParams(vmem_limit_bytes=32 << 20),
+        compiler_params=params(16),
         name="side_by_side",
     )(blocks)
 
@@ -194,6 +202,13 @@
     high = lax.index_in_dim(partial, 1, axis, keepdims=False)
     kept, sent = picked(bits()[step], (low, high))
     return kept + swapped(sent.astype(b16), *AXES[step]).astype(f32)
+
+
+def half_sent(partial, step, axis):
+    low = lax.index_in_dim(partial, 0, axis, keepdims=False)
+    high = lax.index_in_dim(partial, 1, axis, keepdims=False)
+    kept, sent = picked(bits()[step], (low, high))
+    return kept, swapped(sent.astype(b16), *AXES[step])
 
 
 def collect_group(partial, sub, *earlier):
@@ -205,33 +220,129 @@
     return jnp.concatenate([left, right], axis=-1)
 
 
-def spread_group(block, *earlier):
+SMEM = pltpu.SMEM
+VMEM = pltpu.VMEM
+
+
+def params(megabytes=48):
+    return pltpu.CompilerParams(vmem_limit_bytes=megabytes << 20)
+
+
+def scalar(value):
+    return value.astype(jnp.int32).reshape(1)
+
+
+def whole(shape):
+    return pl.BlockSpec(shape, lambda *_: (0,) * len(shape))
+
+
+def fused(function, flags, *args):
+    shapes = jax.eval_shape(function, *flags, *args)
+    leaves, tree = jax.tree.flatten(shapes)
+    size = sum(math.prod(v.shape) * v.dtype.itemsize for v in (*args, *leaves))
+    if size > 32 << 20:
+        return function(*flags, *args)
+    count = len(flags)
+
+    def kernel(*refs):
+        given = [ref[0] == 1 for ref in refs[:count]]
+        given += [ref[...] for ref in refs[count : count + len(args)]]
+        results = jax.tree.leaves(function(*given))
+        for ref, result in zip(refs[count + len(args) :], results):
+            ref[...] = result
+
+    out = pl.pallas_call(
+        kernel,
+        in_specs=[pl.BlockSpec(memory_space=SMEM)] * count
+        + [pl.BlockSpec(memory_space=VMEM)] * len(args),
+        out_specs=[pl.BlockSpec(memory_space=VMEM)] * len(leaves),
+        out_shape=leaves,
+        compiler_params=params(8 + (size >> 20)),
+        name="fused_" + getattr(function, "__name__", "part").strip("<>_"),
+    )(*[scalar(flag) for flag in flags], *args)
+    return jax.tree.unflatten(tree, out)
+
+
+def join_kernel(own, step, axis):
+    other = swapped(own, *AXES[step])
+    first = bits()[step]
+    if own.ndim < 2 or own.shape[-2] % 16:
+        return jnp.stack(picked(first, (own, other)), axis=axis)
+    shape = own.shape[:axis] + (2,) + own.shape[axis:]
+
+    def kernel(place, own_ref, other_ref, out):
+        lead = (slice(None),) * axis
+        out[(*lead, place[0])] = own_ref[...]
+        out[(*lead, 1 - place[0])] = other_ref[...]
+
+    return pl.pallas_call(
+        kernel,
+        in_specs=[pl.BlockSpec(memory_space=SMEM)] + [pl.BlockSpec(memory_space=VMEM)] * 2,
+        out_specs=pl.BlockSpec(memory_space=VMEM),
+        out_shape=jax.ShapeDtypeStruct(shape, own.dtype),
+        compiler_params=params(8),
+        name="join",
+    )(1 - scalar(first), own, other)
+
+
+def parted(first, low, high):
+    kept, sent = picked(first, (low, high))
+    return kept, sent.astype(b16)
+
+
+def core_parted(low_core, out, sub):
+    parts = [out[k * sub : (k + 1) * sub] for k in range(8)]
+    pairs = [parted(low_core, parts[2 * k], parts[2 * k + 1]) for k in range(4)]
+    return tuple(
+        jnp.concatenate([pair[which] for pair in pairs], axis=0).reshape(2, 2, sub, -1)
+        for which in range(2)
+    )
+
+
+def collect_halves(kept, sent, *earlier):
+    half = kept.shape[-1] // 2
+    context, high, low = bits()
+
+    def halve(context, high, kept, got):
+        total = kept + got.astype(f32)
+        left, right = total[..., :half], total[..., half:]
+        left = parted(context, left[0], left[1])
+        right = parted(high, right[:, 0], right[:, 1])
+        return *left, *right
+
+    def again(context, high, left, left_got, right, right_got):
+        left = left + left_got.astype(f32)
+        right = right + right_got.astype(f32)
+        return *parted(high, left[0], left[1]), *parted(context, right[0], right[1])
+
+    got = swapped(sent, *AXES[2])
+    left, left_sent, right, right_sent = fused(halve, (context, high), kept, got)
+    left_sent, right_sent = after((left_sent, right_sent), *earlier)
+    left_got, right_got = swapped(left_sent, *AXES[0]), swapped(right_sent, *AXES[1])
+    left, left_sent, right, right_sent = fused(
+        again, (context, high), left, left_got, right, right_got
+    )
+    return left, swapped(left_sent, *AXES[1]), right, swapped(right_sent, *AXES[0])
+
+
+def halves_summed(left, left_got, right, right_got):
+    return jnp.concatenate([left + left_got.astype(f32), right + right_got.astype(f32)], axis=-1)
+
+
+def side_by_side_columns(left, right):
+    return jnp.concatenate([left, right], axis=-1)
+
+
+def spread_group(block):
     width = block.shape[-1]
     left, right = block[:, : width // 2], block[:, width // 2 :]
-    left = join(join(left, 0, 0), 1, 1)
-    right = join(join(right, 1, 0), 0, 0)
-    whole = after(jnp.concatenate([left, right], axis=-1), *earlier)
-    whole = join(whole, 2, 2)
-    return whole.reshape(-1, width)
+    left = join_kernel(join_kernel(left, 0, 0), 1, 1)
+    right = join_kernel(join_kernel(right, 1, 0), 0, 0)
+    return join_kernel(fused(side_by_side_columns, (), left, right), 2, 2).reshape(-1, width)
 
 
 def spread_lanes(block):
-    return join(join(block, 1, 0), 2, 1).reshape(-1, block.shape[-1])
-
-
-SMEM = pltpu.SMEM
-
-
-def params(megabytes=48):
-    return pltpu.CompilerParams(vmem_limit_bytes=megabytes << 20)
-
-
-def scalar(value):
-    return value.astype(jnp.int32).reshape(1)
-
-
-def whole(shape):
-    return pl.BlockSpec(shape, lambda *_: (0,) * len(shape))
+    return join_kernel(join_kernel(block, 1, 0), 2, 1).reshape(-1, block.shape[-1])
 
 
 def row_grad(left, right):
@@ -246,7 +357,7 @@
     return pl.pallas_call(
         kernel,
         out_shape=jax.ShapeDtypeStruct((width, right.shape[1]), b16),
-        compiler_params=params(),
+        compiler_params=params(16),
         name="row_grad",
     )(left, right)
 
@@ -327,6 +438,13 @@
     return lax.optimization_barrier(values)
 
 
+def added(terms):
+    total = terms[0].astype(f32)
+    for term in terms[1:]:
+        total = total + term.astype(f32)
+    return total
+
+
 def spread_chunk(block, *earlier):
     block = jnp.concatenate([block, swapped(block, "tensor", 2)], axis=0)
     block = after(block, *earlier)
@@ -349,22 +467,23 @@
         if group[0]:
             sent = after(block, *got)
         rows.append(got)
+    near = rows[1]
     for number, got in enumerate(rows):
         got = jnp.concatenate(got, axis=0) if len(got) > 1 else got[0]
         rows[number] = spread_chunk(got, *partial[:1])
-        first, *others = work(number, after(rows[number], *partial[-1:]))
+        first, *others = work(number, after(rows[number], *partial[-1:]), *near)
         partial.append(first)
         rest.append(others)
 
-    total = 0.0
-    for number, group in enumerate(groups):
-        back = folded(folded(partial[number], 1), 2)
-        for place, steps in enumerate(group):
+    terms, earlier = [], []
+    for number in list(range(1, len(groups))) + [0]:
+        back = after(folded(partial[number], 1), *earlier)
+        back = folded(back, 2)
+        earlier = [back]
+        for place, steps in enumerate(groups[number]):
             part = back[place * sub : (place + 1) * sub]
-            if steps:
-                part = rotated(part.astype(b16), -steps).astype(f32)
-            total = total + part
-    return rows, total, list(zip(*rest)), partial + [back]
+            terms.append(rotated(part.astype(b16), -steps) if steps else part)
+    return rows, terms, list(zip(*rest)), partial + earlier
 
 
 def on_device(
@@ -413,13 +532,13 @@
 
     gains = jnp.concatenate([pre_attn_gain, post_attn_gain, pre_ffw_gain, post_ffw_gain])
     pair_got = ring_blocks(with_rider(jnp.where(is_first, key_weight, value_weight), gains))
-    group_tokens = join(tokens, 0, 0).reshape(group, width).astype(f32)
+    group_tokens = join(tokens, 0, 0).reshape(group, width)
     segment_pair = join(segments[None].astype(b16), 0, 0)
     pair_in, gains = split_rider(in_order(pair_got), 4 * deep)
     pair_in = pair_in.reshape(width, HEAD_SIZE)
     gains = 1.0 + jnp.swapaxes(gains.reshape(n, 4, deep), 0, 1).reshape(4, width).astype(f32)
-    scale_one = rms_scale(group_tokens)
-    normed_one = group_tokens * scale_one
+    normed_one = group_tokens.astype(f32)
+    normed_one = normed_one * rms_scale(normed_one)
     lifted_one = (normed_one * gains[0]).astype(b16)
     positions = place * group + jnp.arange(group, dtype=jnp.int32)
     cosine_table, sine_table = rotary_tables(positions)
@@ -438,9 +557,12 @@
     gate_got = exchange(after(gate_got, *mine), "dp")
     up_got = exchange(after(up_got, gate_got), "dp")
     down_got = exchange(after(down_got, up_got), "dp")
-    gate_w = join(gate_got, 0, 1).reshape(width, units)
-    up_w = join(up_got, 0, 1).reshape(width, units)
-    down_w = join(down_got, 0, 1).reshape(width, units)
+    gate_other, up_other, down_other = [
+        swapped(got, "context", 1) for got in (gate_got, up_got, down_got)
+    ]
+
+    def both_halves(own, other):
+        return jnp.stack(picked(is_first, (own, other)), axis=1).reshape(width, units)
 
     theirs = [swapped(block, "context", 1) for block in mine]
     mine = jnp.concatenate(mine[::-1], axis=0)
@@ -465,111 +587,165 @@
     weights = jnp.exp(masked - jnp.max(masked, axis=-1, keepdims=True))
     probs = weights / jnp.sum(weights, axis=-1, keepdims=True)
     probs_low = probs.astype(b16)
-    mixed = dot(after(probs_low, up_got, gate_w, *out_got), values).astype(b16)
-    branch = collect_group(dot_nt(mixed, w_out), sub, up_w, down_got)
-
-    own_tokens = lax.dynamic_slice_in_dim(tokens, lane * sub, sub).astype(f32)
-    grad_out = lax.dynamic_slice_in_dim(cotangent, lane * sub, sub).astype(f32)
+    mixed = dot(after(probs_low, gate_got, *out_got), values).astype(b16)
+    branch = after(collect_group(dot_nt(mixed, w_out), sub), up_got)
+
+    own_tokens = lax.dynamic_slice_in_dim(tokens, lane * sub, sub)
+    own_cotangent = lax.dynamic_slice_in_dim(cotangent, lane * sub, sub)
+    grad_out = own_cotangent.astype(f32)
     scale_two = rms_scale(branch)
     normed_two = branch * scale_two
-    middle = own_tokens + normed_two * gains[1]
+    middle = own_tokens.astype(f32) + normed_two * gains[1]
     scale_three = rms_scale(middle)
     normed_three = middle * scale_three
-    lifted_two = (normed_three * gains[2]).astype(b16)
-
-    def feed(number, chunk):
+    lifted_two = after((normed_three * gains[2]).astype(b16), down_got)
+    gate_w = both_halves(gate_got, after(gate_other, lifted_two))
+    up_w = both_halves(up_got, after(up_other, lifted_two))
+
+    def feed(number, chunk, *arrived):
+        down_w = both_halves(down_got, after(down_other, *arrived))
         gate = dot(chunk, gate_w)
         upper = dot(chunk, up_w)
         hidden = gated(gate, upper).astype(b16)
         return dot_nt(hidden, down_w), gate, upper, hidden
 
-    lifted_two, down, (gate, upper, hidden), unused = pipelined(lifted_two, feed)
+    lifted_two, terms, (gate, upper, hidden), unused = pipelined(lifted_two, feed)
+    down = added(terms)
     scale_four = rms_scale(down)
     normed_four = down * scale_four
     output = (middle + normed_four * gains[3]).astype(b16)
 
+    grad_gain_four = jnp.sum(grad_out * normed_four, axis=0, keepdims=True)
     def unit_grad(left, right):
         partial = dot_tn(jnp.concatenate(left, axis=0), jnp.concatenate(right, axis=0))
         return partial.reshape(n, 2, deep // 2, units)
 
     grad_down = rms_back(grad_out * gains[3], normed_four, scale_four).astype(b16)
-    def feed_back(number, chunk):
+    down_w = both_halves(down_got, down_other)
+
+    def feed_back(number, chunk, *arrived):
         unused, pull = jax.vjp(gated, gate[number], upper[number])
         grad_gate, grad_upper = [side.astype(b16) for side in pull(dot(chunk, down_w))]
         partial = dot_nt(grad_gate, gate_w) + dot_nt(grad_upper, up_w)
         return partial, grad_gate, grad_upper
 
-    grad_down, lifted_grad, (grad_gate, grad_upper), partial = pipelined(grad_down, feed_back)
+    grad_down, terms, (grad_gate, grad_upper), partial = pipelined(grad_down, feed_back)
     output = spread_lanes(after(output, *grad_down))
     down_sum = unit_grad(grad_down, after(hidden, partial[-3]))
-    down_part = fold(down_sum, 0, 1).astype(b16)
+    down_kept, down_got = half_sent(down_sum, 0, 1)
     gate_sum = unit_grad(lifted_two, after(grad_gate, partial[-1]))
-    gate_part = fold(after(gate_sum, down_part), 0, 1).astype(b16)
     up_sum = unit_grad(lifted_two, after(grad_upper, partial[-1]))
-    up_part = fold(after(up_sum, gate_part), 0, 1).astype(b16)
+    terms, down_got, gate_sum, up_sum = together(terms, down_got, gate_sum, up_sum)
+
+    def two_sided(kept, got):
+        return (kept + got.astype(f32)).astype(b16)
+
+    def middle_back(cotangent, gains, scale_two, normed_two, scale_three, normed_three, *terms):
+        grad_out = cotangent.astype(f32)
+        lifted_grad = added(terms)
+        grad_middle = grad_out + rms_back(lifted_grad * gains[2:3], normed_three, scale_three)
+        grad_branch = rms_back(grad_middle * gains[1:2], normed_two, scale_two).astype(b16)
+        gain_two = jnp.sum(grad_middle * normed_two, axis=0, keepdims=True)
+        gain_three = jnp.sum(lifted_grad * normed_three, axis=0, keepdims=True)
+        return grad_middle, grad_branch, gain_two, gain_three
+
+    down_part = (down_kept + down_got.astype(f32)).astype(b16)
     grad_w_down = exchange(down_part, "dp")
-    lifted_grad = after(lifted_grad, down_part, gate_sum, up_sum)
-    grad_middle = grad_out + rms_back(lifted_grad * gains[2], normed_three, scale_three)
-    grad_branch = rms_back(grad_middle * gains[1], normed_two, scale_two).astype(b16)
-    grad_w_gate = exchange(after(gate_part, grad_w_down), "dp")
-    grad_branch = spread_group(after(grad_branch, output, grad_w_down, gate_part), grad_w_gate, up_part)
+    gate_kept, gate_got = half_sent(gate_sum, 0, 1)
+    grad_middle, grad_branch, grad_gain_two, grad_gain_three = fused(
+        middle_back, (), own_cotangent, gains, scale_two, normed_two, scale_three, normed_three, *terms
+    )
+    grad_branch, grad_w_down, gate_got = together(grad_branch, grad_w_down, gate_got)
+    gate_part = (gate_kept + gate_got.astype(f32)).astype(b16)
+
+    low_core = bits()[2]
 
     def row_blocks(left, right):
         return row_grad(left, right).reshape(n, deep, HEAD_SIZE)
 
-    grad_w_up = exchange(after(up_part, grad_w_gate), "dp")
-    grad_w_out = ring_summed(after(row_blocks(grad_branch, mixed), grad_w_gate))
+    grad_w_gate = exchange(gate_part, "dp")
+    up_kept, up_got = half_sent(up_sum, 0, 1)
+    grad_branch = spread_group(grad_branch)
+    out_blocks = row_blocks(grad_branch, mixed)
     grad_query_pre, kept, sent = attend_back(
         grad_branch, w_out, keys, values, queries, probs, bent, (cosine_table, sine_table), side
     )
+    query_blocks = row_blocks(lifted_one, grad_query_pre)
+    up_got, kept = together(up_got, kept)
+    up_part = (up_kept + up_got.astype(f32)).astype(b16)
+    grad_w_up = exchange(after(up_part, grad_w_gate), "dp")
+    kept, sent, out_blocks, query_blocks, output = together(
+        kept, sent, after(out_blocks, grad_w_gate), query_blocks, output
+    )
     kept = kept.reshape(reach + 1, group, HEAD_SIZE)
     sent = sent.reshape(reach + 1, group, HEAD_SIZE)
+
+    def full(kept, got):
+        return kept + got.astype(f32)
+
     slots = [
-        kept[slot] + swapped(sent[slot], "context", 1).astype(f32) for slot in range(reach + 1)
+        fused(two_sided if slot < reach else full, (), kept[slot], swapped(sent[slot], "context", 1))
+        for slot in range(reach + 1)
     ]
-    slots[0] = after(slots[0], grad_w_up, grad_w_out)
-    mine = slots[reach]
+    grad_w_out = ring_summed(out_blocks)
+    terms = [slots[reach]]
     for steps in range(reach, 0, -1):
-        mine = mine + shifted(slots[reach - steps].astype(b16), "dp", -steps).astype(f32)
-    grad_w_query = ring_summed(after(row_blocks(lifted_one, grad_query_pre), grad_w_out))
-    mine = after(mine, grad_w_query)
-    mine = jnp.where(is_first, rotate_back(mine, cosine_table, sine_table), mine).astype(b16)
-    first_grad = dot_nt(grad_query_pre, query_in) + dot_nt(mine, pair_in)
-    grad_gain_one = jnp.sum(first_grad * normed_one, axis=0)
-    first_grad = collect_group(first_grad, sub)
-    own_scale = rms_scale(own_tokens)
-    own_normed = own_tokens * own_scale
-    grad_inputs = grad_middle + rms_back(first_grad * gains[0], own_normed, own_scale)
-    grad_inputs = grad_inputs.astype(b16)
-    grad_gains = jnp.stack(
-        [
-            grad_gain_one,
-            jnp.sum(grad_middle * normed_two, axis=0),
-            jnp.sum(lifted_grad * normed_three, axis=0),
-            jnp.sum(grad_out * normed_four, axis=0),
-        ]
+        terms.append(shifted(slots[reach - steps], "dp", -steps))
+    terms, grad_w_up, grad_w_out = together(terms, grad_w_up, grad_w_out)
+
+    def unturned(is_first, cosine, sine, *terms):
+        total = added(terms)
+        return jnp.where(is_first, rotate_back(total, cosine, sine), total).astype(b16)
+
+    mine = fused(unturned, (is_first,), cosine_table, sine_table, *terms)
+    pair_blocks = row_blocks(lifted_one, mine)
+
+    def first_product(low_core, tokens, query_grad, query_in, pair_grad, pair_in):
+        out = dot_nt(query_grad, query_in) + dot_nt(pair_grad, pair_in)
+        values = tokens.astype(f32)
+        gain = jnp.sum(out * (values * rms_scale(values)), axis=0, keepdims=True)
+        return *core_parted(low_core, out, sub), gain
+
+    kept, sent, grad_gain_one = fused(
+        first_product,
+        (low_core,),
+        group_tokens,
+        grad_query_pre,
+        query_in,
+        after(mine, pair_blocks),
+        pair_in,
+    )
+    first_grad = collect_halves(kept, sent)
+
+    def first_back(own_tokens, gains, grad_middle, *halves):
+        first_grad = halves_summed(*halves)
+        values = own_tokens.astype(f32)
+        scale = rms_scale(values)
+        return (grad_middle + rms_back(first_grad * gains[:1], values * scale, scale)).astype(b16)
+
+    grad_inputs = fused(first_back, (), own_tokens, gains, grad_middle, *first_grad)
+    grad_gains = jnp.concatenate(
+        [grad_gain_one, grad_gain_two, grad_gain_three, grad_gain_four], axis=0
     )
 
     def halves(total):
         kept, sent = picked(is_first, (total[: deep // 2], total[deep // 2 : deep]))
         return kept, swapped(sent.astype(b16), "context", 1).astype(f32)
 
-    rider = jnp.swapaxes(grad_gains.astype(b16).reshape(4, n, deep), 0, 1).reshape(n, -1)
-    rider = jnp.pad(rider, ((0, 0), (0, 16 * HEAD_SIZE - rider.shape[1])))
-    rider = jnp.concatenate([row_blocks(lifted_one, mine), rider.reshape(n, 16, HEAD_SIZE)], axis=1)
-    grad_pair = ring_summed(rider)
-    grad_inputs, grad_pair = together(grad_inputs, grad_pair)
-    grad_inputs = spread_lanes(grad_inputs).astype(f32)
-    grad_gains = grad_pair[deep:].reshape(-1)[: 4 * deep].reshape(4, 2, deep // 2)
-    grad_gains, sent = picked(is_first, (grad_gains[:, 0], grad_gains[:, 1]))
-    grad_gains = grad_gains + swapped(sent, "context", 1)
+    grad_w_query = ring_summed(after(query_blocks, *terms), grad_inputs)
+    grad_pair = ring_summed(pair_blocks, grad_inputs)
+    grad_gains = after(grad_gains, grad_inputs)
     grad_gains = grad_gains + swapped(grad_gains, "tensor", 2)
     grad_gains = grad_gains + swapped(grad_gains, "tensor", 1)
+    grad_gains = jnp.transpose(grad_gains.reshape(4, n, 2, deep // 2), (2, 1, 0, 3))
+    grad_gains, sent = picked(is_first, (grad_gains[0], grad_gains[1]))
+    grad_gains = ring_summed(grad_gains + swapped(sent, "context", 1))
+    grad_inputs = spread_lanes(grad_inputs).astype(f32)
     grad_w_out = jnp.concatenate(picked(is_first, halves(grad_w_out)), axis=1).T
     grad_w_query = jnp.concatenate(picked(is_first, halves(grad_w_query)), axis=1)
     grad_w_key, grad_w_value = picked(is_first, halves(grad_pair))
     grad_w_down, grad_w_gate, grad_w_up = after(
-        (grad_w_down, grad_w_gate, grad_w_up), grad_w_out
+        (grad_w_down, grad_w_gate, grad_w_up), mine
     )
     grad_w_down = side_by_side(grad_w_down).T
     grad_w_gate = side_by_side(grad_w_gate)

time: 791 us -> 755 us (0.954)
  waiting for transfers between devices: 399 us -> 329 us
  starting transfers between devices: 160 us -> 192 us
  other arithmetic: 94.1 us -> 70.9 us
  local copies, waits for them, and re-layouts: 39.8 us -> 55.4 us
  Pallas kernels: 27.2 us -> 42.5 us
    ppermute x30 -> x33, starting transfers between devices: 43.1 us -> 93.6 us  [rotated(): return lax.ppermute(value, 'dp', [(s, (s + steps) % n) for s in range(n)])]
    ppermute x30 -> x33, waiting for transfers between devices: 171 us -> 125 us  [rotated(): return lax.ppermute(value, 'dp', [(s, (s + steps) % n) for s in range(n)])]
    ppermute x65, waiting for transfers between devices: 172 us -> 139 us  [swapped(): lax.ppermute(value, axis, [(place, place ^ bit) for place in range(count)])]
    all_to_all x6, waiting for transfers between devices: 30.1 us -> 51.6 us  [exchange(): return lax.all_to_all(blocks, axis, 0, 0, tiled=True)]
    unnamed x207 -> x181, local copies, waits for them, and re-layouts: 12.9 us -> 31.7 us
    pallas_call x0 -> x20, Pallas kernels: none -> 15.3 us  [the longest x11 9.22 us: fused(): pl.pallas_call(kernel, in_specs=[pl.BlockSpec(memory_space=SMEM)] * count...]
    ppermute x6, waiting for transfers between devices: 26.7 us -> 14 us  [shifted(): lax.ppermute(value, axis, [(s, s + steps) for s in range(count) if 0 <= s...]
    convert_element_type x13 -> x5, other arithmetic: 14.8 us -> 4.44 us  [fold(): return kept + swapped(sent.astype(b16), *AXES[step]).astype(f32)]
  transfers between devices with their start and end apart: 107 -> 110, of which waited for: 55 -> 51; matrix products, arithmetic and copies ran while one was open for 20% -> 15% of each run, Pallas kernels for 3% -> 5%
where the time goes in v4:
time: 755 us; the launch traced here: 747 us
  waiting for transfers between devices  329 us (44%)
  starting transfers between devices  192 us (25%)
  other arithmetic  70.9 us (9%)
  local copies, waits for them, and re-layouts  55.4 us (7%)
  matrix products  53.9 us (7%)
  Pallas kernels  42.5 us (6%)
    ppermute x65, waiting for transfers between devices, swapped(): lax.ppermute(value, axis, [(place, place ^ bit) for place in range(count)])  139 us
    ppermute x33, waiting for transfers between devices, rotated(): return lax.ppermute(value, 'dp', [(s, (s + steps) % n) for s in range(n)])  125 us
    ppermute x33, starting transfers between devices, rotated(): return lax.ppermute(value, 'dp', [(s, (s + steps) % n) for s in range(n)])  93.6 us
    all_to_all x6, waiting for transfers between devices, exchange(): return lax.all_to_all(blocks, axis, 0, 0, tiled=True)  51.6 us
    ppermute x65, starting transfers between devices, swapped(): lax.ppermute(value, axis, [(place, place ^ bit) for place in range(count)])  45.4 us
    all_to_all x6, starting transfers between devices, exchange(): return lax.all_to_all(blocks, axis, 0, 0, tiled=True)  39.8 us
    unnamed x181, local copies, waits for them, and re-layouts  31.7 us
    dot_general x11, matrix products, dot_nt(): lax.dot_general(left, right, (((1,), (1,)), ((), ())), preferred_element_...  20.2 us
  transfers between devices with their start and end apart: 110, of which 51 were waited for; matrix products, arithmetic and copies ran while one was open for 15% of the time, Pallas kernels for 5%

profile of v4, /device:TPU:0, one launch (start us, length us, event | category | flops | bytes accessed | tf_op | source)
XLA Modules:
  0.0 747.1 jit_solution(1530757987971717358)
XLA Ops:
  0.7 2.8 concatenate.106
  4.5 5.1 collective-permute-start.2
  14.5 2.8 collective-permute-done.2
  17.3 18.2 %collective-permute-done.3 = bf16[592,256]{1,0:T(8,128)(2,1)S(1)} collective-permute-done((bf16[592,256]{1,0:T(8,128)(2,1)S(1)}, bf16[592,256]{1,0:T(8,128)(2,1)S(1)}, u32[]{:S(2)}, u32[]{:S(2)}) %collective-permute-start.3) | collective-permute-done | bytes 303136 | tf_op jit(solution)/shard_map/ppermute | solution.py:99
  43.3 5.1 collective-permute-start.10
  54.5 22.8 %collective-permute-start.7 = (bf16[592,256]{1,0:T(8,128)(2,1)S(1)}, bf16[592,256]{1,0:T(8,128)(2,1)}, u32[]{:S(2)}, u32[]{:S(2)}) collective-permute-start(bf16[592,256]{1,0:T(8,128)(2,1)S(1)} %pad_maximum_fusion.27), channel_id=1, source_target_pairs={{0,8},{8,16},{16,24},{24,0},{1,9},{9,17},{17,25},{25,1},{2,10},{10... | collective-permute-start | bytes 909320 | tf_op jit(solution)/shard_map/ppermute | solution.py:99
  77.3 5.0 unit_blocks.1
  83.9 5.0 all-to-all-start
  96.7 18.6 %collective-permute-start.15 = (bf16[576,256]{1,0:T(8,128)(2,1)S(1)}, bf16[576,256]{1,0:T(8,128)(2,1)S(1)}, u32[]{:S(2)}, u32[]{:S(2)}) collective-permute-start(bf16[576,256]{1,0:T(8,128)(2,1)S(1)} %slice_select_fusion), channel_id=1, source_target_pairs={{0,8},{8,16},{16,24},{24,0},{1,9},{9,17},{17,25},{25,1},{2,10},{10... | collective-permute-start | bytes 884744 | tf_op jit(solution)/shard_map/ppermute | solution.py:99
  118.0 3.1 collective-permute-start.17
  123.8 3.9 fusion.104
  128.4 3.5 fusion.102
  131.9 8.7 %collective-permute-done.16 = bf16[576,256]{1,0:T(8,128)(2,1)S(1)} collective-permute-done((bf16[576,256]{1,0:T(8,128)(2,1)S(1)}, bf16[576,256]{1,0:T(8,128)(2,1)S(1)}, u32[]{:S(2)}, u32[]{:S(2)}) %collective-permute-start.16) | collective-permute-done | bytes 294944 | tf_op jit(solution)/shard_map/ppermute | solution.py:99
  143.3 2.9 fusion.84
  146.2 3.6 fusion.21
  149.8 3.1 collective-permute-done.18
  160.1 16.3 %all-to-all-start.1 = ((bf16[4,288,576]{2,1,0:T(8,128)(2,1)}), bf16[4,288,576]{2,1,0:T(8,128)(2,1)S(1)}, u32[]{:S(2)}, u32[]{:S(2)}) async-start(bf16[4,288,576]{2,1,0:T(8,128)(2,1)} %get-tuple-element.120), calls=%async_computation.1 | async-start | bytes 2949120 | tf_op jit(solution)/shard_map/all_to_all | solution.py:53
  187.6 23.4 %all-to-all-done.1 = bf16[4,288,576]{2,1,0:T(8,128)(2,1)S(1)} async-done(((bf16[4,288,576]{2,1,0:T(8,128)(2,1)}), bf16[4,288,576]{2,1,0:T(8,128)(2,1)S(1)}, u32[]{:S(2)}, u32[]{:S(2)}) %all-to-all-start.1) | async-done | bytes 1327136 | tf_op jit(solution)/shard_map/all_to_all | solution.py:53
  211.0 4.3 all-to-all-start.2
  221.5 28.3 %all-to-all-done.2 = bf16[4,288,576]{2,1,0:T(8,128)(2,1)} async-done(((bf16[4,288,576]{2,1,0:T(8,128)(2,1)}), bf16[4,288,576]{2,1,0:T(8,128)(2,1)}, u32[]{:S(2)}, u32[]{:S(2)}) %all-to-all-start.2) | async-done | bytes 1327136 | tf_op jit(solution)/shard_map/all_to_all | solution.py:53
  249.7 3.8 collective-permute-start.24
  257.5 3.7 collective-permute-done.26
  264.2 2.8 collective-permute-start.36
  267.7 10.7 %collective-permute-done.36 = bf16[64,2304]{1,0:T(8,128)(2,1)S(1)} collective-permute-done((bf16[64,2304]{1,0:T(8,128)(2,1)S(1)}, bf16[64,2304]{1,0:T(8,128)(2,1)S(1)}, u32[]{:S(2)}, u32[]{:S(2)}) %collective-permute-start.36) | collective-permute-done | bytes 294944 | tf_op jit(solution)/shard_map/ppermute | solution.py:99
  278.9 8.0 %collective-permute-done.37 = bf16[64,2304]{1,0:T(8,128)(2,1)S(1)} collective-permute-done((bf16[64,2304]{1,0:T(8,128)(2,1)S(1)}, bf16[64,2304]{1,0:T(8,128)(2,1)S(1)}, u32[]{:S(2)}, u32[]{:S(2)}) %collective-permute-start.37) | collective-permute-done | bytes 294944 | tf_op jit(solution)/shard_map/ppermute | solution.py:63
  313.1 13.7 %collective-permute-done.33 = bf16[128,2304]{1,0:T(8,128)(2,1)S(1)} collective-permute-done((bf16[128,2304]{1,0:T(8,128)(2,1)S(1)}, bf16[128,2304]{1,0:T(8,128)(2,1)S(1)}, u32[]{:S(2)}, u32[]{:S(2)}) %collective-permute-start.33) | collective-permute-done | bytes 589856 | tf_op jit(solution)/shard_map/ppermute | solution.py:63
  330.7 4.6 collective-permute-done.40
  337.1 5.6 collective-permute-done.34
  343.4 10.8 %collective-permute-done.41 = bf16[64,2304]{1,0:T(8,128)(2,1)S(1)} collective-permute-done((bf16[64,2304]{1,0:T(8,128)(2,1)S(1)}, bf16[64,2304]{1,0:T(8,128)(2,1)S(1)}, u32[]{:S(2)}, u32[]{:S(2)}) %collective-permute-start.41) | collective-permute-done | bytes 294944 | tf_op jit(solution)/shard_map/ppermute | solution.py:99
  358.0 3.1 collective-permute-start.45
  362.1 7.0 collective-permute-done.44
  369.0 3.9 collective-permute-done.45
  376.1 11.8 %collective-permute-done.54 = bf16[64,2304]{1,0:T(8,128)(2,1)S(1)} collective-permute-done((bf16[64,2304]{1,0:T(8,128)(2,1)S(1)}, bf16[64,2304]{1,0:T(8,128)(2,1)S(1)}, u32[]{:S(2)}, u32[]{:S(2)}) %collective-permute-start.54) | collective-permute-done | bytes 294944 | tf_op jit(solution)/shard_map/ppermute | solution.py:99
  392.6 4.6 collective-permute-done.55
  398.3 3.7 collective-permute-done.60
  415.8 3.9 fusion.22
  421.1 14.3 %collective-permute-done.51 = bf16[128,2304]{1,0:T(8,128)(2,1)S(1)} collective-permute-done((bf16[128,2304]{1,0:T(8,128)(2,1)S(1)}, bf16[128,2304]{1,0:T(8,128)(2,1)S(1)}, u32[]{:S(2)}, u32[]{:S(2)}) %collective-permute-start.51) | collective-permute-done | bytes 589856 | tf_op jit(solution)/shard_map/ppermute | solution.py:63
  437.4 6.5 collective-permute-done.58
  448.2 3.2 collective-permute-done.61
  452.2 5.8 fusion.34
  458.0 5.8 fusion.28
  463.8 6.4 collective-permute-done.62
  474.2 4.1 all-to-all-start.3
  478.2 4.1 fusion.13
  498.3 17.9 %collective-permute-done.64 = bf16[4,288,576]{2,1,0:T(8,128)(2,1)} collective-permute-done((bf16[4,288,576]{2,1,0:T(8,128)(2,1)}, bf16[4,288,576]{2,1,0:T(8,128)(2,1)}, u32[]{:S(2)}, u32[]{:S(2)}) %collective-permute-start.64) | collective-permute-done | bytes 1327136 | tf_op jit(solution)/shard_map/ppermute | solution.py:63
  520.4 4.7 fusion.9
  525.0 4.8 all-to-all-start.4
  533.9 4.1 fusion.12
  547.7 12.8 %attend_back.1 = (bf16[512,256]{1,0:T(8,128)(2,1)S(1)}, f32[2048,256]{1,0:T(8,128)}, bf16[2048,256]{1,0:T(8,128)(2,1)S(1)}) custom-call(s32[1]{0:T(128)} %bitcast.16.side_ref, bf16[512,2304]{1,0:T(8,128)(2,1)} %bitcast.271, bf16[2304,256]{1,0:T(8,128)(2,1)S(1)} %bitcast.274, bf16[2048,256]{1,0:T(8,128)(2,1)S(1)} %copy-done.18, ...), custom_call_target="tpu_custom_call" | custom-call | tf_op jit(solution)/shard_map/attend_back/pallas_call | solution.py:410
  562.2 7.1 collective-permute-done.63
  569.4 3.1 fusion.8
  573.5 5.3 all-to-all-start.5
  600.5 3.7 collective-permute-done.75.refs_1_
  621.9 19.6 %collective-permute-done.80 = bf16[576,256]{1,0:T(8,128)(2,1)} collective-permute-done((bf16[576,256]{1,0:T(8,128)(2,1)}, bf16[576,256]{1,0:T(8,128)(2,1)}, u32[]{:S(2)}, u32[]{:S(2)}) %collective-permute-start.80) | collective-permute-done | bytes 294944 | tf_op jit(solution)/shard_map/ppermute | solution.py:99
  644.5 13.3 %collective-permute-done.76.refs_5_ = bf16[512,256]{1,0:T(8,128)(2,1)} collective-permute-done((bf16[512,256]{1,0:T(8,128)(2,1)}, bf16[512,256]{1,0:T(8,128)(2,1)}, u32[]{:S(2)}, u32[]{:S(2)}) %collective-permute-start.76) | collective-permute-done | bytes 262176 | tf_op jit(solution)/shard_map/ppermute | solution.py:76
  670.1 3.2 side_by_side.4
  677.2 9.3 %collective-permute-done.83.refs_3_ = bf16[2,64,1152]{2,1,0:T(8,128)(2,1)S(1)} collective-permute-done((bf16[2,64,1152]{2,1,0:T(8,128)(2,1)S(1)}, bf16[2,64,1152]{2,1,0:T(8,128)(2,1)S(1)}, u32[]{:S(2)}, u32[]{:S(2)}) %collective-permute-start.83) | collective-permute-done | bytes 294944 | tf_op jit(solution)/shard_map/ppermute | solution.py:63
  690.8 3.4 collective-permute-done.85.refs_4_
  696.4 2.9 collective-permute-start.91
  699.9 8.8 %collective-permute-done.95 = bf16[576,256]{1,0:T(8,128)(2,1)S(1)} collective-permute-done((bf16[576,256]{1,0:T(8,128)(2,1)S(1)}, bf16[576,256]{1,0:T(8,128)(2,1)S(1)}, u32[]{:S(2)}, u32[]{:S(2)}) %collective-permute-start.95) | collective-permute-done | bytes 294944 | tf_op jit(solution)/shard_map/ppermute | solution.py:99
  708.9 3.8 collective-permute-done.98
  714.0 10.6 %collective-permute-done.90 = bf16[576,256]{1,0:T(8,128)(2,1)S(1)} collective-permute-done((bf16[576,256]{1,0:T(8,128)(2,1)S(1)}, bf16[576,256]{1,0:T(8,128)(2,1)S(1)}, u32[]{:S(2)}, u32[]{:S(2)}) %collective-permute-start.90) | collective-permute-done | bytes 294944 | tf_op jit(solution)/shard_map/ppermute | solution.py:99
  726.6 2.7 collective-permute-done.100
  729.4 6.2 collective-permute-start.101
  (550 shorter events, 258.5 us)
Async XLA Ops:
  9.6 25.8 %collective-permute-start.3 = (bf16[592,256]{1,0:T(8,128)(2,1)S(1)}, bf16[592,256]{1,0:T(8,128)(2,1)S(1)}, u32[]{:S(2)}, u32[]{:S(2)}) collective-permute-start(bf16[592,256]{1,0:T(8,128)(2,1)S(1)} %pad_maximum_fusion.28), channel_id=1, source_target_pairs={{0,16},{8,24},{16,0},{24,8},{1,17},{9,25},{17,1},{25,9},{2,18},{10... | collective-permute-start | bytes 909320 | tf_op jit(solution)/shard_map/ppermute | solution.py:99
  9.6 25.8 %collective-permute-start.4 = (bf16[592,256]{1,0:T(8,128)(2,1)S(1)}, bf16[592,256]{1,0:T(8,128)(2,1)S(1)}, u32[]{:S(2)}, u32[]{:S(2)}) collective-permute-start(bf16[592,256]{1,0:T(8,128)(2,1)S(1)} %pad_maximum_fusion.28), channel_id=1, source_target_pairs={{0,8},{8,16},{16,24},{24,0},{1,9},{9,17},{17,25},{25,1},{2,10},{10... | collective-permute-start | bytes 909320 | tf_op jit(solution)/shard_map/ppermute | solution.py:99
  10.6 27.2 %collective-permute-start.1 = (bf16[256,2304]{1,0:T(8,128)(2,1)}, bf16[256,2304]{1,0:T(8,128)(2,1)}, u32[]{:S(2)}, u32[]{:S(2)}) collective-permute-start(bf16[256,2304]{1,0:T(8,128)(2,1)} %param.14), channel_id=1, source_target_pairs={{0,4},{4,0},{1,5},{5,1},{2,6},{6,2},{3,7},{7,3},{8,12},{12,8},{9,1... | collective-permute-start | bytes 3538952 | tf_op jit(solution)/shard_map/ppermute | solution.py:63
  12.8 35.6 %collective-permute-start = (bf16[1,256]{1,0:T(2,128)(2,1)S(1)}, bf16[1,256]{1,0:T(2,128)(2,1)S(1)}, u32[]{:S(2)}, u32[]{:S(2)}) collective-permute-start(bf16[1,256]{1,0:T(2,128)(2,1)S(1)} %convert_element_type.335), channel_id=1, source_target_pairs={{0,4},{4,0},{1,5},{5,1},{2,6},{6,2},{3,7},{7,3},{8,12},{12,8},{9,1... | collective-permute-start | bytes 1544 | tf_op jit(solution)/shard_map/ppermute | solution.py:63
  48.5 33.8 %collective-permute-start.8 = (bf16[512,256]{1,0:T(8,128)(2,1)S(1)}, bf16[512,256]{1,0:T(8,128)(2,1)}, u32[]{:S(2)}, u32[]{:S(2)}) collective-permute-start(bf16[512,256]{1,0:T(8,128)(2,1)S(1)} %fusion.68), channel_id=1, source_target_pairs={{0,24},{1,25},{2,26},{3,27},{4,28},{5,29},{6,30},{7,31}} | collective-permute-start | bytes 786440 | tf_op jit(solution)/shard_map/ppermute | solution.py:76
  50.5 33.4 %collective-permute-start.9 = (bf16[512,256]{1,0:T(8,128)(2,1)S(1)}, bf16[512,256]{1,0:T(8,128)(2,1)}, u32[]{:S(2)}, u32[]{:S(2)}) collective-permute-start(bf16[512,256]{1,0:T(8,128)(2,1)S(1)} %fusion.68), channel_id=1, source_target_pairs={{0,16},{8,24},{1,17},{9,25},{2,18},{10,26},{3,19},{11,27},{4,20},{... | collective-permute-start | bytes 786440 | tf_op jit(solution)/shard_map/ppermute | solution.py:76
  53.0 37.4 %collective-permute-start.5 = (bf16[592,256]{1,0:T(8,128)(2,1)S(1)}, bf16[592,256]{1,0:T(8,128)(2,1)}, u32[]{:S(2)}, u32[]{:S(2)}) collective-permute-start(bf16[592,256]{1,0:T(8,128)(2,1)S(1)} %pad_maximum_fusion.27), channel_id=1, source_target_pairs={{0,24},{8,0},{16,8},{24,16},{1,25},{9,1},{17,9},{25,17},{2,26},{10... | collective-permute-start | bytes 909320 | tf_op jit(solution)/shard_map/ppermute | solution.py:99
  53.0 37.9 %collective-permute-start.6 = (bf16[592,256]{1,0:T(8,128)(2,1)S(1)}, bf16[592,256]{1,0:T(8,128)(2,1)}, u32[]{:S(2)}, u32[]{:S(2)}) collective-permute-start(bf16[592,256]{1,0:T(8,128)(2,1)S(1)} %pad_maximum_fusion.27), channel_id=1, source_target_pairs={{0,16},{8,24},{16,0},{24,8},{1,17},{9,25},{17,1},{25,9},{2,18},{10... | collective-permute-start | bytes 909320 | tf_op jit(solution)/shard_map/ppermute | solution.py:99
  54.5 38.0 %collective-permute-start.7 = (bf16[592,256]{1,0:T(8,128)(2,1)S(1)}, bf16[592,256]{1,0:T(8,128)(2,1)}, u32[]{:S(2)}, u32[]{:S(2)}) collective-permute-start(bf16[592,256]{1,0:T(8,128)(2,1)S(1)} %pad_maximum_fusion.27), channel_id=1, source_target_pairs={{0,8},{8,16},{16,24},{24,0},{1,9},{9,17},{17,25},{25,1},{2,10},{10... | collective-permute-start | bytes 909320 | tf_op jit(solution)/shard_map/ppermute | solution.py:99
  82.4 38.9 %collective-permute-start.14 = (bf16[512,256]{1,0:T(8,128)(2,1)S(1)}, bf16[512,256]{1,0:T(8,128)(2,1)}, u32[]{:S(2)}, u32[]{:S(2)}) collective-permute-start(bf16[512,256]{1,0:T(8,128)(2,1)S(1)} %fusion.68), channel_id=1, source_target_pairs={{0,4},{4,0},{1,5},{5,1},{2,6},{6,2},{3,7},{7,3},{8,12},{12,8},{9,1... | collective-permute-start | bytes 786440 | tf_op jit(solution)/shard_map/ppermute | solution.py:63
  83.9 57.0 %all-to-all-start = ((bf16[4,288,576]{2,1,0:T(8,128)(2,1)}), bf16[4,288,576]{2,1,0:T(8,128)(2,1)}, u32[]{:S(2)}, u32[]{:S(2)}) async-start(bf16[4,288,576]{2,1,0:T(8,128)(2,1)} %get-tuple-element.116), calls=%async_computation | async-start | bytes 2949120 | tf_op jit(solution)/shard_map/all_to_all | solution.py:53
  88.9 26.5 %collective-permute-start.11 = (bf16[512,256]{1,0:T(8,128)(2,1)}, bf16[512,256]{1,0:T(8,128)(2,1)S(1)}, u32[]{:S(2)}, u32[]{:S(2)}) collective-permute-start(bf16[512,256]{1,0:T(8,128)(2,1)} %collective-permute-done.8), channel_id=1, source_target_pairs={{0,4},{4,0},{1,5},{5,1},{2,6},{6,2},{3,7},{7,3},{8,12},{12,8},{9,1... | collective-permute-start | bytes 786440 | tf_op jit(solution)/shard_map/ppermute | solution.py:63
  90.4 27.6 %collective-permute-start.12 = (bf16[512,256]{1,0:T(8,128)(2,1)}, bf16[512,256]{1,0:T(8,128)(2,1)S(1)}, u32[]{:S(2)}, u32[]{:S(2)}) collective-permute-start(bf16[512,256]{1,0:T(8,128)(2,1)} %collective-permute-done.9), channel_id=1, source_target_pairs={{0,4},{4,0},{1,5},{5,1},{2,6},{6,2},{3,7},{7,3},{8,12},{12,8},{9,1... | collective-permute-start | bytes 786440 | tf_op jit(solution)/shard_map/ppermute | solution.py:63
  90.9 30.3 %collective-permute-start.13 = (bf16[512,256]{1,0:T(8,128)(2,1)}, bf16[512,256]{1,0:T(8,128)(2,1)S(1)}, u32[]{:S(2)}, u32[]{:S(2)}) collective-permute-start(bf16[512,256]{1,0:T(8,128)(2,1)} %collective-permute-done.10), channel_id=1, source_target_pairs={{0,4},{4,0},{1,5},{5,1},{2,6},{6,2},{3,7},{7,3},{8,12},{12,8},{9,1... | collective-permute-start | bytes 786440 | tf_op jit(solution)/shard_map/ppermute | solution.py:63
  96.7 35.3 %collective-permute-start.15 = (bf16[576,256]{1,0:T(8,128)(2,1)S(1)}, bf16[576,256]{1,0:T(8,128)(2,1)S(1)}, u32[]{:S(2)}, u32[]{:S(2)}) collective-permute-start(bf16[576,256]{1,0:T(8,128)(2,1)S(1)} %slice_select_fusion), channel_id=1, source_target_pairs={{0,8},{8,16},{16,24},{24,0},{1,9},{9,17},{17,25},{25,1},{2,10},{10... | collective-permute-start | bytes 884744 | tf_op jit(solution)/shard_map/ppermute | solution.py:99
  115.4 25.2 %collective-permute-start.16 = (bf16[576,256]{1,0:T(8,128)(2,1)S(1)}, bf16[576,256]{1,0:T(8,128)(2,1)S(1)}, u32[]{:S(2)}, u32[]{:S(2)}) collective-permute-start(bf16[576,256]{1,0:T(8,128)(2,1)S(1)} %slice_select_fusion), channel_id=1, source_target_pairs={{0,16},{8,24},{16,0},{24,8},{1,17},{9,25},{17,1},{25,9},{2,18},{10... | collective-permute-start | bytes 884744 | tf_op jit(solution)/shard_map/ppermute | solution.py:99
  118.0 22.6 %collective-permute-start.17 = (bf16[576,256]{1,0:T(8,128)(2,1)S(1)}, bf16[576,256]{1,0:T(8,128)(2,1)S(1)}, u32[]{:S(2)}, u32[]{:S(2)}) collective-permute-start(bf16[576,256]{1,0:T(8,128)(2,1)S(1)} %slice_select_fusion), channel_id=1, source_target_pairs={{0,24},{8,0},{16,8},{24,16},{1,25},{9,1},{17,9},{25,17},{2,26},{10... | collective-permute-start | bytes 884744 | tf_op jit(solution)/shard_map/ppermute | solution.py:99
  157.0 23.4 %collective-permute-start.21 = (bf16[2,64,1152]{2,1,0:T(8,128)(2,1)S(1)}, bf16[2,64,1152]{2,1,0:T(8,128)(2,1)S(1)}, u32[]{:S(2)}, u32[]{:S(2)}) collective-permute-start(bf16[2,64,1152]{2,1,0:T(8,128)(2,1)S(1)} %fusion.79), channel_id=1, source_target_pairs={{0,2},{1,3},{2,0},{3,1},{4,6},{5,7},{6,4},{7,5},{8,10},{9,11},{10,... | collective-permute-start | bytes 884744 | tf_op jit(solution)/shard_map/ppermute | solution.py:63
  158.6 21.8 %collective-permute-start.19 = (bf16[2,64,1152]{2,1,0:T(8,128)(2,1)S(1)}, bf16[2,64,1152]{2,1,0:T(8,128)(2,1)}, u32[]{:S(2)}, u32[]{:S(2)}) collective-permute-start(bf16[2,64,1152]{2,1,0:T(8,128)(2,1)S(1)} %fusion.78), channel_id=1, source_target_pairs={{0,4},{4,0},{1,5},{5,1},{2,6},{6,2},{3,7},{7,3},{8,12},{12,8},{9,1... | collective-permute-start | bytes 884744 | tf_op jit(solution)/shard_map/ppermute | solution.py:63
  160.1 50.9 %all-to-all-start.1 = ((bf16[4,288,576]{2,1,0:T(8,128)(2,1)}), bf16[4,288,576]{2,1,0:T(8,128)(2,1)S(1)}, u32[]{:S(2)}, u32[]{:S(2)}) async-start(bf16[4,288,576]{2,1,0:T(8,128)(2,1)} %get-tuple-element.120), calls=%async_computation.1 | async-start | bytes 2949120 | tf_op jit(solution)/shard_map/all_to_all | solution.py:53
  179.9 74.1 %collective-permute-start.28 = (bf16[4,288,576]{2,1,0:T(8,128)(2,1)}, bf16[4,288,576]{2,1,0:T(8,128)(2,1)}, u32[]{:S(2)}, u32[]{:S(2)}) collective-permute-start(bf16[4,288,576]{2,1,0:T(8,128)(2,1)} %all-to-all-done), channel_id=1, source_target_pairs={{0,4},{4,0},{1,5},{5,1},{2,6},{6,2},{3,7},{7,3},{8,12},{12,8},{9,1... | collective-permute-start | bytes 3981320 | tf_op jit(solution)/shard_map/ppermute | solution.py:63
  183.6 33.3 %collective-permute-start.22 = (bf16[64,1152]{1,0:T(8,128)(2,1)}, bf16[64,1152]{1,0:T(8,128)(2,1)}, u32[]{:S(2)}, u32[]{:S(2)}) collective-permute-start(bf16[64,1152]{1,0:T(8,128)(2,1)} %fusion.87), channel_id=1, source_target_pairs={{0,4},{4,0},{1,5},{5,1},{2,6},{6,2},{3,7},{7,3},{8,12},{12,8},{9,1... | collective-permute-start | bytes 442376 | tf_op jit(solution)/shard_map/ppermute | solution.py:63
  211.0 38.8 %all-to-all-start.2 = ((bf16[4,288,576]{2,1,0:T(8,128)(2,1)}), bf16[4,288,576]{2,1,0:T(8,128)(2,1)}, u32[]{:S(2)}, u32[]{:S(2)}) async-start(bf16[4,288,576]{2,1,0:T(8,128)(2,1)} %get-tuple-element.123), calls=%async_computation.2 | async-start | bytes 2949120 | tf_op jit(solution)/shard_map/all_to_all | solution.py:53
  218.0 38.1 %collective-permute-start.29 = (bf16[4,288,576]{2,1,0:T(8,128)(2,1)S(1)}, bf16[4,288,576]{2,1,0:T(8,128)(2,1)}, u32[]{:S(2)}, u32[]{:S(2)}) collective-permute-start(bf16[4,288,576]{2,1,0:T(8,128)(2,1)S(1)} %all-to-all-done.1), channel_id=1, source_target_pairs={{0,4},{4,0},{1,5},{5,1},{2,6},{6,2},{3,7},{7,3},{8,12},{12,8},{9,1... | collective-permute-start | bytes 3981320 | tf_op jit(solution)/shard_map/ppermute | solution.py:63
  249.7 14.5 %collective-permute-start.24 = (bf16[64,2304]{1,0:T(8,128)(2,1)}, bf16[64,2304]{1,0:T(8,128)(2,1)S(1)}, u32[]{:S(2)}, u32[]{:S(2)}) collective-permute-start(bf16[64,2304]{1,0:T(8,128)(2,1)} %get-tuple-element.130), channel_id=1, source_target_pairs={{0,24},{8,0},{16,8},{24,16},{1,25},{9,1},{17,9},{25,17},{2,26},{10... | collective-permute-start | bytes 884744 | tf_op jit(solution)/shard_map/ppermute | solution.py:99
  256.9 32.7 %collective-permute-start.30 = (bf16[4,288,576]{2,1,0:T(8,128)(2,1)}, bf16[4,288,576]{2,1,0:T(8,128)(2,1)S(1)}, u32[]{:S(2)}, u32[]{:S(2)}) collective-permute-start(bf16[4,288,576]{2,1,0:T(8,128)(2,1)} %all-to-all-done.2), channel_id=1, source_target_pairs={{0,4},{4,0},{1,5},{5,1},{2,6},{6,2},{3,7},{7,3},{8,12},{12,8},{9,1... | collective-permute-start | bytes 3981320 | tf_op jit(solution)/shard_map/ppermute | solution.py:63
  261.2 25.8 %collective-permute-start.27 = (bf16[128,2304]{1,0:T(8,128)(2,1)S(1)}, bf16[128,2304]{1,0:T(8,128)(2,1)S(1)}, u32[]{:S(2)}, u32[]{:S(2)}) collective-permute-start(bf16[128,2304]{1,0:T(8,128)(2,1)S(1)} %pad_maximum_fusion.21), channel_id=1, source_target_pairs={{0,1},{1,0},{2,3},{3,2},{4,5},{5,4},{6,7},{7,6},{8,9},{9,8},{10,11... | collective-permute-start | bytes 1769480 | tf_op jit(solution)/shard_map/ppermute | solution.py:63
  264.2 14.2 %collective-permute-start.36 = (bf16[64,2304]{1,0:T(8,128)(2,1)S(1)}, bf16[64,2304]{1,0:T(8,128)(2,1)S(1)}, u32[]{:S(2)}, u32[]{:S(2)}) collective-permute-start(bf16[64,2304]{1,0:T(8,128)(2,1)S(1)} %copy-done.62), channel_id=1, source_target_pairs={{0,16},{8,24},{16,0},{24,8},{1,17},{9,25},{17,1},{25,9},{2,18},{10... | collective-permute-start | bytes 884744 | tf_op jit(solution)/shard_map/ppermute | solution.py:99
  267.1 21.2 %collective-permute-start.25 = (bf16[128,2304]{1,0:T(8,128)(2,1)S(1)}, bf16[128,2304]{1,0:T(8,128)(2,1)S(1)}, u32[]{:S(2)}, u32[]{:S(2)}) collective-permute-start(bf16[128,2304]{1,0:T(8,128)(2,1)S(1)} %pad_maximum_fusion.20), channel_id=1, source_target_pairs={{0,2},{1,3},{2,0},{3,1},{4,6},{5,7},{6,4},{7,5},{8,10},{9,11},{10,... | collective-permute-start | bytes 1769480 | tf_op jit(solution)/shard_map/ppermute | solution.py:63
  311.4 15.4 %collective-permute-start.33 = (bf16[128,2304]{1,0:T(8,128)(2,1)S(1)}, bf16[128,2304]{1,0:T(8,128)(2,1)S(1)}, u32[]{:S(2)}, u32[]{:S(2)}) collective-permute-start(bf16[128,2304]{1,0:T(8,128)(2,1)S(1)} %slice.599), channel_id=1, source_target_pairs={{0,2},{1,3},{2,0},{3,1},{4,6},{5,7},{6,4},{7,5},{8,10},{9,11},{10,... | collective-permute-start | bytes 1769480 | tf_op jit(solution)/shard_map/ppermute | solution.py:63
  328.7 14.1 %collective-permute-start.34 = (bf16[64,2304]{1,0:T(8,128)(2,1)S(1)}, bf16[64,2304]{1,0:T(8,128)(2,1)S(1)}, u32[]{:S(2)}, u32[]{:S(2)}) collective-permute-start(bf16[64,2304]{1,0:T(8,128)(2,1)S(1)} %get-tuple-element.305), channel_id=1, source_target_pairs={{0,24},{8,0},{16,8},{24,16},{1,25},{9,1},{17,9},{25,17},{2,26},{10... | collective-permute-start | bytes 884744 | tf_op jit(solution)/shard_map/ppermute | solution.py:99
  329.0 14.4 %collective-permute-start.35 = (bf16[64,2304]{1,0:T(8,128)(2,1)S(1)}, bf16[64,2304]{1,0:T(8,128)(2,1)S(1)}, u32[]{:S(2)}, u32[]{:S(2)}) collective-permute-start(bf16[64,2304]{1,0:T(8,128)(2,1)S(1)} %get-tuple-element.306), channel_id=1, source_target_pairs={{0,8},{8,16},{16,24},{24,0},{1,9},{9,17},{17,25},{25,1},{2,10},{10... | collective-permute-start | bytes 884744 | tf_op jit(solution)/shard_map/ppermute | solution.py:99
  335.4 18.8 %collective-permute-start.41 = (bf16[64,2304]{1,0:T(8,128)(2,1)S(1)}, bf16[64,2304]{1,0:T(8,128)(2,1)S(1)}, u32[]{:S(2)}, u32[]{:S(2)}) collective-permute-start(bf16[64,2304]{1,0:T(8,128)(2,1)S(1)} %convert_add_fusion.5), channel_id=1, source_target_pairs={{0,16},{8,24},{16,0},{24,8},{1,17},{9,25},{17,1},{25,9},{2,18},{10... | collective-permute-start | bytes 884744 | tf_op jit(solution)/shard_map/ppermute | solution.py:99
  358.0 15.0 %collective-permute-start.45 = (bf16[64,2304]{1,0:T(8,128)(2,1)S(1)}, bf16[64,2304]{1,0:T(8,128)(2,1)S(1)}, u32[]{:S(2)}, u32[]{:S(2)}) collective-permute-start(bf16[64,2304]{1,0:T(8,128)(2,1)S(1)} %fusion.44), channel_id=1, source_target_pairs={{0,24},{8,0},{16,8},{24,16},{1,25},{9,1},{17,9},{25,17},{2,26},{10... | collective-permute-start | bytes 884744 | tf_op jit(solution)/shard_map/ppermute | solution.py:99
  361.1 13.8 %collective-permute-start.47 = (bf16[64,2304]{1,0:T(8,128)(2,1)S(1)}, bf16[64,2304]{1,0:T(8,128)(2,1)S(1)}, u32[]{:S(2)}, u32[]{:S(2)}) collective-permute-start(bf16[64,2304]{1,0:T(8,128)(2,1)S(1)} %fusion.44), channel_id=1, source_target_pairs={{0,2},{1,3},{2,0},{3,1},{4,6},{5,7},{6,4},{7,5},{8,10},{9,11},{10,... | collective-permute-start | bytes 884744 | tf_op jit(solution)/shard_map/ppermute | solution.py:63
  372.9 15.0 %collective-permute-start.54 = (bf16[64,2304]{1,0:T(8,128)(2,1)S(1)}, bf16[64,2304]{1,0:T(8,128)(2,1)S(1)}, u32[]{:S(2)}, u32[]{:S(2)}) collective-permute-start(bf16[64,2304]{1,0:T(8,128)(2,1)S(1)} %fusion.44), channel_id=1, source_target_pairs={{0,16},{8,24},{16,0},{24,8},{1,17},{9,25},{17,1},{25,9},{2,18},{10... | collective-permute-start | bytes 884744 | tf_op jit(solution)/shard_map/ppermute | solution.py:99
  375.1 22.2 %collective-permute-start.46 = (bf16[128,2304]{1,0:T(8,128)(2,1)S(1)}, bf16[128,2304]{1,0:T(8,128)(2,1)S(1)}, u32[]{:S(2)}, u32[]{:S(2)}) collective-permute-start(bf16[128,2304]{1,0:T(8,128)(2,1)S(1)} %pad_maximum_fusion.23), channel_id=1, source_target_pairs={{0,2},{1,3},{2,0},{3,1},{4,6},{5,7},{6,4},{7,5},{8,10},{9,11},{10,... | collective-permute-start | bytes 1769480 | tf_op jit(solution)/shard_map/ppermute | solution.py:63
  420.0 15.4 %collective-permute-start.51 = (bf16[128,2304]{1,0:T(8,128)(2,1)S(1)}, bf16[128,2304]{1,0:T(8,128)(2,1)S(1)}, u32[]{:S(2)}, u32[]{:S(2)}) collective-permute-start(bf16[128,2304]{1,0:T(8,128)(2,1)S(1)} %slice.596), channel_id=1, source_target_pairs={{0,2},{1,3},{2,0},{3,1},{4,6},{5,7},{6,4},{7,5},{8,10},{9,11},{10,... | collective-permute-start | bytes 1769480 | tf_op jit(solution)/shard_map/ppermute | solution.py:63
  436.9 33.3 %collective-permute-start.62 = (bf16[4,288,576]{2,1,0:T(8,128)(2,1)S(1)}, bf16[4,288,576]{2,1,0:T(8,128)(2,1)S(1)}, u32[]{:S(2)}, u32[]{:S(2)}) collective-permute-start(bf16[4,288,576]{2,1,0:T(8,128)(2,1)S(1)} %fusion.11), channel_id=1, source_target_pairs={{0,4},{4,0},{1,5},{5,1},{2,6},{6,2},{3,7},{7,3},{8,12},{12,8},{9,1... | collective-permute-start | bytes 3981320 | tf_op jit(solution)/shard_map/ppermute | solution.py:63
  445.0 25.1 %collective-permute-start.52 = (bf16[64,2304]{1,0:T(8,128)(2,1)S(1)}, bf16[64,2304]{1,0:T(8,128)(2,1)S(1)}, u32[]{:S(2)}, u32[]{:S(2)}) collective-permute-start(bf16[64,2304]{1,0:T(8,128)(2,1)S(1)} %get-tuple-element.304), channel_id=1, source_target_pairs={{0,24},{8,0},{16,8},{24,16},{1,25},{9,1},{17,9},{25,17},{2,26},{10... | collective-permute-start | bytes 884744 | tf_op jit(solution)/shard_map/ppermute | solution.py:99
  447.3 23.6 %collective-permute-start.53 = (bf16[64,2304]{1,0:T(8,128)(2,1)S(1)}, bf16[64,2304]{1,0:T(8,128)(2,1)S(1)}, u32[]{:S(2)}, u32[]{:S(2)}) collective-permute-start(bf16[64,2304]{1,0:T(8,128)(2,1)S(1)} %get-tuple-element.303), channel_id=1, source_target_pairs={{0,8},{8,16},{16,24},{24,0},{1,9},{9,17},{17,25},{25,1},{2,10},{10... | collective-permute-start | bytes 884744 | tf_op jit(solution)/shard_map/ppermute | solution.py:99
  447.5 24.4 %collective-permute-start.59 = (bf16[64,2304]{1,0:T(8,128)(2,1)S(1)}, bf16[64,2304]{1,0:T(8,128)(2,1)S(1)}, u32[]{:S(2)}, u32[]{:S(2)}) collective-permute-start(bf16[64,2304]{1,0:T(8,128)(2,1)S(1)} %convert_add_fusion.4), channel_id=1, source_target_pairs={{0,16},{8,24},{16,0},{24,8},{1,17},{9,25},{17,1},{25,9},{2,18},{10... | collective-permute-start | bytes 884744 | tf_op jit(solution)/shard_map/ppermute | solution.py:99
  474.2 42.0 %all-to-all-start.3 = ((bf16[4,288,576]{2,1,0:T(8,128)(2,1)}), bf16[4,288,576]{2,1,0:T(8,128)(2,1)S(1)}, u32[]{:S(2)}, u32[]{:S(2)}) async-start(bf16[4,288,576]{2,1,0:T(8,128)(2,1)} %fusion.10), calls=%async_computation.3 | async-start | bytes 2949120 | tf_op jit(solution)/shard_map/all_to_all | solution.py:53
  482.4 33.8 %collective-permute-start.64 = (bf16[4,288,576]{2,1,0:T(8,128)(2,1)}, bf16[4,288,576]{2,1,0:T(8,128)(2,1)}, u32[]{:S(2)}, u32[]{:S(2)}) collective-permute-start(bf16[4,288,576]{2,1,0:T(8,128)(2,1)} %fusion.13), channel_id=1, source_target_pairs={{0,4},{4,0},{1,5},{5,1},{2,6},{6,2},{3,7},{7,3},{8,12},{12,8},{9,1... | collective-permute-start | bytes 3981320 | tf_op jit(solution)/shard_map/ppermute | solution.py:63
  525.0 47.4 %all-to-all-start.4 = ((bf16[4,288,576]{2,1,0:T(8,128)(2,1)}), bf16[4,288,576]{2,1,0:T(8,128)(2,1)S(1)}, u32[]{:S(2)}, u32[]{:S(2)}) async-start(bf16[4,288,576]{2,1,0:T(8,128)(2,1)} %fusion.9), calls=%async_computation.4 | async-start | bytes 2949120 | tf_op jit(solution)/shard_map/all_to_all | solution.py:53
  538.0 31.4 %collective-permute-start.63 = (bf16[4,288,576]{2,1,0:T(8,128)(2,1)}, bf16[4,288,576]{2,1,0:T(8,128)(2,1)}, u32[]{:S(2)}, u32[]{:S(2)}) collective-permute-start(bf16[4,288,576]{2,1,0:T(8,128)(2,1)} %fusion.12), channel_id=1, source_target_pairs={{0,4},{4,0},{1,5},{5,1},{2,6},{6,2},{3,7},{7,3},{8,12},{12,8},{9,1... | collective-permute-start | bytes 3981320 | tf_op jit(solution)/shard_map/ppermute | solution.py:63
  541.3 39.5 %collective-permute-start.70 = (bf16[64,2304]{1,0:T(8,128)(2,1)}, bf16[64,2304]{1,0:T(8,128)(2,1)}, u32[]{:S(2)}, u32[]{:S(2)}) collective-permute-start(bf16[64,2304]{1,0:T(8,128)(2,1)} %get-tuple-element.166.own_ref), channel_id=1, source_target_pairs={{0,2},{1,3},{2,0},{3,1},{4,6},{5,7},{6,4},{7,5},{8,10},{9,11},{10,... | collective-permute-start | bytes 884744 | tf_op jit(solution)/shard_map/ppermute | solution.py:63
  573.5 84.2 %all-to-all-start.5 = ((bf16[4,288,576]{2,1,0:T(8,128)(2,1)}), bf16[4,288,576]{2,1,0:T(8,128)(2,1)}, u32[]{:S(2)}, u32[]{:S(2)}) async-start(bf16[4,288,576]{2,1,0:T(8,128)(2,1)} %fusion.8), calls=%async_computation.5 | async-start | bytes 2949120 | tf_op jit(solution)/shard_map/all_to_all | solution.py:53
  590.6 13.6 %collective-permute-start.75 = (bf16[512,256]{1,0:T(8,128)(2,1)}, bf16[512,256]{1,0:T(8,128)(2,1)}, u32[]{:S(2)}, u32[]{:S(2)}) collective-permute-start(bf16[512,256]{1,0:T(8,128)(2,1)} %get-tuple-element.289), channel_id=1, source_target_pairs={{0,4},{4,0},{1,5},{5,1},{2,6},{6,2},{3,7},{7,3},{8,12},{12,8},{9,1... | collective-permute-start | bytes 786440 | tf_op jit(solution)/shard_map/ppermute | solution.py:63
  593.2 23.8 %collective-permute-start.79 = (bf16[576,256]{1,0:T(8,128)(2,1)S(1)}, bf16[576,256]{1,0:T(8,128)(2,1)S(1)}, u32[]{:S(2)}, u32[]{:S(2)}) collective-permute-start(bf16[576,256]{1,0:T(8,128)(2,1)S(1)} %get-tuple-element.275), channel_id=1, source_target_pairs={{0,8},{8,16},{16,24},{24,0},{1,9},{9,17},{17,25},{25,1},{2,10},{10... | collective-permute-start | bytes 884744 | tf_op jit(solution)/shard_map/ppermute | solution.py:99
  595.3 46.3 %collective-permute-start.80 = (bf16[576,256]{1,0:T(8,128)(2,1)}, bf16[576,256]{1,0:T(8,128)(2,1)}, u32[]{:S(2)}, u32[]{:S(2)}) collective-permute-start(bf16[576,256]{1,0:T(8,128)(2,1)} %get-tuple-element.274), channel_id=1, source_target_pairs={{0,16},{8,24},{16,0},{24,8},{1,17},{9,25},{17,1},{25,9},{2,18},{10... | collective-permute-start | bytes 884744 | tf_op jit(solution)/shard_map/ppermute | solution.py:99
  597.6 43.9 %collective-permute-start.81 = (bf16[576,256]{1,0:T(8,128)(2,1)}, bf16[576,256]{1,0:T(8,128)(2,1)}, u32[]{:S(2)}, u32[]{:S(2)}) collective-permute-start(bf16[576,256]{1,0:T(8,128)(2,1)} %get-tuple-element.273), channel_id=1, source_target_pairs={{0,24},{8,0},{16,8},{24,16},{1,25},{9,1},{17,9},{25,17},{2,26},{10... | collective-permute-start | bytes 884744 | tf_op jit(solution)/shard_map/ppermute | solution.py:99
  610.6 33.2 %collective-permute-start.78 = (bf16[512,256]{1,0:T(8,128)(2,1)}, bf16[512,256]{1,0:T(8,128)(2,1)S(1)}, u32[]{:S(2)}, u32[]{:S(2)}) collective-permute-start(bf16[512,256]{1,0:T(8,128)(2,1)} %fused_two_sided.5), channel_id=1, source_target_pairs={{8,0},{16,8},{24,16},{9,1},{17,9},{25,17},{10,2},{18,10},{26,18},{... | collective-permute-start | bytes 786440 | tf_op jit(solution)/shard_map/ppermute | solution.py:76
  615.8 41.9 %collective-permute-start.76 = (bf16[512,256]{1,0:T(8,128)(2,1)}, bf16[512,256]{1,0:T(8,128)(2,1)}, u32[]{:S(2)}, u32[]{:S(2)}) collective-permute-start(bf16[512,256]{1,0:T(8,128)(2,1)} %fused_two_sided.4), channel_id=1, source_target_pairs={{16,0},{24,8},{17,1},{25,9},{18,2},{26,10},{19,3},{27,11},{20,4},{... | collective-permute-start | bytes 786440 | tf_op jit(solution)/shard_map/ppermute | solution.py:76
  617.8 39.9 %collective-permute-start.74 = (bf16[512,256]{1,0:T(8,128)(2,1)}, bf16[512,256]{1,0:T(8,128)(2,1)}, u32[]{:S(2)}, u32[]{:S(2)}) collective-permute-start(bf16[512,256]{1,0:T(8,128)(2,1)} %fused_two_sided.3), channel_id=1, source_target_pairs={{24,0},{25,1},{26,2},{27,3},{28,4},{29,5},{30,6},{31,7}} | collective-permute-start | bytes 786440 | tf_op jit(solution)/shard_map/ppermute | solution.py:76
  673.4 15.6 %collective-permute-start.97 = (bf16[288,256]{1,0:T(8,128)(2,1)S(1)}, bf16[288,256]{1,0:T(8,128)(2,1)S(1)}, u32[]{:S(2)}, u32[]{:S(2)}) collective-permute-start(bf16[288,256]{1,0:T(8,128)(2,1)S(1)} %select_convert_fusion.6), channel_id=1, source_target_pairs={{0,4},{4,0},{1,5},{5,1},{2,6},{6,2},{3,7},{7,3},{8,12},{12,8},{9,1... | collective-permute-start | bytes 442376 | tf_op jit(solution)/shard_map/ppermute | solution.py:63
  675.7 20.7 %collective-permute-start.93 = (bf16[576,256]{1,0:T(8,128)(2,1)S(1)}, bf16[576,256]{1,0:T(8,128)(2,1)S(1)}, u32[]{:S(2)}, u32[]{:S(2)}) collective-permute-start(bf16[576,256]{1,0:T(8,128)(2,1)S(1)} %get-tuple-element.269), channel_id=1, source_target_pairs={{0,8},{8,16},{16,24},{24,0},{1,9},{9,17},{17,25},{25,1},{2,10},{10... | collective-permute-start | bytes 884744 | tf_op jit(solution)/shard_map/ppermute | solution.py:99
  675.8 24.1 %collective-permute-start.94 = (bf16[576,256]{1,0:T(8,128)(2,1)S(1)}, bf16[576,256]{1,0:T(8,128)(2,1)S(1)}, u32[]{:S(2)}, u32[]{:S(2)}) collective-permute-start(bf16[576,256]{1,0:T(8,128)(2,1)S(1)} %get-tuple-element.268), channel_id=1, source_target_pairs={{0,16},{8,24},{16,0},{24,8},{1,17},{9,25},{17,1},{25,9},{2,18},{10... | collective-permute-start | bytes 884744 | tf_op jit(solution)/shard_map/ppermute | solution.py:99
  686.4 22.3 %collective-permute-start.95 = (bf16[576,256]{1,0:T(8,128)(2,1)S(1)}, bf16[576,256]{1,0:T(8,128)(2,1)S(1)}, u32[]{:S(2)}, u32[]{:S(2)}) collective-permute-start(bf16[576,256]{1,0:T(8,128)(2,1)S(1)} %get-tuple-element.267), channel_id=1, source_target_pairs={{0,24},{8,0},{16,8},{24,16},{1,25},{9,1},{17,9},{25,17},{2,26},{10... | collective-permute-start | bytes 884744 | tf_op jit(solution)/shard_map/ppermute | solution.py:99
  694.2 18.6 %collective-permute-start.89 = (bf16[576,256]{1,0:T(8,128)(2,1)S(1)}, bf16[576,256]{1,0:T(8,128)(2,1)S(1)}, u32[]{:S(2)}, u32[]{:S(2)}) collective-permute-start(bf16[576,256]{1,0:T(8,128)(2,1)S(1)} %get-tuple-element.272), channel_id=1, source_target_pairs={{0,8},{8,16},{16,24},{24,0},{1,9},{9,17},{17,25},{25,1},{2,10},{10... | collective-permute-start | bytes 884744 | tf_op jit(solution)/shard_map/ppermute | solution.py:99
  694.5 30.0 %collective-permute-start.90 = (bf16[576,256]{1,0:T(8,128)(2,1)S(1)}, bf16[576,256]{1,0:T(8,128)(2,1)S(1)}, u32[]{:S(2)}, u32[]{:S(2)}) collective-permute-start(bf16[576,256]{1,0:T(8,128)(2,1)S(1)} %get-tuple-element.271), channel_id=1, source_target_pairs={{0,16},{8,24},{16,0},{24,8},{1,17},{9,25},{17,1},{25,9},{2,18},{10... | collective-permute-start | bytes 884744 | tf_op jit(solution)/shard_map/ppermute | solution.py:99
  696.4 28.1 %collective-permute-start.91 = (bf16[576,256]{1,0:T(8,128)(2,1)S(1)}, bf16[576,256]{1,0:T(8,128)(2,1)S(1)}, u32[]{:S(2)}, u32[]{:S(2)}) collective-permute-start(bf16[576,256]{1,0:T(8,128)(2,1)S(1)} %get-tuple-element.270), channel_id=1, source_target_pairs={{0,24},{8,0},{16,8},{24,16},{1,25},{9,1},{17,9},{25,17},{2,26},{10... | collective-permute-start | bytes 884744 | tf_op jit(solution)/shard_map/ppermute | solution.py:99
  699.9 40.9 %collective-permute-start.87 = (bf16[64,2304]{1,0:T(8,128)(2,1)S(1)}, bf16[64,2304]{1,0:T(8,128)(2,1)S(1)}, u32[]{:S(2)}, u32[]{:S(2)}) collective-permute-start(bf16[64,2304]{1,0:T(8,128)(2,1)S(1)} %fused_first_back.1.own_ref), channel_id=1, source_target_pairs={{0,2},{1,3},{2,0},{3,1},{4,6},{5,7},{6,4},{7,5},{8,10},{9,11},{10,... | collective-permute-start | bytes 884744 | tf_op jit(solution)/shard_map/ppermute | solution.py:63
  712.8 31.5 %collective-permute-start.96 = (bf16[288,256]{1,0:T(8,128)(2,1)S(1)}, bf16[288,256]{1,0:T(8,128)(2,1)S(1)}, u32[]{:S(2)}, u32[]{:S(2)}) collective-permute-start(bf16[288,256]{1,0:T(8,128)(2,1)S(1)} %select_convert_fusion.7), channel_id=1, source_target_pairs={{0,4},{4,0},{1,5},{5,1},{2,6},{6,2},{3,7},{7,3},{8,12},{12,8},{9,1... | collective-permute-start | bytes 442376 | tf_op jit(solution)/shard_map/ppermute | solution.py:63
  (125 other events, 659.6 us)

commit v5 on v4

--- a/solution.py
+++ b/solution.py
@@ -264,8 +264,10 @@
 
 
 def join_kernel(own, step, axis):
-    other = swapped(own, *AXES[step])
-    first = bits()[step]
+    return put_together(own, swapped(own, *AXES[step]), bits()[step], axis)
+
+
+def put_together(own, other, first, axis):
     if own.ndim < 2 or own.shape[-2] % 16:
         return jnp.stack(picked(first, (own, other)), axis=axis)
     shape = own.shape[:axis] + (2,) + own.shape[axis:]
@@ -562,7 +564,7 @@
     ]
 
     def both_halves(own, other):
-        return jnp.stack(picked(is_first, (own, other)), axis=1).reshape(width, units)
+        return put_together(own, other, is_first, 1).reshape(width, units)
 
     theirs = [swapped(block, "context", 1) for block in mine]
     mine = jnp.concatenate(mine[::-1], axis=0)
@@ -588,7 +590,13 @@
     probs = weights / jnp.sum(weights, axis=-1, keepdims=True)
     probs_low = probs.astype(b16)
     mixed = dot(after(probs_low, gate_got, *out_got), values).astype(b16)
-    branch = after(collect_group(dot_nt(mixed, w_out), sub), up_got)
+    low_core = bits()[2]
+
+    def out_product(low_core, mixed, w_out):
+        return core_parted(low_core, dot_nt(mixed, w_out), sub)
+
+    branch = collect_halves(*fused(out_product, (low_core,), mixed, w_out), gate_other)
+    branch = after(halves_summed(*branch), up_got, gate_other)
 
     own_tokens = lax.dynamic_slice_in_dim(tokens, lane * sub, sub)
     own_cotangent = lax.dynamic_slice_in_dim(cotangent, lane * sub, sub)
@@ -598,9 +606,9 @@
     middle = own_tokens.astype(f32) + normed_two * gains[1]
     scale_three = rms_scale(middle)
     normed_three = middle * scale_three
-    lifted_two = after((normed_three * gains[2]).astype(b16), down_got)
-    gate_w = both_halves(gate_got, after(gate_other, lifted_two))
-    up_w = both_halves(up_got, after(up_other, lifted_two))
+    lifted_two = after((normed_three * gains[2]).astype(b16), down_got, up_other)
+    gate_w = both_halves(gate_got, gate_other)
+    up_w = both_halves(up_got, up_other)
 
     def feed(number, chunk, *arrived):
         down_w = both_halves(down_got, after(down_other, *arrived))
@@ -630,12 +638,19 @@
         return partial, grad_gate, grad_upper
 
     grad_down, terms, (grad_gate, grad_upper), partial = pipelined(grad_down, feed_back)
-    output = spread_lanes(after(output, *grad_down))
+    output = spread_lanes(after(output, grad_down[0]))
     down_sum = unit_grad(grad_down, after(hidden, partial[-3]))
     down_kept, down_got = half_sent(down_sum, 0, 1)
+
+    def both_parts(total):
+        kept, sent = picked(is_first, (total[:, 0], total[:, 1]))
+        return kept, sent.astype(b16)
+
     gate_sum = unit_grad(lifted_two, after(grad_gate, partial[-1]))
     up_sum = unit_grad(lifted_two, after(grad_upper, partial[-1]))
-    terms, down_got, gate_sum, up_sum = together(terms, down_got, gate_sum, up_sum)
+    gate_kept, gate_sent = both_parts(gate_sum)
+    up_kept, up_sent = both_parts(up_sum)
+    terms, down_got, gate_sent = together(terms, down_got, gate_sent)
 
     def two_sided(kept, got):
         return (kept + got.astype(f32)).astype(b16)
@@ -651,20 +666,19 @@
 
     down_part = (down_kept + down_got.astype(f32)).astype(b16)
     grad_w_down = exchange(down_part, "dp")
-    gate_kept, gate_got = half_sent(gate_sum, 0, 1)
+    gate_got = swapped(gate_sent, "context", 1)
     grad_middle, grad_branch, grad_gain_two, grad_gain_three = fused(
         middle_back, (), own_cotangent, gains, scale_two, normed_two, scale_three, normed_three, *terms
     )
     grad_branch, grad_w_down, gate_got = together(grad_branch, grad_w_down, gate_got)
     gate_part = (gate_kept + gate_got.astype(f32)).astype(b16)
 
-    low_core = bits()[2]
 
     def row_blocks(left, right):
         return row_grad(left, right).reshape(n, deep, HEAD_SIZE)
 
     grad_w_gate = exchange(gate_part, "dp")
-    up_kept, up_got = half_sent(up_sum, 0, 1)
+    up_got = swapped(after(up_sent, gate_got), "context", 1)
     grad_branch = spread_group(grad_branch)
     out_blocks = row_blocks(grad_branch, mixed)
     grad_query_pre, kept, sent = attend_back(
@@ -674,8 +688,8 @@
     up_got, kept = together(up_got, kept)
     up_part = (up_kept + up_got.astype(f32)).astype(b16)
     grad_w_up = exchange(after(up_part, grad_w_gate), "dp")
-    kept, sent, out_blocks, query_blocks, output = together(
-        kept, sent, after(out_blocks, grad_w_gate), query_blocks, output
+    out_blocks, query_blocks, output = together(
+        after(out_blocks, grad_w_gate), query_blocks, output
     )
     kept = kept.reshape(reach + 1, group, HEAD_SIZE)
     sent = sent.reshape(reach + 1, group, HEAD_SIZE)

time: 755 us -> 739 us (0.979)
  other arithmetic: 70.9 us -> 56.7 us
  starting transfers between devices: 192 us -> 183 us
    all_to_all x6, waiting for transfers between devices: 51.6 us -> 4.45 us  [exchange(): return lax.all_to_all(blocks, axis, 0, 0, tiled=True)]
    ppermute x33, starting transfers between devices: 93.6 us -> 54 us  [rotated(): return lax.ppermute(value, 'dp', [(s, (s + steps) % n) for s in range(n)])]
    ppermute x65, waiting for transfers between devices: 139 us -> 175 us  [swapped(): lax.ppermute(value, axis, [(place, place ^ bit) for place in range(count)])]
    ppermute x6, starting transfers between devices: 13.4 us -> 29.3 us  [shifted(): lax.ppermute(value, axis, [(s, s + steps) for s in range(count) if 0 <= s...]
    ppermute x33, waiting for transfers between devices: 125 us -> 136 us  [rotated(): return lax.ppermute(value, 'dp', [(s, (s + steps) % n) for s in range(n)])]
    ppermute x65, starting transfers between devices: 45.4 us -> 55.8 us  [swapped(): lax.ppermute(value, axis, [(place, place ^ bit) for place in range(count)])]
    convert_element_type x3 -> x1, other arithmetic: 8.53 us -> 0.28 us  [half_sent(): return (kept, swapped(sent.astype(b16), *AXES[step]))]
    unnamed x181 -> x229, local copies, waits for them, and re-layouts: 31.7 us -> 38 us
  transfers between devices with their start and end apart: 110 -> 110, of which waited for: 51 -> 57; matrix products, arithmetic and copies ran while one was open for 15% -> 13% of each run, Pallas kernels for 5% -> 6%
where the time goes in v5:
time: 739 us; the launch traced here: 730 us
  waiting for transfers between devices  332 us (45%)
  starting transfers between devices  183 us (25%)
  other arithmetic  56.7 us (8%)
  local copies, waits for them, and re-layouts  54.9 us (7%)
  matrix products  53.4 us (7%)
  Pallas kernels  47.7 us (6%)
    ppermute x65, waiting for transfers between devices, swapped(): lax.ppermute(value, axis, [(place, place ^ bit) for place in range(count)])  175 us
    ppermute x33, waiting for transfers between devices, rotated(): return lax.ppermute(value, 'dp', [(s, (s + steps) % n) for s in range(n)])  136 us
    ppermute x65, starting transfers between devices, swapped(): lax.ppermute(value, axis, [(place, place ^ bit) for place in range(count)])  55.8 us
    ppermute x33, starting transfers between devices, rotated(): return lax.ppermute(value, 'dp', [(s, (s + steps) % n) for s in range(n)])  54 us
    all_to_all x6, starting transfers between devices, exchange(): return lax.all_to_all(blocks, axis, 0, 0, tiled=True)  43.8 us
    unnamed x229, local copies, waits for them, and re-layouts  38 us
    ppermute x6, starting transfers between devices, shifted(): lax.ppermute(value, axis, [(s, s + steps) for s in range(count) if 0 <= s...  29.3 us
    dot_general x12, matrix products, dot(): return jnp.dot(left, right, preferred_element_type=f32)  19.5 us
  transfers between devices with their start and end apart: 110, of which 57 were waited for; matrix products, arithmetic and copies ran while one was open for 13% of the time, Pallas kernels for 6%

profile of v5, /device:TPU:0, one launch (start us, length us, event | category | flops | bytes accessed | tf_op | source)
XLA Modules:
  0.0 730.5 jit_solution(11614071683847766403)
XLA Ops:
  0.7 2.8 concatenate.104
  4.5 5.1 collective-permute-start
  17.3 18.2 %collective-permute-done.1 = bf16[592,256]{1,0:T(8,128)(2,1)S(1)} collective-permute-done((bf16[592,256]{1,0:T(8,128)(2,1)S(1)}, bf16[592,256]{1,0:T(8,128)(2,1)S(1)}, u32[]{:S(2)}, u32[]{:S(2)}) %collective-permute-start.1) | collective-permute-done | bytes 303136 | tf_op jit(solution)/shard_map/ppermute | solution.py:99
  43.4 5.1 collective-permute-start.10
  51.2 5.0 collective-permute-start.8
  56.1 15.1 %collective-permute-start.9 = (bf16[512,256]{1,0:T(8,128)(2,1)S(1)}, bf16[512,256]{1,0:T(8,128)(2,1)}, u32[]{:S(2)}, u32[]{:S(2)}) collective-permute-start(bf16[512,256]{1,0:T(8,128)(2,1)S(1)} %fusion.65), channel_id=1, source_target_pairs={{0,16},{8,24},{1,17},{9,25},{2,18},{10,26},{3,19},{11,27},{4,20},{... | collective-permute-start | bytes 786440 | tf_op jit(solution)/shard_map/ppermute | solution.py:76
  71.2 3.1 unit_blocks.1
  82.3 17.8 %all-to-all-start = ((bf16[4,288,576]{2,1,0:T(8,128)(2,1)}), bf16[4,288,576]{2,1,0:T(8,128)(2,1)S(1)}, u32[]{:S(2)}, u32[]{:S(2)}) async-start(bf16[4,288,576]{2,1,0:T(8,128)(2,1)} %copy-done.33), calls=%async_computation | async-start | bytes 2949120 | tf_op jit(solution)/shard_map/all_to_all | solution.py:53
  109.6 2.9 collective-permute-start.16
  112.5 2.6 collective-permute-done.12
  115.1 3.7 collective-permute-start.17
  119.9 2.6 broadcast_select_fusion
  122.5 3.9 fusion.95
  127.1 3.5 fusion.93
  130.6 5.2 collective-permute-done.15
  135.9 17.7 %collective-permute-done.16 = bf16[576,256]{1,0:T(8,128)(2,1)S(1)} collective-permute-done((bf16[576,256]{1,0:T(8,128)(2,1)S(1)}, bf16[576,256]{1,0:T(8,128)(2,1)S(1)}, u32[]{:S(2)}, u32[]{:S(2)}) %collective-permute-start.16) | collective-permute-done | bytes 294944 | tf_op jit(solution)/shard_map/ppermute | solution.py:99
  155.5 2.6 convolution_convert_fusion.refs_1_.right_ref
  161.3 8.0 %all-to-all-start.1 = ((bf16[4,288,576]{2,1,0:T(8,128)(2,1)}), bf16[4,288,576]{2,1,0:T(8,128)(2,1)}, u32[]{:S(2)}, u32[]{:S(2)}) async-start(bf16[4,288,576]{2,1,0:T(8,128)(2,1)} %copy-done.32), calls=%async_computation.1 | async-start | bytes 2949120 | tf_op jit(solution)/shard_map/all_to_all | solution.py:53
  172.6 13.9 %collective-permute-done.19.other_ref = bf16[4,288,576]{2,1,0:T(8,128)(2,1)} collective-permute-done((bf16[4,288,576]{2,1,0:T(8,128)(2,1)S(1)}, bf16[4,288,576]{2,1,0:T(8,128)(2,1)}, u32[]{:S(2)}, u32[]{:S(2)}) %collective-permute-start.19) | collective-permute-done | bytes 1327136 | tf_op jit(solution)/shard_map/ppermute | solution.py:63
  189.4 3.7 collective-permute-done.20.refs_3_
  201.3 3.6 all-to-all-done.1.own_ref
  204.9 5.2 all-to-all-start.2
  214.8 28.6 %collective-permute-done.24.other_ref = bf16[4,288,576]{2,1,0:T(8,128)(2,1)S(1)} collective-permute-done((bf16[4,288,576]{2,1,0:T(8,128)(2,1)}, bf16[4,288,576]{2,1,0:T(8,128)(2,1)S(1)}, u32[]{:S(2)}, u32[]{:S(2)}) %collective-permute-start.24) | collective-permute-done | bytes 1327136 | tf_op jit(solution)/shard_map/ppermute | solution.py:63
  246.3 2.5 collective-permute-start.26
  263.1 12.7 %collective-permute-done.36 = bf16[64,2304]{1,0:T(8,128)(2,1)S(1)} collective-permute-done((bf16[64,2304]{1,0:T(8,128)(2,1)S(1)}, bf16[64,2304]{1,0:T(8,128)(2,1)S(1)}, u32[]{:S(2)}, u32[]{:S(2)}) %collective-permute-start.36) | collective-permute-done | bytes 294944 | tf_op jit(solution)/shard_map/ppermute | solution.py:99
  276.4 6.9 collective-permute-done.37
  291.3 2.5 collective-permute-done.42
  295.6 2.7 multiply_convert_fusion.2
  306.9 14.1 %collective-permute-done.33 = bf16[128,2304]{1,0:T(8,128)(2,1)S(1)} collective-permute-done((bf16[128,2304]{1,0:T(8,128)(2,1)S(1)}, bf16[128,2304]{1,0:T(8,128)(2,1)S(1)}, u32[]{:S(2)}, u32[]{:S(2)}) %collective-permute-start.33) | collective-permute-done | bytes 589856 | tf_op jit(solution)/shard_map/ppermute | solution.py:63
  324.2 5.3 collective-permute-done.40
  331.6 6.9 collective-permute-done.35
  338.5 10.5 %collective-permute-done.41 = bf16[64,2304]{1,0:T(8,128)(2,1)S(1)} collective-permute-done((bf16[64,2304]{1,0:T(8,128)(2,1)S(1)}, bf16[64,2304]{1,0:T(8,128)(2,1)S(1)}, u32[]{:S(2)}, u32[]{:S(2)}) %collective-permute-start.41) | collective-permute-done | bytes 294944 | tf_op jit(solution)/shard_map/ppermute | solution.py:99
  349.3 2.5 fusion.44
  353.2 3.8 collective-permute-start.45
  357.0 3.6 collective-permute-done.47
  360.7 4.2 collective-permute-done.44
  371.5 10.2 %collective-permute-done.54 = bf16[64,2304]{1,0:T(8,128)(2,1)S(1)} collective-permute-done((bf16[64,2304]{1,0:T(8,128)(2,1)S(1)}, bf16[64,2304]{1,0:T(8,128)(2,1)S(1)}, u32[]{:S(2)}, u32[]{:S(2)}) %collective-permute-start.54) | collective-permute-done | bytes 294944 | tf_op jit(solution)/shard_map/ppermute | solution.py:99
  387.5 3.0 collective-permute-done.55
  406.3 3.9 fusion.21
  412.4 13.5 %collective-permute-done.51 = bf16[128,2304]{1,0:T(8,128)(2,1)S(1)} collective-permute-done((bf16[128,2304]{1,0:T(8,128)(2,1)S(1)}, bf16[128,2304]{1,0:T(8,128)(2,1)S(1)}, u32[]{:S(2)}, u32[]{:S(2)}) %collective-permute-start.51) | collective-permute-done | bytes 589856 | tf_op jit(solution)/shard_map/ppermute | solution.py:63
  428.8 5.6 collective-permute-done.58
  438.6 3.2 collective-permute-done.61
  442.7 3.9 fusion.27
  448.3 13.2 %collective-permute-done.62 = bf16[4,288,576]{2,1,0:T(8,128)(2,1)S(1)} collective-permute-done((bf16[4,288,576]{2,1,0:T(8,128)(2,1)S(1)}, bf16[4,288,576]{2,1,0:T(8,128)(2,1)S(1)}, u32[]{:S(2)}, u32[]{:S(2)}) %collective-permute-start.62) | collective-permute-done | bytes 1327136 | tf_op jit(solution)/shard_map/ppermute | solution.py:63
  465.2 3.7 all-to-all-start.3
  484.9 8.8 %fusion.33 = f32[2304,576]{1,0:T(8,128)} fusion(bf16[1024,2304]{1,0:T(8,128)(2,1)} %copy-done.83, bf16[256,576]{0,1:T(8,128)(2,1)S(1)} %copy-done.77, bf16[512,576]{0,1:T(8,128)(2,1)S(1)} %copy-done.97, bf16[256,576]{0,1:T(8,128)(2,1)S(1)} %copy-done.75), kind=kOutput, calls=%fused_computation.90 | convolution fusion | flops 2721447936 | bytes 11206656 | tf_op jit(solution)/shard_map/dot_general | solution.py:94
  493.6 8.4 %collective-permute-done.63 = bf16[4,288,576]{2,1,0:T(8,128)(2,1)} collective-permute-done((bf16[4,288,576]{2,1,0:T(8,128)(2,1)}, bf16[4,288,576]{2,1,0:T(8,128)(2,1)}, u32[]{:S(2)}, u32[]{:S(2)}) %collective-permute-start.63) | collective-permute-done | bytes 1327136 | tf_op jit(solution)/shard_map/ppermute | solution.py:63
  506.0 4.7 fusion.9
  510.6 4.2 all-to-all-start.4
  520.0 4.1 fusion.13
  532.6 12.8 %attend_back.1 = (bf16[512,256]{1,0:T(8,128)(2,1)S(1)}, f32[2048,256]{1,0:T(8,128)}, bf16[2048,256]{1,0:T(8,128)(2,1)S(1)}) custom-call(s32[1]{0:T(128)} %bitcast.19.side_ref, bf16[512,2304]{1,0:T(8,128)(2,1)} %bitcast.262, bf16[2304,256]{1,0:T(8,128)(2,1)S(1)} %bitcast.265, bf16[2048,256]{1,0:T(8,128)(2,1)S(1)} %copy-done.19, ...), custom_call_target="tpu_custom_call" | custom-call | tf_op jit(solution)/shard_map/attend_back/pallas_call | solution.py:412
  547.1 9.0 %collective-permute-done.71 = bf16[4,288,576]{2,1,0:T(8,128)(2,1)} collective-permute-done((bf16[4,288,576]{2,1,0:T(8,128)(2,1)}, bf16[4,288,576]{2,1,0:T(8,128)(2,1)}, u32[]{:S(2)}, u32[]{:S(2)}) %collective-permute-start.71) | collective-permute-done | bytes 1327136 | tf_op jit(solution)/shard_map/ppermute | solution.py:63
  556.1 3.1 fusion.8
  560.4 4.8 all-to-all-start.5
  588.0 4.7 collective-permute-done.73.refs_1_
  598.4 2.5 collective-permute-done.79
  606.0 21.8 %collective-permute-done.80 = bf16[576,256]{1,0:T(8,128)(2,1)} collective-permute-done((bf16[576,256]{1,0:T(8,128)(2,1)}, bf16[576,256]{1,0:T(8,128)(2,1)}, u32[]{:S(2)}, u32[]{:S(2)}) %collective-permute-start.80) | collective-permute-done | bytes 294944 | tf_op jit(solution)/shard_map/ppermute | solution.py:99
  630.0 14.3 %collective-permute-done.76.refs_5_ = bf16[512,256]{1,0:T(8,128)(2,1)} collective-permute-done((bf16[512,256]{1,0:T(8,128)(2,1)}, bf16[512,256]{1,0:T(8,128)(2,1)}, u32[]{:S(2)}, u32[]{:S(2)}) %collective-permute-start.76) | collective-permute-done | bytes 262176 | tf_op jit(solution)/shard_map/ppermute | solution.py:76
  655.9 3.2 side_by_side.4
  662.3 9.5 %collective-permute-done.83.refs_3_ = bf16[2,64,1152]{2,1,0:T(8,128)(2,1)S(1)} collective-permute-done((bf16[2,64,1152]{2,1,0:T(8,128)(2,1)S(1)}, bf16[2,64,1152]{2,1,0:T(8,128)(2,1)S(1)}, u32[]{:S(2)}, u32[]{:S(2)}) %collective-permute-start.83) | collective-permute-done | bytes 294944 | tf_op jit(solution)/shard_map/ppermute | solution.py:63
  685.4 8.0 %collective-permute-done.95 = bf16[576,256]{1,0:T(8,128)(2,1)S(1)} collective-permute-done((bf16[576,256]{1,0:T(8,128)(2,1)S(1)}, bf16[576,256]{1,0:T(8,128)(2,1)S(1)}, u32[]{:S(2)}, u32[]{:S(2)}) %collective-permute-start.95) | collective-permute-done | bytes 294944 | tf_op jit(solution)/shard_map/ppermute | solution.py:99
  694.4 2.9 collective-permute-done.98
  698.5 10.1 %collective-permute-done.90 = bf16[576,256]{1,0:T(8,128)(2,1)S(1)} collective-permute-done((bf16[576,256]{1,0:T(8,128)(2,1)S(1)}, bf16[576,256]{1,0:T(8,128)(2,1)S(1)}, u32[]{:S(2)}, u32[]{:S(2)}) %collective-permute-start.90) | collective-permute-done | bytes 294944 | tf_op jit(solution)/shard_map/ppermute | solution.py:99
  713.5 5.5 collective-permute-start.101
  (589 shorter events, 266.8 us)
Async XLA Ops:
  4.5 12.7 %collective-permute-start = (bf16[592,256]{1,0:T(8,128)(2,1)S(1)}, bf16[592,256]{1,0:T(8,128)(2,1)S(1)}, u32[]{:S(2)}, u32[]{:S(2)}) collective-permute-start(bf16[592,256]{1,0:T(8,128)(2,1)S(1)} %pad_maximum_fusion.25), channel_id=1, source_target_pairs={{0,24},{8,0},{16,8},{24,16},{1,25},{9,1},{17,9},{25,17},{2,26},{10... | collective-permute-start | bytes 909320 | tf_op jit(solution)/shard_map/ppermute | solution.py:99
  9.6 25.8 %collective-permute-start.1 = (bf16[592,256]{1,0:T(8,128)(2,1)S(1)}, bf16[592,256]{1,0:T(8,128)(2,1)S(1)}, u32[]{:S(2)}, u32[]{:S(2)}) collective-permute-start(bf16[592,256]{1,0:T(8,128)(2,1)S(1)} %pad_maximum_fusion.25), channel_id=1, source_target_pairs={{0,16},{8,24},{16,0},{24,8},{1,17},{9,25},{17,1},{25,9},{2,18},{10... | collective-permute-start | bytes 909320 | tf_op jit(solution)/shard_map/ppermute | solution.py:99
  9.6 25.8 %collective-permute-start.2 = (bf16[592,256]{1,0:T(8,128)(2,1)S(1)}, bf16[592,256]{1,0:T(8,128)(2,1)S(1)}, u32[]{:S(2)}, u32[]{:S(2)}) collective-permute-start(bf16[592,256]{1,0:T(8,128)(2,1)S(1)} %pad_maximum_fusion.25), channel_id=1, source_target_pairs={{0,8},{8,16},{16,24},{24,0},{1,9},{9,17},{17,25},{25,1},{2,10},{10... | collective-permute-start | bytes 909320 | tf_op jit(solution)/shard_map/ppermute | solution.py:99
  10.6 27.2 %collective-permute-start.4 = (bf16[256,2304]{1,0:T(8,128)(2,1)}, bf16[256,2304]{1,0:T(8,128)(2,1)}, u32[]{:S(2)}, u32[]{:S(2)}) collective-permute-start(bf16[256,2304]{1,0:T(8,128)(2,1)} %param.14), channel_id=1, source_target_pairs={{0,4},{4,0},{1,5},{5,1},{2,6},{6,2},{3,7},{7,3},{8,12},{12,8},{9,1... | collective-permute-start | bytes 3538952 | tf_op jit(solution)/shard_map/ppermute | solution.py:63
  12.8 35.6 %collective-permute-start.3 = (bf16[1,256]{1,0:T(2,128)(2,1)S(1)}, bf16[1,256]{1,0:T(2,128)(2,1)S(1)}, u32[]{:S(2)}, u32[]{:S(2)}) collective-permute-start(bf16[1,256]{1,0:T(2,128)(2,1)S(1)} %convert_element_type.307), channel_id=1, source_target_pairs={{0,4},{4,0},{1,5},{5,1},{2,6},{6,2},{3,7},{7,3},{8,12},{12,8},{9,1... | collective-permute-start | bytes 1544 | tf_op jit(solution)/shard_map/ppermute | solution.py:63
  43.4 12.7 %collective-permute-start.10 = (bf16[512,256]{1,0:T(8,128)(2,1)S(1)}, bf16[512,256]{1,0:T(8,128)(2,1)}, u32[]{:S(2)}, u32[]{:S(2)}) collective-permute-start(bf16[512,256]{1,0:T(8,128)(2,1)S(1)} %fusion.65), channel_id=1, source_target_pairs={{0,8},{8,16},{16,24},{1,9},{9,17},{17,25},{2,10},{10,18},{18,26},{... | collective-permute-start | bytes 786440 | tf_op jit(solution)/shard_map/ppermute | solution.py:76
  48.6 53.1 %collective-permute-start.5 = (bf16[592,256]{1,0:T(8,128)(2,1)S(1)}, bf16[592,256]{1,0:T(8,128)(2,1)S(1)}, u32[]{:S(2)}, u32[]{:S(2)}) collective-permute-start(bf16[592,256]{1,0:T(8,128)(2,1)S(1)} %pad_maximum_fusion.26), channel_id=1, source_target_pairs={{0,24},{8,0},{16,8},{24,16},{1,25},{9,1},{17,9},{25,17},{2,26},{10... | collective-permute-start | bytes 909320 | tf_op jit(solution)/shard_map/ppermute | solution.py:99
  48.6 53.5 %collective-permute-start.6 = (bf16[592,256]{1,0:T(8,128)(2,1)S(1)}, bf16[592,256]{1,0:T(8,128)(2,1)S(1)}, u32[]{:S(2)}, u32[]{:S(2)}) collective-permute-start(bf16[592,256]{1,0:T(8,128)(2,1)S(1)} %pad_maximum_fusion.26), channel_id=1, source_target_pairs={{0,16},{8,24},{16,0},{24,8},{1,17},{9,25},{17,1},{25,9},{2,18},{10... | collective-permute-start | bytes 909320 | tf_op jit(solution)/shard_map/ppermute | solution.py:99
  49.7 54.0 %collective-permute-start.7 = (bf16[592,256]{1,0:T(8,128)(2,1)S(1)}, bf16[592,256]{1,0:T(8,128)(2,1)S(1)}, u32[]{:S(2)}, u32[]{:S(2)}) collective-permute-start(bf16[592,256]{1,0:T(8,128)(2,1)S(1)} %pad_maximum_fusion.26), channel_id=1, source_target_pairs={{0,8},{8,16},{16,24},{24,0},{1,9},{9,17},{17,25},{25,1},{2,10},{10... | collective-permute-start | bytes 909320 | tf_op jit(solution)/shard_map/ppermute | solution.py:99
  51.2 28.4 %collective-permute-start.8 = (bf16[512,256]{1,0:T(8,128)(2,1)S(1)}, bf16[512,256]{1,0:T(8,128)(2,1)}, u32[]{:S(2)}, u32[]{:S(2)}) collective-permute-start(bf16[512,256]{1,0:T(8,128)(2,1)S(1)} %fusion.65), channel_id=1, source_target_pairs={{0,24},{1,25},{2,26},{3,27},{4,28},{5,29},{6,30},{7,31}} | collective-permute-start | bytes 786440 | tf_op jit(solution)/shard_map/ppermute | solution.py:76
  56.1 26.2 %collective-permute-start.9 = (bf16[512,256]{1,0:T(8,128)(2,1)S(1)}, bf16[512,256]{1,0:T(8,128)(2,1)}, u32[]{:S(2)}, u32[]{:S(2)}) collective-permute-start(bf16[512,256]{1,0:T(8,128)(2,1)S(1)} %fusion.65), channel_id=1, source_target_pairs={{0,16},{8,24},{1,17},{9,25},{2,18},{10,26},{3,19},{11,27},{4,20},{... | collective-permute-start | bytes 786440 | tf_op jit(solution)/shard_map/ppermute | solution.py:76
  79.5 39.4 %collective-permute-start.14 = (bf16[512,256]{1,0:T(8,128)(2,1)S(1)}, bf16[512,256]{1,0:T(8,128)(2,1)}, u32[]{:S(2)}, u32[]{:S(2)}) collective-permute-start(bf16[512,256]{1,0:T(8,128)(2,1)S(1)} %fusion.65), channel_id=1, source_target_pairs={{0,4},{4,0},{1,5},{5,1},{2,6},{6,2},{3,7},{7,3},{8,12},{12,8},{9,1... | collective-permute-start | bytes 786440 | tf_op jit(solution)/shard_map/ppermute | solution.py:63
  82.3 71.6 %all-to-all-start = ((bf16[4,288,576]{2,1,0:T(8,128)(2,1)}), bf16[4,288,576]{2,1,0:T(8,128)(2,1)S(1)}, u32[]{:S(2)}, u32[]{:S(2)}) async-start(bf16[4,288,576]{2,1,0:T(8,128)(2,1)} %copy-done.33), calls=%async_computation | async-start | bytes 2949120 | tf_op jit(solution)/shard_map/all_to_all | solution.py:53
  101.6 13.5 %collective-permute-start.12 = (bf16[512,256]{1,0:T(8,128)(2,1)}, bf16[512,256]{1,0:T(8,128)(2,1)S(1)}, u32[]{:S(2)}, u32[]{:S(2)}) collective-permute-start(bf16[512,256]{1,0:T(8,128)(2,1)} %collective-permute-done.9), channel_id=1, source_target_pairs={{0,4},{4,0},{1,5},{5,1},{2,6},{6,2},{3,7},{7,3},{8,12},{12,8},{9,1... | collective-permute-start | bytes 786440 | tf_op jit(solution)/shard_map/ppermute | solution.py:63
  102.2 16.7 %collective-permute-start.13 = (bf16[512,256]{1,0:T(8,128)(2,1)}, bf16[512,256]{1,0:T(8,128)(2,1)S(1)}, u32[]{:S(2)}, u32[]{:S(2)}) collective-permute-start(bf16[512,256]{1,0:T(8,128)(2,1)} %collective-permute-done.10), channel_id=1, source_target_pairs={{0,4},{4,0},{1,5},{5,1},{2,6},{6,2},{3,7},{7,3},{8,12},{12,8},{9,1... | collective-permute-start | bytes 786440 | tf_op jit(solution)/shard_map/ppermute | solution.py:63
  103.9 32.0 %collective-permute-start.15 = (bf16[576,256]{1,0:T(8,128)(2,1)S(1)}, bf16[576,256]{1,0:T(8,128)(2,1)S(1)}, u32[]{:S(2)}, u32[]{:S(2)}) collective-permute-start(bf16[576,256]{1,0:T(8,128)(2,1)S(1)} %slice_select_fusion), channel_id=1, source_target_pairs={{0,8},{8,16},{16,24},{24,0},{1,9},{9,17},{17,25},{25,1},{2,10},{10... | collective-permute-start | bytes 884744 | tf_op jit(solution)/shard_map/ppermute | solution.py:99
  109.6 44.0 %collective-permute-start.16 = (bf16[576,256]{1,0:T(8,128)(2,1)S(1)}, bf16[576,256]{1,0:T(8,128)(2,1)S(1)}, u32[]{:S(2)}, u32[]{:S(2)}) collective-permute-start(bf16[576,256]{1,0:T(8,128)(2,1)S(1)} %slice_select_fusion), channel_id=1, source_target_pairs={{0,16},{8,24},{16,0},{24,8},{1,17},{9,25},{17,1},{25,9},{2,18},{10... | collective-permute-start | bytes 884744 | tf_op jit(solution)/shard_map/ppermute | solution.py:99
  115.1 38.5 %collective-permute-start.17 = (bf16[576,256]{1,0:T(8,128)(2,1)S(1)}, bf16[576,256]{1,0:T(8,128)(2,1)S(1)}, u32[]{:S(2)}, u32[]{:S(2)}) collective-permute-start(bf16[576,256]{1,0:T(8,128)(2,1)S(1)} %slice_select_fusion), channel_id=1, source_target_pairs={{0,24},{8,0},{16,8},{24,16},{1,25},{9,1},{17,9},{25,17},{2,26},{10... | collective-permute-start | bytes 884744 | tf_op jit(solution)/shard_map/ppermute | solution.py:99
  153.9 32.5 %collective-permute-start.19 = (bf16[4,288,576]{2,1,0:T(8,128)(2,1)S(1)}, bf16[4,288,576]{2,1,0:T(8,128)(2,1)}, u32[]{:S(2)}, u32[]{:S(2)}) collective-permute-start(bf16[4,288,576]{2,1,0:T(8,128)(2,1)S(1)} %all-to-all-done.own_ref), channel_id=1, source_target_pairs={{0,4},{4,0},{1,5},{5,1},{2,6},{6,2},{3,7},{7,3},{8,12},{12,8},{9,1... | collective-permute-start | bytes 3981320 | tf_op jit(solution)/shard_map/ppermute | solution.py:63
  161.3 43.6 %all-to-all-start.1 = ((bf16[4,288,576]{2,1,0:T(8,128)(2,1)}), bf16[4,288,576]{2,1,0:T(8,128)(2,1)}, u32[]{:S(2)}, u32[]{:S(2)}) async-start(bf16[4,288,576]{2,1,0:T(8,128)(2,1)} %copy-done.32), calls=%async_computation.1 | async-start | bytes 2949120 | tf_op jit(solution)/shard_map/all_to_all | solution.py:53
  204.9 39.6 %all-to-all-start.2 = ((bf16[4,288,576]{2,1,0:T(8,128)(2,1)}), bf16[4,288,576]{2,1,0:T(8,128)(2,1)S(1)}, u32[]{:S(2)}, u32[]{:S(2)}) async-start(bf16[4,288,576]{2,1,0:T(8,128)(2,1)} %copy-done.31), calls=%async_computation.2 | async-start | bytes 2949120 | tf_op jit(solution)/shard_map/all_to_all | solution.py:53
  211.1 32.3 %collective-permute-start.24 = (bf16[4,288,576]{2,1,0:T(8,128)(2,1)}, bf16[4,288,576]{2,1,0:T(8,128)(2,1)S(1)}, u32[]{:S(2)}, u32[]{:S(2)}) collective-permute-start(bf16[4,288,576]{2,1,0:T(8,128)(2,1)} %all-to-all-done.1.own_ref), channel_id=1, source_target_pairs={{0,4},{4,0},{1,5},{5,1},{2,6},{6,2},{3,7},{7,3},{8,12},{12,8},{9,1... | collective-permute-start | bytes 3981320 | tf_op jit(solution)/shard_map/ppermute | solution.py:63
  244.5 12.6 %collective-permute-start.25 = (bf16[64,2304]{1,0:T(8,128)(2,1)}, bf16[64,2304]{1,0:T(8,128)(2,1)}, u32[]{:S(2)}, u32[]{:S(2)}) collective-permute-start(bf16[64,2304]{1,0:T(8,128)(2,1)} %get-tuple-element.148), channel_id=1, source_target_pairs={{0,8},{8,16},{16,24},{24,0},{1,9},{9,17},{17,25},{25,1},{2,10},{10... | collective-permute-start | bytes 884744 | tf_op jit(solution)/shard_map/ppermute | solution.py:99
  246.3 12.3 %collective-permute-start.26 = (bf16[64,2304]{1,0:T(8,128)(2,1)}, bf16[64,2304]{1,0:T(8,128)(2,1)}, u32[]{:S(2)}, u32[]{:S(2)}) collective-permute-start(bf16[64,2304]{1,0:T(8,128)(2,1)} %get-tuple-element.148), channel_id=1, source_target_pairs={{0,24},{8,0},{16,8},{24,16},{1,25},{9,1},{17,9},{25,17},{2,26},{10... | collective-permute-start | bytes 884744 | tf_op jit(solution)/shard_map/ppermute | solution.py:99
  256.6 31.1 %collective-permute-start.30 = (bf16[4,288,576]{2,1,0:T(8,128)(2,1)S(1)}, bf16[4,288,576]{2,1,0:T(8,128)(2,1)S(1)}, u32[]{:S(2)}, u32[]{:S(2)}) collective-permute-start(bf16[4,288,576]{2,1,0:T(8,128)(2,1)S(1)} %all-to-all-done.2.own_ref), channel_id=1, source_target_pairs={{0,4},{4,0},{1,5},{5,1},{2,6},{6,2},{3,7},{7,3},{8,12},{12,8},{9,1... | collective-permute-start | bytes 3981320 | tf_op jit(solution)/shard_map/ppermute | solution.py:63
  259.7 25.0 %collective-permute-start.27 = (bf16[128,2304]{1,0:T(8,128)(2,1)S(1)}, bf16[128,2304]{1,0:T(8,128)(2,1)S(1)}, u32[]{:S(2)}, u32[]{:S(2)}) collective-permute-start(bf16[128,2304]{1,0:T(8,128)(2,1)S(1)} %pad_maximum_fusion.18), channel_id=1, source_target_pairs={{0,2},{1,3},{2,0},{3,1},{4,6},{5,7},{6,4},{7,5},{8,10},{9,11},{10,... | collective-permute-start | bytes 1769480 | tf_op jit(solution)/shard_map/ppermute | solution.py:63
  261.2 14.6 %collective-permute-start.36 = (bf16[64,2304]{1,0:T(8,128)(2,1)S(1)}, bf16[64,2304]{1,0:T(8,128)(2,1)S(1)}, u32[]{:S(2)}, u32[]{:S(2)}) collective-permute-start(bf16[64,2304]{1,0:T(8,128)(2,1)S(1)} %copy-done.71), channel_id=1, source_target_pairs={{0,16},{8,24},{16,0},{24,8},{1,17},{9,25},{17,1},{25,9},{2,18},{10... | collective-permute-start | bytes 884744 | tf_op jit(solution)/shard_map/ppermute | solution.py:99
  263.0 20.3 %collective-permute-start.29 = (bf16[128,2304]{1,0:T(8,128)(2,1)S(1)}, bf16[128,2304]{1,0:T(8,128)(2,1)S(1)}, u32[]{:S(2)}, u32[]{:S(2)}) collective-permute-start(bf16[128,2304]{1,0:T(8,128)(2,1)S(1)} %pad_maximum_fusion.19), channel_id=1, source_target_pairs={{0,1},{1,0},{2,3},{3,2},{4,5},{5,4},{6,7},{7,6},{8,9},{9,8},{10,11... | collective-permute-start | bytes 1769480 | tf_op jit(solution)/shard_map/ppermute | solution.py:63
  305.5 15.4 %collective-permute-start.33 = (bf16[128,2304]{1,0:T(8,128)(2,1)S(1)}, bf16[128,2304]{1,0:T(8,128)(2,1)S(1)}, u32[]{:S(2)}, u32[]{:S(2)}) collective-permute-start(bf16[128,2304]{1,0:T(8,128)(2,1)S(1)} %slice.515), channel_id=1, source_target_pairs={{0,2},{1,3},{2,0},{3,1},{4,6},{5,7},{6,4},{7,5},{8,10},{9,11},{10,... | collective-permute-start | bytes 1769480 | tf_op jit(solution)/shard_map/ppermute | solution.py:63
  324.1 14.3 %collective-permute-start.35 = (bf16[64,2304]{1,0:T(8,128)(2,1)S(1)}, bf16[64,2304]{1,0:T(8,128)(2,1)S(1)}, u32[]{:S(2)}, u32[]{:S(2)}) collective-permute-start(bf16[64,2304]{1,0:T(8,128)(2,1)S(1)} %get-tuple-element.302), channel_id=1, source_target_pairs={{0,8},{8,16},{16,24},{24,0},{1,9},{9,17},{17,25},{25,1},{2,10},{10... | collective-permute-start | bytes 884744 | tf_op jit(solution)/shard_map/ppermute | solution.py:99
  329.5 19.5 %collective-permute-start.41 = (bf16[64,2304]{1,0:T(8,128)(2,1)S(1)}, bf16[64,2304]{1,0:T(8,128)(2,1)S(1)}, u32[]{:S(2)}, u32[]{:S(2)}) collective-permute-start(bf16[64,2304]{1,0:T(8,128)(2,1)S(1)} %convert_add_fusion.5), channel_id=1, source_target_pairs={{0,16},{8,24},{16,0},{24,8},{1,17},{9,25},{17,1},{25,9},{2,18},{10... | collective-permute-start | bytes 884744 | tf_op jit(solution)/shard_map/ppermute | solution.py:99
  353.2 14.1 %collective-permute-start.45 = (bf16[64,2304]{1,0:T(8,128)(2,1)S(1)}, bf16[64,2304]{1,0:T(8,128)(2,1)S(1)}, u32[]{:S(2)}, u32[]{:S(2)}) collective-permute-start(bf16[64,2304]{1,0:T(8,128)(2,1)S(1)} %fusion.43), channel_id=1, source_target_pairs={{0,24},{8,0},{16,8},{24,16},{1,25},{9,1},{17,9},{25,17},{2,26},{10... | collective-permute-start | bytes 884744 | tf_op jit(solution)/shard_map/ppermute | solution.py:99
  360.7 22.6 %collective-permute-start.48 = (bf16[128,2304]{1,0:T(8,128)(2,1)S(1)}, bf16[128,2304]{1,0:T(8,128)(2,1)S(1)}, u32[]{:S(2)}, u32[]{:S(2)}) collective-permute-start(bf16[128,2304]{1,0:T(8,128)(2,1)S(1)} %pad_maximum_fusion.22), channel_id=1, source_target_pairs={{0,1},{1,0},{2,3},{3,2},{4,5},{5,4},{6,7},{7,6},{8,9},{9,8},{10,11... | collective-permute-start | bytes 1769480 | tf_op jit(solution)/shard_map/ppermute | solution.py:63
  367.4 14.3 %collective-permute-start.54 = (bf16[64,2304]{1,0:T(8,128)(2,1)S(1)}, bf16[64,2304]{1,0:T(8,128)(2,1)S(1)}, u32[]{:S(2)}, u32[]{:S(2)}) collective-permute-start(bf16[64,2304]{1,0:T(8,128)(2,1)S(1)} %fusion.43), channel_id=1, source_target_pairs={{0,16},{8,24},{16,0},{24,8},{1,17},{9,25},{17,1},{25,9},{2,18},{10... | collective-permute-start | bytes 884744 | tf_op jit(solution)/shard_map/ppermute | solution.py:99
  369.8 20.8 %collective-permute-start.46 = (bf16[128,2304]{1,0:T(8,128)(2,1)S(1)}, bf16[128,2304]{1,0:T(8,128)(2,1)S(1)}, u32[]{:S(2)}, u32[]{:S(2)}) collective-permute-start(bf16[128,2304]{1,0:T(8,128)(2,1)S(1)} %pad_maximum_fusion.21), channel_id=1, source_target_pairs={{0,2},{1,3},{2,0},{3,1},{4,6},{5,7},{6,4},{7,5},{8,10},{9,11},{10,... | collective-permute-start | bytes 1769480 | tf_op jit(solution)/shard_map/ppermute | solution.py:63
  410.5 15.4 %collective-permute-start.51 = (bf16[128,2304]{1,0:T(8,128)(2,1)S(1)}, bf16[128,2304]{1,0:T(8,128)(2,1)S(1)}, u32[]{:S(2)}, u32[]{:S(2)}) collective-permute-start(bf16[128,2304]{1,0:T(8,128)(2,1)S(1)} %slice.512), channel_id=1, source_target_pairs={{0,2},{1,3},{2,0},{3,1},{4,6},{5,7},{6,4},{7,5},{8,10},{9,11},{10,... | collective-permute-start | bytes 1769480 | tf_op jit(solution)/shard_map/ppermute | solution.py:63
  428.2 33.3 %collective-permute-start.62 = (bf16[4,288,576]{2,1,0:T(8,128)(2,1)S(1)}, bf16[4,288,576]{2,1,0:T(8,128)(2,1)S(1)}, u32[]{:S(2)}, u32[]{:S(2)}) collective-permute-start(bf16[4,288,576]{2,1,0:T(8,128)(2,1)S(1)} %fusion.11), channel_id=1, source_target_pairs={{0,4},{4,0},{1,5},{5,1},{2,6},{6,2},{3,7},{7,3},{8,12},{12,8},{9,1... | collective-permute-start | bytes 3981320 | tf_op jit(solution)/shard_map/ppermute | solution.py:63
  436.4 25.2 %collective-permute-start.52 = (bf16[64,2304]{1,0:T(8,128)(2,1)S(1)}, bf16[64,2304]{1,0:T(8,128)(2,1)S(1)}, u32[]{:S(2)}, u32[]{:S(2)}) collective-permute-start(bf16[64,2304]{1,0:T(8,128)(2,1)S(1)} %get-tuple-element.300), channel_id=1, source_target_pairs={{0,24},{8,0},{16,8},{24,16},{1,25},{9,1},{17,9},{25,17},{2,26},{10... | collective-permute-start | bytes 884744 | tf_op jit(solution)/shard_map/ppermute | solution.py:99
  437.8 24.4 %collective-permute-start.53 = (bf16[64,2304]{1,0:T(8,128)(2,1)S(1)}, bf16[64,2304]{1,0:T(8,128)(2,1)S(1)}, u32[]{:S(2)}, u32[]{:S(2)}) collective-permute-start(bf16[64,2304]{1,0:T(8,128)(2,1)S(1)} %get-tuple-element.299), channel_id=1, source_target_pairs={{0,8},{8,16},{16,24},{24,0},{1,9},{9,17},{17,25},{25,1},{2,10},{10... | collective-permute-start | bytes 884744 | tf_op jit(solution)/shard_map/ppermute | solution.py:99
  438.6 24.4 %collective-permute-start.59 = (bf16[64,2304]{1,0:T(8,128)(2,1)S(1)}, bf16[64,2304]{1,0:T(8,128)(2,1)S(1)}, u32[]{:S(2)}, u32[]{:S(2)}) collective-permute-start(bf16[64,2304]{1,0:T(8,128)(2,1)S(1)} %convert_add_fusion.4), channel_id=1, source_target_pairs={{0,16},{8,24},{16,0},{24,8},{1,17},{9,25},{17,1},{25,9},{2,18},{10... | collective-permute-start | bytes 884744 | tf_op jit(solution)/shard_map/ppermute | solution.py:99
  465.2 37.6 %all-to-all-start.3 = ((bf16[4,288,576]{2,1,0:T(8,128)(2,1)}), bf16[4,288,576]{2,1,0:T(8,128)(2,1)S(1)}, u32[]{:S(2)}, u32[]{:S(2)}) async-start(bf16[4,288,576]{2,1,0:T(8,128)(2,1)} %fusion.10), calls=%async_computation.3 | async-start | bytes 2949120 | tf_op jit(solution)/shard_map/all_to_all | solution.py:53
  468.9 33.1 %collective-permute-start.63 = (bf16[4,288,576]{2,1,0:T(8,128)(2,1)}, bf16[4,288,576]{2,1,0:T(8,128)(2,1)}, u32[]{:S(2)}, u32[]{:S(2)}) collective-permute-start(bf16[4,288,576]{2,1,0:T(8,128)(2,1)} %fusion.12), channel_id=1, source_target_pairs={{0,4},{4,0},{1,5},{5,1},{2,6},{6,2},{3,7},{7,3},{8,12},{12,8},{9,1... | collective-permute-start | bytes 3981320 | tf_op jit(solution)/shard_map/ppermute | solution.py:63
  510.6 48.6 %all-to-all-start.4 = ((bf16[4,288,576]{2,1,0:T(8,128)(2,1)}), bf16[4,288,576]{2,1,0:T(8,128)(2,1)S(1)}, u32[]{:S(2)}, u32[]{:S(2)}) async-start(bf16[4,288,576]{2,1,0:T(8,128)(2,1)} %fusion.9), calls=%async_computation.4 | async-start | bytes 2949120 | tf_op jit(solution)/shard_map/all_to_all | solution.py:53
  524.2 32.0 %collective-permute-start.71 = (bf16[4,288,576]{2,1,0:T(8,128)(2,1)}, bf16[4,288,576]{2,1,0:T(8,128)(2,1)}, u32[]{:S(2)}, u32[]{:S(2)}) collective-permute-start(bf16[4,288,576]{2,1,0:T(8,128)(2,1)} %fusion.13), channel_id=1, source_target_pairs={{0,4},{4,0},{1,5},{5,1},{2,6},{6,2},{3,7},{7,3},{8,12},{12,8},{9,1... | collective-permute-start | bytes 3981320 | tf_op jit(solution)/shard_map/ppermute | solution.py:63
  526.2 40.9 %collective-permute-start.69 = (bf16[64,2304]{1,0:T(8,128)(2,1)}, bf16[64,2304]{1,0:T(8,128)(2,1)}, u32[]{:S(2)}, u32[]{:S(2)}) collective-permute-start(bf16[64,2304]{1,0:T(8,128)(2,1)} %get-tuple-element.177.own_ref), channel_id=1, source_target_pairs={{0,2},{1,3},{2,0},{3,1},{4,6},{5,7},{6,4},{7,5},{8,10},{9,11},{10,... | collective-permute-start | bytes 884744 | tf_op jit(solution)/shard_map/ppermute | solution.py:63
  560.4 84.0 %all-to-all-start.5 = ((bf16[4,288,576]{2,1,0:T(8,128)(2,1)}), bf16[4,288,576]{2,1,0:T(8,128)(2,1)}, u32[]{:S(2)}, u32[]{:S(2)}) async-start(bf16[4,288,576]{2,1,0:T(8,128)(2,1)} %fusion.8), calls=%async_computation.5 | async-start | bytes 2949120 | tf_op jit(solution)/shard_map/all_to_all | solution.py:53
  568.3 15.2 %collective-permute-start.77 = (bf16[512,256]{1,0:T(8,128)(2,1)S(1)}, bf16[512,256]{1,0:T(8,128)(2,1)S(1)}, u32[]{:S(2)}, u32[]{:S(2)}) collective-permute-start(bf16[512,256]{1,0:T(8,128)(2,1)S(1)} %get-tuple-element.288), channel_id=1, source_target_pairs={{0,4},{4,0},{1,5},{5,1},{2,6},{6,2},{3,7},{7,3},{8,12},{12,8},{9,1... | collective-permute-start | bytes 786440 | tf_op jit(solution)/shard_map/ppermute | solution.py:63
  568.8 15.2 %collective-permute-start.75 = (bf16[512,256]{1,0:T(8,128)(2,1)S(1)}, bf16[512,256]{1,0:T(8,128)(2,1)S(1)}, u32[]{:S(2)}, u32[]{:S(2)}) collective-permute-start(bf16[512,256]{1,0:T(8,128)(2,1)S(1)} %get-tuple-element.289), channel_id=1, source_target_pairs={{0,4},{4,0},{1,5},{5,1},{2,6},{6,2},{3,7},{7,3},{8,12},{12,8},{9,1... | collective-permute-start | bytes 786440 | tf_op jit(solution)/shard_map/ppermute | solution.py:63
  577.7 23.2 %collective-permute-start.79 = (bf16[576,256]{1,0:T(8,128)(2,1)S(1)}, bf16[576,256]{1,0:T(8,128)(2,1)S(1)}, u32[]{:S(2)}, u32[]{:S(2)}) collective-permute-start(bf16[576,256]{1,0:T(8,128)(2,1)S(1)} %get-tuple-element.279), channel_id=1, source_target_pairs={{0,8},{8,16},{16,24},{24,0},{1,9},{9,17},{17,25},{25,1},{2,10},{10... | collective-permute-start | bytes 884744 | tf_op jit(solution)/shard_map/ppermute | solution.py:99
  579.7 48.2 %collective-permute-start.80 = (bf16[576,256]{1,0:T(8,128)(2,1)}, bf16[576,256]{1,0:T(8,128)(2,1)}, u32[]{:S(2)}, u32[]{:S(2)}) collective-permute-start(bf16[576,256]{1,0:T(8,128)(2,1)} %get-tuple-element.278), channel_id=1, source_target_pairs={{0,16},{8,24},{16,0},{24,8},{1,17},{9,25},{17,1},{25,9},{2,18},{10... | collective-permute-start | bytes 884744 | tf_op jit(solution)/shard_map/ppermute | solution.py:99
  582.0 45.8 %collective-permute-start.81 = (bf16[576,256]{1,0:T(8,128)(2,1)}, bf16[576,256]{1,0:T(8,128)(2,1)}, u32[]{:S(2)}, u32[]{:S(2)}) collective-permute-start(bf16[576,256]{1,0:T(8,128)(2,1)} %get-tuple-element.277), channel_id=1, source_target_pairs={{0,24},{8,0},{16,8},{24,16},{1,25},{9,1},{17,9},{25,17},{2,26},{10... | collective-permute-start | bytes 884744 | tf_op jit(solution)/shard_map/ppermute | solution.py:99
  584.0 12.4 %collective-permute-start.72 = (bf16[512,256]{1,0:T(8,128)(2,1)S(1)}, bf16[512,256]{1,0:T(8,128)(2,1)S(1)}, u32[]{:S(2)}, u32[]{:S(2)}) collective-permute-start(bf16[512,256]{1,0:T(8,128)(2,1)S(1)} %get-tuple-element.291), channel_id=1, source_target_pairs={{0,4},{4,0},{1,5},{5,1},{2,6},{6,2},{3,7},{7,3},{8,12},{12,8},{9,1... | collective-permute-start | bytes 786440 | tf_op jit(solution)/shard_map/ppermute | solution.py:63
  592.8 37.3 %collective-permute-start.78 = (bf16[512,256]{1,0:T(8,128)(2,1)}, bf16[512,256]{1,0:T(8,128)(2,1)}, u32[]{:S(2)}, u32[]{:S(2)}) collective-permute-start(bf16[512,256]{1,0:T(8,128)(2,1)} %fused_two_sided.5), channel_id=1, source_target_pairs={{8,0},{16,8},{24,16},{9,1},{17,9},{25,17},{10,2},{18,10},{26,18},{... | collective-permute-start | bytes 786440 | tf_op jit(solution)/shard_map/ppermute | solution.py:76
  597.1 47.2 %collective-permute-start.76 = (bf16[512,256]{1,0:T(8,128)(2,1)}, bf16[512,256]{1,0:T(8,128)(2,1)}, u32[]{:S(2)}, u32[]{:S(2)}) collective-permute-start(bf16[512,256]{1,0:T(8,128)(2,1)} %fused_two_sided.4), channel_id=1, source_target_pairs={{16,0},{24,8},{17,1},{25,9},{18,2},{26,10},{19,3},{27,11},{20,4},{... | collective-permute-start | bytes 786440 | tf_op jit(solution)/shard_map/ppermute | solution.py:76
  601.6 42.7 %collective-permute-start.74 = (bf16[512,256]{1,0:T(8,128)(2,1)}, bf16[512,256]{1,0:T(8,128)(2,1)}, u32[]{:S(2)}, u32[]{:S(2)}) collective-permute-start(bf16[512,256]{1,0:T(8,128)(2,1)} %fused_two_sided.3), channel_id=1, source_target_pairs={{24,0},{25,1},{26,2},{27,3},{28,4},{29,5},{30,6},{31,7}} | collective-permute-start | bytes 786440 | tf_op jit(solution)/shard_map/ppermute | solution.py:76
  659.1 15.4 %collective-permute-start.97 = (bf16[288,256]{1,0:T(8,128)(2,1)S(1)}, bf16[288,256]{1,0:T(8,128)(2,1)S(1)}, u32[]{:S(2)}, u32[]{:S(2)}) collective-permute-start(bf16[288,256]{1,0:T(8,128)(2,1)S(1)} %select_convert_fusion.3), channel_id=1, source_target_pairs={{0,4},{4,0},{1,5},{5,1},{2,6},{6,2},{3,7},{7,3},{8,12},{12,8},{9,1... | collective-permute-start | bytes 442376 | tf_op jit(solution)/shard_map/ppermute | solution.py:63
  659.7 22.1 %collective-permute-start.93 = (bf16[576,256]{1,0:T(8,128)(2,1)S(1)}, bf16[576,256]{1,0:T(8,128)(2,1)S(1)}, u32[]{:S(2)}, u32[]{:S(2)}) collective-permute-start(bf16[576,256]{1,0:T(8,128)(2,1)S(1)} %get-tuple-element.273), channel_id=1, source_target_pairs={{0,8},{8,16},{16,24},{24,0},{1,9},{9,17},{17,25},{25,1},{2,10},{10... | collective-permute-start | bytes 884744 | tf_op jit(solution)/shard_map/ppermute | solution.py:99
  659.8 24.1 %collective-permute-start.94 = (bf16[576,256]{1,0:T(8,128)(2,1)S(1)}, bf16[576,256]{1,0:T(8,128)(2,1)S(1)}, u32[]{:S(2)}, u32[]{:S(2)}) collective-permute-start(bf16[576,256]{1,0:T(8,128)(2,1)S(1)} %get-tuple-element.272), channel_id=1, source_target_pairs={{0,16},{8,24},{16,0},{24,8},{1,17},{9,25},{17,1},{25,9},{2,18},{10... | collective-permute-start | bytes 884744 | tf_op jit(solution)/shard_map/ppermute | solution.py:99
  671.8 21.6 %collective-permute-start.95 = (bf16[576,256]{1,0:T(8,128)(2,1)S(1)}, bf16[576,256]{1,0:T(8,128)(2,1)S(1)}, u32[]{:S(2)}, u32[]{:S(2)}) collective-permute-start(bf16[576,256]{1,0:T(8,128)(2,1)S(1)} %get-tuple-element.271), channel_id=1, source_target_pairs={{0,24},{8,0},{16,8},{24,16},{1,25},{9,1},{17,9},{25,17},{2,26},{10... | collective-permute-start | bytes 884744 | tf_op jit(solution)/shard_map/ppermute | solution.py:99
  678.2 19.3 %collective-permute-start.89 = (bf16[576,256]{1,0:T(8,128)(2,1)S(1)}, bf16[576,256]{1,0:T(8,128)(2,1)S(1)}, u32[]{:S(2)}, u32[]{:S(2)}) collective-permute-start(bf16[576,256]{1,0:T(8,128)(2,1)S(1)} %get-tuple-element.276), channel_id=1, source_target_pairs={{0,8},{8,16},{16,24},{24,0},{1,9},{9,17},{17,25},{25,1},{2,10},{10... | collective-permute-start | bytes 884744 | tf_op jit(solution)/shard_map/ppermute | solution.py:99
  679.8 28.8 %collective-permute-start.90 = (bf16[576,256]{1,0:T(8,128)(2,1)S(1)}, bf16[576,256]{1,0:T(8,128)(2,1)S(1)}, u32[]{:S(2)}, u32[]{:S(2)}) collective-permute-start(bf16[576,256]{1,0:T(8,128)(2,1)S(1)} %get-tuple-element.275), channel_id=1, source_target_pairs={{0,16},{8,24},{16,0},{24,8},{1,17},{9,25},{17,1},{25,9},{2,18},{10... | collective-permute-start | bytes 884744 | tf_op jit(solution)/shard_map/ppermute | solution.py:99
  681.9 26.7 %collective-permute-start.91 = (bf16[576,256]{1,0:T(8,128)(2,1)S(1)}, bf16[576,256]{1,0:T(8,128)(2,1)S(1)}, u32[]{:S(2)}, u32[]{:S(2)}) collective-permute-start(bf16[576,256]{1,0:T(8,128)(2,1)S(1)} %get-tuple-element.274), channel_id=1, source_target_pairs={{0,24},{8,0},{16,8},{24,16},{1,25},{9,1},{17,9},{25,17},{2,26},{10... | collective-permute-start | bytes 884744 | tf_op jit(solution)/shard_map/ppermute | solution.py:99
  683.9 40.2 %collective-permute-start.87 = (bf16[64,2304]{1,0:T(8,128)(2,1)S(1)}, bf16[64,2304]{1,0:T(8,128)(2,1)S(1)}, u32[]{:S(2)}, u32[]{:S(2)}) collective-permute-start(bf16[64,2304]{1,0:T(8,128)(2,1)S(1)} %fused_first_back.1.own_ref), channel_id=1, source_target_pairs={{0,2},{1,3},{2,0},{3,1},{4,6},{5,7},{6,4},{7,5},{8,10},{9,11},{10,... | collective-permute-start | bytes 884744 | tf_op jit(solution)/shard_map/ppermute | solution.py:63
  697.5 30.1 %collective-permute-start.96 = (bf16[288,256]{1,0:T(8,128)(2,1)S(1)}, bf16[288,256]{1,0:T(8,128)(2,1)S(1)}, u32[]{:S(2)}, u32[]{:S(2)}) collective-permute-start(bf16[288,256]{1,0:T(8,128)(2,1)S(1)} %select_convert_fusion.4), channel_id=1, source_target_pairs={{0,4},{4,0},{1,5},{5,1},{2,6},{6,2},{3,7},{7,3},{8,12},{12,8},{9,1... | collective-permute-start | bytes 442376 | tf_op jit(solution)/shard_map/ppermute | solution.py:63
  (149 other events, 847.6 us)

commit v6 on v5

--- a/solution.py
+++ b/solution.py
@@ -533,10 +533,11 @@
         return blocks[:, :size], rider
 
     gains = jnp.concatenate([pre_attn_gain, post_attn_gain, pre_ffw_gain, post_ffw_gain])
-    pair_got = ring_blocks(with_rider(jnp.where(is_first, key_weight, value_weight), gains))
+    pair_got = ring_blocks(jnp.where(is_first, key_weight, value_weight))
     group_tokens = join(tokens, 0, 0).reshape(group, width)
     segment_pair = join(segments[None].astype(b16), 0, 0)
-    pair_in, gains = split_rider(in_order(pair_got), 4 * deep)
+    gains = in_order(ring_blocks(after(gains, segment_pair)))
+    pair_in = in_order(pair_got)
     pair_in = pair_in.reshape(width, HEAD_SIZE)
     gains = 1.0 + jnp.swapaxes(gains.reshape(n, 4, deep), 0, 1).reshape(4, width).astype(f32)
     normed_one = group_tokens.astype(f32)
@@ -746,14 +747,14 @@
         kept, sent = picked(is_first, (total[: deep // 2], total[deep // 2 : deep]))
         return kept, swapped(sent.astype(b16), "context", 1).astype(f32)
 
-    grad_w_query = ring_summed(after(query_blocks, *terms), grad_inputs)
-    grad_pair = ring_summed(pair_blocks, grad_inputs)
     grad_gains = after(grad_gains, grad_inputs)
     grad_gains = grad_gains + swapped(grad_gains, "tensor", 2)
     grad_gains = grad_gains + swapped(grad_gains, "tensor", 1)
+    grad_w_query = ring_summed(after(query_blocks, *terms), grad_inputs, grad_gains)
     grad_gains = jnp.transpose(grad_gains.reshape(4, n, 2, deep // 2), (2, 1, 0, 3))
     grad_gains, sent = picked(is_first, (grad_gains[0], grad_gains[1]))
     grad_gains = ring_summed(grad_gains + swapped(sent, "context", 1))
+    grad_pair = ring_summed(pair_blocks, grad_inputs)
     grad_inputs = spread_lanes(grad_inputs).astype(f32)
     grad_w_out = jnp.concatenate(picked(is_first, halves(grad_w_out)), axis=1).T
     grad_w_query = jnp.concatenate(picked(is_first, halves(grad_w_query)), axis=1)

time: 739 us -> 734 us (level)
  starting transfers between devices: 183 us -> 167 us
  waiting for transfers between devices: 332 us -> 344 us
    ppermute x6, starting transfers between devices: 29.3 us -> 11.5 us  [shifted(): lax.ppermute(value, axis, [(s, s + steps) for s in range(count) if 0 <= s...]
    ppermute x6, waiting for transfers between devices: 17.4 us -> 31.9 us  [shifted(): lax.ppermute(value, axis, [(s, s + steps) for s in range(count) if 0 <= s...]
    ppermute x33 -> x36, starting transfers between devices: 54 us -> 59 us  [rotated(): return lax.ppermute(value, 'dp', [(s, (s + steps) % n) for s in range(n)])]
    ppermute x33 -> x36, waiting for transfers between devices: 136 us -> 135 us  [rotated(): return lax.ppermute(value, 'dp', [(s, (s + steps) % n) for s in range(n)])]
    unnamed x229 -> x226, local copies, waits for them, and re-layouts: 38 us -> 37.8 us
  transfers between devices with their start and end apart: 110 -> 113, of which waited for: 57 -> 57; matrix products, arithmetic and copies ran while one was open for 13% -> 13% of each run, Pallas kernels for 6% -> 6%
where the time goes in v6:
time: 734 us; the launch traced here: 726 us
  waiting for transfers between devices  344 us (47%)
  starting transfers between devices  167 us (23%)
  other arithmetic  55.3 us (8%)
  local copies, waits for them, and re-layouts  54.9 us (7%)
  matrix products  53.4 us (7%)
  Pallas kernels  48.1 us (7%)
    ppermute x65, waiting for transfers between devices, swapped(): lax.ppermute(value, axis, [(place, place ^ bit) for place in range(count)])  173 us
    ppermute x36, waiting for transfers between devices, rotated(): return lax.ppermute(value, 'dp', [(s, (s + steps) % n) for s in range(n)])  135 us
    ppermute x36, starting transfers between devices, rotated(): return lax.ppermute(value, 'dp', [(s, (s + steps) % n) for s in range(n)])  59 us
    ppermute x65, starting transfers between devices, swapped(): lax.ppermute(value, axis, [(place, place ^ bit) for place in range(count)])  53.6 us
    all_to_all x6, starting transfers between devices, exchange(): return lax.all_to_all(blocks, axis, 0, 0, tiled=True)  42.7 us
    unnamed x226, local copies, waits for them, and re-layouts  37.8 us
    ppermute x6, waiting for transfers between devices, shifted(): lax.ppermute(value, axis, [(s, s + steps) for s in range(count) if 0 <= s...  31.9 us
    dot_general x12, matrix products, dot(): return jnp.dot(left, right, preferred_element_type=f32)  19.5 us
  transfers between devices with their start and end apart: 113, of which 57 were waited for; matrix products, arithmetic and copies ran while one was open for 13% of the time, Pallas kernels for 6%

profile of v6, /device:TPU:0, one launch (start us, length us, event | category | flops | bytes accessed | tf_op | source)
XLA Modules:
  0.0 725.8 jit_solution(10865513863570012904)
XLA Ops:
  1.7 5.1 collective-permute-start.5
  10.6 2.8 concatenate.102
  21.9 15.8 %collective-permute-done.6 = bf16[576,256]{1,0:T(8,128)(2,1)S(1)} collective-permute-done((bf16[576,256]{1,0:T(8,128)(2,1)S(1)}, bf16[576,256]{1,0:T(8,128)(2,1)S(1)}, u32[]{:S(2)}, u32[]{:S(2)}) %collective-permute-start.6) | collective-permute-done | bytes 294944 | tf_op jit(solution)/shard_map/ppermute | solution.py:99
  43.8 3.8 collective-permute-start.8
  47.6 4.8 collective-permute-start.12
  54.4 4.1 unit_blocks.1
  60.8 14.1 %collective-permute-done.12 = bf16[512,256]{1,0:T(8,128)(2,1)S(1)} collective-permute-done((bf16[512,256]{1,0:T(8,128)(2,1)S(1)}, bf16[512,256]{1,0:T(8,128)(2,1)S(1)}, u32[]{:S(2)}, u32[]{:S(2)}) %collective-permute-start.12) | collective-permute-done | bytes 262176 | tf_op jit(solution)/shard_map/ppermute | solution.py:76
  76.4 3.5 collective-permute-done.13
  80.6 16.7 %all-to-all-start = ((bf16[4,288,576]{2,1,0:T(8,128)(2,1)}), bf16[4,288,576]{2,1,0:T(8,128)(2,1)S(1)}, u32[]{:S(2)}, u32[]{:S(2)}) async-start(bf16[4,288,576]{2,1,0:T(8,128)(2,1)} %get-tuple-element.126), calls=%async_computation | async-start | bytes 2949120 | tf_op jit(solution)/shard_map/all_to_all | solution.py:53
  106.5 3.0 collective-permute-start.19
  109.5 2.6 collective-permute-done.15
  112.1 4.1 collective-permute-start.20
  118.9 3.9 fusion.95
  123.6 3.5 fusion.93
  127.1 5.9 collective-permute-done.18
  133.0 19.3 %collective-permute-done.19 = bf16[576,256]{1,0:T(8,128)(2,1)S(1)} collective-permute-done((bf16[576,256]{1,0:T(8,128)(2,1)S(1)}, bf16[576,256]{1,0:T(8,128)(2,1)S(1)}, u32[]{:S(2)}, u32[]{:S(2)}) %collective-permute-start.19) | collective-permute-done | bytes 294944 | tf_op jit(solution)/shard_map/ppermute | solution.py:99
  154.2 2.6 convolution_convert_fusion.refs_1_.right_ref
  160.0 8.0 %all-to-all-start.1 = ((bf16[4,288,576]{2,1,0:T(8,128)(2,1)}), bf16[4,288,576]{2,1,0:T(8,128)(2,1)}, u32[]{:S(2)}, u32[]{:S(2)}) async-start(bf16[4,288,576]{2,1,0:T(8,128)(2,1)} %copy-done.32), calls=%async_computation.1 | async-start | bytes 2949120 | tf_op jit(solution)/shard_map/all_to_all | solution.py:53
  171.3 13.8 %collective-permute-done.22.other_ref = bf16[4,288,576]{2,1,0:T(8,128)(2,1)} collective-permute-done((bf16[4,288,576]{2,1,0:T(8,128)(2,1)S(1)}, bf16[4,288,576]{2,1,0:T(8,128)(2,1)}, u32[]{:S(2)}, u32[]{:S(2)}) %collective-permute-start.22) | collective-permute-done | bytes 1327136 | tf_op jit(solution)/shard_map/ppermute | solution.py:63
  188.1 3.7 collective-permute-done.23.refs_3_
  191.8 2.6 collective-permute-done.24.refs_5_
  200.6 3.1 all-to-all-done.1.own_ref
  203.6 5.0 all-to-all-start.2
  213.7 28.5 %collective-permute-done.27.other_ref = bf16[4,288,576]{2,1,0:T(8,128)(2,1)S(1)} collective-permute-done((bf16[4,288,576]{2,1,0:T(8,128)(2,1)}, bf16[4,288,576]{2,1,0:T(8,128)(2,1)S(1)}, u32[]{:S(2)}, u32[]{:S(2)}) %collective-permute-start.27) | collective-permute-done | bytes 1327136 | tf_op jit(solution)/shard_map/ppermute | solution.py:63
  245.1 2.5 collective-permute-start.29
  261.8 13.4 %collective-permute-done.39 = bf16[64,2304]{1,0:T(8,128)(2,1)S(1)} collective-permute-done((bf16[64,2304]{1,0:T(8,128)(2,1)S(1)}, bf16[64,2304]{1,0:T(8,128)(2,1)S(1)}, u32[]{:S(2)}, u32[]{:S(2)}) %collective-permute-start.39) | collective-permute-done | bytes 294944 | tf_op jit(solution)/shard_map/ppermute | solution.py:99
  275.8 7.3 %collective-permute-done.40 = bf16[64,2304]{1,0:T(8,128)(2,1)S(1)} collective-permute-done((bf16[64,2304]{1,0:T(8,128)(2,1)S(1)}, bf16[64,2304]{1,0:T(8,128)(2,1)S(1)}, u32[]{:S(2)}, u32[]{:S(2)}) %collective-permute-start.40) | collective-permute-done | bytes 294944 | tf_op jit(solution)/shard_map/ppermute | solution.py:63
  294.8 2.7 multiply_convert_fusion.2
  306.1 14.1 %collective-permute-done.36 = bf16[128,2304]{1,0:T(8,128)(2,1)S(1)} collective-permute-done((bf16[128,2304]{1,0:T(8,128)(2,1)S(1)}, bf16[128,2304]{1,0:T(8,128)(2,1)S(1)}, u32[]{:S(2)}, u32[]{:S(2)}) %collective-permute-start.36) | collective-permute-done | bytes 589856 | tf_op jit(solution)/shard_map/ppermute | solution.py:63
  323.3 5.3 collective-permute-done.43
  330.7 6.9 collective-permute-done.38
  337.6 10.5 %collective-permute-done.44 = bf16[64,2304]{1,0:T(8,128)(2,1)S(1)} collective-permute-done((bf16[64,2304]{1,0:T(8,128)(2,1)S(1)}, bf16[64,2304]{1,0:T(8,128)(2,1)S(1)}, u32[]{:S(2)}, u32[]{:S(2)}) %collective-permute-start.44) | collective-permute-done | bytes 294944 | tf_op jit(solution)/shard_map/ppermute | solution.py:99
  348.5 2.5 fusion.44
  352.4 3.8 collective-permute-start.48
  356.3 3.6 collective-permute-done.50
  360.0 4.2 collective-permute-done.47
  364.2 2.6 collective-permute-done.48
  370.6 10.4 %collective-permute-done.57 = bf16[64,2304]{1,0:T(8,128)(2,1)S(1)} collective-permute-done((bf16[64,2304]{1,0:T(8,128)(2,1)S(1)}, bf16[64,2304]{1,0:T(8,128)(2,1)S(1)}, u32[]{:S(2)}, u32[]{:S(2)}) %collective-permute-start.57) | collective-permute-done | bytes 294944 | tf_op jit(solution)/shard_map/ppermute | solution.py:99
  386.7 3.2 collective-permute-done.58
  405.7 3.9 fusion.21
  411.6 13.8 %collective-permute-done.54 = bf16[128,2304]{1,0:T(8,128)(2,1)S(1)} collective-permute-done((bf16[128,2304]{1,0:T(8,128)(2,1)S(1)}, bf16[128,2304]{1,0:T(8,128)(2,1)S(1)}, u32[]{:S(2)}, u32[]{:S(2)}) %collective-permute-start.54) | collective-permute-done | bytes 589856 | tf_op jit(solution)/shard_map/ppermute | solution.py:63
  428.0 5.9 collective-permute-done.61
  437.9 3.5 collective-permute-done.64
  442.2 3.9 fusion.27
  447.8 12.9 %collective-permute-done.65 = bf16[4,288,576]{2,1,0:T(8,128)(2,1)S(1)} collective-permute-done((bf16[4,288,576]{2,1,0:T(8,128)(2,1)S(1)}, bf16[4,288,576]{2,1,0:T(8,128)(2,1)S(1)}, u32[]{:S(2)}, u32[]{:S(2)}) %collective-permute-start.65) | collective-permute-done | bytes 1327136 | tf_op jit(solution)/shard_map/ppermute | solution.py:63
  464.5 3.7 all-to-all-start.3
  484.1 8.8 %fusion.33 = f32[2304,576]{1,0:T(8,128)} fusion(bf16[1024,2304]{1,0:T(8,128)(2,1)} %copy-done.86, bf16[256,576]{0,1:T(8,128)(2,1)S(1)} %copy-done.77, bf16[512,576]{0,1:T(8,128)(2,1)S(1)} %copy-done.96, bf16[256,576]{0,1:T(8,128)(2,1)S(1)} %copy-done.75), kind=kOutput, calls=%fused_computation.88 | convolution fusion | flops 2721447936 | bytes 11206656 | tf_op jit(solution)/shard_map/dot_general | solution.py:94
  492.9 8.4 %collective-permute-done.66 = bf16[4,288,576]{2,1,0:T(8,128)(2,1)} collective-permute-done((bf16[4,288,576]{2,1,0:T(8,128)(2,1)}, bf16[4,288,576]{2,1,0:T(8,128)(2,1)}, u32[]{:S(2)}, u32[]{:S(2)}) %collective-permute-start.66) | collective-permute-done | bytes 1327136 | tf_op jit(solution)/shard_map/ppermute | solution.py:63
  504.9 4.7 fusion.9
  509.6 4.5 all-to-all-start.4
  519.2 4.1 fusion.13
  532.3 12.8 %attend_back.1 = (bf16[512,256]{1,0:T(8,128)(2,1)S(1)}, f32[2048,256]{1,0:T(8,128)}, bf16[2048,256]{1,0:T(8,128)(2,1)S(1)}) custom-call(s32[1]{0:T(128)} %bitcast.19.side_ref, bf16[512,2304]{1,0:T(8,128)(2,1)} %bitcast.260, bf16[2304,256]{1,0:T(8,128)(2,1)S(1)} %bitcast.263, bf16[2048,256]{1,0:T(8,128)(2,1)S(1)} %copy-done.19, ...), custom_call_target="tpu_custom_call" | custom-call | tf_op jit(solution)/shard_map/attend_back/pallas_call | solution.py:412
  546.8 8.5 %collective-permute-done.74 = bf16[4,288,576]{2,1,0:T(8,128)(2,1)} collective-permute-done((bf16[4,288,576]{2,1,0:T(8,128)(2,1)}, bf16[4,288,576]{2,1,0:T(8,128)(2,1)}, u32[]{:S(2)}, u32[]{:S(2)}) %collective-permute-start.74) | collective-permute-done | bytes 1327136 | tf_op jit(solution)/shard_map/ppermute | solution.py:63
  555.3 3.1 fusion.8
  559.5 4.8 all-to-all-start.5
  587.2 4.7 collective-permute-done.76.refs_1_
  605.2 21.8 %collective-permute-done.83 = bf16[576,256]{1,0:T(8,128)(2,1)} collective-permute-done((bf16[576,256]{1,0:T(8,128)(2,1)}, bf16[576,256]{1,0:T(8,128)(2,1)}, u32[]{:S(2)}, u32[]{:S(2)}) %collective-permute-start.83) | collective-permute-done | bytes 294944 | tf_op jit(solution)/shard_map/ppermute | solution.py:99
  629.2 14.3 %collective-permute-done.79.refs_5_ = bf16[512,256]{1,0:T(8,128)(2,1)} collective-permute-done((bf16[512,256]{1,0:T(8,128)(2,1)}, bf16[512,256]{1,0:T(8,128)(2,1)}, u32[]{:S(2)}, u32[]{:S(2)}) %collective-permute-start.79) | collective-permute-done | bytes 262176 | tf_op jit(solution)/shard_map/ppermute | solution.py:76
  655.0 3.2 side_by_side.4
  663.9 7.0 collective-permute-done.86.refs_3_
  683.4 15.4 %collective-permute-done.99 = bf16[576,256]{1,0:T(8,128)(2,1)S(1)} collective-permute-done((bf16[576,256]{1,0:T(8,128)(2,1)S(1)}, bf16[576,256]{1,0:T(8,128)(2,1)S(1)}, u32[]{:S(2)}, u32[]{:S(2)}) %collective-permute-start.99) | collective-permute-done | bytes 294944 | tf_op jit(solution)/shard_map/ppermute | solution.py:99
  707.6 3.1 collective-permute-done.103
  710.8 2.7 collective-permute-start.104
  713.4 3.1 collective-permute-start.105
  (592 shorter events, 266.8 us)
Async XLA Ops:
  1.7 20.2 %collective-permute-start.5 = (bf16[576,256]{1,0:T(8,128)(2,1)S(1)}, bf16[576,256]{1,0:T(8,128)(2,1)S(1)}, u32[]{:S(2)}, u32[]{:S(2)}) collective-permute-start(bf16[576,256]{1,0:T(8,128)(2,1)S(1)} %broadcast_select_fusion.14), channel_id=1, source_target_pairs={{0,24},{8,0},{16,8},{24,16},{1,25},{9,1},{17,9},{25,17},{2,26},{10... | collective-permute-start | bytes 884744 | tf_op jit(solution)/shard_map/ppermute | solution.py:99
  8.9 29.0 %collective-permute-start.4 = (bf16[256,2304]{1,0:T(8,128)(2,1)}, bf16[256,2304]{1,0:T(8,128)(2,1)S(1)}, u32[]{:S(2)}, u32[]{:S(2)}) collective-permute-start(bf16[256,2304]{1,0:T(8,128)(2,1)} %param.14), channel_id=1, source_target_pairs={{0,4},{4,0},{1,5},{5,1},{2,6},{6,2},{3,7},{7,3},{8,12},{12,8},{9,1... | collective-permute-start | bytes 3538952 | tf_op jit(solution)/shard_map/ppermute | solution.py:63
  17.1 20.6 %collective-permute-start.6 = (bf16[576,256]{1,0:T(8,128)(2,1)S(1)}, bf16[576,256]{1,0:T(8,128)(2,1)S(1)}, u32[]{:S(2)}, u32[]{:S(2)}) collective-permute-start(bf16[576,256]{1,0:T(8,128)(2,1)S(1)} %broadcast_select_fusion.14), channel_id=1, source_target_pairs={{0,16},{8,24},{16,0},{24,8},{1,17},{9,25},{17,1},{25,9},{2,18},{10... | collective-permute-start | bytes 884744 | tf_op jit(solution)/shard_map/ppermute | solution.py:99
  18.5 19.2 %collective-permute-start.7 = (bf16[576,256]{1,0:T(8,128)(2,1)S(1)}, bf16[576,256]{1,0:T(8,128)(2,1)S(1)}, u32[]{:S(2)}, u32[]{:S(2)}) collective-permute-start(bf16[576,256]{1,0:T(8,128)(2,1)S(1)} %broadcast_select_fusion.14), channel_id=1, source_target_pairs={{0,8},{8,16},{16,24},{24,0},{1,9},{9,17},{17,25},{25,1},{2,10},{10... | collective-permute-start | bytes 884744 | tf_op jit(solution)/shard_map/ppermute | solution.py:99
  43.8 55.0 %collective-permute-start.10 = (bf16[592,256]{1,0:T(8,128)(2,1)S(1)}, bf16[592,256]{1,0:T(8,128)(2,1)S(1)}, u32[]{:S(2)}, u32[]{:S(2)}) collective-permute-start(bf16[592,256]{1,0:T(8,128)(2,1)S(1)} %pad_maximum_fusion.23), channel_id=1, source_target_pairs={{0,8},{8,16},{16,24},{24,0},{1,9},{9,17},{17,25},{25,1},{2,10},{10... | collective-permute-start | bytes 909320 | tf_op jit(solution)/shard_map/ppermute | solution.py:99
  43.8 55.5 %collective-permute-start.8 = (bf16[592,256]{1,0:T(8,128)(2,1)S(1)}, bf16[592,256]{1,0:T(8,128)(2,1)S(1)}, u32[]{:S(2)}, u32[]{:S(2)}) collective-permute-start(bf16[592,256]{1,0:T(8,128)(2,1)S(1)} %pad_maximum_fusion.23), channel_id=1, source_target_pairs={{0,24},{8,0},{16,8},{24,16},{1,25},{9,1},{17,9},{25,17},{2,26},{10... | collective-permute-start | bytes 909320 | tf_op jit(solution)/shard_map/ppermute | solution.py:99
  47.6 53.2 %collective-permute-start.9 = (bf16[592,256]{1,0:T(8,128)(2,1)S(1)}, bf16[592,256]{1,0:T(8,128)(2,1)S(1)}, u32[]{:S(2)}, u32[]{:S(2)}) collective-permute-start(bf16[592,256]{1,0:T(8,128)(2,1)S(1)} %pad_maximum_fusion.23), channel_id=1, source_target_pairs={{0,16},{8,24},{16,0},{24,8},{1,17},{9,25},{17,1},{25,9},{2,18},{10... | collective-permute-start | bytes 909320 | tf_op jit(solution)/shard_map/ppermute | solution.py:99
  47.6 27.3 %collective-permute-start.12 = (bf16[512,256]{1,0:T(8,128)(2,1)S(1)}, bf16[512,256]{1,0:T(8,128)(2,1)S(1)}, u32[]{:S(2)}, u32[]{:S(2)}) collective-permute-start(bf16[512,256]{1,0:T(8,128)(2,1)S(1)} %fusion.65), channel_id=1, source_target_pairs={{0,16},{8,24},{1,17},{9,25},{2,18},{10,26},{3,19},{11,27},{4,20},{... | collective-permute-start | bytes 786440 | tf_op jit(solution)/shard_map/ppermute | solution.py:76
  52.5 27.4 %collective-permute-start.13 = (bf16[512,256]{1,0:T(8,128)(2,1)S(1)}, bf16[512,256]{1,0:T(8,128)(2,1)S(1)}, u32[]{:S(2)}, u32[]{:S(2)}) collective-permute-start(bf16[512,256]{1,0:T(8,128)(2,1)S(1)} %fusion.65), channel_id=1, source_target_pairs={{0,8},{8,16},{16,24},{1,9},{9,17},{17,25},{2,10},{10,18},{18,26},{... | collective-permute-start | bytes 786440 | tf_op jit(solution)/shard_map/ppermute | solution.py:76
  74.9 41.6 %collective-permute-start.17 = (bf16[512,256]{1,0:T(8,128)(2,1)S(1)}, bf16[512,256]{1,0:T(8,128)(2,1)}, u32[]{:S(2)}, u32[]{:S(2)}) collective-permute-start(bf16[512,256]{1,0:T(8,128)(2,1)S(1)} %fusion.65), channel_id=1, source_target_pairs={{0,4},{4,0},{1,5},{5,1},{2,6},{6,2},{3,7},{7,3},{8,12},{12,8},{9,1... | collective-permute-start | bytes 786440 | tf_op jit(solution)/shard_map/ppermute | solution.py:63
  80.6 72.0 %all-to-all-start = ((bf16[4,288,576]{2,1,0:T(8,128)(2,1)}), bf16[4,288,576]{2,1,0:T(8,128)(2,1)S(1)}, u32[]{:S(2)}, u32[]{:S(2)}) async-start(bf16[4,288,576]{2,1,0:T(8,128)(2,1)} %get-tuple-element.126), calls=%async_computation | async-start | bytes 2949120 | tf_op jit(solution)/shard_map/all_to_all | solution.py:53
  98.8 13.3 %collective-permute-start.15 = (bf16[512,256]{1,0:T(8,128)(2,1)}, bf16[512,256]{1,0:T(8,128)(2,1)S(1)}, u32[]{:S(2)}, u32[]{:S(2)}) collective-permute-start(bf16[512,256]{1,0:T(8,128)(2,1)} %copy-done.79), channel_id=1, source_target_pairs={{0,4},{4,0},{1,5},{5,1},{2,6},{6,2},{3,7},{7,3},{8,12},{12,8},{9,1... | collective-permute-start | bytes 786440 | tf_op jit(solution)/shard_map/ppermute | solution.py:63
  99.3 17.1 %collective-permute-start.16 = (bf16[512,256]{1,0:T(8,128)(2,1)}, bf16[512,256]{1,0:T(8,128)(2,1)S(1)}, u32[]{:S(2)}, u32[]{:S(2)}) collective-permute-start(bf16[512,256]{1,0:T(8,128)(2,1)} %copy-done.81), channel_id=1, source_target_pairs={{0,4},{4,0},{1,5},{5,1},{2,6},{6,2},{3,7},{7,3},{8,12},{12,8},{9,1... | collective-permute-start | bytes 786440 | tf_op jit(solution)/shard_map/ppermute | solution.py:63
  101.1 31.9 %collective-permute-start.18 = (bf16[576,256]{1,0:T(8,128)(2,1)S(1)}, bf16[576,256]{1,0:T(8,128)(2,1)S(1)}, u32[]{:S(2)}, u32[]{:S(2)}) collective-permute-start(bf16[576,256]{1,0:T(8,128)(2,1)S(1)} %slice_select_fusion), channel_id=1, source_target_pairs={{0,8},{8,16},{16,24},{24,0},{1,9},{9,17},{17,25},{25,1},{2,10},{10... | collective-permute-start | bytes 884744 | tf_op jit(solution)/shard_map/ppermute | solution.py:99
  106.5 45.8 %collective-permute-start.19 = (bf16[576,256]{1,0:T(8,128)(2,1)S(1)}, bf16[576,256]{1,0:T(8,128)(2,1)S(1)}, u32[]{:S(2)}, u32[]{:S(2)}) collective-permute-start(bf16[576,256]{1,0:T(8,128)(2,1)S(1)} %slice_select_fusion), channel_id=1, source_target_pairs={{0,16},{8,24},{16,0},{24,8},{1,17},{9,25},{17,1},{25,9},{2,18},{10... | collective-permute-start | bytes 884744 | tf_op jit(solution)/shard_map/ppermute | solution.py:99
  112.1 40.2 %collective-permute-start.20 = (bf16[576,256]{1,0:T(8,128)(2,1)S(1)}, bf16[576,256]{1,0:T(8,128)(2,1)S(1)}, u32[]{:S(2)}, u32[]{:S(2)}) collective-permute-start(bf16[576,256]{1,0:T(8,128)(2,1)S(1)} %slice_select_fusion), channel_id=1, source_target_pairs={{0,24},{8,0},{16,8},{24,16},{1,25},{9,1},{17,9},{25,17},{2,26},{10... | collective-permute-start | bytes 884744 | tf_op jit(solution)/shard_map/ppermute | solution.py:99
  152.6 32.5 %collective-permute-start.22 = (bf16[4,288,576]{2,1,0:T(8,128)(2,1)S(1)}, bf16[4,288,576]{2,1,0:T(8,128)(2,1)}, u32[]{:S(2)}, u32[]{:S(2)}) collective-permute-start(bf16[4,288,576]{2,1,0:T(8,128)(2,1)S(1)} %all-to-all-done.own_ref), channel_id=1, source_target_pairs={{0,4},{4,0},{1,5},{5,1},{2,6},{6,2},{3,7},{7,3},{8,12},{12,8},{9,1... | collective-permute-start | bytes 3981320 | tf_op jit(solution)/shard_map/ppermute | solution.py:63
  160.0 43.7 %all-to-all-start.1 = ((bf16[4,288,576]{2,1,0:T(8,128)(2,1)}), bf16[4,288,576]{2,1,0:T(8,128)(2,1)}, u32[]{:S(2)}, u32[]{:S(2)}) async-start(bf16[4,288,576]{2,1,0:T(8,128)(2,1)} %copy-done.32), calls=%async_computation.1 | async-start | bytes 2949120 | tf_op jit(solution)/shard_map/all_to_all | solution.py:53
  203.6 39.7 %all-to-all-start.2 = ((bf16[4,288,576]{2,1,0:T(8,128)(2,1)}), bf16[4,288,576]{2,1,0:T(8,128)(2,1)S(1)}, u32[]{:S(2)}, u32[]{:S(2)}) async-start(bf16[4,288,576]{2,1,0:T(8,128)(2,1)} %copy-done.31), calls=%async_computation.2 | async-start | bytes 2949120 | tf_op jit(solution)/shard_map/all_to_all | solution.py:53
  209.6 32.6 %collective-permute-start.27 = (bf16[4,288,576]{2,1,0:T(8,128)(2,1)}, bf16[4,288,576]{2,1,0:T(8,128)(2,1)S(1)}, u32[]{:S(2)}, u32[]{:S(2)}) collective-permute-start(bf16[4,288,576]{2,1,0:T(8,128)(2,1)} %all-to-all-done.1.own_ref), channel_id=1, source_target_pairs={{0,4},{4,0},{1,5},{5,1},{2,6},{6,2},{3,7},{7,3},{8,12},{12,8},{9,1... | collective-permute-start | bytes 3981320 | tf_op jit(solution)/shard_map/ppermute | solution.py:63
  243.3 12.6 %collective-permute-start.28 = (bf16[64,2304]{1,0:T(8,128)(2,1)}, bf16[64,2304]{1,0:T(8,128)(2,1)}, u32[]{:S(2)}, u32[]{:S(2)}) collective-permute-start(bf16[64,2304]{1,0:T(8,128)(2,1)} %get-tuple-element.150), channel_id=1, source_target_pairs={{0,8},{8,16},{16,24},{24,0},{1,9},{9,17},{17,25},{25,1},{2,10},{10... | collective-permute-start | bytes 884744 | tf_op jit(solution)/shard_map/ppermute | solution.py:99
  245.1 12.6 %collective-permute-start.29 = (bf16[64,2304]{1,0:T(8,128)(2,1)}, bf16[64,2304]{1,0:T(8,128)(2,1)}, u32[]{:S(2)}, u32[]{:S(2)}) collective-permute-start(bf16[64,2304]{1,0:T(8,128)(2,1)} %get-tuple-element.150), channel_id=1, source_target_pairs={{0,24},{8,0},{16,8},{24,16},{1,25},{9,1},{17,9},{25,17},{2,26},{10... | collective-permute-start | bytes 884744 | tf_op jit(solution)/shard_map/ppermute | solution.py:99
  255.4 31.5 %collective-permute-start.33 = (bf16[4,288,576]{2,1,0:T(8,128)(2,1)S(1)}, bf16[4,288,576]{2,1,0:T(8,128)(2,1)S(1)}, u32[]{:S(2)}, u32[]{:S(2)}) collective-permute-start(bf16[4,288,576]{2,1,0:T(8,128)(2,1)S(1)} %all-to-all-done.2.own_ref), channel_id=1, source_target_pairs={{0,4},{4,0},{1,5},{5,1},{2,6},{6,2},{3,7},{7,3},{8,12},{12,8},{9,1... | collective-permute-start | bytes 3981320 | tf_op jit(solution)/shard_map/ppermute | solution.py:63
  258.8 25.7 %collective-permute-start.30 = (bf16[128,2304]{1,0:T(8,128)(2,1)S(1)}, bf16[128,2304]{1,0:T(8,128)(2,1)S(1)}, u32[]{:S(2)}, u32[]{:S(2)}) collective-permute-start(bf16[128,2304]{1,0:T(8,128)(2,1)S(1)} %pad_maximum_fusion.16), channel_id=1, source_target_pairs={{0,2},{1,3},{2,0},{3,1},{4,6},{5,7},{6,4},{7,5},{8,10},{9,11},{10,... | collective-permute-start | bytes 1769480 | tf_op jit(solution)/shard_map/ppermute | solution.py:63
  260.4 14.9 %collective-permute-start.39 = (bf16[64,2304]{1,0:T(8,128)(2,1)S(1)}, bf16[64,2304]{1,0:T(8,128)(2,1)S(1)}, u32[]{:S(2)}, u32[]{:S(2)}) collective-permute-start(bf16[64,2304]{1,0:T(8,128)(2,1)S(1)} %copy-done.70), channel_id=1, source_target_pairs={{0,16},{8,24},{16,0},{24,8},{1,17},{9,25},{17,1},{25,9},{2,18},{10... | collective-permute-start | bytes 884744 | tf_op jit(solution)/shard_map/ppermute | solution.py:99
  261.8 21.3 %collective-permute-start.32 = (bf16[128,2304]{1,0:T(8,128)(2,1)S(1)}, bf16[128,2304]{1,0:T(8,128)(2,1)S(1)}, u32[]{:S(2)}, u32[]{:S(2)}) collective-permute-start(bf16[128,2304]{1,0:T(8,128)(2,1)S(1)} %pad_maximum_fusion.17), channel_id=1, source_target_pairs={{0,1},{1,0},{2,3},{3,2},{4,5},{5,4},{6,7},{7,6},{8,9},{9,8},{10,11... | collective-permute-start | bytes 1769480 | tf_op jit(solution)/shard_map/ppermute | solution.py:63
  304.7 15.4 %collective-permute-start.36 = (bf16[128,2304]{1,0:T(8,128)(2,1)S(1)}, bf16[128,2304]{1,0:T(8,128)(2,1)S(1)}, u32[]{:S(2)}, u32[]{:S(2)}) collective-permute-start(bf16[128,2304]{1,0:T(8,128)(2,1)S(1)} %slice.501), channel_id=1, source_target_pairs={{0,2},{1,3},{2,0},{3,1},{4,6},{5,7},{6,4},{7,5},{8,10},{9,11},{10,... | collective-permute-start | bytes 1769480 | tf_op jit(solution)/shard_map/ppermute | solution.py:63
  323.3 14.3 %collective-permute-start.38 = (bf16[64,2304]{1,0:T(8,128)(2,1)S(1)}, bf16[64,2304]{1,0:T(8,128)(2,1)S(1)}, u32[]{:S(2)}, u32[]{:S(2)}) collective-permute-start(bf16[64,2304]{1,0:T(8,128)(2,1)S(1)} %get-tuple-element.304), channel_id=1, source_target_pairs={{0,8},{8,16},{16,24},{24,0},{1,9},{9,17},{17,25},{25,1},{2,10},{10... | collective-permute-start | bytes 884744 | tf_op jit(solution)/shard_map/ppermute | solution.py:99
  328.7 19.5 %collective-permute-start.44 = (bf16[64,2304]{1,0:T(8,128)(2,1)S(1)}, bf16[64,2304]{1,0:T(8,128)(2,1)S(1)}, u32[]{:S(2)}, u32[]{:S(2)}) collective-permute-start(bf16[64,2304]{1,0:T(8,128)(2,1)S(1)} %convert_add_fusion.5), channel_id=1, source_target_pairs={{0,16},{8,24},{16,0},{24,8},{1,17},{9,25},{17,1},{25,9},{2,18},{10... | collective-permute-start | bytes 884744 | tf_op jit(solution)/shard_map/ppermute | solution.py:99
  352.4 11.8 %collective-permute-start.47 = (bf16[64,2304]{1,0:T(8,128)(2,1)S(1)}, bf16[64,2304]{1,0:T(8,128)(2,1)S(1)}, u32[]{:S(2)}, u32[]{:S(2)}) collective-permute-start(bf16[64,2304]{1,0:T(8,128)(2,1)S(1)} %fusion.43), channel_id=1, source_target_pairs={{0,8},{8,16},{16,24},{24,0},{1,9},{9,17},{17,25},{25,1},{2,10},{10... | collective-permute-start | bytes 884744 | tf_op jit(solution)/shard_map/ppermute | solution.py:99
  352.4 14.3 %collective-permute-start.48 = (bf16[64,2304]{1,0:T(8,128)(2,1)S(1)}, bf16[64,2304]{1,0:T(8,128)(2,1)S(1)}, u32[]{:S(2)}, u32[]{:S(2)}) collective-permute-start(bf16[64,2304]{1,0:T(8,128)(2,1)S(1)} %fusion.43), channel_id=1, source_target_pairs={{0,24},{8,0},{16,8},{24,16},{1,25},{9,1},{17,9},{25,17},{2,26},{10... | collective-permute-start | bytes 884744 | tf_op jit(solution)/shard_map/ppermute | solution.py:99
  359.9 22.6 %collective-permute-start.51 = (bf16[128,2304]{1,0:T(8,128)(2,1)S(1)}, bf16[128,2304]{1,0:T(8,128)(2,1)S(1)}, u32[]{:S(2)}, u32[]{:S(2)}) collective-permute-start(bf16[128,2304]{1,0:T(8,128)(2,1)S(1)} %pad_maximum_fusion.20), channel_id=1, source_target_pairs={{0,1},{1,0},{2,3},{3,2},{4,5},{5,4},{6,7},{7,6},{8,9},{9,8},{10,11... | collective-permute-start | bytes 1769480 | tf_op jit(solution)/shard_map/ppermute | solution.py:63
  366.8 14.3 %collective-permute-start.57 = (bf16[64,2304]{1,0:T(8,128)(2,1)S(1)}, bf16[64,2304]{1,0:T(8,128)(2,1)S(1)}, u32[]{:S(2)}, u32[]{:S(2)}) collective-permute-start(bf16[64,2304]{1,0:T(8,128)(2,1)S(1)} %fusion.43), channel_id=1, source_target_pairs={{0,16},{8,24},{16,0},{24,8},{1,17},{9,25},{17,1},{25,9},{2,18},{10... | collective-permute-start | bytes 884744 | tf_op jit(solution)/shard_map/ppermute | solution.py:99
  369.2 20.9 %collective-permute-start.49 = (bf16[128,2304]{1,0:T(8,128)(2,1)S(1)}, bf16[128,2304]{1,0:T(8,128)(2,1)S(1)}, u32[]{:S(2)}, u32[]{:S(2)}) collective-permute-start(bf16[128,2304]{1,0:T(8,128)(2,1)S(1)} %pad_maximum_fusion.19), channel_id=1, source_target_pairs={{0,2},{1,3},{2,0},{3,1},{4,6},{5,7},{6,4},{7,5},{8,10},{9,11},{10,... | collective-permute-start | bytes 1769480 | tf_op jit(solution)/shard_map/ppermute | solution.py:63
  410.0 15.4 %collective-permute-start.54 = (bf16[128,2304]{1,0:T(8,128)(2,1)S(1)}, bf16[128,2304]{1,0:T(8,128)(2,1)S(1)}, u32[]{:S(2)}, u32[]{:S(2)}) collective-permute-start(bf16[128,2304]{1,0:T(8,128)(2,1)S(1)} %slice.498), channel_id=1, source_target_pairs={{0,2},{1,3},{2,0},{3,1},{4,6},{5,7},{6,4},{7,5},{8,10},{9,11},{10,... | collective-permute-start | bytes 1769480 | tf_op jit(solution)/shard_map/ppermute | solution.py:63
  427.4 33.3 %collective-permute-start.65 = (bf16[4,288,576]{2,1,0:T(8,128)(2,1)S(1)}, bf16[4,288,576]{2,1,0:T(8,128)(2,1)S(1)}, u32[]{:S(2)}, u32[]{:S(2)}) collective-permute-start(bf16[4,288,576]{2,1,0:T(8,128)(2,1)S(1)} %fusion.11), channel_id=1, source_target_pairs={{0,4},{4,0},{1,5},{5,1},{2,6},{6,2},{3,7},{7,3},{8,12},{12,8},{9,1... | collective-permute-start | bytes 3981320 | tf_op jit(solution)/shard_map/ppermute | solution.py:63
  435.6 25.2 %collective-permute-start.55 = (bf16[64,2304]{1,0:T(8,128)(2,1)S(1)}, bf16[64,2304]{1,0:T(8,128)(2,1)S(1)}, u32[]{:S(2)}, u32[]{:S(2)}) collective-permute-start(bf16[64,2304]{1,0:T(8,128)(2,1)S(1)} %get-tuple-element.302), channel_id=1, source_target_pairs={{0,24},{8,0},{16,8},{24,16},{1,25},{9,1},{17,9},{25,17},{2,26},{10... | collective-permute-start | bytes 884744 | tf_op jit(solution)/shard_map/ppermute | solution.py:99
  437.1 24.3 %collective-permute-start.56 = (bf16[64,2304]{1,0:T(8,128)(2,1)S(1)}, bf16[64,2304]{1,0:T(8,128)(2,1)S(1)}, u32[]{:S(2)}, u32[]{:S(2)}) collective-permute-start(bf16[64,2304]{1,0:T(8,128)(2,1)S(1)} %get-tuple-element.301), channel_id=1, source_target_pairs={{0,8},{8,16},{16,24},{24,0},{1,9},{9,17},{17,25},{25,1},{2,10},{10... | collective-permute-start | bytes 884744 | tf_op jit(solution)/shard_map/ppermute | solution.py:99
  437.8 24.4 %collective-permute-start.62 = (bf16[64,2304]{1,0:T(8,128)(2,1)S(1)}, bf16[64,2304]{1,0:T(8,128)(2,1)S(1)}, u32[]{:S(2)}, u32[]{:S(2)}) collective-permute-start(bf16[64,2304]{1,0:T(8,128)(2,1)S(1)} %convert_add_fusion.4), channel_id=1, source_target_pairs={{0,16},{8,24},{16,0},{24,8},{1,17},{9,25},{17,1},{25,9},{2,18},{10... | collective-permute-start | bytes 884744 | tf_op jit(solution)/shard_map/ppermute | solution.py:99
  464.5 37.6 %all-to-all-start.3 = ((bf16[4,288,576]{2,1,0:T(8,128)(2,1)}), bf16[4,288,576]{2,1,0:T(8,128)(2,1)S(1)}, u32[]{:S(2)}, u32[]{:S(2)}) async-start(bf16[4,288,576]{2,1,0:T(8,128)(2,1)} %fusion.10), calls=%async_computation.3 | async-start | bytes 2949120 | tf_op jit(solution)/shard_map/all_to_all | solution.py:53
  468.1 33.1 %collective-permute-start.66 = (bf16[4,288,576]{2,1,0:T(8,128)(2,1)}, bf16[4,288,576]{2,1,0:T(8,128)(2,1)}, u32[]{:S(2)}, u32[]{:S(2)}) collective-permute-start(bf16[4,288,576]{2,1,0:T(8,128)(2,1)} %fusion.12), channel_id=1, source_target_pairs={{0,4},{4,0},{1,5},{5,1},{2,6},{6,2},{3,7},{7,3},{8,12},{12,8},{9,1... | collective-permute-start | bytes 3981320 | tf_op jit(solution)/shard_map/ppermute | solution.py:63
  504.9 12.1 %collective-permute-start.67 = (bf16[64,1152]{1,0:T(8,128)(2,1)}, bf16[64,1152]{1,0:T(8,128)(2,1)}, u32[]{:S(2)}, u32[]{:S(2)}) collective-permute-start(bf16[64,1152]{1,0:T(8,128)(2,1)} %get-tuple-element.310.own_ref), channel_id=1, source_target_pairs={{0,4},{4,0},{1,5},{5,1},{2,6},{6,2},{3,7},{7,3},{8,12},{12,8},{9,1... | collective-permute-start | bytes 442376 | tf_op jit(solution)/shard_map/ppermute | solution.py:63
  509.6 48.8 %all-to-all-start.4 = ((bf16[4,288,576]{2,1,0:T(8,128)(2,1)}), bf16[4,288,576]{2,1,0:T(8,128)(2,1)S(1)}, u32[]{:S(2)}, u32[]{:S(2)}) async-start(bf16[4,288,576]{2,1,0:T(8,128)(2,1)} %fusion.9), calls=%async_computation.4 | async-start | bytes 2949120 | tf_op jit(solution)/shard_map/all_to_all | solution.py:53
  523.3 32.0 %collective-permute-start.74 = (bf16[4,288,576]{2,1,0:T(8,128)(2,1)}, bf16[4,288,576]{2,1,0:T(8,128)(2,1)}, u32[]{:S(2)}, u32[]{:S(2)}) collective-permute-start(bf16[4,288,576]{2,1,0:T(8,128)(2,1)} %fusion.13), channel_id=1, source_target_pairs={{0,4},{4,0},{1,5},{5,1},{2,6},{6,2},{3,7},{7,3},{8,12},{12,8},{9,1... | collective-permute-start | bytes 3981320 | tf_op jit(solution)/shard_map/ppermute | solution.py:63
  525.9 40.3 %collective-permute-start.72 = (bf16[64,2304]{1,0:T(8,128)(2,1)}, bf16[64,2304]{1,0:T(8,128)(2,1)}, u32[]{:S(2)}, u32[]{:S(2)}) collective-permute-start(bf16[64,2304]{1,0:T(8,128)(2,1)} %get-tuple-element.179.own_ref), channel_id=1, source_target_pairs={{0,2},{1,3},{2,0},{3,1},{4,6},{5,7},{6,4},{7,5},{8,10},{9,11},{10,... | collective-permute-start | bytes 884744 | tf_op jit(solution)/shard_map/ppermute | solution.py:63
  559.5 84.0 %all-to-all-start.5 = ((bf16[4,288,576]{2,1,0:T(8,128)(2,1)}), bf16[4,288,576]{2,1,0:T(8,128)(2,1)}, u32[]{:S(2)}, u32[]{:S(2)}) async-start(bf16[4,288,576]{2,1,0:T(8,128)(2,1)} %fusion.8), calls=%async_computation.5 | async-start | bytes 2949120 | tf_op jit(solution)/shard_map/all_to_all | solution.py:53
  567.4 15.2 %collective-permute-start.80 = (bf16[512,256]{1,0:T(8,128)(2,1)S(1)}, bf16[512,256]{1,0:T(8,128)(2,1)S(1)}, u32[]{:S(2)}, u32[]{:S(2)}) collective-permute-start(bf16[512,256]{1,0:T(8,128)(2,1)S(1)} %get-tuple-element.290), channel_id=1, source_target_pairs={{0,4},{4,0},{1,5},{5,1},{2,6},{6,2},{3,7},{7,3},{8,12},{12,8},{9,1... | collective-permute-start | bytes 786440 | tf_op jit(solution)/shard_map/ppermute | solution.py:63
  568.0 15.2 %collective-permute-start.78 = (bf16[512,256]{1,0:T(8,128)(2,1)S(1)}, bf16[512,256]{1,0:T(8,128)(2,1)S(1)}, u32[]{:S(2)}, u32[]{:S(2)}) collective-permute-start(bf16[512,256]{1,0:T(8,128)(2,1)S(1)} %get-tuple-element.291), channel_id=1, source_target_pairs={{0,4},{4,0},{1,5},{5,1},{2,6},{6,2},{3,7},{7,3},{8,12},{12,8},{9,1... | collective-permute-start | bytes 786440 | tf_op jit(solution)/shard_map/ppermute | solution.py:63
  576.8 23.2 %collective-permute-start.82 = (bf16[576,256]{1,0:T(8,128)(2,1)S(1)}, bf16[576,256]{1,0:T(8,128)(2,1)S(1)}, u32[]{:S(2)}, u32[]{:S(2)}) collective-permute-start(bf16[576,256]{1,0:T(8,128)(2,1)S(1)} %get-tuple-element.277), channel_id=1, source_target_pairs={{0,8},{8,16},{16,24},{24,0},{1,9},{9,17},{17,25},{25,1},{2,10},{10... | collective-permute-start | bytes 884744 | tf_op jit(solution)/shard_map/ppermute | solution.py:99
  578.8 48.2 %collective-permute-start.83 = (bf16[576,256]{1,0:T(8,128)(2,1)}, bf16[576,256]{1,0:T(8,128)(2,1)}, u32[]{:S(2)}, u32[]{:S(2)}) collective-permute-start(bf16[576,256]{1,0:T(8,128)(2,1)} %get-tuple-element.276), channel_id=1, source_target_pairs={{0,16},{8,24},{16,0},{24,8},{1,17},{9,25},{17,1},{25,9},{2,18},{10... | collective-permute-start | bytes 884744 | tf_op jit(solution)/shard_map/ppermute | solution.py:99
  581.2 45.8 %collective-permute-start.84 = (bf16[576,256]{1,0:T(8,128)(2,1)}, bf16[576,256]{1,0:T(8,128)(2,1)}, u32[]{:S(2)}, u32[]{:S(2)}) collective-permute-start(bf16[576,256]{1,0:T(8,128)(2,1)} %get-tuple-element.275), channel_id=1, source_target_pairs={{0,24},{8,0},{16,8},{24,16},{1,25},{9,1},{17,9},{25,17},{2,26},{10... | collective-permute-start | bytes 884744 | tf_op jit(solution)/shard_map/ppermute | solution.py:99
  583.1 12.4 %collective-permute-start.75 = (bf16[512,256]{1,0:T(8,128)(2,1)S(1)}, bf16[512,256]{1,0:T(8,128)(2,1)S(1)}, u32[]{:S(2)}, u32[]{:S(2)}) collective-permute-start(bf16[512,256]{1,0:T(8,128)(2,1)S(1)} %get-tuple-element.293), channel_id=1, source_target_pairs={{0,4},{4,0},{1,5},{5,1},{2,6},{6,2},{3,7},{7,3},{8,12},{12,8},{9,1... | collective-permute-start | bytes 786440 | tf_op jit(solution)/shard_map/ppermute | solution.py:63
  591.9 37.3 %collective-permute-start.81 = (bf16[512,256]{1,0:T(8,128)(2,1)}, bf16[512,256]{1,0:T(8,128)(2,1)}, u32[]{:S(2)}, u32[]{:S(2)}) collective-permute-start(bf16[512,256]{1,0:T(8,128)(2,1)} %fused_two_sided.5), channel_id=1, source_target_pairs={{8,0},{16,8},{24,16},{9,1},{17,9},{25,17},{10,2},{18,10},{26,18},{... | collective-permute-start | bytes 786440 | tf_op jit(solution)/shard_map/ppermute | solution.py:76
  596.3 47.2 %collective-permute-start.79 = (bf16[512,256]{1,0:T(8,128)(2,1)}, bf16[512,256]{1,0:T(8,128)(2,1)}, u32[]{:S(2)}, u32[]{:S(2)}) collective-permute-start(bf16[512,256]{1,0:T(8,128)(2,1)} %fused_two_sided.4), channel_id=1, source_target_pairs={{16,0},{24,8},{17,1},{25,9},{18,2},{26,10},{19,3},{27,11},{20,4},{... | collective-permute-start | bytes 786440 | tf_op jit(solution)/shard_map/ppermute | solution.py:76
  600.8 42.7 %collective-permute-start.77 = (bf16[512,256]{1,0:T(8,128)(2,1)}, bf16[512,256]{1,0:T(8,128)(2,1)}, u32[]{:S(2)}, u32[]{:S(2)}) collective-permute-start(bf16[512,256]{1,0:T(8,128)(2,1)} %fused_two_sided.3), channel_id=1, source_target_pairs={{24,0},{25,1},{26,2},{27,3},{28,4},{29,5},{30,6},{31,7}} | collective-permute-start | bytes 786440 | tf_op jit(solution)/shard_map/ppermute | solution.py:76
  658.3 13.9 %collective-permute-start.102 = (bf16[288,256]{1,0:T(8,128)(2,1)S(1)}, bf16[288,256]{1,0:T(8,128)(2,1)S(1)}, u32[]{:S(2)}, u32[]{:S(2)}) collective-permute-start(bf16[288,256]{1,0:T(8,128)(2,1)S(1)} %select_convert_fusion.3), channel_id=1, source_target_pairs={{0,4},{4,0},{1,5},{5,1},{2,6},{6,2},{3,7},{7,3},{8,12},{12,8},{9,1... | collective-permute-start | bytes 442376 | tf_op jit(solution)/shard_map/ppermute | solution.py:63
  658.9 21.6 %collective-permute-start.100 = (bf16[576,256]{1,0:T(8,128)(2,1)S(1)}, bf16[576,256]{1,0:T(8,128)(2,1)S(1)}, u32[]{:S(2)}, u32[]{:S(2)}) collective-permute-start(bf16[576,256]{1,0:T(8,128)(2,1)S(1)} %get-tuple-element.269), channel_id=1, source_target_pairs={{0,24},{8,0},{16,8},{24,16},{1,25},{9,1},{17,9},{25,17},{2,26},{10... | collective-permute-start | bytes 884744 | tf_op jit(solution)/shard_map/ppermute | solution.py:99
  658.9 23.7 %collective-permute-start.98 = (bf16[576,256]{1,0:T(8,128)(2,1)S(1)}, bf16[576,256]{1,0:T(8,128)(2,1)S(1)}, u32[]{:S(2)}, u32[]{:S(2)}) collective-permute-start(bf16[576,256]{1,0:T(8,128)(2,1)S(1)} %get-tuple-element.271), channel_id=1, source_target_pairs={{0,8},{8,16},{16,24},{24,0},{1,9},{9,17},{17,25},{25,1},{2,10},{10... | collective-permute-start | bytes 884744 | tf_op jit(solution)/shard_map/ppermute | solution.py:99
  670.9 27.9 %collective-permute-start.99 = (bf16[576,256]{1,0:T(8,128)(2,1)S(1)}, bf16[576,256]{1,0:T(8,128)(2,1)S(1)}, u32[]{:S(2)}, u32[]{:S(2)}) collective-permute-start(bf16[576,256]{1,0:T(8,128)(2,1)S(1)} %get-tuple-element.270), channel_id=1, source_target_pairs={{0,16},{8,24},{16,0},{24,8},{1,17},{9,25},{17,1},{25,9},{2,18},{10... | collective-permute-start | bytes 884744 | tf_op jit(solution)/shard_map/ppermute | solution.py:99
  676.6 29.2 %collective-permute-start.92 = (bf16[576,256]{1,0:T(8,128)(2,1)S(1)}, bf16[576,256]{1,0:T(8,128)(2,1)}, u32[]{:S(2)}, u32[]{:S(2)}) collective-permute-start(bf16[576,256]{1,0:T(8,128)(2,1)S(1)} %get-tuple-element.274), channel_id=1, source_target_pairs={{0,8},{8,16},{16,24},{24,0},{1,9},{9,17},{17,25},{25,1},{2,10},{10... | collective-permute-start | bytes 884744 | tf_op jit(solution)/shard_map/ppermute | solution.py:99
  678.0 28.4 %collective-permute-start.93 = (bf16[576,256]{1,0:T(8,128)(2,1)S(1)}, bf16[576,256]{1,0:T(8,128)(2,1)}, u32[]{:S(2)}, u32[]{:S(2)}) collective-permute-start(bf16[576,256]{1,0:T(8,128)(2,1)S(1)} %get-tuple-element.273), channel_id=1, source_target_pairs={{0,16},{8,24},{16,0},{24,8},{1,17},{9,25},{17,1},{25,9},{2,18},{10... | collective-permute-start | bytes 884744 | tf_op jit(solution)/shard_map/ppermute | solution.py:99
  680.4 25.9 %collective-permute-start.94 = (bf16[576,256]{1,0:T(8,128)(2,1)S(1)}, bf16[576,256]{1,0:T(8,128)(2,1)}, u32[]{:S(2)}, u32[]{:S(2)}) collective-permute-start(bf16[576,256]{1,0:T(8,128)(2,1)S(1)} %get-tuple-element.272), channel_id=1, source_target_pairs={{0,24},{8,0},{16,8},{24,16},{1,25},{9,1},{17,9},{25,17},{2,26},{10... | collective-permute-start | bytes 884744 | tf_op jit(solution)/shard_map/ppermute | solution.py:99
  682.6 38.1 %collective-permute-start.90 = (bf16[64,2304]{1,0:T(8,128)(2,1)S(1)}, bf16[64,2304]{1,0:T(8,128)(2,1)S(1)}, u32[]{:S(2)}, u32[]{:S(2)}) collective-permute-start(bf16[64,2304]{1,0:T(8,128)(2,1)S(1)} %fused_first_back.1.own_ref), channel_id=1, source_target_pairs={{0,2},{1,3},{2,0},{3,1},{4,6},{5,7},{6,4},{7,5},{8,10},{9,11},{10,... | collective-permute-start | bytes 884744 | tf_op jit(solution)/shard_map/ppermute | solution.py:63
  704.0 16.8 %collective-permute-start.101 = (bf16[288,256]{1,0:T(8,128)(2,1)}, bf16[288,256]{1,0:T(8,128)(2,1)S(1)}, u32[]{:S(2)}, u32[]{:S(2)}) collective-permute-start(bf16[288,256]{1,0:T(8,128)(2,1)} %select_convert_fusion.4), channel_id=1, source_target_pairs={{0,4},{4,0},{1,5},{5,1},{2,6},{6,2},{3,7},{7,3},{8,12},{12,8},{9,1... | collective-permute-start | bytes 442376 | tf_op jit(solution)/shard_map/ppermute | solution.py:63
  (151 other events, 807.2 us)

commit v7 on v6

--- a/solution.py
+++ b/solution.py
@@ -552,7 +552,7 @@
     query_in, all_segments = split_rider(in_order(query_got), group)
     query_in = query_in.reshape(width, HEAD_SIZE)
     all_segments = all_segments.reshape(-1).astype(jnp.int32)
-    out_got = ring_blocks(after(half_of(w_output.T, side, 1), *query_got))
+    out_got = ring_blocks(after(half_of(w_output.T, side, 1), *mine))
     w_out = in_order(out_got).reshape(width, HEAD_SIZE)
 
     units = w_gate.shape[1] // n

time: 734 us -> 726 us (0.989)
  waiting for transfers between devices: 344 us -> 330 us
    ppermute x65, waiting for transfers between devices: 173 us -> 156 us  [swapped(): lax.ppermute(value, axis, [(place, place ^ bit) for place in range(count)])]
    ppermute x6, waiting for transfers between devices: 31.9 us -> 15.3 us  [shifted(): lax.ppermute(value, axis, [(s, s + steps) for s in range(count) if 0 <= s...]
    all_to_all x6, waiting for transfers between devices: 3.9 us -> 17.6 us  [exchange(): return lax.all_to_all(blocks, axis, 0, 0, tiled=True)]
    unnamed x226 -> x240, local copies, waits for them, and re-layouts: 37.8 us -> 38.8 us
  transfers between devices with their start and end apart: 113 -> 113, of which waited for: 57 -> 54; matrix products, arithmetic and copies ran while one was open for 13% -> 13% of each run, Pallas kernels for 6% -> 6%
where the time goes in v7:
time: 726 us; the launch traced here: 718 us
  waiting for transfers between devices  330 us (45%)
  starting transfers between devices  173 us (24%)
  local copies, waits for them, and re-layouts  55.8 us (8%)
  other arithmetic  54.7 us (8%)
  matrix products  53.3 us (7%)
  Pallas kernels  48.1 us (7%)
    ppermute x65, waiting for transfers between devices, swapped(): lax.ppermute(value, axis, [(place, place ^ bit) for place in range(count)])  156 us
    ppermute x36, waiting for transfers between devices, rotated(): return lax.ppermute(value, 'dp', [(s, (s + steps) % n) for s in range(n)])  140 us
    ppermute x36, starting transfers between devices, rotated(): return lax.ppermute(value, 'dp', [(s, (s + steps) % n) for s in range(n)])  62.5 us
    ppermute x65, starting transfers between devices, swapped(): lax.ppermute(value, axis, [(place, place ^ bit) for place in range(count)])  53.7 us
    all_to_all x6, starting transfers between devices, exchange(): return lax.all_to_all(blocks, axis, 0, 0, tiled=True)  47.7 us
    unnamed x240, local copies, waits for them, and re-layouts  38.8 us
    dot_general x12, matrix products, dot(): return jnp.dot(left, right, preferred_element_type=f32)  19.5 us
    all_to_all x6, waiting for transfers between devices, exchange(): return lax.all_to_all(blocks, axis, 0, 0, tiled=True)  17.6 us
  transfers between devices with their start and end apart: 113, of which 54 were waited for; matrix products, arithmetic and copies ran while one was open for 13% of the time, Pallas kernels for 6%

profile of v7, /device:TPU:0, one launch (start us, length us, event | category | flops | bytes accessed | tf_op | source)
XLA Modules:
  0.0 717.8 jit_solution(6998625204452963268)
XLA Ops:
  1.7 5.1 collective-permute-start.5
  9.5 2.8 concatenate.102
  20.8 15.8 %collective-permute-done.6 = bf16[576,256]{1,0:T(8,128)(2,1)S(1)} collective-permute-done((bf16[576,256]{1,0:T(8,128)(2,1)S(1)}, bf16[576,256]{1,0:T(8,128)(2,1)S(1)}, u32[]{:S(2)}, u32[]{:S(2)}) %collective-permute-start.6) | collective-permute-done | bytes 294944 | tf_op jit(solution)/shard_map/ppermute | solution.py:99
  43.1 2.5 collective-permute-start.12
  47.6 3.3 collective-permute-start.8
  51.5 4.1 unit_blocks.1
  60.9 6.3 collective-permute-start.18
  67.2 4.1 all-to-all-start
  75.1 15.8 %collective-permute-done.9 = bf16[592,256]{1,0:T(8,128)(2,1)S(1)} collective-permute-done((bf16[592,256]{1,0:T(8,128)(2,1)S(1)}, bf16[592,256]{1,0:T(8,128)(2,1)S(1)}, u32[]{:S(2)}, u32[]{:S(2)}) %collective-permute-start.9) | collective-permute-done | bytes 303136 | tf_op jit(solution)/shard_map/ppermute | solution.py:99
  98.1 5.0 collective-permute-start.20
  105.6 3.9 fusion.95
  110.2 3.5 fusion.93
  113.7 13.5 %collective-permute-done.19 = bf16[576,256]{1,0:T(8,128)(2,1)S(1)} collective-permute-done((bf16[576,256]{1,0:T(8,128)(2,1)S(1)}, bf16[576,256]{1,0:T(8,128)(2,1)S(1)}, u32[]{:S(2)}, u32[]{:S(2)}) %collective-permute-start.19) | collective-permute-done | bytes 294944 | tf_op jit(solution)/shard_map/ppermute | solution.py:99
  129.1 2.6 convolution_convert_fusion.refs_1_.right_ref
  134.9 25.8 %all-to-all-start.1 = ((bf16[4,288,576]{2,1,0:T(8,128)(2,1)}), bf16[4,288,576]{2,1,0:T(8,128)(2,1)}, u32[]{:S(2)}, u32[]{:S(2)}) async-start(bf16[4,288,576]{2,1,0:T(8,128)(2,1)} %copy-done.32), calls=%async_computation.1 | async-start | bytes 2949120 | tf_op jit(solution)/shard_map/all_to_all | solution.py:53
  166.2 7.1 collective-permute-done.23.refs_3_
  179.6 16.8 %all-to-all-done.1.own_ref = bf16[4,288,576]{2,1,0:T(8,128)(2,1)} async-done(((bf16[4,288,576]{2,1,0:T(8,128)(2,1)}), bf16[4,288,576]{2,1,0:T(8,128)(2,1)}, u32[]{:S(2)}, u32[]{:S(2)}) %all-to-all-start.1) | async-done | bytes 1327136 | tf_op jit(solution)/shard_map/all_to_all | solution.py:53
  196.4 5.0 all-to-all-start.2
  205.9 28.9 %collective-permute-done.27.other_ref = bf16[4,288,576]{2,1,0:T(8,128)(2,1)S(1)} collective-permute-done((bf16[4,288,576]{2,1,0:T(8,128)(2,1)}, bf16[4,288,576]{2,1,0:T(8,128)(2,1)S(1)}, u32[]{:S(2)}, u32[]{:S(2)}) %collective-permute-start.27) | collective-permute-done | bytes 1327136 | tf_op jit(solution)/shard_map/ppermute | solution.py:63
  237.6 2.6 collective-permute-start.29
  254.4 13.1 %collective-permute-done.39 = bf16[64,2304]{1,0:T(8,128)(2,1)S(1)} collective-permute-done((bf16[64,2304]{1,0:T(8,128)(2,1)S(1)}, bf16[64,2304]{1,0:T(8,128)(2,1)S(1)}, u32[]{:S(2)}, u32[]{:S(2)}) %collective-permute-start.39) | collective-permute-done | bytes 294944 | tf_op jit(solution)/shard_map/ppermute | solution.py:99
  268.0 7.0 collective-permute-done.40
  282.7 2.5 collective-permute-done.45
  287.0 2.7 multiply_convert_fusion.2
  298.3 14.1 %collective-permute-done.36 = bf16[128,2304]{1,0:T(8,128)(2,1)S(1)} collective-permute-done((bf16[128,2304]{1,0:T(8,128)(2,1)S(1)}, bf16[128,2304]{1,0:T(8,128)(2,1)S(1)}, u32[]{:S(2)}, u32[]{:S(2)}) %collective-permute-start.36) | collective-permute-done | bytes 589856 | tf_op jit(solution)/shard_map/ppermute | solution.py:63
  313.2 2.7 collective-permute-start.37
  315.8 5.0 collective-permute-done.43
  323.3 6.9 collective-permute-done.38
  330.2 10.4 %collective-permute-done.44 = bf16[64,2304]{1,0:T(8,128)(2,1)S(1)} collective-permute-done((bf16[64,2304]{1,0:T(8,128)(2,1)S(1)}, bf16[64,2304]{1,0:T(8,128)(2,1)S(1)}, u32[]{:S(2)}, u32[]{:S(2)}) %collective-permute-start.44) | collective-permute-done | bytes 294944 | tf_op jit(solution)/shard_map/ppermute | solution.py:99
  340.8 2.5 fusion.44
  344.8 3.8 collective-permute-start.48
  348.6 3.4 collective-permute-done.50
  352.2 4.4 collective-permute-done.47
  358.9 2.6 collective-permute-start.57
  363.1 10.1 %collective-permute-done.57 = bf16[64,2304]{1,0:T(8,128)(2,1)S(1)} collective-permute-done((bf16[64,2304]{1,0:T(8,128)(2,1)S(1)}, bf16[64,2304]{1,0:T(8,128)(2,1)S(1)}, u32[]{:S(2)}, u32[]{:S(2)}) %collective-permute-start.57) | collective-permute-done | bytes 294944 | tf_op jit(solution)/shard_map/ppermute | solution.py:99
  378.8 3.1 collective-permute-done.58
  397.7 3.9 fusion.21
  403.6 13.8 %collective-permute-done.54 = bf16[128,2304]{1,0:T(8,128)(2,1)S(1)} collective-permute-done((bf16[128,2304]{1,0:T(8,128)(2,1)S(1)}, bf16[128,2304]{1,0:T(8,128)(2,1)S(1)}, u32[]{:S(2)}, u32[]{:S(2)}) %collective-permute-start.54) | collective-permute-done | bytes 589856 | tf_op jit(solution)/shard_map/ppermute | solution.py:63
  420.0 5.9 collective-permute-done.61
  429.9 3.5 collective-permute-done.64
  434.2 3.9 fusion.27
  439.8 12.9 %collective-permute-done.65 = bf16[4,288,576]{2,1,0:T(8,128)(2,1)S(1)} collective-permute-done((bf16[4,288,576]{2,1,0:T(8,128)(2,1)S(1)}, bf16[4,288,576]{2,1,0:T(8,128)(2,1)S(1)}, u32[]{:S(2)}, u32[]{:S(2)}) %collective-permute-start.65) | collective-permute-done | bytes 1327136 | tf_op jit(solution)/shard_map/ppermute | solution.py:63
  456.4 3.7 all-to-all-start.3
  476.1 8.7 %fusion.33 = f32[2304,576]{1,0:T(8,128)} fusion(bf16[1024,2304]{1,0:T(8,128)(2,1)} %copy-done.89, bf16[256,576]{0,1:T(8,128)(2,1)S(1)} %copy-done.78, bf16[512,576]{0,1:T(8,128)(2,1)S(1)} %copy-done.103, bf16[256,576]{0,1:T(8,128)(2,1)S(1)} %copy-done.76), kind=kOutput, calls=%fused_computation.88 | convolution fusion | flops 2721447936 | bytes 11206656 | tf_op jit(solution)/shard_map/dot_general | solution.py:94
  484.8 8.2 %collective-permute-done.66 = bf16[4,288,576]{2,1,0:T(8,128)(2,1)} collective-permute-done((bf16[4,288,576]{2,1,0:T(8,128)(2,1)}, bf16[4,288,576]{2,1,0:T(8,128)(2,1)}, u32[]{:S(2)}, u32[]{:S(2)}) %collective-permute-start.66) | collective-permute-done | bytes 1327136 | tf_op jit(solution)/shard_map/ppermute | solution.py:63
  497.4 4.7 fusion.9
  502.1 4.2 all-to-all-start.4
  511.0 4.1 fusion.13
  524.3 12.8 %attend_back.1 = (bf16[512,256]{1,0:T(8,128)(2,1)S(1)}, f32[2048,256]{1,0:T(8,128)}, bf16[2048,256]{1,0:T(8,128)(2,1)S(1)}) custom-call(s32[1]{0:T(128)} %bitcast.19.side_ref, bf16[512,2304]{1,0:T(8,128)(2,1)} %bitcast.260, bf16[2304,256]{1,0:T(8,128)(2,1)S(1)} %bitcast.263, bf16[2048,256]{1,0:T(8,128)(2,1)S(1)} %copy-done.19, ...), custom_call_target="tpu_custom_call" | custom-call | tf_op jit(solution)/shard_map/attend_back/pallas_call | solution.py:412
  538.8 8.4 %collective-permute-done.74 = bf16[4,288,576]{2,1,0:T(8,128)(2,1)} collective-permute-done((bf16[4,288,576]{2,1,0:T(8,128)(2,1)}, bf16[4,288,576]{2,1,0:T(8,128)(2,1)}, u32[]{:S(2)}, u32[]{:S(2)}) %collective-permute-start.74) | collective-permute-done | bytes 1327136 | tf_op jit(solution)/shard_map/ppermute | solution.py:63
  547.1 3.1 fusion.8
  551.3 4.8 all-to-all-start.5
  579.0 4.7 collective-permute-done.76.refs_1_
  589.4 2.5 collective-permute-done.82
  597.0 21.8 %collective-permute-done.83 = bf16[576,256]{1,0:T(8,128)(2,1)} collective-permute-done((bf16[576,256]{1,0:T(8,128)(2,1)}, bf16[576,256]{1,0:T(8,128)(2,1)}, u32[]{:S(2)}, u32[]{:S(2)}) %collective-permute-start.83) | collective-permute-done | bytes 294944 | tf_op jit(solution)/shard_map/ppermute | solution.py:99
  621.0 14.3 %collective-permute-done.79.refs_5_ = bf16[512,256]{1,0:T(8,128)(2,1)} collective-permute-done((bf16[512,256]{1,0:T(8,128)(2,1)}, bf16[512,256]{1,0:T(8,128)(2,1)}, u32[]{:S(2)}, u32[]{:S(2)}) %collective-permute-start.79) | collective-permute-done | bytes 262176 | tf_op jit(solution)/shard_map/ppermute | solution.py:76
  646.8 3.2 side_by_side.4
  655.9 6.9 collective-permute-done.86.refs_3_
  665.7 2.7 collective-permute-done.88.refs_4_
  675.4 15.5 %collective-permute-done.99 = bf16[576,256]{1,0:T(8,128)(2,1)S(1)} collective-permute-done((bf16[576,256]{1,0:T(8,128)(2,1)S(1)}, bf16[576,256]{1,0:T(8,128)(2,1)S(1)}, u32[]{:S(2)}, u32[]{:S(2)}) %collective-permute-start.99) | collective-permute-done | bytes 294944 | tf_op jit(solution)/shard_map/ppermute | solution.py:99
  691.9 2.9 collective-permute-done.95
  699.7 3.1 collective-permute-done.103
  702.8 2.7 collective-permute-start.104
  705.5 3.1 collective-permute-start.105
  (605 shorter events, 256.4 us)
Async XLA Ops:
  1.7 19.2 %collective-permute-start.5 = (bf16[576,256]{1,0:T(8,128)(2,1)S(1)}, bf16[576,256]{1,0:T(8,128)(2,1)S(1)}, u32[]{:S(2)}, u32[]{:S(2)}) collective-permute-start(bf16[576,256]{1,0:T(8,128)(2,1)S(1)} %broadcast_select_fusion.14), channel_id=1, source_target_pairs={{0,24},{8,0},{16,8},{24,16},{1,25},{9,1},{17,9},{25,17},{2,26},{10... | collective-permute-start | bytes 884744 | tf_op jit(solution)/shard_map/ppermute | solution.py:99
  8.9 27.9 %collective-permute-start.4 = (bf16[256,2304]{1,0:T(8,128)(2,1)}, bf16[256,2304]{1,0:T(8,128)(2,1)S(1)}, u32[]{:S(2)}, u32[]{:S(2)}) collective-permute-start(bf16[256,2304]{1,0:T(8,128)(2,1)} %param.14), channel_id=1, source_target_pairs={{0,4},{4,0},{1,5},{5,1},{2,6},{6,2},{3,7},{7,3},{8,12},{12,8},{9,1... | collective-permute-start | bytes 3538952 | tf_op jit(solution)/shard_map/ppermute | solution.py:63
  16.0 20.6 %collective-permute-start.6 = (bf16[576,256]{1,0:T(8,128)(2,1)S(1)}, bf16[576,256]{1,0:T(8,128)(2,1)S(1)}, u32[]{:S(2)}, u32[]{:S(2)}) collective-permute-start(bf16[576,256]{1,0:T(8,128)(2,1)S(1)} %broadcast_select_fusion.14), channel_id=1, source_target_pairs={{0,16},{8,24},{16,0},{24,8},{1,17},{9,25},{17,1},{25,9},{2,18},{10... | collective-permute-start | bytes 884744 | tf_op jit(solution)/shard_map/ppermute | solution.py:99
  17.4 19.2 %collective-permute-start.7 = (bf16[576,256]{1,0:T(8,128)(2,1)S(1)}, bf16[576,256]{1,0:T(8,128)(2,1)S(1)}, u32[]{:S(2)}, u32[]{:S(2)}) collective-permute-start(bf16[576,256]{1,0:T(8,128)(2,1)S(1)} %broadcast_select_fusion.14), channel_id=1, source_target_pairs={{0,8},{8,16},{16,24},{24,0},{1,9},{9,17},{17,25},{25,1},{2,10},{10... | collective-permute-start | bytes 884744 | tf_op jit(solution)/shard_map/ppermute | solution.py:99
  43.1 15.2 %collective-permute-start.12 = (bf16[512,256]{1,0:T(8,128)(2,1)S(1)}, bf16[512,256]{1,0:T(8,128)(2,1)S(1)}, u32[]{:S(2)}, u32[]{:S(2)}) collective-permute-start(bf16[512,256]{1,0:T(8,128)(2,1)S(1)} %fusion.65), channel_id=1, source_target_pairs={{0,16},{8,24},{1,17},{9,25},{2,18},{10,26},{3,19},{11,27},{4,20},{... | collective-permute-start | bytes 786440 | tf_op jit(solution)/shard_map/ppermute | solution.py:76
  45.7 15.3 %collective-permute-start.13 = (bf16[512,256]{1,0:T(8,128)(2,1)S(1)}, bf16[512,256]{1,0:T(8,128)(2,1)S(1)}, u32[]{:S(2)}, u32[]{:S(2)}) collective-permute-start(bf16[512,256]{1,0:T(8,128)(2,1)S(1)} %fusion.65), channel_id=1, source_target_pairs={{0,8},{8,16},{16,24},{1,9},{9,17},{17,25},{2,10},{10,18},{18,26},{... | collective-permute-start | bytes 786440 | tf_op jit(solution)/shard_map/ppermute | solution.py:76
  47.0 24.4 %collective-permute-start.10 = (bf16[592,256]{1,0:T(8,128)(2,1)S(1)}, bf16[592,256]{1,0:T(8,128)(2,1)S(1)}, u32[]{:S(2)}, u32[]{:S(2)}) collective-permute-start(bf16[592,256]{1,0:T(8,128)(2,1)S(1)} %pad_maximum_fusion.23), channel_id=1, source_target_pairs={{0,8},{8,16},{16,24},{24,0},{1,9},{9,17},{17,25},{25,1},{2,10},{10... | collective-permute-start | bytes 909320 | tf_op jit(solution)/shard_map/ppermute | solution.py:99
  47.6 26.4 %collective-permute-start.8 = (bf16[592,256]{1,0:T(8,128)(2,1)S(1)}, bf16[592,256]{1,0:T(8,128)(2,1)S(1)}, u32[]{:S(2)}, u32[]{:S(2)}) collective-permute-start(bf16[592,256]{1,0:T(8,128)(2,1)S(1)} %pad_maximum_fusion.23), channel_id=1, source_target_pairs={{0,24},{8,0},{16,8},{24,16},{1,25},{9,1},{17,9},{25,17},{2,26},{10... | collective-permute-start | bytes 909320 | tf_op jit(solution)/shard_map/ppermute | solution.py:99
  50.8 40.0 %collective-permute-start.9 = (bf16[592,256]{1,0:T(8,128)(2,1)S(1)}, bf16[592,256]{1,0:T(8,128)(2,1)S(1)}, u32[]{:S(2)}, u32[]{:S(2)}) collective-permute-start(bf16[592,256]{1,0:T(8,128)(2,1)S(1)} %pad_maximum_fusion.23), channel_id=1, source_target_pairs={{0,16},{8,24},{16,0},{24,8},{1,17},{9,25},{17,1},{25,9},{2,18},{10... | collective-permute-start | bytes 909320 | tf_op jit(solution)/shard_map/ppermute | solution.py:99
  58.4 44.8 %collective-permute-start.17 = (bf16[512,256]{1,0:T(8,128)(2,1)S(1)}, bf16[512,256]{1,0:T(8,128)(2,1)}, u32[]{:S(2)}, u32[]{:S(2)}) collective-permute-start(bf16[512,256]{1,0:T(8,128)(2,1)S(1)} %fusion.65), channel_id=1, source_target_pairs={{0,4},{4,0},{1,5},{5,1},{2,6},{6,2},{3,7},{7,3},{8,12},{12,8},{9,1... | collective-permute-start | bytes 786440 | tf_op jit(solution)/shard_map/ppermute | solution.py:63
  60.9 52.8 %collective-permute-start.18 = (bf16[576,256]{1,0:T(8,128)(2,1)S(1)}, bf16[576,256]{1,0:T(8,128)(2,1)S(1)}, u32[]{:S(2)}, u32[]{:S(2)}) collective-permute-start(bf16[576,256]{1,0:T(8,128)(2,1)S(1)} %get-tuple-element.127), channel_id=1, source_target_pairs={{0,8},{8,16},{16,24},{24,0},{1,9},{9,17},{17,25},{25,1},{2,10},{10... | collective-permute-start | bytes 884744 | tf_op jit(solution)/shard_map/ppermute | solution.py:99
  67.2 60.3 %all-to-all-start = ((bf16[4,288,576]{2,1,0:T(8,128)(2,1)}), bf16[4,288,576]{2,1,0:T(8,128)(2,1)S(1)}, u32[]{:S(2)}, u32[]{:S(2)}) async-start(bf16[4,288,576]{2,1,0:T(8,128)(2,1)} %get-tuple-element.126), calls=%async_computation | async-start | bytes 2949120 | tf_op jit(solution)/shard_map/all_to_all | solution.py:53
  71.4 26.2 %collective-permute-start.14 = (bf16[512,256]{1,0:T(8,128)(2,1)}, bf16[512,256]{1,0:T(8,128)(2,1)S(1)}, u32[]{:S(2)}, u32[]{:S(2)}) collective-permute-start(bf16[512,256]{1,0:T(8,128)(2,1)} %copy-done.80), channel_id=1, source_target_pairs={{0,4},{4,0},{1,5},{5,1},{2,6},{6,2},{3,7},{7,3},{8,12},{12,8},{9,1... | collective-permute-start | bytes 786440 | tf_op jit(solution)/shard_map/ppermute | solution.py:63
  74.0 24.1 %collective-permute-start.15 = (bf16[512,256]{1,0:T(8,128)(2,1)}, bf16[512,256]{1,0:T(8,128)(2,1)S(1)}, u32[]{:S(2)}, u32[]{:S(2)}) collective-permute-start(bf16[512,256]{1,0:T(8,128)(2,1)} %copy-done.82), channel_id=1, source_target_pairs={{0,4},{4,0},{1,5},{5,1},{2,6},{6,2},{3,7},{7,3},{8,12},{12,8},{9,1... | collective-permute-start | bytes 786440 | tf_op jit(solution)/shard_map/ppermute | solution.py:63
  97.5 29.7 %collective-permute-start.19 = (bf16[576,256]{1,0:T(8,128)(2,1)S(1)}, bf16[576,256]{1,0:T(8,128)(2,1)S(1)}, u32[]{:S(2)}, u32[]{:S(2)}) collective-permute-start(bf16[576,256]{1,0:T(8,128)(2,1)S(1)} %get-tuple-element.127), channel_id=1, source_target_pairs={{0,16},{8,24},{16,0},{24,8},{1,17},{9,25},{17,1},{25,9},{2,18},{10... | collective-permute-start | bytes 884744 | tf_op jit(solution)/shard_map/ppermute | solution.py:99
  98.1 29.1 %collective-permute-start.20 = (bf16[576,256]{1,0:T(8,128)(2,1)S(1)}, bf16[576,256]{1,0:T(8,128)(2,1)S(1)}, u32[]{:S(2)}, u32[]{:S(2)}) collective-permute-start(bf16[576,256]{1,0:T(8,128)(2,1)S(1)} %get-tuple-element.127), channel_id=1, source_target_pairs={{0,24},{8,0},{16,8},{24,16},{1,25},{9,1},{17,9},{25,17},{2,26},{10... | collective-permute-start | bytes 884744 | tf_op jit(solution)/shard_map/ppermute | solution.py:99
  127.5 36.5 %collective-permute-start.22 = (bf16[4,288,576]{2,1,0:T(8,128)(2,1)S(1)}, bf16[4,288,576]{2,1,0:T(8,128)(2,1)}, u32[]{:S(2)}, u32[]{:S(2)}) collective-permute-start(bf16[4,288,576]{2,1,0:T(8,128)(2,1)S(1)} %all-to-all-done.own_ref), channel_id=1, source_target_pairs={{0,4},{4,0},{1,5},{5,1},{2,6},{6,2},{3,7},{7,3},{8,12},{12,8},{9,1... | collective-permute-start | bytes 3981320 | tf_op jit(solution)/shard_map/ppermute | solution.py:63
  134.9 25.8 %collective-permute-start.21 = (bf16[2,2,64,2304]{3,2,1,0:T(8,128)(2,1)}, bf16[2,2,64,2304]{3,2,1,0:T(8,128)(2,1)}, u32[]{:S(2)}, u32[]{:S(2)}) collective-permute-start(bf16[2,2,64,2304]{3,2,1,0:T(8,128)(2,1)} %get-tuple-element.130), channel_id=1, source_target_pairs={{0,1},{1,0},{2,3},{3,2},{4,5},{5,4},{6,7},{7,6},{8,9},{9,8},{10,11... | collective-permute-start | bytes 3538952 | tf_op jit(solution)/shard_map/ppermute | solution.py:63
  134.9 61.5 %all-to-all-start.1 = ((bf16[4,288,576]{2,1,0:T(8,128)(2,1)}), bf16[4,288,576]{2,1,0:T(8,128)(2,1)}, u32[]{:S(2)}, u32[]{:S(2)}) async-start(bf16[4,288,576]{2,1,0:T(8,128)(2,1)} %copy-done.32), calls=%async_computation.1 | async-start | bytes 2949120 | tf_op jit(solution)/shard_map/all_to_all | solution.py:53
  176.0 25.4 %collective-permute-start.26 = (bf16[64,1152]{1,0:T(8,128)(2,1)S(1)}, bf16[64,1152]{1,0:T(8,128)(2,1)}, u32[]{:S(2)}, u32[]{:S(2)}) collective-permute-start(bf16[64,1152]{1,0:T(8,128)(2,1)S(1)} %get-tuple-element.140), channel_id=1, source_target_pairs={{0,4},{4,0},{1,5},{5,1},{2,6},{6,2},{3,7},{7,3},{8,12},{12,8},{9,1... | collective-permute-start | bytes 442376 | tf_op jit(solution)/shard_map/ppermute | solution.py:63
  196.4 39.6 %all-to-all-start.2 = ((bf16[4,288,576]{2,1,0:T(8,128)(2,1)}), bf16[4,288,576]{2,1,0:T(8,128)(2,1)S(1)}, u32[]{:S(2)}, u32[]{:S(2)}) async-start(bf16[4,288,576]{2,1,0:T(8,128)(2,1)} %copy-done.31), calls=%async_computation.2 | async-start | bytes 2949120 | tf_op jit(solution)/shard_map/all_to_all | solution.py:53
  202.4 32.5 %collective-permute-start.27 = (bf16[4,288,576]{2,1,0:T(8,128)(2,1)}, bf16[4,288,576]{2,1,0:T(8,128)(2,1)S(1)}, u32[]{:S(2)}, u32[]{:S(2)}) collective-permute-start(bf16[4,288,576]{2,1,0:T(8,128)(2,1)} %all-to-all-done.1.own_ref), channel_id=1, source_target_pairs={{0,4},{4,0},{1,5},{5,1},{2,6},{6,2},{3,7},{7,3},{8,12},{12,8},{9,1... | collective-permute-start | bytes 3981320 | tf_op jit(solution)/shard_map/ppermute | solution.py:63
  235.9 12.6 %collective-permute-start.28 = (bf16[64,2304]{1,0:T(8,128)(2,1)}, bf16[64,2304]{1,0:T(8,128)(2,1)}, u32[]{:S(2)}, u32[]{:S(2)}) collective-permute-start(bf16[64,2304]{1,0:T(8,128)(2,1)} %get-tuple-element.150), channel_id=1, source_target_pairs={{0,8},{8,16},{16,24},{24,0},{1,9},{9,17},{17,25},{25,1},{2,10},{10... | collective-permute-start | bytes 884744 | tf_op jit(solution)/shard_map/ppermute | solution.py:99
  237.6 12.5 %collective-permute-start.29 = (bf16[64,2304]{1,0:T(8,128)(2,1)}, bf16[64,2304]{1,0:T(8,128)(2,1)}, u32[]{:S(2)}, u32[]{:S(2)}) collective-permute-start(bf16[64,2304]{1,0:T(8,128)(2,1)} %get-tuple-element.150), channel_id=1, source_target_pairs={{0,24},{8,0},{16,8},{24,16},{1,25},{9,1},{17,9},{25,17},{2,26},{10... | collective-permute-start | bytes 884744 | tf_op jit(solution)/shard_map/ppermute | solution.py:99
  248.0 31.1 %collective-permute-start.33 = (bf16[4,288,576]{2,1,0:T(8,128)(2,1)S(1)}, bf16[4,288,576]{2,1,0:T(8,128)(2,1)S(1)}, u32[]{:S(2)}, u32[]{:S(2)}) collective-permute-start(bf16[4,288,576]{2,1,0:T(8,128)(2,1)S(1)} %all-to-all-done.2.own_ref), channel_id=1, source_target_pairs={{0,4},{4,0},{1,5},{5,1},{2,6},{6,2},{3,7},{7,3},{8,12},{12,8},{9,1... | collective-permute-start | bytes 3981320 | tf_op jit(solution)/shard_map/ppermute | solution.py:63
  251.2 25.2 %collective-permute-start.30 = (bf16[128,2304]{1,0:T(8,128)(2,1)S(1)}, bf16[128,2304]{1,0:T(8,128)(2,1)S(1)}, u32[]{:S(2)}, u32[]{:S(2)}) collective-permute-start(bf16[128,2304]{1,0:T(8,128)(2,1)S(1)} %pad_maximum_fusion.16), channel_id=1, source_target_pairs={{0,2},{1,3},{2,0},{3,1},{4,6},{5,7},{6,4},{7,5},{8,10},{9,11},{10,... | collective-permute-start | bytes 1769480 | tf_op jit(solution)/shard_map/ppermute | solution.py:63
  252.8 14.7 %collective-permute-start.39 = (bf16[64,2304]{1,0:T(8,128)(2,1)S(1)}, bf16[64,2304]{1,0:T(8,128)(2,1)S(1)}, u32[]{:S(2)}, u32[]{:S(2)}) collective-permute-start(bf16[64,2304]{1,0:T(8,128)(2,1)S(1)} %copy-done.70), channel_id=1, source_target_pairs={{0,16},{8,24},{16,0},{24,8},{1,17},{9,25},{17,1},{25,9},{2,18},{10... | collective-permute-start | bytes 884744 | tf_op jit(solution)/shard_map/ppermute | solution.py:99
  254.3 20.7 %collective-permute-start.32 = (bf16[128,2304]{1,0:T(8,128)(2,1)S(1)}, bf16[128,2304]{1,0:T(8,128)(2,1)S(1)}, u32[]{:S(2)}, u32[]{:S(2)}) collective-permute-start(bf16[128,2304]{1,0:T(8,128)(2,1)S(1)} %pad_maximum_fusion.17), channel_id=1, source_target_pairs={{0,1},{1,0},{2,3},{3,2},{4,5},{5,4},{6,7},{7,6},{8,9},{9,8},{10,11... | collective-permute-start | bytes 1769480 | tf_op jit(solution)/shard_map/ppermute | solution.py:63
  296.9 15.4 %collective-permute-start.36 = (bf16[128,2304]{1,0:T(8,128)(2,1)S(1)}, bf16[128,2304]{1,0:T(8,128)(2,1)S(1)}, u32[]{:S(2)}, u32[]{:S(2)}) collective-permute-start(bf16[128,2304]{1,0:T(8,128)(2,1)S(1)} %slice.501), channel_id=1, source_target_pairs={{0,2},{1,3},{2,0},{3,1},{4,6},{5,7},{6,4},{7,5},{8,10},{9,11},{10,... | collective-permute-start | bytes 1769480 | tf_op jit(solution)/shard_map/ppermute | solution.py:63
  315.8 14.3 %collective-permute-start.38 = (bf16[64,2304]{1,0:T(8,128)(2,1)S(1)}, bf16[64,2304]{1,0:T(8,128)(2,1)S(1)}, u32[]{:S(2)}, u32[]{:S(2)}) collective-permute-start(bf16[64,2304]{1,0:T(8,128)(2,1)S(1)} %get-tuple-element.304), channel_id=1, source_target_pairs={{0,8},{8,16},{16,24},{24,0},{1,9},{9,17},{17,25},{25,1},{2,10},{10... | collective-permute-start | bytes 884744 | tf_op jit(solution)/shard_map/ppermute | solution.py:99
  320.9 19.6 %collective-permute-start.44 = (bf16[64,2304]{1,0:T(8,128)(2,1)S(1)}, bf16[64,2304]{1,0:T(8,128)(2,1)S(1)}, u32[]{:S(2)}, u32[]{:S(2)}) collective-permute-start(bf16[64,2304]{1,0:T(8,128)(2,1)S(1)} %convert_add_fusion.5), channel_id=1, source_target_pairs={{0,16},{8,24},{16,0},{24,8},{1,17},{9,25},{17,1},{25,9},{2,18},{10... | collective-permute-start | bytes 884744 | tf_op jit(solution)/shard_map/ppermute | solution.py:99
  344.8 14.1 %collective-permute-start.48 = (bf16[64,2304]{1,0:T(8,128)(2,1)S(1)}, bf16[64,2304]{1,0:T(8,128)(2,1)S(1)}, u32[]{:S(2)}, u32[]{:S(2)}) collective-permute-start(bf16[64,2304]{1,0:T(8,128)(2,1)S(1)} %fusion.43), channel_id=1, source_target_pairs={{0,24},{8,0},{16,8},{24,16},{1,25},{9,1},{17,9},{25,17},{2,26},{10... | collective-permute-start | bytes 884744 | tf_op jit(solution)/shard_map/ppermute | solution.py:99
  352.1 22.5 %collective-permute-start.51 = (bf16[128,2304]{1,0:T(8,128)(2,1)S(1)}, bf16[128,2304]{1,0:T(8,128)(2,1)S(1)}, u32[]{:S(2)}, u32[]{:S(2)}) collective-permute-start(bf16[128,2304]{1,0:T(8,128)(2,1)S(1)} %pad_maximum_fusion.20), channel_id=1, source_target_pairs={{0,1},{1,0},{2,3},{3,2},{4,5},{5,4},{6,7},{7,6},{8,9},{9,8},{10,11... | collective-permute-start | bytes 1769480 | tf_op jit(solution)/shard_map/ppermute | solution.py:63
  358.9 14.2 %collective-permute-start.57 = (bf16[64,2304]{1,0:T(8,128)(2,1)S(1)}, bf16[64,2304]{1,0:T(8,128)(2,1)S(1)}, u32[]{:S(2)}, u32[]{:S(2)}) collective-permute-start(bf16[64,2304]{1,0:T(8,128)(2,1)S(1)} %fusion.43), channel_id=1, source_target_pairs={{0,16},{8,24},{16,0},{24,8},{1,17},{9,25},{17,1},{25,9},{2,18},{10... | collective-permute-start | bytes 884744 | tf_op jit(solution)/shard_map/ppermute | solution.py:99
  361.6 20.5 %collective-permute-start.49 = (bf16[128,2304]{1,0:T(8,128)(2,1)S(1)}, bf16[128,2304]{1,0:T(8,128)(2,1)S(1)}, u32[]{:S(2)}, u32[]{:S(2)}) collective-permute-start(bf16[128,2304]{1,0:T(8,128)(2,1)S(1)} %pad_maximum_fusion.19), channel_id=1, source_target_pairs={{0,2},{1,3},{2,0},{3,1},{4,6},{5,7},{6,4},{7,5},{8,10},{9,11},{10,... | collective-permute-start | bytes 1769480 | tf_op jit(solution)/shard_map/ppermute | solution.py:63
  402.0 15.4 %collective-permute-start.54 = (bf16[128,2304]{1,0:T(8,128)(2,1)S(1)}, bf16[128,2304]{1,0:T(8,128)(2,1)S(1)}, u32[]{:S(2)}, u32[]{:S(2)}) collective-permute-start(bf16[128,2304]{1,0:T(8,128)(2,1)S(1)} %slice.498), channel_id=1, source_target_pairs={{0,2},{1,3},{2,0},{3,1},{4,6},{5,7},{6,4},{7,5},{8,10},{9,11},{10,... | collective-permute-start | bytes 1769480 | tf_op jit(solution)/shard_map/ppermute | solution.py:63
  419.4 33.3 %collective-permute-start.65 = (bf16[4,288,576]{2,1,0:T(8,128)(2,1)S(1)}, bf16[4,288,576]{2,1,0:T(8,128)(2,1)S(1)}, u32[]{:S(2)}, u32[]{:S(2)}) collective-permute-start(bf16[4,288,576]{2,1,0:T(8,128)(2,1)S(1)} %fusion.11), channel_id=1, source_target_pairs={{0,4},{4,0},{1,5},{5,1},{2,6},{6,2},{3,7},{7,3},{8,12},{12,8},{9,1... | collective-permute-start | bytes 3981320 | tf_op jit(solution)/shard_map/ppermute | solution.py:63
  427.5 25.2 %collective-permute-start.55 = (bf16[64,2304]{1,0:T(8,128)(2,1)S(1)}, bf16[64,2304]{1,0:T(8,128)(2,1)S(1)}, u32[]{:S(2)}, u32[]{:S(2)}) collective-permute-start(bf16[64,2304]{1,0:T(8,128)(2,1)S(1)} %get-tuple-element.302), channel_id=1, source_target_pairs={{0,24},{8,0},{16,8},{24,16},{1,25},{9,1},{17,9},{25,17},{2,26},{10... | collective-permute-start | bytes 884744 | tf_op jit(solution)/shard_map/ppermute | solution.py:99
  429.1 24.3 %collective-permute-start.56 = (bf16[64,2304]{1,0:T(8,128)(2,1)S(1)}, bf16[64,2304]{1,0:T(8,128)(2,1)S(1)}, u32[]{:S(2)}, u32[]{:S(2)}) collective-permute-start(bf16[64,2304]{1,0:T(8,128)(2,1)S(1)} %get-tuple-element.301), channel_id=1, source_target_pairs={{0,8},{8,16},{16,24},{24,0},{1,9},{9,17},{17,25},{25,1},{2,10},{10... | collective-permute-start | bytes 884744 | tf_op jit(solution)/shard_map/ppermute | solution.py:99
  429.7 24.4 %collective-permute-start.62 = (bf16[64,2304]{1,0:T(8,128)(2,1)S(1)}, bf16[64,2304]{1,0:T(8,128)(2,1)S(1)}, u32[]{:S(2)}, u32[]{:S(2)}) collective-permute-start(bf16[64,2304]{1,0:T(8,128)(2,1)S(1)} %convert_add_fusion.4), channel_id=1, source_target_pairs={{0,16},{8,24},{16,0},{24,8},{1,17},{9,25},{17,1},{25,9},{2,18},{10... | collective-permute-start | bytes 884744 | tf_op jit(solution)/shard_map/ppermute | solution.py:99
  456.4 37.5 %all-to-all-start.3 = ((bf16[4,288,576]{2,1,0:T(8,128)(2,1)}), bf16[4,288,576]{2,1,0:T(8,128)(2,1)S(1)}, u32[]{:S(2)}, u32[]{:S(2)}) async-start(bf16[4,288,576]{2,1,0:T(8,128)(2,1)} %fusion.10), calls=%async_computation.3 | async-start | bytes 2949120 | tf_op jit(solution)/shard_map/all_to_all | solution.py:53
  460.1 33.0 %collective-permute-start.66 = (bf16[4,288,576]{2,1,0:T(8,128)(2,1)}, bf16[4,288,576]{2,1,0:T(8,128)(2,1)}, u32[]{:S(2)}, u32[]{:S(2)}) collective-permute-start(bf16[4,288,576]{2,1,0:T(8,128)(2,1)} %fusion.12), channel_id=1, source_target_pairs={{0,4},{4,0},{1,5},{5,1},{2,6},{6,2},{3,7},{7,3},{8,12},{12,8},{9,1... | collective-permute-start | bytes 3981320 | tf_op jit(solution)/shard_map/ppermute | solution.py:63
  502.1 48.2 %all-to-all-start.4 = ((bf16[4,288,576]{2,1,0:T(8,128)(2,1)}), bf16[4,288,576]{2,1,0:T(8,128)(2,1)S(1)}, u32[]{:S(2)}, u32[]{:S(2)}) async-start(bf16[4,288,576]{2,1,0:T(8,128)(2,1)} %fusion.9), calls=%async_computation.4 | async-start | bytes 2949120 | tf_op jit(solution)/shard_map/all_to_all | solution.py:53
  515.1 32.0 %collective-permute-start.74 = (bf16[4,288,576]{2,1,0:T(8,128)(2,1)}, bf16[4,288,576]{2,1,0:T(8,128)(2,1)}, u32[]{:S(2)}, u32[]{:S(2)}) collective-permute-start(bf16[4,288,576]{2,1,0:T(8,128)(2,1)} %fusion.13), channel_id=1, source_target_pairs={{0,4},{4,0},{1,5},{5,1},{2,6},{6,2},{3,7},{7,3},{8,12},{12,8},{9,1... | collective-permute-start | bytes 3981320 | tf_op jit(solution)/shard_map/ppermute | solution.py:63
  517.9 40.2 %collective-permute-start.72 = (bf16[64,2304]{1,0:T(8,128)(2,1)}, bf16[64,2304]{1,0:T(8,128)(2,1)}, u32[]{:S(2)}, u32[]{:S(2)}) collective-permute-start(bf16[64,2304]{1,0:T(8,128)(2,1)} %get-tuple-element.179.own_ref), channel_id=1, source_target_pairs={{0,2},{1,3},{2,0},{3,1},{4,6},{5,7},{6,4},{7,5},{8,10},{9,11},{10,... | collective-permute-start | bytes 884744 | tf_op jit(solution)/shard_map/ppermute | solution.py:63
  551.3 84.0 %all-to-all-start.5 = ((bf16[4,288,576]{2,1,0:T(8,128)(2,1)}), bf16[4,288,576]{2,1,0:T(8,128)(2,1)}, u32[]{:S(2)}, u32[]{:S(2)}) async-start(bf16[4,288,576]{2,1,0:T(8,128)(2,1)} %fusion.8), calls=%async_computation.5 | async-start | bytes 2949120 | tf_op jit(solution)/shard_map/all_to_all | solution.py:53
  559.3 15.2 %collective-permute-start.80 = (bf16[512,256]{1,0:T(8,128)(2,1)S(1)}, bf16[512,256]{1,0:T(8,128)(2,1)S(1)}, u32[]{:S(2)}, u32[]{:S(2)}) collective-permute-start(bf16[512,256]{1,0:T(8,128)(2,1)S(1)} %get-tuple-element.290), channel_id=1, source_target_pairs={{0,4},{4,0},{1,5},{5,1},{2,6},{6,2},{3,7},{7,3},{8,12},{12,8},{9,1... | collective-permute-start | bytes 786440 | tf_op jit(solution)/shard_map/ppermute | solution.py:63
  560.0 15.2 %collective-permute-start.78 = (bf16[512,256]{1,0:T(8,128)(2,1)S(1)}, bf16[512,256]{1,0:T(8,128)(2,1)S(1)}, u32[]{:S(2)}, u32[]{:S(2)}) collective-permute-start(bf16[512,256]{1,0:T(8,128)(2,1)S(1)} %get-tuple-element.291), channel_id=1, source_target_pairs={{0,4},{4,0},{1,5},{5,1},{2,6},{6,2},{3,7},{7,3},{8,12},{12,8},{9,1... | collective-permute-start | bytes 786440 | tf_op jit(solution)/shard_map/ppermute | solution.py:63
  568.6 23.2 %collective-permute-start.82 = (bf16[576,256]{1,0:T(8,128)(2,1)S(1)}, bf16[576,256]{1,0:T(8,128)(2,1)S(1)}, u32[]{:S(2)}, u32[]{:S(2)}) collective-permute-start(bf16[576,256]{1,0:T(8,128)(2,1)S(1)} %get-tuple-element.277), channel_id=1, source_target_pairs={{0,8},{8,16},{16,24},{24,0},{1,9},{9,17},{17,25},{25,1},{2,10},{10... | collective-permute-start | bytes 884744 | tf_op jit(solution)/shard_map/ppermute | solution.py:99
  570.7 48.2 %collective-permute-start.83 = (bf16[576,256]{1,0:T(8,128)(2,1)}, bf16[576,256]{1,0:T(8,128)(2,1)}, u32[]{:S(2)}, u32[]{:S(2)}) collective-permute-start(bf16[576,256]{1,0:T(8,128)(2,1)} %get-tuple-element.276), channel_id=1, source_target_pairs={{0,16},{8,24},{16,0},{24,8},{1,17},{9,25},{17,1},{25,9},{2,18},{10... | collective-permute-start | bytes 884744 | tf_op jit(solution)/shard_map/ppermute | solution.py:99
  573.0 45.8 %collective-permute-start.84 = (bf16[576,256]{1,0:T(8,128)(2,1)}, bf16[576,256]{1,0:T(8,128)(2,1)}, u32[]{:S(2)}, u32[]{:S(2)}) collective-permute-start(bf16[576,256]{1,0:T(8,128)(2,1)} %get-tuple-element.275), channel_id=1, source_target_pairs={{0,24},{8,0},{16,8},{24,16},{1,25},{9,1},{17,9},{25,17},{2,26},{10... | collective-permute-start | bytes 884744 | tf_op jit(solution)/shard_map/ppermute | solution.py:99
  575.2 12.2 %collective-permute-start.75 = (bf16[512,256]{1,0:T(8,128)(2,1)S(1)}, bf16[512,256]{1,0:T(8,128)(2,1)S(1)}, u32[]{:S(2)}, u32[]{:S(2)}) collective-permute-start(bf16[512,256]{1,0:T(8,128)(2,1)S(1)} %get-tuple-element.293), channel_id=1, source_target_pairs={{0,4},{4,0},{1,5},{5,1},{2,6},{6,2},{3,7},{7,3},{8,12},{12,8},{9,1... | collective-permute-start | bytes 786440 | tf_op jit(solution)/shard_map/ppermute | solution.py:63
  583.7 37.3 %collective-permute-start.81 = (bf16[512,256]{1,0:T(8,128)(2,1)}, bf16[512,256]{1,0:T(8,128)(2,1)}, u32[]{:S(2)}, u32[]{:S(2)}) collective-permute-start(bf16[512,256]{1,0:T(8,128)(2,1)} %fused_two_sided.5), channel_id=1, source_target_pairs={{8,0},{16,8},{24,16},{9,1},{17,9},{25,17},{10,2},{18,10},{26,18},{... | collective-permute-start | bytes 786440 | tf_op jit(solution)/shard_map/ppermute | solution.py:76
  588.1 47.2 %collective-permute-start.79 = (bf16[512,256]{1,0:T(8,128)(2,1)}, bf16[512,256]{1,0:T(8,128)(2,1)}, u32[]{:S(2)}, u32[]{:S(2)}) collective-permute-start(bf16[512,256]{1,0:T(8,128)(2,1)} %fused_two_sided.4), channel_id=1, source_target_pairs={{16,0},{24,8},{17,1},{25,9},{18,2},{26,10},{19,3},{27,11},{20,4},{... | collective-permute-start | bytes 786440 | tf_op jit(solution)/shard_map/ppermute | solution.py:76
  592.6 42.7 %collective-permute-start.77 = (bf16[512,256]{1,0:T(8,128)(2,1)}, bf16[512,256]{1,0:T(8,128)(2,1)}, u32[]{:S(2)}, u32[]{:S(2)}) collective-permute-start(bf16[512,256]{1,0:T(8,128)(2,1)} %fused_two_sided.3), channel_id=1, source_target_pairs={{24,0},{25,1},{26,2},{27,3},{28,4},{29,5},{30,6},{31,7}} | collective-permute-start | bytes 786440 | tf_op jit(solution)/shard_map/ppermute | solution.py:76
  650.1 14.1 %collective-permute-start.102 = (bf16[288,256]{1,0:T(8,128)(2,1)S(1)}, bf16[288,256]{1,0:T(8,128)(2,1)S(1)}, u32[]{:S(2)}, u32[]{:S(2)}) collective-permute-start(bf16[288,256]{1,0:T(8,128)(2,1)S(1)} %select_convert_fusion.3), channel_id=1, source_target_pairs={{0,4},{4,0},{1,5},{5,1},{2,6},{6,2},{3,7},{7,3},{8,12},{12,8},{9,1... | collective-permute-start | bytes 442376 | tf_op jit(solution)/shard_map/ppermute | solution.py:63
  650.9 21.5 %collective-permute-start.100 = (bf16[576,256]{1,0:T(8,128)(2,1)S(1)}, bf16[576,256]{1,0:T(8,128)(2,1)S(1)}, u32[]{:S(2)}, u32[]{:S(2)}) collective-permute-start(bf16[576,256]{1,0:T(8,128)(2,1)S(1)} %get-tuple-element.269), channel_id=1, source_target_pairs={{0,24},{8,0},{16,8},{24,16},{1,25},{9,1},{17,9},{25,17},{2,26},{10... | collective-permute-start | bytes 884744 | tf_op jit(solution)/shard_map/ppermute | solution.py:99
  651.0 23.4 %collective-permute-start.98 = (bf16[576,256]{1,0:T(8,128)(2,1)S(1)}, bf16[576,256]{1,0:T(8,128)(2,1)S(1)}, u32[]{:S(2)}, u32[]{:S(2)}) collective-permute-start(bf16[576,256]{1,0:T(8,128)(2,1)S(1)} %get-tuple-element.271), channel_id=1, source_target_pairs={{0,8},{8,16},{16,24},{24,0},{1,9},{9,17},{17,25},{25,1},{2,10},{10... | collective-permute-start | bytes 884744 | tf_op jit(solution)/shard_map/ppermute | solution.py:99
  662.8 28.1 %collective-permute-start.99 = (bf16[576,256]{1,0:T(8,128)(2,1)S(1)}, bf16[576,256]{1,0:T(8,128)(2,1)S(1)}, u32[]{:S(2)}, u32[]{:S(2)}) collective-permute-start(bf16[576,256]{1,0:T(8,128)(2,1)S(1)} %get-tuple-element.270), channel_id=1, source_target_pairs={{0,16},{8,24},{16,0},{24,8},{1,17},{9,25},{17,1},{25,9},{2,18},{10... | collective-permute-start | bytes 884744 | tf_op jit(solution)/shard_map/ppermute | solution.py:99
  668.4 29.3 %collective-permute-start.92 = (bf16[576,256]{1,0:T(8,128)(2,1)S(1)}, bf16[576,256]{1,0:T(8,128)(2,1)}, u32[]{:S(2)}, u32[]{:S(2)}) collective-permute-start(bf16[576,256]{1,0:T(8,128)(2,1)S(1)} %get-tuple-element.274), channel_id=1, source_target_pairs={{0,8},{8,16},{16,24},{24,0},{1,9},{9,17},{17,25},{25,1},{2,10},{10... | collective-permute-start | bytes 884744 | tf_op jit(solution)/shard_map/ppermute | solution.py:99
  670.0 28.4 %collective-permute-start.93 = (bf16[576,256]{1,0:T(8,128)(2,1)S(1)}, bf16[576,256]{1,0:T(8,128)(2,1)}, u32[]{:S(2)}, u32[]{:S(2)}) collective-permute-start(bf16[576,256]{1,0:T(8,128)(2,1)S(1)} %get-tuple-element.273), channel_id=1, source_target_pairs={{0,16},{8,24},{16,0},{24,8},{1,17},{9,25},{17,1},{25,9},{2,18},{10... | collective-permute-start | bytes 884744 | tf_op jit(solution)/shard_map/ppermute | solution.py:99
  672.4 26.0 %collective-permute-start.94 = (bf16[576,256]{1,0:T(8,128)(2,1)S(1)}, bf16[576,256]{1,0:T(8,128)(2,1)}, u32[]{:S(2)}, u32[]{:S(2)}) collective-permute-start(bf16[576,256]{1,0:T(8,128)(2,1)S(1)} %get-tuple-element.272), channel_id=1, source_target_pairs={{0,24},{8,0},{16,8},{24,16},{1,25},{9,1},{17,9},{25,17},{2,26},{10... | collective-permute-start | bytes 884744 | tf_op jit(solution)/shard_map/ppermute | solution.py:99
  674.4 38.4 %collective-permute-start.90 = (bf16[64,2304]{1,0:T(8,128)(2,1)S(1)}, bf16[64,2304]{1,0:T(8,128)(2,1)S(1)}, u32[]{:S(2)}, u32[]{:S(2)}) collective-permute-start(bf16[64,2304]{1,0:T(8,128)(2,1)S(1)} %fused_first_back.1.own_ref), channel_id=1, source_target_pairs={{0,2},{1,3},{2,0},{3,1},{4,6},{5,7},{6,4},{7,5},{8,10},{9,11},{10,... | collective-permute-start | bytes 884744 | tf_op jit(solution)/shard_map/ppermute | solution.py:63
  696.1 16.8 %collective-permute-start.101 = (bf16[288,256]{1,0:T(8,128)(2,1)}, bf16[288,256]{1,0:T(8,128)(2,1)S(1)}, u32[]{:S(2)}, u32[]{:S(2)}) collective-permute-start(bf16[288,256]{1,0:T(8,128)(2,1)} %select_convert_fusion.4), channel_id=1, source_target_pairs={{0,4},{4,0},{1,5},{5,1},{2,6},{6,2},{3,7},{7,3},{8,12},{12,8},{9,1... | collective-permute-start | bytes 442376 | tf_op jit(solution)/shard_map/ppermute | solution.py:63
  (158 other events, 890.3 us)
